TPU v7x, 32 devices: a whole 2x2x4 slice. The times are simulated.
32 devices in a mesh: dp: 16 (over z, x, core), rank: 2 (over y).
Axes of the slice: x: 2, y: 2, z: 4, core: 2. Of those that a mesh axis runs over, the one named last changes fastest.
Arguments:
- block_input: bfloat16 [8192, 2048], P(('dp', 'rank')), may hold values from -6 to 6
- seq_lens: int32 [32, 3], P(('dp', 'rank')), may hold values from 1 to 170, 256 in all within a row
- attn_gain: float32 [2048], P(('dp', 'rank')), may hold values from 0.1 to 1.9
- latent_down: float32 [1024, 2048], P('rank', 'dp'), may hold values from -0.30935922 to 0.30935922
- latent_gain: float32 [1024], P('rank'), may hold values from 0.1 to 1.9
- latent_up: float32 [1024, 4096], P('rank', 'dp'), may hold values from -0.1875 to 0.1875
- shared_kv: float32 [2048, 256], P(('dp', 'rank')), may hold values from -0.125 to 0.125
- out_proj: float32 [4096, 2048], P(('dp', 'rank')), may hold values from -0.25 to 0.25
- mlp_gain: float32 [2048], P(('dp', 'rank')), may hold values from 0.1 to 1.9
- gate_weight: float32 [2048, 5632], P(('dp', 'rank')), may hold values from -0.125 to 0.125
- up_weight: float32 [2048, 5632], P(('dp', 'rank')), may hold values from -0.125 to 0.125
- down_weight: float32 [5632, 2048], P(('dp', 'rank')), may hold values from -0.078125 to 0.078125
- out_cotangent: bfloat16 [8192, 2048], P(('dp', 'rank')), may hold values from -6 to 6
Outputs:
- block_output: bfloat16 [8192, 2048], P(('dp', 'rank'))
- input_grad: bfloat16 [8192, 2048], P(('dp', 'rank'))
- attn_gain_grad: float32 [2048], P(('dp', 'rank'))
- latent_down_grad: float32 [1024, 2048], P('rank', 'dp')
- latent_gain_grad: float32 [1024], P('rank')
- latent_up_grad: float32 [1024, 4096], P('rank', 'dp')
- shared_kv_grad: float32 [2048, 256], P(('dp', 'rank'))
- out_proj_grad: float32 [4096, 2048], P(('dp', 'rank'))
- mlp_gain_grad: float32 [2048], P(('dp', 'rank'))
- gate_grad: float32 [2048, 5632], P(('dp', 'rank'))
- up_grad: float32 [2048, 5632], P(('dp', 'rank'))
- down_grad: float32 [5632, 2048], P(('dp', 'rank'))
Inputs may be any that keep to these rules, and one draw needn't show every extreme that they name: `seq_lens`: row b lists the lengths of the 3 sequences of block b in order; they sum to 256 and the longest of each row is exactly 170.
All inputs are finite; a program needn't handle non-finite values.
Results may differ from a plain program's by a relative error of at most 0.015.
The roundings to bfloat16 on the way count: a program that leaves them out, or rounds other values in their place, can miss the bound.
Values may be sent and summed in bfloat16 or wider, within the bound.
A program may use at most 384 MiB of HBM per device.

v0:
```python
import math

import jax
import jax.numpy as jnp
from jax import lax
from jax.sharding import PartitionSpec as P

LATENT = 1024
HEADS = 16
HEAD_DIM = 256


EPS = 1e-06
NEGATIVE = -1e30


def contract(left, right, left_dim, right_dim):
    return lax.dot_general(
        left, right, (((left_dim,), (right_dim,)), ((), ())), preferred_element_type=jnp.float32
    )


def layout(lengths, count):
    ends = jnp.cumsum(lengths)
    starts = ends - lengths
    places = jnp.arange(count, dtype=jnp.int32)
    segment = jnp.sum((places[:, None] >= ends[None, :]).astype(jnp.int32), axis=1)
    member = segment[:, None] == jnp.arange(lengths.shape[0], dtype=jnp.int32)[None, :]
    offset = jnp.sum(jnp.where(member, starts[None, :], 0), axis=1)
    position = (places - offset).astype(jnp.float32)
    allowed = (segment[:, None] == segment[None, :]) & (places[None, :] <= places[:, None])
    return (position, allowed)


def rope_tables(position, width):
    half = width // 2
    steps = jnp.arange(half, dtype=jnp.float32)
    freqs = jnp.exp(steps * (-math.log(10000.0) / half))
    angles = position[:, None] * freqs[None, :]
    return (jnp.cos(angles), jnp.sin(angles))


def rotate(values, cosine, sine):
    half = values.shape[-1] // 2
    first = values[..., :half]
    second = values[..., half:]
    return jnp.concatenate(
        [first * cosine - second * sine, second * cosine + first * sine], axis=-1
    )


def unrotate(grads, cosine, sine):
    half = grads.shape[-1] // 2
    first = grads[..., :half]
    second = grads[..., half:]
    return jnp.concatenate(
        [first * cosine + second * sine, second * cosine - first * sine], axis=-1
    )


def scores_of(q_rot, k_rot, allowed):
    raw = jnp.einsum("thd,sd->hts", q_rot, k_rot, preferred_element_type=jnp.float32) * q_rot.shape[
        -1
    ] ** (-0.5)
    return jnp.where(allowed[None], raw, NEGATIVE)


def per_device(
    block_input,
    seq_lens,
    attn_gain,
    latent_down,
    latent_gain,
    latent_up,
    shared_kv,
    out_proj,
    mlp_gain,
    gate_weight,
    up_weight,
    down_weight,
    out_cotangent,
):
    count = block_input.shape[0]
    block_parts = (
        shared_kv.astype(jnp.bfloat16),
        attn_gain.astype(jnp.bfloat16),
        out_proj.astype(jnp.bfloat16),
        mlp_gain.astype(jnp.bfloat16),
        gate_weight.astype(jnp.bfloat16),
        up_weight.astype(jnp.bfloat16),
        down_weight.astype(jnp.bfloat16),
    )
    query_parts = (latent_down.astype(jnp.bfloat16), latent_up.astype(jnp.bfloat16))
    kv_full, gain_one, out_full, gain_two, gate_full, up_full, down_full = (
        lax.all_gather(block_parts[0], ("dp", "rank"), axis=0, tiled=True),
        lax.all_gather(block_parts[1], ("dp", "rank"), axis=0, tiled=True),
        lax.all_gather(block_parts[2], ("dp", "rank"), axis=0, tiled=True),
        lax.all_gather(block_parts[3], ("dp", "rank"), axis=0, tiled=True),
        lax.all_gather(block_parts[4], ("dp", "rank"), axis=0, tiled=True),
        lax.all_gather(block_parts[5], ("dp", "rank"), axis=0, tiled=True),
        lax.all_gather(block_parts[6], ("dp", "rank"), axis=0, tiled=True),
    )
    down_half, up_half = (
        lax.all_gather(query_parts[0], "dp", axis=1, tiled=True),
        lax.all_gather(query_parts[1], "dp", axis=1, tiled=True),
    )
    inputs = block_input.astype(jnp.float32)
    rms_one = lax.rsqrt(jnp.mean(inputs * inputs, axis=-1, keepdims=True) + EPS)
    normed = (inputs * rms_one * gain_one.astype(jnp.float32)).astype(jnp.bfloat16)
    paired = lax.all_gather(normed, "rank", axis=0, tiled=True)
    latent = contract(paired, down_half, 1, 1)
    squares = lax.psum(jnp.sum(latent * latent, axis=-1), "rank")
    rms_lat = lax.rsqrt(squares / LATENT + EPS)[:, None]
    latent_n = (latent * rms_lat * latent_gain).astype(jnp.bfloat16)
    partial_q = jnp.dot(latent_n, up_half, preferred_element_type=jnp.float32)
    queries = lax.psum_scatter(partial_q, "rank", scatter_dimension=0, tiled=True)
    shared = jnp.dot(normed, kv_full, preferred_element_type=jnp.float32)
    position, allowed = layout(seq_lens[0], count)
    cosine, sine = rope_tables(position, HEAD_DIM)
    q_rot = rotate(queries.reshape(count, HEADS, HEAD_DIM), cosine[:, None], sine[:, None]).astype(
        jnp.bfloat16
    )
    k_rot = rotate(shared, cosine, sine).astype(jnp.bfloat16)
    values = shared.astype(jnp.bfloat16)
    scores = scores_of(q_rot, k_rot, allowed)
    peak = jnp.max(scores, axis=-1, keepdims=True)
    log_total = peak + jnp.log(jnp.sum(jnp.exp(scores - peak), axis=-1, keepdims=True))
    probs_low = jnp.exp(scores - log_total).astype(jnp.bfloat16)
    attended = jnp.einsum("hts,sd->thd", probs_low, values, preferred_element_type=jnp.float32)
    attended = attended.reshape(count, HEADS * HEAD_DIM).astype(jnp.bfloat16)
    branch = jnp.dot(attended, out_full, preferred_element_type=jnp.float32)
    middle = inputs + branch
    rms_two = lax.rsqrt(jnp.mean(middle * middle, axis=-1, keepdims=True) + EPS)
    normed_two = (middle * rms_two * gain_two.astype(jnp.float32)).astype(jnp.bfloat16)
    gate = jnp.dot(normed_two, gate_full, preferred_element_type=jnp.float32)
    upval = jnp.dot(normed_two, up_full, preferred_element_type=jnp.float32)
    sigma = jax.nn.sigmoid(gate)
    hidden = (gate * sigma * upval).astype(jnp.bfloat16)
    result = middle + jnp.dot(hidden, down_full, preferred_element_type=jnp.float32)
    block_output = result.astype(jnp.bfloat16)
    block_back, query_back, result = lax.optimization_barrier((block_parts, query_parts, result))
    kv_full, gain_one, out_full, gain_two, gate_full, up_full, down_full = (
        lax.all_gather(block_back[0], ("dp", "rank"), axis=0, tiled=True),
        lax.all_gather(block_back[1], ("dp", "rank"), axis=0, tiled=True),
        lax.all_gather(block_back[2], ("dp", "rank"), axis=0, tiled=True),
        lax.all_gather(block_back[3], ("dp", "rank"), axis=0, tiled=True),
        lax.all_gather(block_back[4], ("dp", "rank"), axis=0, tiled=True),
        lax.all_gather(block_back[5], ("dp", "rank"), axis=0, tiled=True),
        lax.all_gather(block_back[6], ("dp", "rank"), axis=0, tiled=True),
    )
    down_half, up_half = (
        lax.all_gather(query_back[0], "dp", axis=1, tiled=True),
        lax.all_gather(query_back[1], "dp", axis=1, tiled=True),
    )
    upstream = out_cotangent.astype(jnp.float32)
    d_hidden = contract(out_cotangent, down_full, 1, 1)
    down_grad = contract(hidden, out_cotangent, 0, 0)
    d_gate = (d_hidden * upval * sigma * (1.0 + gate * (1.0 - sigma))).astype(jnp.bfloat16)
    d_up = (d_hidden * gate * sigma).astype(jnp.bfloat16)
    gate_grad = contract(normed_two, d_gate, 0, 0)
    up_grad = contract(normed_two, d_up, 0, 0)
    d_normed_two = contract(d_gate, gate_full, 1, 1) + contract(d_up, up_full, 1, 1)
    gain_two_grad = jnp.sum(d_normed_two * middle * rms_two, axis=0)
    scaled_two = d_normed_two * gain_two.astype(jnp.float32)
    d_middle = (
        upstream
        + rms_two * scaled_two
        - middle
        * (rms_two * rms_two * rms_two)
        * jnp.mean(scaled_two * middle, axis=-1, keepdims=True)
    )
    mlp_gain_grad, gate_grad, up_grad, down_grad = (
        lax.psum_scatter(gain_two_grad, ("dp", "rank"), scatter_dimension=0, tiled=True),
        lax.psum_scatter(gate_grad, ("dp", "rank"), scatter_dimension=0, tiled=True),
        lax.psum_scatter(up_grad, ("dp", "rank"), scatter_dimension=0, tiled=True),
        lax.psum_scatter(down_grad, ("dp", "rank"), scatter_dimension=0, tiled=True),
    )
    d_branch = d_middle.astype(jnp.bfloat16)
    out_grad = contract(attended, d_branch, 0, 0)
    d_attended = (
        contract(d_branch, out_full, 1, 1).astype(jnp.bfloat16).reshape(count, HEADS, HEAD_DIM)
    )
    scores = scores_of(q_rot, k_rot, allowed)
    probs = jnp.exp(scores - log_total)
    d_probs = jnp.einsum("thd,sd->hts", d_attended, values, preferred_element_type=jnp.float32)
    value_grad = jnp.einsum(
        "hts,thd->sd", probs.astype(jnp.bfloat16), d_attended, preferred_element_type=jnp.float32
    )
    inner = jnp.sum(probs * d_probs, axis=-1, keepdims=True)
    d_scores = (probs * (d_probs - inner)).astype(jnp.bfloat16)
    scale = HEAD_DIM ** (-0.5)
    d_qrot = jnp.einsum("hts,sd->thd", d_scores, k_rot, preferred_element_type=jnp.float32) * scale
    d_krot = jnp.einsum("hts,thd->sd", d_scores, q_rot, preferred_element_type=jnp.float32) * scale
    d_queries = (
        unrotate(d_qrot, cosine[:, None], sine[:, None])
        .reshape(count, HEADS * HEAD_DIM)
        .astype(jnp.bfloat16)
    )
    d_shared = (unrotate(d_krot, cosine, sine) + value_grad).astype(jnp.bfloat16)
    kv_grad = contract(normed, d_shared, 0, 0)
    d_normed = contract(d_shared, kv_full, 1, 1)
    d_paired = lax.all_gather(d_queries, "rank", axis=0, tiled=True)
    up_half_grad = contract(latent_n, d_paired, 0, 0)
    d_latent_n = contract(d_paired, up_half, 1, 1)
    lgain_part = jnp.sum(d_latent_n * latent * rms_lat, axis=0)
    scaled_lat = d_latent_n * latent_gain
    inner_lat = lax.psum(jnp.sum(scaled_lat * latent, axis=-1), "rank")[:, None]
    d_latent = (
        rms_lat * scaled_lat - latent * (rms_lat * rms_lat * rms_lat) * inner_lat / LATENT
    ).astype(jnp.bfloat16)
    down_half_grad = contract(d_latent, paired, 0, 0)
    partial_in = jnp.dot(d_latent, down_half, preferred_element_type=jnp.float32)
    d_normed = d_normed + lax.psum_scatter(
        partial_in.astype(jnp.bfloat16), "rank", scatter_dimension=0, tiled=True
    ).astype(jnp.float32)
    gain_one_grad = jnp.sum(d_normed * inputs * rms_one, axis=0)
    scaled_one = d_normed * gain_one.astype(jnp.float32)
    input_grad = (
        d_middle
        + rms_one * scaled_one
        - inputs
        * (rms_one * rms_one * rms_one)
        * jnp.mean(scaled_one * inputs, axis=-1, keepdims=True)
    ).astype(jnp.bfloat16)
    shared_kv_grad, attn_gain_grad, out_proj_grad = (
        lax.psum_scatter(kv_grad, ("dp", "rank"), scatter_dimension=0, tiled=True),
        lax.psum_scatter(gain_one_grad, ("dp", "rank"), scatter_dimension=0, tiled=True),
        lax.psum_scatter(out_grad, ("dp", "rank"), scatter_dimension=0, tiled=True),
    )
    latent_down_grad, latent_up_grad = (
        lax.psum_scatter(down_half_grad, "dp", scatter_dimension=1, tiled=True),
        lax.psum_scatter(up_half_grad, "dp", scatter_dimension=1, tiled=True),
    )
    latent_gain_grad = lax.psum(lgain_part, "dp")
    return (
        block_output,
        input_grad,
        attn_gain_grad,
        latent_down_grad,
        latent_gain_grad,
        latent_up_grad,
        shared_kv_grad,
        out_proj_grad,
        mlp_gain_grad,
        gate_grad,
        up_grad,
        down_grad,
    )


def solution(mesh):
    return jax.shard_map(
        per_device,
        mesh=mesh,
        in_specs=(
            P(("dp", "rank"), None),
            P(("dp", "rank"), None),
            P(("dp", "rank")),
            P("rank", "dp"),
            P("rank"),
            P("rank", "dp"),
            P(("dp", "rank"), None),
            P(("dp", "rank"), None),
            P(("dp", "rank")),
            P(("dp", "rank"), None),
            P(("dp", "rank"), None),
            P(("dp", "rank"), None),
            P(("dp", "rank"), None),
        ),
        out_specs=(
            P(("dp", "rank"), None),
            P(("dp", "rank"), None),
            P(("dp", "rank")),
            P("rank", "dp"),
            P("rank"),
            P("rank", "dp"),
            P(("dp", "rank"), None),
            P(("dp", "rank"), None),
            P(("dp", "rank")),
            P(("dp", "rank"), None),
            P(("dp", "rank"), None),
            P(("dp", "rank"), None),
        ),
        check_vma=False,
    )
```

profile of v0, /device:TPU:10, one launch (start us, length us, event | category | flops | bytes accessed | tf_op | source)
XLA Modules:
  0.0 5658.8 jit_solution(2487369754109241219)
XLA Ops:
  9.3 41.4 all-reduce.8
  58.3 29.9 all-gather.19.cloned.1.call-done
  88.2 43.0 all-gather.21.cloned.1.call-done
  140.2 43.6 all-gather.23.cloned.1.call-done
  200.1 40.3 all-gather.17.cloned.1.call-done
  243.0 98.6 %reduce-scatter.10.cloned.1.call-done = f32[256,4096]{1,0:T(8,128)} async-done(((f32[512,4096]{1,0:T(8,128)}), f32[256,4096]{1,0:T(8,128)}) %reduce-scatter.10.cloned.1.call-update) | async-done | bytes 4194320 | tf_op jit(solution)/shard_map/reduce_scatter | solution.py:116
  351.9 107.0 %all-gather.25.cloned.1.call-done = bf16[4096,2048]{1,0:T(8,128)(2,1)} async-done(((bf16[128,2048]{1,0:T(8,128)(2,1)}), bf16[4096,2048]{1,0:T(8,128)(2,1)}) %all-gather.25.cloned.1.call-update) | async-done | bytes 16777232 | tf_op jit(solution)/shard_map/all_gather | solution.py:97
  469.4 135.0 %all-gather.27.cloned.1.call-done = bf16[2048,5632]{1,0:T(8,128)(2,1)} async-done(((bf16[64,5632]{1,0:T(8,128)(2,1)}), bf16[2048,5632]{1,0:T(8,128)(2,1)}) %all-gather.27.cloned.1.call-update) | async-done | bytes 23068688 | tf_op jit(solution)/shard_map/all_gather | solution.py:99
  617.6 133.0 %all-gather.29.cloned.1.call-done = bf16[2048,5632]{1,0:T(8,128)(2,1)} async-done(((bf16[64,5632]{1,0:T(8,128)(2,1)}), bf16[2048,5632]{1,0:T(8,128)(2,1)}) %all-gather.29.cloned.1.call-update) | async-done | bytes 23068688 | tf_op jit(solution)/shard_map/all_gather | solution.py:100
  769.0 127.7 %all-gather.31.cloned.1.call-done = bf16[5632,2048]{1,0:T(8,128)(2,1)} async-done(((bf16[176,2048]{1,0:T(8,128)(2,1)}), bf16[5632,2048]{1,0:T(8,128)(2,1)}) %all-gather.31.cloned.1.call-update) | async-done | bytes 23068688 | tf_op jit(solution)/shard_map/all_gather | solution.py:101
  915.2 42.1 all-reduce.7
  958.7 94.5 %all-gather.33.cloned.1.call-done = bf16[5632,2048]{1,0:T(8,128)(2,1)} async-done(((bf16[176,2048]{1,0:T(8,128)(2,1)}), bf16[5632,2048]{1,0:T(8,128)(2,1)}) %all-gather.33.cloned.1.call-update) | async-done | bytes 23068688 | tf_op jit(solution)/shard_map/all_gather | solution.py:149
  1080.3 119.0 %all-gather.35.cloned.1.call-done = bf16[2048,5632]{1,0:T(8,128)(2,1)} async-done(((bf16[64,5632]{1,0:T(8,128)(2,1)}), bf16[2048,5632]{1,0:T(8,128)(2,1)}) %all-gather.35.cloned.1.call-update) | async-done | bytes 23068688 | tf_op jit(solution)/shard_map/all_gather | solution.py:147
  1211.9 133.4 %all-gather.37.cloned.1.call-done = bf16[2048,5632]{1,0:T(8,128)(2,1)} async-done(((bf16[64,5632]{1,0:T(8,128)(2,1)}), bf16[2048,5632]{1,0:T(8,128)(2,1)}) %all-gather.37.cloned.1.call-update) | async-done | bytes 23068688 | tf_op jit(solution)/shard_map/all_gather | solution.py:148
  1362.7 100.3 %all-gather.39.cloned.1.call-done = bf16[4096,2048]{1,0:T(8,128)(2,1)} async-done(((bf16[128,2048]{1,0:T(8,128)(2,1)}), bf16[4096,2048]{1,0:T(8,128)(2,1)}) %all-gather.39.cloned.1.call-update) | async-done | bytes 16777232 | tf_op jit(solution)/shard_map/all_gather | solution.py:145
  1515.8 59.1 %all-gather.43.cloned.1.call-done = bf16[512,4096]{0,1:T(8,128)(2,1)} async-done(((bf16[256,4096]{0,1:T(8,128)(2,1)}), bf16[512,4096]{0,1:T(8,128)(2,1)}) %all-gather.43.cloned.1.call-update) | async-done | bytes 4194320 | tf_op jit(solution)/shard_map/all_gather | solution.py:202
  1588.9 29.0 all-gather.47.cloned.1.call-done
  1748.0 48.5 all-reduce.6
  1827.1 93.4 %reduce-scatter.14.cloned.1.call-done = f32[512,128]{1,0:T(8,128)} async-done(((f32[512,2048]{1,0:T(8,128)}), f32[512,128]{1,0:T(8,128)}) %reduce-scatter.14.cloned.1.call-update) | async-done | bytes 262160 | tf_op jit(solution)/shard_map/reduce_scatter | solution.py:231
  1920.5 109.3 %reduce-scatter.16.cloned.1.call-done = f32[512,256]{1,0:T(8,128)} async-done(((f32[512,4096]{1,0:T(8,128)}), f32[512,256]{1,0:T(8,128)}) %reduce-scatter.16.cloned.1.call-update) | async-done | bytes 524304 | tf_op jit(solution)/shard_map/reduce_scatter | solution.py:232
  2029.8 969.8 %reduce-scatter.26.cloned.1.call-done = f32[176,2048]{1,0:T(8,128)} async-done(((f32[5632,2048]{1,0:T(8,128)}), f32[176,2048]{1,0:T(8,128)}) %reduce-scatter.26.cloned.1.call-update) | async-done | bytes 1441808 | tf_op jit(solution)/shard_map/reduce_scatter | solution.py:176
  2999.6 709.8 %reduce-scatter.20.cloned.1.call-done = f32[128,2048]{1,0:T(8,128)} async-done(((f32[4096,2048]{1,0:T(8,128)}), f32[128,2048]{1,0:T(8,128)}) %reduce-scatter.20.cloned.1.call-update) | async-done | bytes 1048592 | tf_op jit(solution)/shard_map/reduce_scatter | solution.py:228
  3709.4 971.4 %reduce-scatter.22.cloned.1.call-done = f32[64,5632]{1,0:T(8,128)} async-done(((f32[2048,5632]{1,0:T(8,128)}), f32[64,5632]{1,0:T(8,128)}) %reduce-scatter.22.cloned.1.call-update) | async-done | bytes 1441808 | tf_op jit(solution)/shard_map/reduce_scatter | solution.py:174
  4680.8 971.3 %reduce-scatter.24.cloned.1.call-done = f32[64,5632]{1,0:T(8,128)} async-done(((f32[2048,5632]{1,0:T(8,128)}), f32[64,5632]{1,0:T(8,128)}) %reduce-scatter.24.cloned.1.call-update) | async-done | bytes 1441808 | tf_op jit(solution)/shard_map/reduce_scatter | solution.py:175
  (244 shorter events, 393.5 us)
Async XLA Ops:
  7.2 81.0 %all-gather.19.cloned.1.call-start = ((), (), s32[]{:S(2)}) async-start(), calls=%async_computation.10 | async-start | bytes 3145728 | tf_op jit(solution)/shard_map/all_gather | solution.py:110
  56.7 127.1 %all-gather.23.cloned.1.call-start = ((), (), s32[]{:S(2)}) async-start(), calls=%async_computation.12 | async-start | bytes 4456448 | tf_op jit(solution)/shard_map/all_gather | solution.py:105
  57.5 182.9 %all-gather.17.cloned.1.call-start = ((), (), s32[]{:S(2)}) async-start(), calls=%async_computation.9 | async-start | bytes 1081344 | tf_op jit(solution)/shard_map/all_gather | solution.py:95
  58.2 283.4 %reduce-scatter.10.cloned.1.call-start = ((), (), s32[]{:S(2)}) async-start(), calls=%async_computation.13 | async-start | bytes 12582912 | tf_op jit(solution)/shard_map/reduce_scatter | solution.py:116
  191.9 267.0 %all-gather.25.cloned.1.call-start = ((), (), s32[]{:S(2)}) async-start(), calls=%async_computation.14 | async-start | bytes 17301504 | tf_op jit(solution)/shard_map/all_gather | solution.py:97
  194.2 410.2 %all-gather.27.cloned.1.call-start = ((), (), s32[]{:S(2)}) async-start(), calls=%async_computation.15 | async-start | bytes 23789568 | tf_op jit(solution)/shard_map/all_gather | solution.py:99
  195.3 555.3 %all-gather.29.cloned.1.call-start = ((), (), s32[]{:S(2)}) async-start(), calls=%async_computation.16 | async-start | bytes 23789568 | tf_op jit(solution)/shard_map/all_gather | solution.py:100
  196.3 700.4 %all-gather.31.cloned.1.call-start = ((), (), s32[]{:S(2)}) async-start(), calls=%async_computation.17 | async-start | bytes 23789568 | tf_op jit(solution)/shard_map/all_gather | solution.py:101
  198.7 854.4 %all-gather.33.cloned.1.call-start = ((), (), s32[]{:S(2)}) async-start(), calls=%async_computation.18 | async-start | bytes 23789568 | tf_op jit(solution)/shard_map/all_gather | solution.py:149
  909.1 290.3 %all-gather.35.cloned.1.call-start = ((), (), s32[]{:S(2)}) async-start(), calls=%async_computation.19 | async-start | bytes 23789568 | tf_op jit(solution)/shard_map/all_gather | solution.py:147
  909.8 435.5 %all-gather.37.cloned.1.call-start = ((), (), s32[]{:S(2)}) async-start(), calls=%async_computation.20 | async-start | bytes 23789568 | tf_op jit(solution)/shard_map/all_gather | solution.py:148
  910.4 552.6 %all-gather.39.cloned.1.call-start = ((), (), s32[]{:S(2)}) async-start(), calls=%async_computation.21 | async-start | bytes 17301504 | tf_op jit(solution)/shard_map/all_gather | solution.py:145
  911.1 604.7 %all-gather.45.cloned.1.call-start = ((), (), s32[]{:S(2)}) async-start(), calls=%async_computation.24 | async-start | bytes 4456448 | tf_op jit(solution)/shard_map/all_gather | solution.py:153
  958.6 616.2 %all-gather.43.cloned.1.call-start = ((), (), s32[]{:S(2)}) async-start(), calls=%async_computation.23 | async-start | bytes 6291456 | tf_op jit(solution)/shard_map/all_gather | solution.py:202
  1494.2 123.7 %all-gather.47.cloned.1.call-start = ((), (), s32[]{:S(2)}) async-start(), calls=%async_computation.25 | async-start | bytes 2228224 | tf_op jit(solution)/shard_map/all_gather | solution.py:152
  1494.8 249.4 %all-gather.41.cloned.1.call-start = ((), (), s32[]{:S(2)}) async-start(), calls=%async_computation.22 | async-start | bytes 1081344 | tf_op jit(solution)/shard_map/all_gather | solution.py:143
  1495.4 248.9 %reduce-scatter.12.cloned.1.call-start = ((), (), s32[]{:S(2)}) async-start(), calls=%async_computation.26 | async-start | bytes 3145728 | tf_op jit(solution)/shard_map/reduce_scatter | solution.py:213
  1622.3 204.8 %reduce-scatter.18.cloned.1.call-start = ((), (), s32[]{:S(2)}) async-start(), calls=%async_computation.29 | async-start | bytes 2162688 | tf_op jit(solution)/shard_map/reduce_scatter | solution.py:226
  1629.5 291.0 %reduce-scatter.14.cloned.1.call-start = ((), (), s32[]{:S(2)}) async-start(), calls=%async_computation.27 | async-start | bytes 4456448 | tf_op jit(solution)/shard_map/reduce_scatter | solution.py:231
  1633.9 395.9 %reduce-scatter.16.cloned.1.call-start = ((), (), s32[]{:S(2)}) async-start(), calls=%async_computation.28 | async-start | bytes 8912896 | tf_op jit(solution)/shard_map/reduce_scatter | solution.py:232
  1641.8 1357.8 %reduce-scatter.26.cloned.1.call-start = ((), (), s32[]{:S(2)}) async-start(), calls=%async_computation.33 | async-start | bytes 47579136 | tf_op jit(solution)/shard_map/reduce_scatter | solution.py:176
  1662.7 2046.7 %reduce-scatter.20.cloned.1.call-start = ((), (), s32[]{:S(2)}) async-start(), calls=%async_computation.30 | async-start | bytes 34603008 | tf_op jit(solution)/shard_map/reduce_scatter | solution.py:228
  1679.2 3001.6 %reduce-scatter.22.cloned.1.call-start = ((), (), s32[]{:S(2)}) async-start(), calls=%async_computation.31 | async-start | bytes 47579136 | tf_op jit(solution)/shard_map/reduce_scatter | solution.py:174
  1700.8 3951.3 %reduce-scatter.24.cloned.1.call-start = ((), (), s32[]{:S(2)}) async-start(), calls=%async_computation.32 | async-start | bytes 47579136 | tf_op jit(solution)/shard_map/reduce_scatter | solution.py:175
  (54 other events, 2740.3 us)
Sparse Core Ops, SparseCore 0:
  56.1 32.1 all-gather.18
  90.4 40.7 all-gather.20
  133.9 49.8 all-gather.22
  186.6 53.7 all-gather.16
  242.6 98.9 reduce-scatter.9
  345.3 113.5 all-gather.24
  462.2 142.1 all-gather.26
  607.7 142.7 all-gather.28
  753.9 142.7 all-gather.30
  909.2 143.9 all-gather.32
  1056.5 142.7 all-gather.34
  1202.5 142.7 all-gather.36
  1349.2 113.6 all-gather.38
  1465.7 50.0 all-gather.44
  1517.2 57.5 all-gather.42
  1577.1 40.7 all-gather.46
  1621.0 52.2 all-gather.40
  1710.0 117.1 reduce-scatter.17
  1831.9 88.5 reduce-scatter.13
  1925.1 104.6 reduce-scatter.15
  2032.7 966.8 reduce-scatter.25
  3002.5 706.8 reduce-scatter.19
  3712.1 968.6 reduce-scatter.21
  4683.7 968.3 reduce-scatter.23
  (1 shorter events, 31.5 us)
where the time goes:
time: 5670 us; the launch traced here: 5660 us
  waiting for transfers between devices  5170 us (91%)
  matrix products  252 us (4%)
  blocking collectives  165 us (3%)
    reduce_scatter x1, waiting for transfers between devices, per_device(): lax.psum_scatter(gate_grad, ('dp', 'rank'), scatter_dimension=0, tiled=True)  971 us
    reduce_scatter x1, waiting for transfers between devices, per_device(): lax.psum_scatter(up_grad, ('dp', 'rank'), scatter_dimension=0, tiled=True)  971 us
    reduce_scatter x1, waiting for transfers between devices, per_device(): lax.psum_scatter(down_grad, ('dp', 'rank'), scatter_dimension=0, tiled=True)  970 us
    reduce_scatter x1, waiting for transfers between devices, per_device(): lax.psum_scatter(out_grad, ('dp', 'rank'), scatter_dimension=0, tiled=True)  710 us
    dot_general x14, matrix products, contract(): lax.dot_general(left, right, (((left_dim,), (right_dim,)), ((), ())), pre...  174 us
    all_gather x1, waiting for transfers between devices, per_device(): lax.all_gather(block_parts[4], ('dp', 'rank'), axis=0, tiled=True)  135 us
    all_gather x1, waiting for transfers between devices, per_device(): lax.all_gather(block_back[5], ('dp', 'rank'), axis=0, tiled=True)  133 us
    all_gather x1, waiting for transfers between devices, per_device(): lax.all_gather(block_parts[5], ('dp', 'rank'), axis=0, tiled=True)  133 us
  transfers between devices with their start and end apart: 25, of which 23 were waited for; matrix products, arithmetic and copies ran while one was open for 5% of the time, Pallas kernels for 0%

commit v1 on v0

v1 whole, which is shorter than its diff:
```python
import functools
import math

import jax
import jax.numpy as jnp
from jax import lax
from jax.sharding import Mesh
from jax.sharding import PartitionSpec as P

HEADS = 16
HEAD_DIM = 256
EPS = 1e-06
NEGATIVE = -1e30
F32 = jnp.float32
BF16 = jnp.bfloat16


def contract(left, right, left_dim, right_dim):
    return lax.dot_general(
        left, right, (((left_dim,), (right_dim,)), ((), ())), preferred_element_type=F32
    )


def after(value, *first):
    return lax.optimization_barrier((value, *first))[0]


def layout(lengths, count):
    spots = jnp.arange(lengths.shape[-1], dtype=jnp.int32)
    ends = jnp.sum(jnp.where(spots[None, :] <= spots[:, None], lengths[..., None, :], 0), axis=-1)
    places = jnp.arange(count, dtype=jnp.int32)
    passed = places[:, None] >= ends[..., None, :]
    segment = jnp.sum(passed.astype(jnp.int32), axis=-1)
    offset = jnp.sum(jnp.where(passed, lengths[..., None, :], 0), axis=-1)
    position = (places - offset).astype(F32)
    same = segment[..., :, None] == segment[..., None, :]
    return position, same & (places[None, :] <= places[:, None])


def rope_tables(position, width):
    half = width // 2
    steps = jnp.arange(half, dtype=F32)
    freqs = jnp.exp(steps * (-math.log(10000.0) / half))
    angles = position[..., None] * freqs
    return jnp.cos(angles), jnp.sin(angles)


def rotate(values, cosine, sine):
    half = values.shape[-1] // 2
    first, second = values[..., :half], values[..., half:]
    return jnp.concatenate(
        [first * cosine - second * sine, second * cosine + first * sine], axis=-1
    )


def unrotate(grads, cosine, sine):
    return rotate(grads, cosine, -sine)


def line_gather(block, count):
    place = lax.axis_index("f")
    full = lax.dynamic_update_index_in_dim(
        jnp.zeros((count, *block.shape), block.dtype), block, place, 0
    )
    ups, downs = [block], [block]
    for step in range(1, count):
        ups.append(
            lax.ppermute(ups[-1], "f", [(i, i + 1) for i in range(step - 1, count - 1)])
        )
        downs.append(
            lax.ppermute(downs[-1], "f", [(i, i - 1) for i in range(1, count - step + 1)])
        )
    for step in range(1, count):
        got = jnp.where(place >= step, ups[step], downs[count - step])
        full = lax.dynamic_update_index_in_dim(full, got, lax.rem(place - step + count, count), 0)
    return full


def line_scatter(parts, count):
    place = lax.axis_index("f")

    def part(at):
        return lax.dynamic_index_in_dim(parts, lax.rem(at + 2 * count, count), 0, keepdims=False)

    up = down = None
    for step in range(1, count):
        mine_up, mine_down = part(place - step), part(place + step)
        if up is not None:
            mine_up, mine_down = mine_up + up.astype(F32), mine_down + down.astype(F32)
        up = lax.ppermute(mine_up.astype(BF16), "f", [(i, i + 1) for i in range(min(step, count - 1))])
        down = lax.ppermute(
            mine_down.astype(BF16), "f", [(i, i - 1) for i in range(count - step, count)]
        )
    return part(place) + up.astype(F32) + down.astype(F32)


SWAP = [(0, 1), (1, 0)]
DIAGONAL = [(0, 3), (3, 0), (1, 2), (2, 1)]


def plane_gather(block):
    half = block.shape[0] // 2
    by_x, by_y = lax.ppermute(block, "x", SWAP), lax.ppermute(block, "y", SWAP)
    by_both = jnp.concatenate(
        [lax.ppermute(by_x[:half], "y", SWAP), lax.ppermute(by_y[half:], "x", SWAP)], axis=0
    )
    chips = [block, by_y, by_x, by_both]
    others = [lax.ppermute(a, "c", SWAP) for a in chips]
    order = [chips[0], chips[1], others[0], others[1], chips[2], chips[3], others[2], others[3]]
    return jnp.stack(order)


def plane_scatter(parts):
    low = parts.astype(BF16)
    sums = []
    for chip, (near, far) in enumerate(((0, 2), (1, 3), (4, 6), (5, 7))):
        sums.append(parts[near].astype(F32) + lax.ppermute(low[far], "c", SWAP).astype(F32))
    by_y = lax.ppermute(sums[1].astype(BF16), "y", SWAP)
    by_x = lax.ppermute(sums[2].astype(BF16), "x", SWAP)
    by_both = lax.ppermute(sums[3].astype(BF16), ("x", "y"), DIAGONAL)
    return sums[0] + by_x.astype(F32) + by_y.astype(F32) + by_both.astype(F32)


def place_in_plane():
    return 4 * lax.axis_index("x") + 2 * lax.axis_index("c") + lax.axis_index("y")


def relabel(blocks):
    place = place_in_plane()
    full = jnp.zeros_like(blocks)
    for i in range(8):
        full = lax.dynamic_update_index_in_dim(full, blocks[i], place ^ i, 0)
    return full


def by_owner(array, axis, count, f_first):
    lead, size, tail = array.shape[:axis], array.shape[axis], array.shape[axis + 1 :]
    part = size // (8 * count)
    n = len(lead)
    rest = [*range(n), n + 4, *range(n + 5, n + 5 + len(tail))]
    if f_first:
        array = array.reshape(*lead, count, 2, 2, 2, part, *tail)
        array = array.transpose(n, n + 1, n + 2, n + 3, *rest)
    else:
        array = array.reshape(*lead, 2, 2, count, 2, part, *tail)
        array = array.transpose(n + 2, n, n + 1, n + 3, *rest)
    return array.reshape(count, 8, *lead, part, *tail)


def from_owner(array, axis, f_first):
    count, _, *body = array.shape
    lead, part, tail = body[:axis], body[axis], body[axis + 1 :]
    n = axis
    array = array.reshape(count, 2, 2, 2, *body)
    inner = (0, 1, 2, 3) if f_first else (1, 2, 0, 3)
    array = array.transpose(
        *range(4, 4 + n), *inner, 4 + n, *range(5 + n, 5 + n + len(tail))
    )
    return array.reshape(*lead, 8 * count * part, *tail)


def scores_of(q_rot, k_rot, allowed):
    raw = jnp.einsum("bthd,bsd->bhts", q_rot, k_rot, preferred_element_type=F32)
    return jnp.where(allowed[:, None], raw * HEAD_DIM**-0.5, NEGATIVE)


def per_device(
    count,
    f_first,
    block_input,
    seq_lens,
    attn_gain,
    latent_down,
    latent_gain,
    latent_up,
    shared_kv,
    out_proj,
    mlp_gain,
    gate_weight,
    up_weight,
    down_weight,
    out_cotangent,
):
    tokens, width = block_input.shape
    rank = 2 * latent_down.shape[0]
    half_rank = latent_down.shape[0]
    units = down_weight.shape[0]
    mine = units * count
    padded = -(-mine // 256) * 256
    y = lax.axis_index("y")
    place = lax.axis_index("f")
    x_c = 2 * lax.axis_index("x") + lax.axis_index("c")

    def rows_of(array):
        flat = array.reshape(-1)
        lines = -(-flat.shape[0] // 128)
        return jnp.pad(flat, (0, lines * 128 - flat.shape[0])).reshape(lines, 128)

    gain_high = latent_gain.astype(BF16)
    gain_low = (latent_gain - gain_high.astype(F32)).astype(BF16)
    pieces = [
        latent_down.astype(BF16).reshape(-1, 128),
        shared_kv.astype(BF16).reshape(-1, 2, 128).transpose(1, 0, 2).reshape(-1, 128),
        rows_of(gain_high),
        rows_of(gain_low),
        rows_of(attn_gain.astype(BF16)),
        rows_of(mlp_gain.astype(BF16)),
        rows_of(seq_lens.astype(BF16)),
    ]
    marks = [0]
    for piece in pieces:
        marks.append(marks[-1] + piece.shape[0])
    total = -(-marks[-1] // 32) * 32
    first = jnp.pad(jnp.concatenate(pieces), ((0, total - marks[-1]), (0, 0)))
    first = line_gather(first, count)
    first = plane_gather(first.reshape(count * total, 128)).reshape(8, count, total, 128)
    lengths = lax.dynamic_index_in_dim(first[:, :, marks[6], :3], place, 1, keepdims=False)
    lengths = lengths.astype(jnp.int32)
    first = relabel(first)
    owned = first.transpose(1, 0, 2, 3)

    def piece_of(i):
        return owned[:, :, marks[i] : marks[i + 1]]

    columns = width // (4 * count)
    down_full = piece_of(0).reshape(count, 2, 2, 2, half_rank, columns)
    down_full = down_full.transpose((3, 4, 0, 1, 2, 5) if f_first else (3, 4, 1, 2, 0, 5))
    down_full = down_full.reshape(rank, width)
    kv_rows = shared_kv.shape[0]
    kv_full = piece_of(1).reshape(count, 8, 2, kv_rows, 128).transpose(0, 1, 3, 2, 4)
    kv_full = from_owner(kv_full.reshape(count, 8, kv_rows, HEAD_DIM), 0, f_first)
    gain_lat = (piece_of(2)[0, :2].astype(F32) + piece_of(3)[0, :2].astype(F32)).reshape(rank)
    gain_rows = attn_gain.shape[0]

    def gain_of(i):
        return from_owner(piece_of(i).reshape(count, 8, -1)[:, :, :gain_rows], 0, f_first)

    gain_one, gain_two = gain_of(4).astype(F32), gain_of(5).astype(F32)

    up_line = line_gather(after(latent_up.astype(BF16), first), count)
    out_line = line_gather(after(out_proj.astype(BF16), first), count)
    up_heads = up_line.transpose(1, 0, 2).reshape(half_rank, 4, HEAD_DIM)
    per_head = count // 4
    out_heads = out_line.reshape(4, per_head, -1, width)

    def own_heads(array, axis):
        return lax.dynamic_slice_in_dim(array, 2 * y, 2, axis)

    def other_heads(array, axis):
        return lax.dynamic_slice_in_dim(array, 2 - 2 * y, 2, axis)

    def join(own, other, axis):
        low = jnp.where(y == 0, own, other)
        high = jnp.where(y == 0, other, own)
        return jnp.stack([low, high], axis)

    up_full = join(own_heads(up_heads, 1), lax.ppermute(other_heads(up_heads, 1), "y", SWAP), 0)
    up_full = up_full.reshape(rank, 2 * HEAD_DIM)
    out_full = join(own_heads(out_heads, 0), lax.ppermute(other_heads(out_heads, 0), "y", SWAP), 2)
    out_full = out_full.reshape(2 * HEAD_DIM, width)

    def unit_blocks(weight):
        blocks = by_owner(weight.astype(BF16), 1, count, f_first)
        blocks = blocks.transpose(1, 2, 0, 3).reshape(8, -1, mine)
        return jnp.pad(blocks, ((0, 0), (0, 0), (0, padded - mine)))

    both = jnp.concatenate([unit_blocks(gate_weight), unit_blocks(up_weight)], axis=2)
    both = lax.all_to_all(both, ("x", "c", "y"), 0, 0, tiled=True)
    both = line_gather(after(both, up_line, out_line), count)
    both = from_owner(both, 0, f_first)
    ff_down = line_gather(after(down_weight.astype(BF16), up_line, out_line), count)
    ff_down = jnp.pad(ff_down.reshape(mine, width), ((0, padded - mine), (0, 0)))

    inputs = block_input.astype(F32)
    rms_one = lax.rsqrt(jnp.mean(inputs * inputs, axis=-1, keepdims=True) + EPS)
    normed = (inputs * rms_one * gain_one).astype(BF16)
    latent = contract(normed, down_full, 1, 1)
    rms_lat = lax.rsqrt(jnp.mean(latent * latent, axis=-1, keepdims=True) + EPS)
    latent_n = (latent * rms_lat * gain_lat).astype(BF16)
    shared = jnp.dot(normed, kv_full, preferred_element_type=F32)
    position, allowed = layout(lengths, tokens)
    cosine, sine = rope_tables(position, HEAD_DIM)
    k_own = rotate(shared, cosine[0], sine[0]).astype(BF16)

    parcel = plane_gather(jnp.concatenate([latent_n, k_own, shared.astype(BF16)], axis=1))
    lat_all = parcel[:, :, :rank].reshape(8 * tokens, rank)
    k_rot = parcel[:, :, rank : rank + HEAD_DIM]
    values = parcel[:, :, rank + HEAD_DIM :]
    g_all = plane_gather(after(out_cotangent, parcel)).reshape(8 * tokens, width)
    queries = jnp.dot(lat_all, up_full, preferred_element_type=F32)
    wide_cos, wide_sin = cosine[:, :, None], sine[:, :, None]
    q_rot = rotate(queries.reshape(8, tokens, 2, HEAD_DIM), wide_cos, wide_sin).astype(BF16)
    scores = scores_of(q_rot, k_rot, allowed)
    peak = jnp.max(scores, axis=-1, keepdims=True)
    log_total = peak + jnp.log(jnp.sum(jnp.exp(scores - peak), axis=-1, keepdims=True))
    probs = jnp.exp(scores - log_total)
    attended = jnp.einsum("bhts,bsd->bthd", probs.astype(BF16), values, preferred_element_type=F32)
    attended = attended.reshape(8 * tokens, 2 * HEAD_DIM).astype(BF16)
    branch = jnp.dot(attended, out_full, preferred_element_type=F32)
    branch = plane_scatter(branch.reshape(8, tokens, width))

    middle = inputs + branch
    rms_two = lax.rsqrt(jnp.mean(middle * middle, axis=-1, keepdims=True) + EPS)
    normed_two = (middle * rms_two * gain_two).astype(BF16)
    two_all = plane_gather(normed_two).reshape(8 * tokens, width)
    gate_up = jnp.dot(two_all, both, preferred_element_type=F32)
    gate, upval = gate_up[:, :padded], gate_up[:, padded:]
    sigma = jax.nn.sigmoid(gate)
    hidden = (gate * sigma * upval).astype(BF16)

    d_hidden = contract(g_all, ff_down, 1, 1)
    d_gate = (d_hidden * upval * sigma * (1.0 + gate * (1.0 - sigma))).astype(BF16)
    d_up = (d_hidden * gate * sigma).astype(BF16)
    d_both = jnp.concatenate([d_gate, d_up], axis=1)
    d_two = plane_scatter(contract(d_both, both, 1, 1).reshape(8, tokens, width))

    result = jnp.dot(hidden, ff_down, preferred_element_type=F32)
    result = plane_scatter(after(result.reshape(8, tokens, width), d_two))
    block_output = (middle + result).astype(BF16)

    both_grad = contract(two_all, d_both, 0, 0)
    both_grad = line_scatter(by_owner(both_grad, 0, count, f_first), count)
    both_grad = lax.all_to_all(both_grad.astype(BF16), ("x", "c", "y"), 0, 0, tiled=True)

    def whole_rows(blocks):
        blocks = blocks[:, :, :mine].astype(F32).reshape(8, -1, count, units)
        return from_owner(blocks.transpose(2, 0, 1, 3), 1, f_first)

    gate_grad, up_grad = whole_rows(both_grad[..., :padded]), whole_rows(both_grad[..., padded:])
    down_grad = contract(hidden, g_all, 0, 0)[:mine].reshape(count, units, width)
    down_grad = line_scatter(down_grad, count)

    upstream = out_cotangent.astype(F32)
    gain_two_part = jnp.sum(d_two * middle * rms_two, axis=0)
    scaled_two = d_two * gain_two
    d_middle = (
        upstream
        + rms_two * scaled_two
        - middle * (rms_two**3) * jnp.mean(scaled_two * middle, axis=-1, keepdims=True)
    )

    d_branch = plane_gather(d_middle.astype(BF16)).reshape(8 * tokens, width)
    d_attended = contract(d_branch, out_full, 1, 1).astype(BF16)
    d_attended = d_attended.reshape(8, tokens, 2, HEAD_DIM)
    d_probs = jnp.einsum("bthd,bsd->bhts", d_attended, values, preferred_element_type=F32)
    inner = jnp.sum(probs * d_probs, axis=-1, keepdims=True)
    d_scores = (probs * (d_probs - inner)).astype(BF16)
    scale = HEAD_DIM**-0.5
    d_qrot = jnp.einsum("bhts,bsd->bthd", d_scores, k_rot, preferred_element_type=F32) * scale
    d_queries = unrotate(d_qrot, wide_cos, wide_sin).astype(BF16)
    d_queries = d_queries.reshape(8 * tokens, 2 * HEAD_DIM)
    d_krot = jnp.einsum("bhts,bthd->bsd", d_scores, q_rot, preferred_element_type=F32) * scale
    value_part = jnp.einsum(
        "bhts,bthd->bsd", probs.astype(BF16), d_attended, preferred_element_type=F32
    )
    shared_part = unrotate(d_krot, cosine, sine) + value_part
    lat_part = contract(d_queries, up_full, 1, 1).reshape(8, tokens, rank)
    back = plane_scatter(jnp.concatenate([lat_part, shared_part], axis=2))
    d_lat_n, d_shared = back[:, :rank], back[:, rank:].astype(BF16)

    up_grad_heads = contract(lat_all, d_queries, 0, 0).reshape(2, half_rank, 2, HEAD_DIM)
    out_grad_heads = contract(attended, d_branch, 0, 0).reshape(2, per_head, 2, -1, width)

    def swap_halves(array, axis):
        own = lax.dynamic_index_in_dim(array, y, axis, keepdims=False)
        other = lax.dynamic_index_in_dim(array, 1 - y, axis, keepdims=False).astype(BF16)
        return own, lax.ppermute(other, "y", SWAP).astype(F32)

    up_line_grad = join(*swap_halves(up_grad_heads, 0), 1).reshape(half_rank, count, -1)
    latent_up_grad = line_scatter(up_line_grad.transpose(1, 0, 2), count)
    out_line_grad = join(*swap_halves(out_grad_heads, 2), 0)
    out_proj_grad = line_scatter(out_line_grad.reshape(count, -1, width), count)

    gain_lat_part = jnp.sum(d_lat_n * latent * rms_lat, axis=0)
    scaled_lat = d_lat_n * gain_lat
    inner_lat = jnp.sum(scaled_lat * latent, axis=-1, keepdims=True)
    d_latent = (rms_lat * scaled_lat - latent * (rms_lat**3) * inner_lat / rank).astype(BF16)
    d_normed = contract(d_shared, kv_full, 1, 1) + jnp.dot(
        d_latent, down_full, preferred_element_type=F32
    )
    gain_one_part = jnp.sum(d_normed * inputs * rms_one, axis=0)
    scaled_one = d_normed * gain_one
    input_grad = (
        d_middle
        + rms_one * scaled_one
        - inputs * (rms_one**3) * jnp.mean(scaled_one * inputs, axis=-1, keepdims=True)
    ).astype(BF16)

    down_part = contract(d_latent, normed, 0, 0)
    if f_first:
        down_part = down_part.reshape(2, half_rank, count, 2, 2, columns).transpose(2, 3, 4, 0, 1, 5)
    else:
        down_part = down_part.reshape(2, half_rank, 2, 2, count, columns).transpose(4, 2, 3, 0, 1, 5)
    down_part = down_part.reshape(count, 8, -1, 128)
    kv_part = by_owner(contract(normed, d_shared, 0, 0), 0, count, f_first)
    kv_part = kv_part.reshape(count, 8, kv_rows, 2, 128).transpose(0, 1, 3, 2, 4)
    kv_part = kv_part.reshape(count, 8, -1, 128)

    def gain_rows_of(part):
        part = by_owner(part, 0, count, f_first)
        return jnp.pad(part, ((0, 0), (0, 0), (0, 128 - gain_rows)))[:, :, None]

    lat_rows = jnp.broadcast_to(
        gain_lat_part.reshape(1, 1, 2, -1, 128), (count, 4, 2, half_rank // 128, 128)
    )
    lat_rows = lat_rows.reshape(count, 8, -1, 128)
    pieces = [down_part, kv_part, lat_rows, gain_rows_of(gain_one_part), gain_rows_of(gain_two_part)]
    marks = [0]
    for piece in pieces:
        marks.append(marks[-1] + piece.shape[2])
    last_rows = -(-marks[-1] // 32) * 32
    last = jnp.pad(jnp.concatenate(pieces, axis=2), ((0, 0), (0, 0), (0, last_rows - marks[-1]), (0, 0)))
    last = relabel(last.transpose(1, 0, 2, 3).astype(BF16))
    last = line_scatter(plane_scatter(last), count)
    latent_down_grad = last[marks[0] : marks[1]].reshape(half_rank, columns)
    shared_kv_grad = last[marks[1] : marks[2]].reshape(2, kv_rows, 128).transpose(1, 0, 2)
    shared_kv_grad = shared_kv_grad.reshape(kv_rows, HEAD_DIM)
    latent_gain_grad = last[marks[2] : marks[3]].reshape(half_rank)
    attn_gain_grad = last[marks[3], :gain_rows]
    mlp_gain_grad = last[marks[4], :gain_rows]
    return (
        block_output,
        input_grad,
        attn_gain_grad,
        latent_down_grad,
        latent_gain_grad,
        latent_up_grad,
        shared_kv_grad,
        out_proj_grad,
        mlp_gain_grad,
        gate_grad,
        up_grad,
        down_grad,
    )


def solution(mesh):
    devices = mesh.devices
    split = devices.shape[0]
    count = split // 4
    f_first = split == HEADS
    if f_first:
        names, sizes = ("f", "x", "c", "y"), (count, 2, 2, 2)
    else:
        names, sizes = ("x", "c", "f", "y"), (2, 2, count, 2)
    fine = Mesh(devices.reshape(sizes), names)
    dp = names[:3]
    return jax.shard_map(
        functools.partial(per_device, count, f_first),
        mesh=fine,
        in_specs=(
            P(names, None),
            P(names, None),
            P(names),
            P("y", dp),
            P("y"),
            P("y", dp),
            P(names, None),
            P(names, None),
            P(names),
            P(names, None),
            P(names, None),
            P(names, None),
            P(names, None),
        ),
        out_specs=(
            P(names, None),
            P(names, None),
            P(names),
            P("y", dp),
            P("y"),
            P("y", dp),
            P(names, None),
            P(names, None),
            P(names),
            P(names, None),
            P(names, None),
            P(names, None),
        ),
        check_vma=False,
    )
```

time: 5670 us -> 1730 us (0.31)
  waiting for transfers between devices: 5170 us -> 304 us
  local copies, waits for them, and re-layouts: 22.6 us -> 830 us
  starting transfers between devices: 1.89 us -> 228 us
  blocking collectives: 165 us -> 0 us
  other arithmetic: 34 us -> 176 us
  matrix products: 252 us -> 156 us
    reduce_scatter x9 -> x0, waiting for transfers between devices: 3950 us -> none  [the longest x1 971 us: per_device(): lax.psum_scatter(gate_grad, ('dp', 'rank'), scatter_dimension=0, tiled=True)]
    all_gather x16 -> x0, waiting for transfers between devices: 1220 us -> none  [the longest x1 135 us: per_device(): lax.all_gather(block_parts[4], ('dp', 'rank'), axis=0, tiled=True)]
    dynamic_update_slice x0 -> x21, local copies, waits for them, and re-layouts: none -> 554 us  [the longest x16 548 us: relabel(): full = lax.dynamic_update_index_in_dim(full, blocks[i], place ^ i, 0)]
    ppermute x0 -> x139, waiting for transfers between devices: none -> 304 us  [the longest x5 63.4 us: plane_scatter(): by_y = lax.ppermute(sums[1].astype(BF16), 'y', SWAP)]
    ppermute x0 -> x139, starting transfers between devices: none -> 217 us  [the longest x15 58 us: line_scatter(): lax.ppermute(mine_up.astype(BF16), 'f', [(i, i + 1) for i in range(min(st...]
    unnamed x3 -> x0, blocking collectives: 132 us -> none
    dot_general x14 -> x12, matrix products: 174 us -> 100 us  [contract(): lax.dot_general(left, right, (((left_dim,), (right_dim,)), ((), ())), pre...]
    reshape x0 -> x22, local copies, waits for them, and re-layouts: none -> 60.2 us  [the longest x6 20.7 us: from_owner(): return array.reshape(*lead, 8 * count * part, *tail)]
  transfers between devices with their start and end apart: 25 -> 141, of which waited for: 23 -> 37; matrix products, arithmetic and copies ran while one was open for 5% -> 65% of each run, Pallas kernels for 0% -> 0%
where the time goes in v1:
time: 1730 us; the launch traced here: 1700 us
  local copies, waits for them, and re-layouts  830 us (48%)
  waiting for transfers between devices  304 us (18%)
  starting transfers between devices  228 us (13%)
  other arithmetic  176 us (10%)
  matrix products  156 us (9%)
    dynamic_update_slice x16, local copies, waits for them, and re-layouts, relabel(): full = lax.dynamic_update_index_in_dim(full, blocks[i], place ^ i, 0)  548 us
    dot_general x12, matrix products, contract(): lax.dot_general(left, right, (((left_dim,), (right_dim,)), ((), ())), pre...  100 us
    unnamed x265, local copies, waits for them, and re-layouts  75.9 us
    ppermute x5, waiting for transfers between devices, plane_scatter(): by_y = lax.ppermute(sums[1].astype(BF16), 'y', SWAP)  63.4 us
    ppermute x15, starting transfers between devices, line_scatter(): lax.ppermute(mine_up.astype(BF16), 'f', [(i, i + 1) for i in range(min(st...  58 us
    ppermute x15, waiting for transfers between devices, line_gather(): lax.ppermute(downs[-1], 'f', [(i, i - 1) for i in range(1, count - step +...  55.8 us
    ppermute x15, starting transfers between devices, line_gather(): lax.ppermute(downs[-1], 'f', [(i, i - 1) for i in range(1, count - step +...  48.1 us
    ppermute x15, waiting for transfers between devices, line_scatter(): lax.ppermute(mine_up.astype(BF16), 'f', [(i, i + 1) for i in range(min(st...  38 us
  transfers between devices with their start and end apart: 141, of which 37 were waited for; matrix products, arithmetic and copies ran while one was open for 65% of the time, Pallas kernels for 0%

profile of v1, /device:TPU:10, one launch (start us, length us, event | category | flops | bytes accessed | tf_op | source)
XLA Modules:
  0.0 1699.0 jit_solution(4294003709991796848)
XLA Ops:
  56.7 21.4 %collective-permute-done.6 = bf16[2688,128]{1,0:T(8,128)(2,1)S(1)} collective-permute-done((bf16[2688,128]{1,0:T(8,128)(2,1)S(1)}, bf16[2688,128]{1,0:T(8,128)(2,1)S(1)}, u32[]{:S(2)}, u32[]{:S(2)}) %collective-permute-start.6) | collective-permute-done | bytes 688160 | tf_op jit(solution)/shard_map/ppermute | solution.py:103
  84.6 34.1 %dynamic_update_slice.118 = bf16[8,4,672,128]{3,0,1,2:T(8,128)(2,1)} dynamic-update-slice(bf16[8,4,672,128]{3,0,1,2:T(8,128)(2,1)} %broadcast.164.clone, bf16[1,4,672,128]{3,0,1,2:T(2,128)(2,1)S(1)} %copy.363, s32[]{:T(128)S(6)} %select_n.306, s32[]{:T(128)} %constant.267.clone.1, s32[]{:T(128)} %constant.267.clone.1, s32[]{:T(128)} %constant.267.clone.1) | dynamic-update-slice | bytes 1376260 | tf_op jit(solution)/shard_map/jit(dynamic_update_index_in_dim)/dynamic_update_slice | solution.py:132
  131.2 34.3 %dynamic_update_slice.119 = bf16[8,4,672,128]{3,0,1,2:T(8,128)(2,1)} dynamic-update-slice(bf16[8,4,672,128]{3,0,1,2:T(8,128)(2,1)} %dynamic_update_slice.118, bf16[1,4,672,128]{3,0,1,2:T(2,128)(2,1)} %copy.364, s32[]{:T(128)S(6)} %select_n.307, s32[]{:T(128)} %constant.267.clone.1, s32[]{:T(128)} %constant.267.clone.1, s32[]{:T(128)} %constant.267.clone.1) | dynamic-update-slice | bytes 1376260 | tf_op jit(solution)/shard_map/jit(dynamic_update_index_in_dim)/dynamic_update_slice | solution.py:132
  165.5 34.2 %dynamic_update_slice.120 = bf16[8,4,672,128]{3,0,1,2:T(8,128)(2,1)} dynamic-update-slice(bf16[8,4,672,128]{3,0,1,2:T(8,128)(2,1)} %dynamic_update_slice.119, bf16[1,4,672,128]{3,0,1,2:T(2,128)(2,1)} %copy.365, s32[]{:T(128)S(6)} %select_n.308, s32[]{:T(128)} %constant.267.clone.1, s32[]{:T(128)} %constant.267.clone.1, s32[]{:T(128)} %constant.267.clone.1) | dynamic-update-slice | bytes 1376260 | tf_op jit(solution)/shard_map/jit(dynamic_update_index_in_dim)/dynamic_update_slice | solution.py:132
  211.4 34.6 %dynamic_update_slice.121 = bf16[8,4,672,128]{3,0,1,2:T(8,128)(2,1)} dynamic-update-slice(bf16[8,4,672,128]{3,0,1,2:T(8,128)(2,1)} %dynamic_update_slice.120, bf16[1,4,672,128]{3,0,1,2:T(2,128)(2,1)} %copy.366, s32[]{:T(128)S(6)} %select_n.309, s32[]{:T(128)} %constant.267.clone.1, s32[]{:T(128)} %constant.267.clone.1, s32[]{:T(128)} %constant.267.clone.1) | dynamic-update-slice | bytes 1376260 | tf_op jit(solution)/shard_map/jit(dynamic_update_index_in_dim)/dynamic_update_slice | solution.py:132
  246.1 34.1 %dynamic_update_slice.122 = bf16[8,4,672,128]{3,0,1,2:T(8,128)(2,1)} dynamic-update-slice(bf16[8,4,672,128]{3,0,1,2:T(8,128)(2,1)} %dynamic_update_slice.121, bf16[1,4,672,128]{3,0,1,2:T(2,128)(2,1)S(1)} %copy.367, s32[]{:T(128)S(6)} %select_n.310, s32[]{:T(128)} %constant.267.clone.1, s32[]{:T(128)} %constant.267.clone.1, s32[]{:T(128)} %constant.267.clone.1) | dynamic-update-slice | bytes 1376260 | tf_op jit(solution)/shard_map/jit(dynamic_update_index_in_dim)/dynamic_update_slice | solution.py:132
  280.2 34.3 %dynamic_update_slice.123 = bf16[8,4,672,128]{3,0,1,2:T(8,128)(2,1)} dynamic-update-slice(bf16[8,4,672,128]{3,0,1,2:T(8,128)(2,1)} %dynamic_update_slice.122, bf16[1,4,672,128]{3,0,1,2:T(2,128)(2,1)} %copy.368, s32[]{:T(128)S(6)} %select_n.311, s32[]{:T(128)} %constant.267.clone.1, s32[]{:T(128)} %constant.267.clone.1, s32[]{:T(128)} %constant.267.clone.1) | dynamic-update-slice | bytes 1376260 | tf_op jit(solution)/shard_map/jit(dynamic_update_index_in_dim)/dynamic_update_slice | solution.py:132
  314.5 34.1 %dynamic_update_slice.124 = bf16[8,4,672,128]{3,0,1,2:T(8,128)(2,1)} dynamic-update-slice(bf16[8,4,672,128]{3,0,1,2:T(8,128)(2,1)} %dynamic_update_slice.123, bf16[1,4,672,128]{3,0,1,2:T(2,128)(2,1)S(1)} %copy-done.35, s32[]{:T(128)S(6)} %select_n.312, s32[]{:T(128)} %constant.267.clone.1, s32[]{:T(128)} %constant.267.clone.1, s32[]{:T(128)} %constant.267.clone.1) | dynamic-update-slice | bytes 1376260 | tf_op jit(solution)/shard_map/jit(dynamic_update_index_in_dim)/dynamic_update_slice | solution.py:132
  357.8 34.1 %dynamic_update_slice.125 = bf16[8,4,672,128]{3,0,1,2:T(8,128)(2,1)} dynamic-update-slice(bf16[8,4,672,128]{3,0,1,2:T(8,128)(2,1)} %dynamic_update_slice.124, bf16[1,4,672,128]{3,0,1,2:T(2,128)(2,1)S(1)} %copy.370, s32[]{:T(128)S(6)} %select_n.313, s32[]{:T(128)} %constant.267.clone.1, s32[]{:T(128)} %constant.267.clone.1, s32[]{:T(128)} %constant.267.clone.1) | dynamic-update-slice | bytes 1376260 | tf_op jit(solution)/shard_map/jit(dynamic_update_index_in_dim)/dynamic_update_slice | solution.py:132
  661.8 26.7 %collective-permute-done.52 = bf16[8,64,1536]{2,1,0:T(8,128)(2,1)S(1)} collective-permute-done((bf16[8,64,1536]{2,1,0:T(8,128)(2,1)}, bf16[8,64,1536]{2,1,0:T(8,128)(2,1)S(1)}, u32[]{:S(2)}, u32[]{:S(2)}) %collective-permute-start.52) | collective-permute-done | bytes 1572896 | tf_op jit(solution)/shard_map/ppermute | solution.py:71
  716.1 19.0 %collective-permute-done.42 = bf16[256,2048]{1,0:T(8,128)(2,1)S(1)} collective-permute-done((bf16[256,2048]{1,0:T(8,128)(2,1)S(1)}, bf16[256,2048]{1,0:T(8,128)(2,1)S(1)}, u32[]{:S(2)}, u32[]{:S(2)}) %collective-permute-start.42) | collective-permute-done | bytes 1048608 | tf_op jit(solution)/shard_map/ppermute | solution.py:120
  847.5 21.8 %fusion.141 = (bf16[2048,2048]{1,0:T(8,128)(2,1)}, f32[2048,2048]{1,0:T(8,128)}) fusion(bf16[2048,1536]{1,0:T(8,128)(2,1)} %bitcast.668, bf16[2048,768]{0,1:T(8,128)(2,1)} %get-tuple-element.41, bf16[2048,768]{0,1:T(8,128)(2,1)} %get-tuple-element.40), kind=kOutput, calls=%fused_computation.406 | convolution fusion | flops 12901679104 | bytes 37748736 | tf_op jit(solution)/shard_map/dot_general | solution.py:19
  873.5 18.4 %fusion.1 = f32[4,8,64,1536]{3,2,1,0:T(8,128)S(1)} fusion(bf16[4,8,64,2048]{3,2,1,0:T(8,128)(2,1)} %bitcast.661, bf16[2048,768]{0,1:T(8,128)(2,1)} %get-tuple-element.41, bf16[2048,768]{0,1:T(8,128)(2,1)} %get-tuple-element.40), kind=kOutput, calls=%fused_computation.11 | convolution fusion | flops 12897484800 | bytes 27262976 | tf_op jit(solution)/shard_map/dot_general | solution.py:19
  938.5 19.8 %collective-permute-done.75 = bf16[256,2048]{1,0:T(8,128)(2,1)S(1)} collective-permute-done((bf16[256,2048]{1,0:T(8,128)(2,1)S(1)}, bf16[256,2048]{1,0:T(8,128)(2,1)S(1)}, u32[]{:S(2)}, u32[]{:S(2)}) %collective-permute-start.75) | collective-permute-done | bytes 1048608 | tf_op jit(solution)/shard_map/ppermute | solution.py:118
  1052.4 36.1 %collective-permute-done.82 = bf16[256,2048]{1,0:T(8,128)(2,1)S(1)} collective-permute-done((bf16[256,2048]{1,0:T(8,128)(2,1)S(1)}, bf16[256,2048]{1,0:T(8,128)(2,1)S(1)}, u32[]{:S(2)}, u32[]{:S(2)}) %collective-permute-start.82) | collective-permute-done | bytes 1048608 | tf_op jit(solution)/shard_map/ppermute | solution.py:118
  1264.7 34.2 %dynamic_update_slice.142 = bf16[8,4,672,128]{3,0,1,2:T(8,128)(2,1)} dynamic-update-slice(bf16[8,4,672,128]{3,0,1,2:T(8,128)(2,1)} %broadcast.164, bf16[1,4,672,128]{3,0,1,2:T(2,128)(2,1)} %get-tuple-element.94, s32[]{:T(128)S(6)} %select_n.306, s32[]{:T(128)} %constant.267.clone.1, s32[]{:T(128)} %constant.267.clone.1, s32[]{:T(128)} %constant.267.clone.1) | dynamic-update-slice | bytes 1376260 | tf_op jit(solution)/shard_map/jit(dynamic_update_index_in_dim)/dynamic_update_slice | solution.py:132
  1298.9 34.2 %dynamic_update_slice.143 = bf16[8,4,672,128]{3,0,1,2:T(8,128)(2,1)} dynamic-update-slice(bf16[8,4,672,128]{3,0,1,2:T(8,128)(2,1)} %dynamic_update_slice.142, bf16[1,4,672,128]{3,0,1,2:T(2,128)(2,1)} %get-tuple-element.93, s32[]{:T(128)S(6)} %select_n.307, s32[]{:T(128)} %constant.267.clone.1, s32[]{:T(128)} %constant.267.clone.1, s32[]{:T(128)} %constant.267.clone.1) | dynamic-update-slice | bytes 1376260 | tf_op jit(solution)/shard_map/jit(dynamic_update_index_in_dim)/dynamic_update_slice | solution.py:132
  1333.1 34.2 %dynamic_update_slice.144 = bf16[8,4,672,128]{3,0,1,2:T(8,128)(2,1)} dynamic-update-slice(bf16[8,4,672,128]{3,0,1,2:T(8,128)(2,1)} %dynamic_update_slice.143, bf16[1,4,672,128]{3,0,1,2:T(2,128)(2,1)} %get-tuple-element.92, s32[]{:T(128)S(6)} %select_n.308, s32[]{:T(128)} %constant.267.clone.1, s32[]{:T(128)} %constant.267.clone.1, s32[]{:T(128)} %constant.267.clone.1) | dynamic-update-slice | bytes 1376260 | tf_op jit(solution)/shard_map/jit(dynamic_update_index_in_dim)/dynamic_update_slice | solution.py:132
  1367.3 34.2 %dynamic_update_slice.145 = bf16[8,4,672,128]{3,0,1,2:T(8,128)(2,1)} dynamic-update-slice(bf16[8,4,672,128]{3,0,1,2:T(8,128)(2,1)} %dynamic_update_slice.144, bf16[1,4,672,128]{3,0,1,2:T(2,128)(2,1)} %get-tuple-element.91, s32[]{:T(128)S(6)} %select_n.309, s32[]{:T(128)} %constant.267.clone.1, s32[]{:T(128)} %constant.267.clone.1, s32[]{:T(128)} %constant.267.clone.1) | dynamic-update-slice | bytes 1376260 | tf_op jit(solution)/shard_map/jit(dynamic_update_index_in_dim)/dynamic_update_slice | solution.py:132
  1401.6 34.2 %dynamic_update_slice.146 = bf16[8,4,672,128]{3,0,1,2:T(8,128)(2,1)} dynamic-update-slice(bf16[8,4,672,128]{3,0,1,2:T(8,128)(2,1)} %dynamic_update_slice.145, bf16[1,4,672,128]{3,0,1,2:T(2,128)(2,1)} %get-tuple-element.90, s32[]{:T(128)S(6)} %select_n.310, s32[]{:T(128)} %constant.267.clone.1, s32[]{:T(128)} %constant.267.clone.1, s32[]{:T(128)} %constant.267.clone.1) | dynamic-update-slice | bytes 1376260 | tf_op jit(solution)/shard_map/jit(dynamic_update_index_in_dim)/dynamic_update_slice | solution.py:132
  1435.8 34.2 %dynamic_update_slice.147 = bf16[8,4,672,128]{3,0,1,2:T(8,128)(2,1)} dynamic-update-slice(bf16[8,4,672,128]{3,0,1,2:T(8,128)(2,1)} %dynamic_update_slice.146, bf16[1,4,672,128]{3,0,1,2:T(2,128)(2,1)} %get-tuple-element.89, s32[]{:T(128)S(6)} %select_n.311, s32[]{:T(128)} %constant.267.clone.1, s32[]{:T(128)} %constant.267.clone.1, s32[]{:T(128)} %constant.267.clone.1) | dynamic-update-slice | bytes 1376260 | tf_op jit(solution)/shard_map/jit(dynamic_update_index_in_dim)/dynamic_update_slice | solution.py:132
  1470.0 34.2 %dynamic_update_slice.148 = bf16[8,4,672,128]{3,0,1,2:T(8,128)(2,1)} dynamic-update-slice(bf16[8,4,672,128]{3,0,1,2:T(8,128)(2,1)} %dynamic_update_slice.147, bf16[1,4,672,128]{3,0,1,2:T(2,128)(2,1)} %get-tuple-element.88, s32[]{:T(128)S(6)} %select_n.312, s32[]{:T(128)} %constant.267.clone.1, s32[]{:T(128)} %constant.267.clone.1, s32[]{:T(128)} %constant.267.clone.1) | dynamic-update-slice | bytes 1376260 | tf_op jit(solution)/shard_map/jit(dynamic_update_index_in_dim)/dynamic_update_slice | solution.py:132
  1504.3 34.1 %dynamic_update_slice.149 = bf16[8,4,672,128]{3,0,1,2:T(8,128)(2,1)} dynamic-update-slice(bf16[8,4,672,128]{3,0,1,2:T(8,128)(2,1)} %dynamic_update_slice.148, bf16[1,4,672,128]{3,0,1,2:T(2,128)(2,1)S(1)} %get-tuple-element.87, s32[]{:T(128)S(6)} %select_n.313, s32[]{:T(128)} %constant.267.clone.1, s32[]{:T(128)} %constant.267.clone.1, s32[]{:T(128)} %constant.267.clone.1) | dynamic-update-slice | bytes 1376260 | tf_op jit(solution)/shard_map/jit(dynamic_update_index_in_dim)/dynamic_update_slice | solution.py:132
  1538.4 26.1 %fusion.137 = (bf16[1,4,672,128]{3,0,1,2:T(2,128)(2,1)}, bf16[1,4,672,128]{3,0,1,2:T(2,128)(2,1)}, bf16[1,4,672,128]{3,0,1,2:T(2,128)(2,1)S(1)}, bf16[1,4,672,12...) fusion(bf16[8,4,672,128]{3,0,1,2:T(8,128)(2,1)} %dynamic_update, ...), kind=kLoop, calls=%fused_computation.402 | loop fusion | flops 344064 | bytes 11698176 | tf_op jit(solution)/shard_map/slice | solution.py:117
  (788 shorter events, 958.3 us)
Async XLA Ops:
  37.3 512.3 %all-to-all-start = ((bf16[8,64,1536]{2,1,0:T(8,128)(2,1)}), bf16[8,64,1536]{2,1,0:T(8,128)(2,1)}, u32[]{:S(2)}, u32[]{:S(2)}) async-start(bf16[8,64,1536]{2,1,0:T(8,128)(2,1)} %fusion.57), calls=%async_computation | async-start | bytes 3145728 | tf_op jit(solution)/shard_map/all_to_all | solution.py:268
  54.7 64.6 %collective-permute-start.10 = (bf16[1344,128]{1,0:T(8,128)(2,1)}, bf16[1344,128]{1,0:T(8,128)(2,1)}, u32[]{:S(2)}, u32[]{:S(2)}) collective-permute-start(bf16[1344,128]{1,0:T(8,128)(2,1)} %slice.434), channel_id=1, source_target_pairs={{0,1},{1,0},{2,3},{3,2},{4,5},{5,4},{6,7},{7,6},{8,9},{9,8},{10,11... | collective-permute-start | bytes 1032200 | tf_op jit(solution)/shard_map/ppermute | solution.py:105
  56.7 70.2 %collective-permute-start.7 = (bf16[2688,128]{1,0:T(8,128)(2,1)S(1)}, bf16[2688,128]{1,0:T(8,128)(2,1)}, u32[]{:S(2)}, u32[]{:S(2)}) collective-permute-start(bf16[2688,128]{1,0:T(8,128)(2,1)S(1)} %bitcast.671), channel_id=1, source_target_pairs={{0,2},{2,0},{1,3},{3,1},{4,6},{6,4},{5,7},{7,5},{8,10},{10,8},{9,1... | collective-permute-start | bytes 2064392 | tf_op jit(solution)/shard_map/ppermute | solution.py:108
  118.7 86.2 %collective-permute-start.8 = (bf16[2688,128]{1,0:T(8,128)(2,1)}, bf16[2688,128]{1,0:T(8,128)(2,1)}, u32[]{:S(2)}, u32[]{:S(2)}) collective-permute-start(bf16[2688,128]{1,0:T(8,128)(2,1)} %copy-done.42), channel_id=1, source_target_pairs={{0,2},{2,0},{1,3},{3,1},{4,6},{6,4},{5,7},{7,5},{8,10},{10,8},{9,1... | collective-permute-start | bytes 2064392 | tf_op jit(solution)/shard_map/ppermute | solution.py:108
  118.7 89.5 %collective-permute-start.12 = (bf16[2688,128]{1,0:T(8,128)(2,1)}, bf16[2688,128]{1,0:T(8,128)(2,1)}, u32[]{:S(2)}, u32[]{:S(2)}) collective-permute-start(bf16[2688,128]{1,0:T(8,128)(2,1)} %copy-done.40), channel_id=1, source_target_pairs={{0,2},{2,0},{1,3},{3,1},{4,6},{6,4},{5,7},{7,5},{8,10},{10,8},{9,1... | collective-permute-start | bytes 2064392 | tf_op jit(solution)/shard_map/ppermute | solution.py:108
  122.7 232.9 %collective-permute-start.13 = (bf16[2688,128]{1,0:T(8,128)(2,1)}, bf16[2688,128]{1,0:T(8,128)(2,1)}, u32[]{:S(2)}, u32[]{:S(2)}) collective-permute-start(bf16[2688,128]{1,0:T(8,128)(2,1)} %constant_dynamic-update-slice_fusion), channel_id=1, source_target_pairs={{0,2},{2,0},{1,3},{3,1},{4,6},{6,4},{5,7},{7,5},{8,10},{10,8},{9,1... | collective-permute-start | bytes 2064392 | tf_op jit(solution)/shard_map/ppermute | solution.py:108
  391.9 82.0 %collective-permute-start.30 = (bf16[128,2048]{1,0:T(8,128)(2,1)}, bf16[128,2048]{1,0:T(8,128)(2,1)}, u32[]{:S(2)}, u32[]{:S(2)}) collective-permute-start(bf16[128,2048]{1,0:T(8,128)(2,1)} %convert_element_type.641), channel_id=1, source_target_pairs={{8,0},{16,8},{24,16},{9,1},{17,9},{25,17},{10,2},{18,10},{26,18},{... | collective-permute-start | bytes 1572872 | tf_op jit(solution)/shard_map/ppermute | solution.py:71
  393.9 80.1 %collective-permute-start.29 = (bf16[128,2048]{1,0:T(8,128)(2,1)}, bf16[128,2048]{1,0:T(8,128)(2,1)}, u32[]{:S(2)}, u32[]{:S(2)}) collective-permute-start(bf16[128,2048]{1,0:T(8,128)(2,1)} %convert_element_type.641), channel_id=1, source_target_pairs={{0,8},{8,16},{16,24},{1,9},{9,17},{17,25},{2,10},{10,18},{18,26},{... | collective-permute-start | bytes 1572872 | tf_op jit(solution)/shard_map/ppermute | solution.py:68
  397.8 54.4 %collective-permute-start.23 = (bf16[512,256]{1,0:T(8,128)(2,1)S(1)}, bf16[512,256]{1,0:T(8,128)(2,1)}, u32[]{:S(2)}, u32[]{:S(2)}) collective-permute-start(bf16[512,256]{1,0:T(8,128)(2,1)S(1)} %convert_element_type.636), channel_id=1, source_target_pairs={{8,0},{16,8},{24,16},{9,1},{17,9},{25,17},{10,2},{18,10},{26,18},{... | collective-permute-start | bytes 786440 | tf_op jit(solution)/shard_map/ppermute | solution.py:71
  400.5 57.3 %collective-permute-start.22 = (bf16[512,256]{1,0:T(8,128)(2,1)S(1)}, bf16[512,256]{1,0:T(8,128)(2,1)}, u32[]{:S(2)}, u32[]{:S(2)}) collective-permute-start(bf16[512,256]{1,0:T(8,128)(2,1)S(1)} %convert_element_type.636), channel_id=1, source_target_pairs={{0,8},{8,16},{16,24},{1,9},{9,17},{17,25},{2,10},{10,18},{18,26},{... | collective-permute-start | bytes 786440 | tf_op jit(solution)/shard_map/ppermute | solution.py:68
  527.1 81.3 %collective-permute-start.58 = (bf16[176,2048]{1,0:T(8,128)(2,1)}, bf16[176,2048]{1,0:T(8,128)(2,1)}, u32[]{:S(2)}, u32[]{:S(2)}) collective-permute-start(bf16[176,2048]{1,0:T(8,128)(2,1)} %convert_element_type.659), channel_id=1, source_target_pairs={{8,0},{16,8},{24,16},{9,1},{17,9},{25,17},{10,2},{18,10},{26,18},{... | collective-permute-start | bytes 2162696 | tf_op jit(solution)/shard_map/ppermute | solution.py:71
  531.5 77.0 %collective-permute-start.57 = (bf16[176,2048]{1,0:T(8,128)(2,1)}, bf16[176,2048]{1,0:T(8,128)(2,1)}, u32[]{:S(2)}, u32[]{:S(2)}) collective-permute-start(bf16[176,2048]{1,0:T(8,128)(2,1)} %convert_element_type.659), channel_id=1, source_target_pairs={{0,8},{8,16},{16,24},{1,9},{9,17},{17,25},{2,10},{10,18},{18,26},{... | collective-permute-start | bytes 2162696 | tf_op jit(solution)/shard_map/ppermute | solution.py:68
  555.4 57.0 %collective-permute-start.64 = (bf16[256,2048]{1,0:T(8,128)(2,1)}, bf16[256,2048]{1,0:T(8,128)(2,1)}, u32[]{:S(2)}, u32[]{:S(2)}) collective-permute-start(bf16[256,2048]{1,0:T(8,128)(2,1)} %param.25), channel_id=1, source_target_pairs={{0,2},{2,0},{1,3},{3,1},{4,6},{6,4},{5,7},{7,5},{8,10},{10,8},{9,1... | collective-permute-start | bytes 3145736 | tf_op jit(solution)/shard_map/ppermute | solution.py:108
  642.3 56.8 %collective-permute-start.51 = (bf16[8,64,1536]{2,1,0:T(8,128)(2,1)}, bf16[8,64,1536]{2,1,0:T(8,128)(2,1)S(1)}, u32[]{:S(2)}, u32[]{:S(2)}) collective-permute-start(bf16[8,64,1536]{2,1,0:T(8,128)(2,1)} %all-to-all-done), channel_id=1, source_target_pairs={{0,8},{8,16},{16,24},{1,9},{9,17},{17,25},{2,10},{10,18},{18,26},{... | collective-permute-start | bytes 4718600 | tf_op jit(solution)/shard_map/ppermute | solution.py:68
  832.0 60.0 %collective-permute-start.133 = (bf16[176,2048]{1,0:T(8,128)(2,1)}, bf16[176,2048]{1,0:T(8,128)(2,1)S(1)}, u32[]{:S(2)}, u32[]{:S(2)}) collective-permute-start(bf16[176,2048]{1,0:T(8,128)(2,1)} %get-tuple-element.77), channel_id=1, source_target_pairs={{0,8},{1,9},{2,10},{3,11},{4,12},{5,13},{6,14},{7,15}} | collective-permute-start | bytes 2162696 | tf_op jit(solution)/shard_map/ppermute | solution.py:90
  833.3 79.5 %collective-permute-start.136 = (bf16[176,2048]{1,0:T(8,128)(2,1)}, bf16[176,2048]{1,0:T(8,128)(2,1)}, u32[]{:S(2)}, u32[]{:S(2)}) collective-permute-start(bf16[176,2048]{1,0:T(8,128)(2,1)} %get-tuple-element.78), channel_id=1, source_target_pairs={{24,16},{25,17},{26,18},{27,19},{28,20},{29,21},{30,22},{31,23}} | collective-permute-start | bytes 2162696 | tf_op jit(solution)/shard_map/ppermute | solution.py:91
  1050.5 109.0 %collective-permute-start.131 = (bf16[8,64,1536]{2,1,0:T(8,128)(2,1)}, bf16[8,64,1536]{2,1,0:T(8,128)(2,1)}, u32[]{:S(2)}, u32[]{:S(2)}) collective-permute-start(bf16[8,64,1536]{2,1,0:T(8,128)(2,1)} %get-tuple-element.52), channel_id=1, source_target_pairs={{16,8},{24,16},{17,9},{25,17},{18,10},{26,18},{19,11},{27,19},{20,... | collective-permute-start | bytes 4718600 | tf_op jit(solution)/shard_map/ppermute | solution.py:91
  1189.4 387.0 %collective-permute-start.129 = (bf16[8,64,1536]{2,1,0:T(8,128)(2,1)}, bf16[8,64,1536]{2,1,0:T(8,128)(2,1)}, u32[]{:S(2)}, u32[]{:S(2)}) collective-permute-start(bf16[8,64,1536]{2,1,0:T(8,128)(2,1)} %get-tuple-element.51), channel_id=1, source_target_pairs={{0,8},{8,16},{16,24},{1,9},{9,17},{17,25},{2,10},{10,18},{18,26},{... | collective-permute-start | bytes 4718600 | tf_op jit(solution)/shard_map/ppermute | solution.py:90
  1192.5 383.8 %collective-permute-start.132 = (bf16[8,64,1536]{2,1,0:T(8,128)(2,1)}, bf16[8,64,1536]{2,1,0:T(8,128)(2,1)}, u32[]{:S(2)}, u32[]{:S(2)}) collective-permute-start(bf16[8,64,1536]{2,1,0:T(8,128)(2,1)} %fusion.11), channel_id=1, source_target_pairs={{8,0},{16,8},{24,16},{9,1},{17,9},{25,17},{10,2},{18,10},{26,18},{... | collective-permute-start | bytes 4718600 | tf_op jit(solution)/shard_map/ppermute | solution.py:91
  1197.3 389.4 %collective-permute-start.121 = (bf16[128,2048]{1,0:T(8,128)(2,1)}, bf16[128,2048]{1,0:T(8,128)(2,1)}, u32[]{:S(2)}, u32[]{:S(2)}) collective-permute-start(bf16[128,2048]{1,0:T(8,128)(2,1)} %get-tuple-element.103), channel_id=1, source_target_pairs={{0,8},{1,9},{2,10},{3,11},{4,12},{5,13},{6,14},{7,15}} | collective-permute-start | bytes 1572872 | tf_op jit(solution)/shard_map/ppermute | solution.py:90
  1204.9 394.1 %collective-permute-start.124 = (bf16[128,2048]{1,0:T(8,128)(2,1)}, bf16[128,2048]{1,0:T(8,128)(2,1)}, u32[]{:S(2)}, u32[]{:S(2)}) collective-permute-start(bf16[128,2048]{1,0:T(8,128)(2,1)} %get-tuple-element.104), channel_id=1, source_target_pairs={{24,16},{25,17},{26,18},{27,19},{28,20},{29,21},{30,22},{31,23}} | collective-permute-start | bytes 1572872 | tf_op jit(solution)/shard_map/ppermute | solution.py:91
  1206.4 362.8 %collective-permute-start.118 = (bf16[512,256]{1,0:T(8,128)(2,1)}, bf16[512,256]{1,0:T(8,128)(2,1)S(1)}, u32[]{:S(2)}, u32[]{:S(2)}) collective-permute-start(bf16[512,256]{1,0:T(8,128)(2,1)} %get-tuple-element.114), channel_id=1, source_target_pairs={{16,8},{24,16},{17,9},{25,17},{18,10},{26,18},{19,11},{27,19},{20,... | collective-permute-start | bytes 786440 | tf_op jit(solution)/shard_map/ppermute | solution.py:91
  1581.5 69.0 %all-to-all-start.1 = ((bf16[8,64,1536]{2,1,0:T(8,128)(2,1)}), bf16[8,64,1536]{2,1,0:T(8,128)(2,1)}, u32[]{:S(2)}, u32[]{:S(2)}) async-start(bf16[8,64,1536]{2,1,0:T(8,128)(2,1)} %fusion.15), calls=%async_computation.1 | async-start | bytes 3145728 | tf_op jit(solution)/shard_map/all_to_all | solution.py:323
  1615.5 74.5 %collective-permute-start.123 = (bf16[128,2048]{1,0:T(8,128)(2,1)}, bf16[128,2048]{1,0:T(8,128)(2,1)}, u32[]{:S(2)}, u32[]{:S(2)}) collective-permute-start(bf16[128,2048]{1,0:T(8,128)(2,1)} %get-tuple-element.101), channel_id=1, source_target_pairs={{0,8},{8,16},{16,24},{1,9},{9,17},{17,25},{2,10},{10,18},{18,26},{... | collective-permute-start | bytes 1572872 | tf_op jit(solution)/shard_map/ppermute | solution.py:90
  (224 other events, 4923.5 us)

commit v2 on v1

--- a/solution.py
+++ b/solution.py
@@ -4,6 +4,8 @@
 import jax
 import jax.numpy as jnp
 from jax import lax
+from jax.experimental import pallas as pl
+from jax.experimental.pallas import tpu as pltpu
 from jax.sharding import Mesh
 from jax.sharding import PartitionSpec as P
 
@@ -57,63 +59,14 @@
     return rotate(grads, cosine, -sine)
 
 
-def line_gather(block, count):
-    place = lax.axis_index("f")
-    full = lax.dynamic_update_index_in_dim(
-        jnp.zeros((count, *block.shape), block.dtype), block, place, 0
-    )
-    ups, downs = [block], [block]
-    for step in range(1, count):
-        ups.append(
-            lax.ppermute(ups[-1], "f", [(i, i + 1) for i in range(step - 1, count - 1)])
-        )
-        downs.append(
-            lax.ppermute(downs[-1], "f", [(i, i - 1) for i in range(1, count - step + 1)])
-        )
-    for step in range(1, count):
-        got = jnp.where(place >= step, ups[step], downs[count - step])
-        full = lax.dynamic_update_index_in_dim(full, got, lax.rem(place - step + count, count), 0)
-    return full
-
-
-def line_scatter(parts, count):
-    place = lax.axis_index("f")
-
-    def part(at):
-        return lax.dynamic_index_in_dim(parts, lax.rem(at + 2 * count, count), 0, keepdims=False)
-
-    up = down = None
-    for step in range(1, count):
-        mine_up, mine_down = part(place - step), part(place + step)
-        if up is not None:
-            mine_up, mine_down = mine_up + up.astype(F32), mine_down + down.astype(F32)
-        up = lax.ppermute(mine_up.astype(BF16), "f", [(i, i + 1) for i in range(min(step, count - 1))])
-        down = lax.ppermute(
-            mine_down.astype(BF16), "f", [(i, i - 1) for i in range(count - step, count)]
-        )
-    return part(place) + up.astype(F32) + down.astype(F32)
-
-
 SWAP = [(0, 1), (1, 0)]
 DIAGONAL = [(0, 3), (3, 0), (1, 2), (2, 1)]
-
-
-def plane_gather(block):
-    half = block.shape[0] // 2
-    by_x, by_y = lax.ppermute(block, "x", SWAP), lax.ppermute(block, "y", SWAP)
-    by_both = jnp.concatenate(
-        [lax.ppermute(by_x[:half], "y", SWAP), lax.ppermute(by_y[half:], "x", SWAP)], axis=0
-    )
-    chips = [block, by_y, by_x, by_both]
-    others = [lax.ppermute(a, "c", SWAP) for a in chips]
-    order = [chips[0], chips[1], others[0], others[1], chips[2], chips[3], others[2], others[3]]
-    return jnp.stack(order)
 
 
 def plane_scatter(parts):
     low = parts.astype(BF16)
     sums = []
-    for chip, (near, far) in enumerate(((0, 2), (1, 3), (4, 6), (5, 7))):
+    for near, far in ((0, 2), (1, 3), (4, 6), (5, 7)):
         sums.append(parts[near].astype(F32) + lax.ppermute(low[far], "c", SWAP).astype(F32))
     by_y = lax.ppermute(sums[1].astype(BF16), "y", SWAP)
     by_x = lax.ppermute(sums[2].astype(BF16), "x", SWAP)
@@ -121,16 +74,564 @@
     return sums[0] + by_x.astype(F32) + by_y.astype(F32) + by_both.astype(F32)
 
 
-def place_in_plane():
+X_BIT, C_BIT, Y_BIT = 4, 2, 1
+VMEM_MOST = 56 * 2**20
+
+
+def other(bits):
+    flips = {"x": bits // 4, "c": bits // 2 % 2, "y": bits % 2}
+    return {name: 1 - lax.axis_index(name) for name, flip in flips.items() if flip}
+
+
+def greet(partners):
+    barrier = pltpu.get_barrier_semaphore()
+    for partner in partners:
+        pl.semaphore_signal(barrier, inc=1, device_id=partner)
+    pl.semaphore_wait(barrier, len(partners))
+
+
+def send(source, target, send_sem, recv_sem, device):
+    return pltpu.make_async_remote_copy(
+        src_ref=source, dst_ref=target, send_sem=send_sem, recv_sem=recv_sem, device_id=device
+    )
+
+
+def gathering(chunks, in_ref, out_ref, send_sem, recv_sem):
+    rows = in_ref.shape[0] // chunks
+    both = X_BIT | Y_BIT
+
+    def to(slot, k, bits, source):
+        part = pl.ds(k * rows, rows)
+        return send(
+            source.at[part], out_ref.at[slot, part], send_sem.at[slot, k], recv_sem.at[slot, k], other(bits)
+        )
+
+    def own():
+        for k in range(chunks):
+            to(X_BIT, k, X_BIT, in_ref).start()
+            to(Y_BIT, k, Y_BIT, in_ref).start()
+        for k in range(chunks):
+            to(C_BIT, k, C_BIT, in_ref).start()
+
+    def relay(first, last):
+        for k in range(first, last):
+            to(X_BIT, k, X_BIT, in_ref).wait_recv()
+            if k < chunks // 2:
+                to(both, k, Y_BIT, out_ref.at[X_BIT]).start()
+            to(X_BIT | C_BIT, k, C_BIT, out_ref.at[X_BIT]).start()
+            to(Y_BIT, k, Y_BIT, in_ref).wait_recv()
+            if k >= chunks // 2:
+                to(both, k, X_BIT, out_ref.at[Y_BIT]).start()
+            to(Y_BIT | C_BIT, k, C_BIT, out_ref.at[Y_BIT]).start()
+
+    def far():
+        for k in range(chunks):
+            to(both, k, Y_BIT, in_ref).wait_recv()
+            to(7, k, C_BIT, out_ref.at[both]).start()
+
+    def end():
+        for slot in range(1, 8):
+            for k in range(chunks):
+                copy = to(slot, k, slot, in_ref)
+                if slot & C_BIT:
+                    copy.wait_recv()
+                copy.wait_send()
+
+    return own, relay, far, end
+
+
+def gather_kernel(chunks, in_ref, out_ref, own_sem, send_sem, recv_sem):
+    greet([other(C_BIT), other(X_BIT), other(Y_BIT)])
+    copy = pltpu.make_async_copy(in_ref, out_ref.at[0], own_sem)
+    copy.start()
+    own, relay, far, end = gathering(chunks, in_ref, out_ref, send_sem, recv_sem)
+    own()
+    relay(0, chunks)
+    far()
+    copy.wait()
+    end()
+
+
+def plane_gather(block, name, chunks=4):
+    return pl.pallas_call(
+        functools.partial(gather_kernel, chunks),
+        out_shape=jax.ShapeDtypeStruct((8, *block.shape), block.dtype),
+        in_specs=[pl.BlockSpec(memory_space=pl.ANY)],
+        out_specs=pl.BlockSpec(memory_space=pl.ANY),
+        scratch_shapes=[
+            pltpu.SemaphoreType.DMA,
+            pltpu.SemaphoreType.DMA((8, chunks)),
+            pltpu.SemaphoreType.DMA((8, chunks)),
+        ],
+        compiler_params=pltpu.CompilerParams(collective_id=name, has_side_effects=True),
+        cost_estimate=pl.CostEstimate(flops=0, bytes_accessed=160 * 2**20, transcendentals=0),
+    )(block)
+
+
+def matmul_scatter_kernel(flip, wide, *refs):
+    left_ref, right_ref, *more_ref, out_ref, part_ref, near_ref, sum_ref, far_ref = refs[:-4]
+    near_send, near_recv, chip_send, chip_recv = refs[-4:]
+    tokens = out_ref.shape[0]
+    step = 256
+    greet([other(C_BIT), other(X_BIT), other(Y_BIT), other(X_BIT | Y_BIT)])
+
+    def product(slot, target):
+        @pl.loop(0, wide // step)
+        def _(i):
+            at = pl.ds(pl.multiple_of(i * step, step), step)
+            rows = left_ref[slot * tokens : (slot + 1) * tokens, :]
+            if flip:
+                got = contract(rows, right_ref[at, :], 1, 1)
+            else:
+                got = contract(rows, right_ref[:, at], 1, 0)
+            target[:, at] = got.astype(BF16)
+
+        for ref in more_ref:
+            target[:, wide:] = ref[slot * tokens : (slot + 1) * tokens, :].astype(BF16)
+
+    chips = (X_BIT | Y_BIT, X_BIT, Y_BIT, 0)
+    near, far = [], []
+    for i, chip in enumerate(chips):
+        product(chip | C_BIT, part_ref.at[i])
+        copy = send(part_ref.at[i], near_ref.at[i], near_send.at[i], near_recv.at[i], other(C_BIT))
+        copy.start()
+        near.append(copy)
+        product(chip, sum_ref.at[i])
+        copy.wait_recv()
+
+        @pl.loop(0, tokens // 32)
+        def _(r):
+            at = pl.ds(pl.multiple_of(r * 32, 32), 32)
+            total = sum_ref[i, at, :].astype(F32) + near_ref[i, at, :].astype(F32)
+            if chip:
+                sum_ref[i, at, :] = total.astype(BF16)
+            else:
+                out_ref[at, :] = total
+
+        if chip:
+            copy = send(sum_ref.at[i], far_ref.at[i], chip_send.at[i], chip_recv.at[i], other(chip))
+            copy.start()
+            far.append(copy)
+    for copy in far:
+        copy.wait_recv()
+
+    @pl.loop(0, tokens // 32)
+    def _(r):
+        at = pl.ds(pl.multiple_of(r * 32, 32), 32)
+        total = out_ref[at, :]
+        for i in range(3):
+            total = total + far_ref[i, at, :].astype(F32)
+        out_ref[at, :] = total
+
+    for copy in (*near, *far):
+        copy.wait_send()
+
+
+def matmul_scatter(left, right, name, flip=False, *more):
+    tokens, depth = left.shape[0] // 8, left.shape[1]
+    wide = right.shape[0 if flip else 1]
+    full = wide + sum(array.shape[1] for array in more)
+    block = pltpu.VMEM((4, tokens, full), BF16)
+    return pl.pallas_call(
+        functools.partial(matmul_scatter_kernel, flip, wide),
+        out_shape=jax.ShapeDtypeStruct((tokens, full), F32),
+        in_specs=[pl.BlockSpec(memory_space=pltpu.VMEM)] * (2 + len(more)),
+        out_specs=pl.BlockSpec(memory_space=pltpu.VMEM),
+        scratch_shapes=[
+            block,
+            block,
+            block,
+            pltpu.VMEM((3, tokens, full), BF16),
+            *[pltpu.SemaphoreType.DMA((4,))] * 2,
+            *[pltpu.SemaphoreType.DMA((3,))] * 2,
+        ],
+        compiler_params=pltpu.CompilerParams(
+            collective_id=name, has_side_effects=True, vmem_limit_bytes=VMEM_MOST
+        ),
+        cost_estimate=pl.CostEstimate(
+            flops=16 * tokens * wide * depth, bytes_accessed=160 * 2**20, transcendentals=0
+        ),
+    )(left, right, *more)
+
+
+def in_plane():
     return 4 * lax.axis_index("x") + 2 * lax.axis_index("c") + lax.axis_index("y")
 
 
-def relabel(blocks):
-    place = place_in_plane()
-    full = jnp.zeros_like(blocks)
-    for i in range(8):
-        full = lax.dynamic_update_index_in_dim(full, blocks[i], place ^ i, 0)
-    return full
+def start_kernel(
+    count, chunks, first_ref, up_ref, out_ref, wide_ref, rows_ref,
+    first_all, up_line, out_line, up_far, out_far, wide_all, rows_all,
+    local_sem, line_send, line_recv, plane_send, plane_recv, far_send, far_recv, wide_send, wide_recv,
+    rows_send, rows_recv,
+):
+    f, y, me = lax.axis_index("f"), lax.axis_index("y"), in_plane()
+    half = count // 2
+    barrier = pltpu.get_barrier_semaphore()
+    for bits in range(1, 8):
+        pl.semaphore_signal(barrier, inc=1, device_id=other(bits))
+    lower, upper = f > 0, f < count - 1
+
+    @pl.when(lower)
+    def _():
+        pl.semaphore_signal(barrier, inc=1, device_id={"f": f - 1})
+
+    @pl.when(upper)
+    def _():
+        pl.semaphore_signal(barrier, inc=1, device_id={"f": f + 1})
+
+    pl.semaphore_wait(barrier, 7 + lower.astype(jnp.int32) + upper.astype(jnp.int32))
+
+    locals_ = [
+        pltpu.make_async_copy(source, target, local_sem.at[i])
+        for i, (source, target) in enumerate(
+            (
+                (first_ref, first_all.at[me, f]),
+                (up_ref, up_line.at[f]),
+                (out_ref, out_line.at[f]),
+                (wide_ref.at[me], wide_all.at[me]),
+                (rows_ref, rows_all.at[0]),
+            )
+        )
+    ]
+    for copy in locals_:
+        copy.start()
+
+    own = (first_ref, up_ref, out_ref)
+    lines = (first_all.at[me], up_line, out_line)
+    fars = (None, up_far, out_far)
+
+    def hop(i, j, up, source):
+        return send(
+            source, lines[i].at[j], line_send.at[i, 0 if up else 1, j], line_recv.at[i, j],
+            {"f": f + 1 if up else f - 1},
+        )
+
+    def line_own(i):
+        pl.when(upper)(lambda: hop(i, f, True, own[i]).start())
+        pl.when(lower)(lambda: hop(i, f, False, own[i]).start())
+
+    def line_step(i, step, then):
+        @pl.when(f - step >= 0)
+        def _():
+            j = f - step
+            hop(i, j, True, lines[i].at[j]).wait_recv()
+            pl.when(upper)(lambda: hop(i, j, True, lines[i].at[j]).start())
+            then(j, lines[i].at[j])
+
+        @pl.when(f + step <= count - 1)
+        def _():
+            j = f + step
+            hop(i, j, False, lines[i].at[j]).wait_recv()
+            pl.when(lower)(lambda: hop(i, j, False, lines[i].at[j]).start())
+            then(j, lines[i].at[j])
+
+    def line_end(i):
+        for j in range(count):
+            pl.when(upper & (f >= j))(lambda: hop(i, j, True, own[i]).wait_send())
+            pl.when(lower & (f <= j))(lambda: hop(i, j, False, own[i]).wait_send())
+
+    def spread(slot, bits, j, source):
+        return send(
+            source, first_all.at[me ^ bits ^ slot, j], plane_send.at[slot, j], plane_recv.at[slot, j], other(bits)
+        )
+
+    def to_plane(j, source):
+        spread(X_BIT, X_BIT, j, source).start()
+        spread(Y_BIT, Y_BIT, j, source).start()
+        spread(C_BIT, C_BIT, j, source).start()
+
+    def relay(j):
+        by_x, by_y = first_all.at[me ^ X_BIT, j], first_all.at[me ^ Y_BIT, j]
+        spread(X_BIT, X_BIT, j, by_x).wait_recv()
+        pl.when(j % 2 == 0)(lambda: spread(5, Y_BIT, j, by_x).start())
+        spread(6, C_BIT, j, by_x).start()
+        spread(Y_BIT, Y_BIT, j, by_y).wait_recv()
+        pl.when(j % 2 == 1)(lambda: spread(5, X_BIT, j, by_y).start())
+        spread(3, C_BIT, j, by_y).start()
+
+    def relay_far(j):
+        by_both = first_all.at[me ^ 5, j]
+        spread(5, Y_BIT, j, by_both).wait_recv()
+        spread(7, C_BIT, j, by_both).start()
+
+    def in_order(do):
+        do(f)
+        for step in range(1, count):
+            pl.when(f - step >= 0)(lambda: do(f - step))
+            pl.when(f + step <= count - 1)(lambda: do(f + step))
+
+    def across(i, slot, source):
+        return send(source, fars[i].at[slot], far_send.at[i, slot], far_recv.at[i, slot], other(Y_BIT))
+
+    def swap(i):
+        return lambda j, source: pl.when(j // half != y)(lambda: across(i, j % half, source).start())
+
+    def wide(bits):
+        return send(wide_ref.at[me ^ bits], wide_all.at[me], wide_send.at[bits], wide_recv.at[bits], other(bits))
+
+    rows_own, rows_relay, rows_far, rows_end = gathering(
+        chunks, rows_ref, rows_all, rows_send, rows_recv
+    )
+    line_own(0)
+    to_plane(f, first_ref)
+    for step in range(1, count):
+        line_step(0, step, to_plane)
+        if step == min(2, count - 1):
+            line_own(1)
+            line_own(2)
+    in_order(relay)
+    for i in (1, 2):
+        swap(i)(f, own[i])
+    for bits in (5, 7, 4, 6, 1, 3, 2):
+        wide(bits).start()
+    rows_own()
+    for step in range(1, count):
+        line_step(1, step, swap(1))
+        line_step(2, step, swap(2))
+        if step == 1:
+            in_order(relay_far)
+        if step == count - 2:
+            rows_relay(0, chunks // 2)
+    rows_relay(chunks // 2, chunks)
+    rows_far()
+    for copy in locals_:
+        copy.wait()
+    rows_end()
+    for i in range(3):
+        line_end(i)
+    for slot in range(1, 8):
+        for j in range(count):
+            copy = spread(slot, slot, j, first_ref)
+            if slot & C_BIT:
+                copy.wait_recv()
+            copy.wait_send()
+    for i in (1, 2):
+        for slot in range(half):
+            copy = across(i, slot, own[i])
+            copy.wait_recv()
+            copy.wait_send()
+    for bits in range(1, 8):
+        wide(bits).wait_recv()
+        wide(bits).wait_send()
+
+
+def start(first, up, out, wide, rows, count, name, chunks=4):
+    half = count // 2
+    any_space = pl.BlockSpec(memory_space=pl.ANY)
+    dma = pltpu.SemaphoreType.DMA
+    return pl.pallas_call(
+        functools.partial(start_kernel, count, chunks),
+        out_shape=[
+            jax.ShapeDtypeStruct((8, count, *first.shape), BF16),
+            jax.ShapeDtypeStruct((count, *up.shape), BF16),
+            jax.ShapeDtypeStruct((count, *out.shape), BF16),
+            jax.ShapeDtypeStruct((half, *up.shape), BF16),
+            jax.ShapeDtypeStruct((half, *out.shape), BF16),
+            jax.ShapeDtypeStruct(wide.shape, BF16),
+            jax.ShapeDtypeStruct((8, *rows.shape), BF16),
+        ],
+        in_specs=[any_space] * 5,
+        out_specs=[any_space] * 7,
+        scratch_shapes=[
+            dma((5,)),
+            dma((3, 2, count)), dma((3, count)),
+            dma((8, count)), dma((8, count)),
+            dma((3, half)), dma((3, half)),
+            dma((8,)), dma((8,)),
+            dma((8, chunks)), dma((8, chunks)),
+        ],
+        compiler_params=pltpu.CompilerParams(collective_id=name, has_side_effects=True),
+        cost_estimate=pl.CostEstimate(flops=0, bytes_accessed=240 * 2**20, transcendentals=0),
+    )(first, up, out, wide, rows)
+
+
+def end_kernel(
+    count, last_ref, up_ref, out_ref, wide_ref,
+    last_sum, up_sum, out_sum, wide_all,
+    total_ref, near_ref, chip_ref, far_ref, *rest,
+):
+    grown = [rest[4 * i : 4 * i + 4] for i in range(3)]
+    local_sem, near_send, near_recv, chip_send, chip_recv, line_send, line_recv, wide_send, wide_recv = rest[12:]
+    f, me = lax.axis_index("f"), in_plane()
+    barrier = pltpu.get_barrier_semaphore()
+    for bits in range(1, 8):
+        pl.semaphore_signal(barrier, inc=1, device_id=other(bits))
+    lower, upper = f > 0, f < count - 1
+
+    @pl.when(lower)
+    def _():
+        pl.semaphore_signal(barrier, inc=1, device_id={"f": f - 1})
+
+    @pl.when(upper)
+    def _():
+        pl.semaphore_signal(barrier, inc=1, device_id={"f": f + 1})
+
+    pl.semaphore_wait(barrier, 7 + lower.astype(jnp.int32) + upper.astype(jnp.int32))
+
+    def rows(ref_rows, do):
+        size = 16 if ref_rows % 32 else 32
+
+        @pl.loop(0, ref_rows // size)
+        def _(r):
+            do(pl.ds(pl.multiple_of(r * size, size), size))
+
+    parts = (total_ref, up_ref, out_ref)
+    sums = (last_sum, up_sum, out_sum)
+
+    def hop(i, d, up):
+        outgoing, incoming = grown[i][0 if up else 2], grown[i][1 if up else 3]
+        way = 0 if up else 1
+        return send(
+            outgoing.at[d], incoming.at[d], line_send.at[i, way, d], line_recv.at[i, way, d],
+            {"f": f + 1 if up else f - 1},
+        )
+
+    def pass_on(i, d, up):
+        outgoing, incoming = grown[i][0 if up else 2], grown[i][1 if up else 3]
+        behind = lower if up else upper
+
+        @pl.when((d > f) if up else (d < f))
+        def _():
+            @pl.when(behind)
+            def _():
+                hop(i, d, up).wait_recv()
+
+                def add(at):
+                    total = parts[i][d, at, :].astype(F32) + incoming[d, at, :].astype(F32)
+                    outgoing[d, at, :] = total.astype(BF16)
+
+                rows(parts[i].shape[1], add)
+
+            @pl.when(jnp.logical_not(behind))
+            def _():
+                def keep(at):
+                    outgoing[d, at, :] = parts[i][d, at, :].astype(BF16)
+
+                rows(parts[i].shape[1], keep)
+
+            hop(i, d, up).start()
+
+    def line_step(i, step):
+        pass_on(i, count - step, True)
+        pass_on(i, step - 1, False)
+
+    def line_end(i):
+        def keep(at):
+            sums[i][at, :] = parts[i][f, at, :].astype(F32)
+
+        rows(parts[i].shape[1], keep)
+        for up, there in ((True, lower), (False, upper)):
+            incoming = grown[i][1 if up else 3]
+
+            @pl.when(there)
+            def _(up=up, incoming=incoming):
+                hop(i, f, up).wait_recv()
+
+                def add(at):
+                    sums[i][at, :] = sums[i][at, :] + incoming[f, at, :].astype(F32)
+
+                rows(parts[i].shape[1], add)
+
+        for d in range(count):
+            pl.when(f < d)(lambda: hop(i, d, True).wait_send())
+            pl.when(f > d)(lambda: hop(i, d, False).wait_send())
+
+    def wide(bits):
+        return send(wide_ref.at[me ^ bits], wide_all.at[me], wide_send.at[bits], wide_recv.at[bits], other(bits))
+
+    chips = (X_BIT | Y_BIT, X_BIT, Y_BIT, 0)
+
+    def near(i):
+        return send(
+            last_ref.at[me ^ (chips[i] | C_BIT)], near_ref.at[i], near_send.at[i], near_recv.at[i], other(C_BIT)
+        )
+
+    def far(i):
+        return send(chip_ref.at[i], far_ref.at[i], chip_send.at[i], chip_recv.at[i], other(chips[i]))
+
+    local = pltpu.make_async_copy(wide_ref.at[me], wide_all.at[me], local_sem)
+    local.start()
+    for i in range(4):
+        near(i).start()
+    line_step(1, 1)
+    line_step(2, 1)
+    for i in range(4):
+        near(i).wait_recv()
+        for j in range(count):
+
+            def add(at, i=i, j=j):
+                total = last_ref[me ^ chips[i], j, at, :].astype(F32) + near_ref[i, j, at, :].astype(F32)
+                if i < 3:
+                    chip_ref[i, j, at, :] = total.astype(BF16)
+                else:
+                    total_ref[j, at, :] = total
+
+            rows(total_ref.shape[1], add)
+        if i < 3:
+            far(i).start()
+    for bits in (5, 7, 4, 6, 1, 3, 2):
+        wide(bits).start()
+    for step in range(2, count):
+        line_step(1, step)
+        line_step(2, step)
+    for i in range(3):
+        far(i).wait_recv()
+    for j in range(count):
+
+        def add(at, j=j):
+            total = total_ref[j, at, :]
+            for i in range(3):
+                total = total + far_ref[i, j, at, :].astype(F32)
+            total_ref[j, at, :] = total
+
+        rows(total_ref.shape[1], add)
+    for step in range(1, count):
+        line_step(0, step)
+    for i in (1, 2, 0):
+        line_end(i)
+    local.wait()
+    for i in range(4):
+        near(i).wait_send()
+    for i in range(3):
+        far(i).wait_send()
+    for bits in range(1, 8):
+        wide(bits).wait_recv()
+        wide(bits).wait_send()
+
+
+def end(last, up, out, wide, count, name):
+    any_space, vmem = pl.BlockSpec(memory_space=pl.ANY), pl.BlockSpec(memory_space=pltpu.VMEM)
+    dma = pltpu.SemaphoreType.DMA
+    body = last.shape[1:]
+    return pl.pallas_call(
+        functools.partial(end_kernel, count),
+        out_shape=[
+            jax.ShapeDtypeStruct(body[1:], F32),
+            jax.ShapeDtypeStruct(up.shape[1:], F32),
+            jax.ShapeDtypeStruct(out.shape[1:], F32),
+            jax.ShapeDtypeStruct(wide.shape, BF16),
+        ],
+        in_specs=[vmem, vmem, vmem, any_space],
+        out_specs=[vmem, vmem, vmem, any_space],
+        scratch_shapes=[
+            pltpu.VMEM(body, F32),
+            pltpu.VMEM((4, *body), BF16),
+            pltpu.VMEM((3, *body), BF16),
+            pltpu.VMEM((3, *body), BF16),
+            *[pltpu.VMEM(body, BF16)] * 4,
+            *[pltpu.VMEM(up.shape, BF16)] * 4,
+            *[pltpu.VMEM(out.shape, BF16)] * 4,
+            dma,
+            dma((4,)), dma((4,)),
+            dma((3,)), dma((3,)),
+            dma((3, 2, count)), dma((3, 2, count)),
+            dma((8,)), dma((8,)),
+        ],
+        compiler_params=pltpu.CompilerParams(
+            collective_id=name, has_side_effects=True, vmem_limit_bytes=VMEM_MOST
+        ),
+        cost_estimate=pl.CostEstimate(flops=0, bytes_accessed=240 * 2**20, transcendentals=0),
+    )(last, up, out, wide)
 
 
 def by_owner(array, axis, count, f_first):
@@ -212,11 +713,26 @@
         marks.append(marks[-1] + piece.shape[0])
     total = -(-marks[-1] // 32) * 32
     first = jnp.pad(jnp.concatenate(pieces), ((0, total - marks[-1]), (0, 0)))
-    first = line_gather(first, count)
-    first = plane_gather(first.reshape(count * total, 128)).reshape(8, count, total, 128)
+
+    def unit_blocks(weight):
+        blocks = by_owner(weight.astype(BF16), 1, count, f_first)
+        blocks = blocks.transpose(1, 2, 0, 3).reshape(8, -1, mine)
+        return jnp.pad(blocks, ((0, 0), (0, 0), (0, padded - mine)))
+
+    both = jnp.concatenate([unit_blocks(gate_weight), unit_blocks(up_weight)], axis=2)
+    first, up_line, out_line, up_far, out_far, both, g_all = start(
+        first, latent_up.astype(BF16), out_proj.astype(BF16), both, out_cotangent, count, 0
+    )
+    g_all = g_all.reshape(8 * tokens, width)
+    both = lax.all_gather(both, "f", axis=0)
+    both = from_owner(both, 0, f_first)
+    ff_down = lax.all_gather(after(down_weight.astype(BF16), up_line, both), "f", axis=0)
+    ff_down = jnp.pad(ff_down.reshape(mine, width), ((0, padded - mine), (0, 0)))
+
     lengths = lax.dynamic_index_in_dim(first[:, :, marks[6], :3], place, 1, keepdims=False)
-    lengths = lengths.astype(jnp.int32)
-    first = relabel(first)
+    lengths = jnp.stack(
+        [lax.dynamic_index_in_dim(lengths, in_plane() ^ i, 0, keepdims=False) for i in range(8)]
+    ).astype(jnp.int32)
     owned = first.transpose(1, 0, 2, 3)
 
     def piece_of(i):
@@ -237,39 +753,18 @@
 
     gain_one, gain_two = gain_of(4).astype(F32), gain_of(5).astype(F32)
 
-    up_line = line_gather(after(latent_up.astype(BF16), first), count)
-    out_line = line_gather(after(out_proj.astype(BF16), first), count)
-    up_heads = up_line.transpose(1, 0, 2).reshape(half_rank, 4, HEAD_DIM)
+    half = count // 2
     per_head = count // 4
-    out_heads = out_line.reshape(4, per_head, -1, width)
-
-    def own_heads(array, axis):
-        return lax.dynamic_slice_in_dim(array, 2 * y, 2, axis)
-
-    def other_heads(array, axis):
-        return lax.dynamic_slice_in_dim(array, 2 - 2 * y, 2, axis)
-
-    def join(own, other, axis):
-        low = jnp.where(y == 0, own, other)
-        high = jnp.where(y == 0, other, own)
+
+    def join(own, other_part, axis):
+        low = jnp.where(y == 0, own, other_part)
+        high = jnp.where(y == 0, other_part, own)
         return jnp.stack([low, high], axis)
 
-    up_full = join(own_heads(up_heads, 1), lax.ppermute(other_heads(up_heads, 1), "y", SWAP), 0)
-    up_full = up_full.reshape(rank, 2 * HEAD_DIM)
-    out_full = join(own_heads(out_heads, 0), lax.ppermute(other_heads(out_heads, 0), "y", SWAP), 2)
-    out_full = out_full.reshape(2 * HEAD_DIM, width)
-
-    def unit_blocks(weight):
-        blocks = by_owner(weight.astype(BF16), 1, count, f_first)
-        blocks = blocks.transpose(1, 2, 0, 3).reshape(8, -1, mine)
-        return jnp.pad(blocks, ((0, 0), (0, 0), (0, padded - mine)))
-
-    both = jnp.concatenate([unit_blocks(gate_weight), unit_blocks(up_weight)], axis=2)
-    both = lax.all_to_all(both, ("x", "c", "y"), 0, 0, tiled=True)
-    both = line_gather(after(both, up_line, out_line), count)
-    both = from_owner(both, 0, f_first)
-    ff_down = line_gather(after(down_weight.astype(BF16), up_line, out_line), count)
-    ff_down = jnp.pad(ff_down.reshape(mine, width), ((0, padded - mine), (0, 0)))
+    up_own = lax.dynamic_slice_in_dim(up_line, half * y, half, 0)
+    out_own = lax.dynamic_slice_in_dim(out_line, half * y, half, 0)
+    up_full = join(up_own, up_far, 0).transpose(0, 2, 1, 3).reshape(rank, 2 * HEAD_DIM)
+    out_full = join(out_own, out_far, 1).reshape(2 * HEAD_DIM, width)
 
     inputs = block_input.astype(F32)
     rms_one = lax.rsqrt(jnp.mean(inputs * inputs, axis=-1, keepdims=True) + EPS)
@@ -282,11 +777,10 @@
     cosine, sine = rope_tables(position, HEAD_DIM)
     k_own = rotate(shared, cosine[0], sine[0]).astype(BF16)
 
-    parcel = plane_gather(jnp.concatenate([latent_n, k_own, shared.astype(BF16)], axis=1))
+    parcel = plane_gather(jnp.concatenate([latent_n, k_own, shared.astype(BF16)], axis=1), 1)
     lat_all = parcel[:, :, :rank].reshape(8 * tokens, rank)
     k_rot = parcel[:, :, rank : rank + HEAD_DIM]
     values = parcel[:, :, rank + HEAD_DIM :]
-    g_all = plane_gather(after(out_cotangent, parcel)).reshape(8 * tokens, width)
     queries = jnp.dot(lat_all, up_full, preferred_element_type=F32)
     wide_cos, wide_sin = cosine[:, :, None], sine[:, :, None]
     q_rot = rotate(queries.reshape(8, tokens, 2, HEAD_DIM), wide_cos, wide_sin).astype(BF16)
@@ -296,13 +790,12 @@
     probs = jnp.exp(scores - log_total)
     attended = jnp.einsum("bhts,bsd->bthd", probs.astype(BF16), values, preferred_element_type=F32)
     attended = attended.reshape(8 * tokens, 2 * HEAD_DIM).astype(BF16)
-    branch = jnp.dot(attended, out_full, preferred_element_type=F32)
-    branch = plane_scatter(branch.reshape(8, tokens, width))
+    branch = matmul_scatter(attended, out_full, 2)
 
     middle = inputs + branch
     rms_two = lax.rsqrt(jnp.mean(middle * middle, axis=-1, keepdims=True) + EPS)
     normed_two = (middle * rms_two * gain_two).astype(BF16)
-    two_all = plane_gather(normed_two).reshape(8 * tokens, width)
+    two_all = plane_gather(normed_two, 3).reshape(8 * tokens, width)
     gate_up = jnp.dot(two_all, both, preferred_element_type=F32)
     gate, upval = gate_up[:, :padded], gate_up[:, padded:]
     sigma = jax.nn.sigmoid(gate)
@@ -312,23 +805,18 @@
     d_gate = (d_hidden * upval * sigma * (1.0 + gate * (1.0 - sigma))).astype(BF16)
     d_up = (d_hidden * gate * sigma).astype(BF16)
     d_both = jnp.concatenate([d_gate, d_up], axis=1)
-    d_two = plane_scatter(contract(d_both, both, 1, 1).reshape(8, tokens, width))
+    d_two = matmul_scatter(d_both, both, 4, True)
 
     result = jnp.dot(hidden, ff_down, preferred_element_type=F32)
     result = plane_scatter(after(result.reshape(8, tokens, width), d_two))
     block_output = (middle + result).astype(BF16)
 
     both_grad = contract(two_all, d_both, 0, 0)
-    both_grad = line_scatter(by_owner(both_grad, 0, count, f_first), count)
-    both_grad = lax.all_to_all(both_grad.astype(BF16), ("x", "c", "y"), 0, 0, tiled=True)
-
-    def whole_rows(blocks):
-        blocks = blocks[:, :, :mine].astype(F32).reshape(8, -1, count, units)
-        return from_owner(blocks.transpose(2, 0, 1, 3), 1, f_first)
-
-    gate_grad, up_grad = whole_rows(both_grad[..., :padded]), whole_rows(both_grad[..., padded:])
+    both_grad = by_owner(both_grad.astype(BF16), 0, count, f_first)
+    both_grad = lax.psum_scatter(both_grad, "f", scatter_dimension=0)
+
     down_grad = contract(hidden, g_all, 0, 0)[:mine].reshape(count, units, width)
-    down_grad = line_scatter(down_grad, count)
+    down_grad = lax.psum_scatter(down_grad.astype(BF16), "f", scatter_dimension=0).astype(F32)
 
     upstream = out_cotangent.astype(F32)
     gain_two_part = jnp.sum(d_two * middle * rms_two, axis=0)
@@ -339,7 +827,7 @@
         - middle * (rms_two**3) * jnp.mean(scaled_two * middle, axis=-1, keepdims=True)
     )
 
-    d_branch = plane_gather(d_middle.astype(BF16)).reshape(8 * tokens, width)
+    d_branch = plane_gather(d_middle.astype(BF16), 5).reshape(8 * tokens, width)
     d_attended = contract(d_branch, out_full, 1, 1).astype(BF16)
     d_attended = d_attended.reshape(8, tokens, 2, HEAD_DIM)
     d_probs = jnp.einsum("bthd,bsd->bhts", d_attended, values, preferred_element_type=F32)
@@ -354,8 +842,7 @@
         "bhts,bthd->bsd", probs.astype(BF16), d_attended, preferred_element_type=F32
     )
     shared_part = unrotate(d_krot, cosine, sine) + value_part
-    lat_part = contract(d_queries, up_full, 1, 1).reshape(8, tokens, rank)
-    back = plane_scatter(jnp.concatenate([lat_part, shared_part], axis=2))
+    back = matmul_scatter(d_queries, up_full, 6, True, shared_part.reshape(8 * tokens, HEAD_DIM))
     d_lat_n, d_shared = back[:, :rank], back[:, rank:].astype(BF16)
 
     up_grad_heads = contract(lat_all, d_queries, 0, 0).reshape(2, half_rank, 2, HEAD_DIM)
@@ -367,9 +854,9 @@
         return own, lax.ppermute(other, "y", SWAP).astype(F32)
 
     up_line_grad = join(*swap_halves(up_grad_heads, 0), 1).reshape(half_rank, count, -1)
-    latent_up_grad = line_scatter(up_line_grad.transpose(1, 0, 2), count)
+    up_line_grad = up_line_grad.transpose(1, 0, 2).astype(BF16)
     out_line_grad = join(*swap_halves(out_grad_heads, 2), 0)
-    out_proj_grad = line_scatter(out_line_grad.reshape(count, -1, width), count)
+    out_line_grad = out_line_grad.reshape(count, -1, width).astype(BF16)
 
     gain_lat_part = jnp.sum(d_lat_n * latent * rms_lat, axis=0)
     scaled_lat = d_lat_n * gain_lat
@@ -410,8 +897,16 @@
         marks.append(marks[-1] + piece.shape[2])
     last_rows = -(-marks[-1] // 32) * 32
     last = jnp.pad(jnp.concatenate(pieces, axis=2), ((0, 0), (0, 0), (0, last_rows - marks[-1]), (0, 0)))
-    last = relabel(last.transpose(1, 0, 2, 3).astype(BF16))
-    last = line_scatter(plane_scatter(last), count)
+    last = last.transpose(1, 0, 2, 3).astype(BF16)
+    last, latent_up_grad, out_proj_grad, both_grad = end(
+        last, up_line_grad, out_line_grad, both_grad.astype(BF16), count, 7
+    )
+
+    def whole_rows(blocks):
+        blocks = blocks[:, :, :mine].astype(F32).reshape(8, -1, count, units)
+        return from_owner(blocks.transpose(2, 0, 1, 3), 1, f_first)
+
+    gate_grad, up_grad = whole_rows(both_grad[..., :padded]), whole_rows(both_grad[..., padded:])
     latent_down_grad = last[marks[0] : marks[1]].reshape(half_rank, columns)
     shared_kv_grad = last[marks[1] : marks[2]].reshape(2, kv_rows, 128).transpose(1, 0, 2)
     shared_kv_grad = shared_kv_grad.reshape(kv_rows, HEAD_DIM)

time: 1730 us -> 931 us (0.54); the launches traced: 1700 us -> 918 us
  local copies, waits for them, and re-layouts: 830 us -> 163 us
  Pallas kernels: 0 us -> 488 us
  waiting for transfers between devices: 304 us -> 34.2 us
  starting transfers between devices: 228 us -> 7.41 us
  other arithmetic: 176 us -> 79.2 us
  matrix products: 156 us -> 131 us
    dynamic_update_slice x21 -> x0, local copies, waits for them, and re-layouts: 554 us -> none  [the longest x16 548 us: relabel(): full = lax.dynamic_update_index_in_dim(full, blocks[i], place ^ i, 0)]
    pallas_call x0 -> x8, Pallas kernels: none -> 488 us  [the longest x3 160 us: matmul_scatter(): pl.pallas_call(functools.partial(matmul_scatter_kernel, flip, wide), out_...]
    ppermute x102 -> x0, waiting for transfers between devices: 194 us -> none  [the longest x15 55.8 us: line_gather(): lax.ppermute(downs[-1], 'f', [(i, i - 1) for i in range(1, count - step +...]
    ppermute x102 -> x0, starting transfers between devices: 193 us -> none  [the longest x15 58 us: line_scatter(): lax.ppermute(mine_up.astype(BF16), 'f', [(i, i + 1) for i in range(min(st...]
    unnamed x265 -> x163, local copies, waits for them, and re-layouts: 75.9 us -> 12.6 us
    slice x22 -> x1, local copies, waits for them, and re-layouts: 45.9 us -> 1.78 us  [per_device(): contract(hidden, g_all, 0, 0)[:mine].reshape(count, units, width)]
    ppermute x5 -> x1, waiting for transfers between devices: 63.4 us -> 22.6 us  [plane_scatter(): by_y = lax.ppermute(sums[1].astype(BF16), 'y', SWAP)]
    ppermute x5 -> x1, waiting for transfers between devices: 33.4 us -> 0.01 us  [plane_scatter(): by_both = lax.ppermute(sums[3].astype(BF16), ('x', 'y'), DIAGONAL)]
  transfers between devices with their start and end apart: 141 -> 13, of which waited for: 37 -> 3; matrix products, arithmetic and copies ran while one was open for 65% -> 31% of each run, Pallas kernels for 0% -> 29%
where the time goes in v2:
time: 931 us; the launch traced here: 918 us
  Pallas kernels  488 us (52%)
  local copies, waits for them, and re-layouts  163 us (18%)
  matrix products  131 us (14%)
  other arithmetic  79.2 us (9%)
  waiting for transfers between devices  34.2 us (4%)
  between operations  15.4 us (2%)
    pallas_call x3, Pallas kernels, matmul_scatter(): pl.pallas_call(functools.partial(matmul_scatter_kernel, flip, wide), out_...  160 us
    pallas_call x1, Pallas kernels, start(): pl.pallas_call(functools.partial(start_kernel, count, chunks), out_shape=...  115 us
    pallas_call x3, Pallas kernels, plane_gather(): pl.pallas_call(functools.partial(gather_kernel, chunks), out_shape=jax.Sh...  111 us
    pallas_call x1, Pallas kernels, end(): pl.pallas_call(functools.partial(end_kernel, count), out_shape=[jax.Shape...  102 us
    dot_general x10, matrix products, contract(): lax.dot_general(left, right, (((left_dim,), (right_dim,)), ((), ())), pre...  78 us
    concatenate x1, local copies, waits for them, and re-layouts, per_device(): jnp.concatenate(pieces, axis=2)  23.9 us
    ppermute x1, waiting for transfers between devices, plane_scatter(): by_y = lax.ppermute(sums[1].astype(BF16), 'y', SWAP)  22.6 us
    reshape x6, local copies, waits for them, and re-layouts, from_owner(): return array.reshape(*lead, 8 * count * part, *tail)  20.8 us
  transfers between devices with their start and end apart: 13, of which 3 were waited for; matrix products, arithmetic and copies ran while one was open for 31% of the time, Pallas kernels for 29%

profile of v2, /device:TPU:10, one launch (start us, length us, event | category | flops | bytes accessed | tf_op | source)
XLA Modules:
  0.0 918.3 jit_solution(10229541223193418914)
XLA Ops:
  27.5 115.0 %shard_map.220 = (bf16[8,4,672,128]{3,2,1,0:T(8,128)(2,1)}, bf16[4,512,256]{2,1,0:T(8,128)(2,1)}, bf16[4,128,2048]{2,1,0:T(8,128)(2,1)}, bf16[2,512,256]{2,1,0:T...) custom-call(bf16[672,128]{1,0:T(8,128)(2,1)} %pad.43.first_ref, ...), custom_call_target="tpu_custom_call" | custom-call | bytes 251658240 | tf_op jit(solution)/shard_map/pallas_call | solution.py:422
  152.9 8.9 copy.259
  161.8 8.1 reshape.415
  187.0 32.1 %shard_map.221 = bf16[8,256,1536]{2,1,0:T(8,128)(2,1)} custom-call(bf16[256,1536]{1,0:T(8,128)(2,1)} %pad_maximum_fusion.8.in_ref), custom_call_target="tpu_custom_call" | custom-call | bytes 167772160 | tf_op jit(solution)/shard_map/pallas_call | solution.py:156
  249.8 7.8 all-gather.5.cloned.1.call-done
  257.7 57.9 %shard_map.222 = f32[256,2048]{1,0:T(8,128)} custom-call(bf16[2048,512]{1,0:T(8,128)(2,1)} %bitcast.349, bf16[512,2048]{1,0:T(8,128)(2,1)} %bitcast.373), custom_call_target="tpu_custom_call" | custom-call | flops 4294967296 | bytes 167772160 | tf_op jit(solution)/shard_map/pallas_call | solution.py:235
  320.0 39.7 %shard_map.223 = bf16[8,256,2048]{2,1,0:T(8,128)(2,1)} custom-call(bf16[256,2048]{1,0:T(8,128)(2,1)} %multiply_convert_fusion.3.in_ref), custom_call_target="tpu_custom_call" | custom-call | bytes 167772160 | tf_op jit(solution)/shard_map/pallas_call | solution.py:156
  359.7 19.2 %fusion.86 = f32[2048,1536]{1,0:T(8,128)} fusion(bf16[2048,2048]{1,0:T(8,128)(2,1)} %bitcast.341, bf16[2048,1536]{1,0:T(8,128)(2,1)} %bitcast.397), kind=kOutput, calls=%fused_computation.206 | convolution fusion | flops 12884901888 | bytes 27262976 | tf_op jit(solution)/shard_map/dot_general | solution.py:799
  378.9 16.9 %multiply_convert_fusion.1 = (bf16[2048,768]{1,0:T(8,128)(2,1)S(1)}, bf16[2048,768]{1,0:T(8,128)(2,1)}, bf16[2048,768]{1,0:T(8,128)(2,1)S(1)}) fusion(f32[2048,1536]{1,0:T(8,128)} %fusion.86, bf16[2048,2048]{1,0:T(8,128)(2,1)} %bitcast.395, bf16[704,2048]{1,0:T(8,128)(2,1)} %all-gather.7.cloned.1.call-done), kind=kOutput, calls=%fused_computation.3 | convolution fusion | flops 6467616768 | bytes 33292288 | tf_op jit(solution)/shard_map/dot_general | solution.py:21
  395.8 11.4 %fusion.90 = bf16[768,2048]{1,0:T(8,128)(2,1)S(1)} fusion(bf16[2048,768]{1,0:T(8,128)(2,1)S(1)} %get-tuple-element.55, bf16[2048,2048]{1,0:T(8,128)(2,1)} %bitcast.396), kind=kOutput, calls=%fused_computation.210 | convolution fusion | flops 6442450944 | bytes 14680064 | tf_op jit(solution)/shard_map/dot_general | solution.py:21
  414.5 9.6 %fusion.10 = f32[2048,2048]{1,0:T(8,128)} fusion(bf16[2048,768]{1,0:T(8,128)(2,1)S(1)} %copy-done.78, bf16[704,2048]{1,0:T(8,128)(2,1)S(1)} %copy-done.76), kind=kOutput, calls=%fused_computation.35 | convolution fusion | flops 6442450944 | bytes 22806528 | tf_op jit(solution)/shard_map/dot_general | solution.py:810
  424.1 62.2 %shard_map.224 = f32[256,2048]{1,0:T(8,128)} custom-call(bf16[2048,1536]{1,0:T(8,128)(2,1)} %pad_maximum_fusion.refs_0_, bf16[2048,1536]{1,0:T(8,128)(2,1)} %bitcast.398), custom_call_target="tpu_custom_call" | custom-call | flops 12884901888 | bytes 167772160 | tf_op jit(solution)/shard_map/pallas_call | solution.py:235
  486.3 6.6 convert_element_type.283
  503.0 6.5 copy.191
  519.4 18.3 %convolution_convert_fusion = bf16[2048,1536]{1,0:T(8,128)(2,1)} fusion(bf16[2048,2048]{1,0:T(8,128)(2,1)} %bitcast.342, bf16[2048,768]{1,0:T(8,128)(2,1)S(1)} %copy-done.33, bf16[2048,768]{1,0:T(8,128)(2,1)S(1)} %copy-done.32), kind=kOutput, calls=%fused_computation | convolution fusion | flops 12900630528 | bytes 20971520 | tf_op jit(solution)/shard_map/dot_general | solution.py:21
  542.2 22.6 %collective-permute-done.4 = bf16[256,2048]{1,0:T(8,128)(2,1)} collective-permute-done((bf16[256,2048]{1,0:T(8,128)(2,1)}, bf16[256,2048]{1,0:T(8,128)(2,1)}, u32[]{:S(2)}, u32[]{:S(2)}) %collective-permute-start.4) | collective-permute-done | bytes 1048608 | tf_op jit(solution)/shard_map/ppermute | solution.py:71
  564.8 6.4 fusion.83
  571.3 38.9 %shard_map.225 = bf16[8,256,2048]{2,1,0:T(8,128)(2,1)} custom-call(bf16[256,2048]{1,0:T(8,128)(2,1)} %get-tuple-element.46.in_ref), custom_call_target="tpu_custom_call" | custom-call | bytes 167772160 | tf_op jit(solution)/shard_map/pallas_call | solution.py:156
  610.1 8.2 fusion.89
  622.2 6.2 convolution_convert_fusion.2
  668.2 40.0 %shard_map.226 = f32[256,1280]{1,0:T(8,128)} custom-call(bf16[2048,512]{1,0:T(8,128)(2,1)} %bitcast.352, bf16[1024,512]{1,0:T(8,128)(2,1)} %bitcast.367, f32[2048,256]{1,0:T(8,128)} %bitcast.399), custom_call_target="tpu_custom_call" | custom-call | flops 2147483648 | bytes 167772160 | tf_op jit(solution)/shard_map/pallas_call | solution.py:235
  720.4 7.7 reshape.427
  737.0 23.9 %concatenate.41 = bf16[4,8,646,128]{3,2,0,1:T(8,128)(2,1)} concatenate(bf16[4,8,512,128]{3,2,0,1:T(8,128)(2,1)} %bitcast.338, bf16[4,8,128,128]{3,2,0,1:T(8,128)(2,1)} %bitcast.372, bf16[4,8,4,128]{3,2,0,1:T(4,128)(2,1)S(1)} %broadcast_in_dim.98, bf16[4,8,1,128]{3,2,0,1:T(2,128)(2,1)S(1)} %copy.189, bf16[4,8,1,128]{3,2,0,1:T(2,128)(2,1)S(1)} %copy.190), dimensions={2} | concatenate | bytes 10584064 | tf_op jit(solution)/shard_map/concatenate | solution.py:899
  777.7 102.0 %shard_map.227 = (f32[672,128]{1,0:T(8,128)}, f32[512,256]{1,0:T(8,128)}, f32[128,2048]{1,0:T(8,128)}, bf16[8,64,1536]{2,1,0:T(8,128)(2,1)}) custom-call(bf16[8,4,672,128]{3,2,1,0:T(8,128)(2,1)} %pad_bitcast_fusion.last_ref, bf16[4,512,256]{2,1,0:T(8,128)(2,1)} %bitcast.360, bf16[4,128,2048]{2,1,0:T(8,128)(2,1)} %bitcast.340, bf16[8,64,1536]{2,1,0:T(8,128)(2,1)} %bitcast.377), custom_call_target="tpu_custom_call" | custom-call | bytes 251658240 | tf_op jit(solution)/shard_map/pallas_call | solution.py:606
  (325 shorter events, 226.7 us)
Async XLA Ops:
  7.2 250.4 %all-gather.5.cloned.1.call-start = ((), (), s32[]{:S(2)}) async-start(), calls=%async_computation.4 | async-start | bytes 7864320 | tf_op jit(solution)/shard_map/all_gather | solution.py:727
  142.6 236.3 %all-gather.7.cloned.1.call-start = ((), (), s32[]{:S(2)}) async-start(), calls=%async_computation.5 | async-start | bytes 3604480 | tf_op jit(solution)/shard_map/all_gather | solution.py:729
  150.9 33.5 %copy-start.53 = (f32[2048]{0:T(1024)}, f32[2048]{0:T(1024)S(1)}, u32[]{:S(2)}) copy-start(f32[2048]{0:T(1024)S(1)} %reshape.443) | copy-start | bytes 24580
  177.1 52.2 %copy-start.9 = (f32[8,256,128]{1,2,0:T(8,128)}, f32[8,256,128]{1,2,0:T(8,128)S(1)}, u32[]{:S(2)}) copy-start(f32[8,256,128]{1,2,0:T(8,128)S(1)} %copy.167) | copy-start | bytes 3145732
  187.0 32.1 %copy-start.52 = (bf16[2,512,256]{2,1,0:T(8,128)(2,1)S(1)}, bf16[2,512,256]{2,1,0:T(8,128)(2,1)}, u32[]{:S(2)}) copy-start(bf16[2,512,256]{2,1,0:T(8,128)(2,1)} %get-tuple-element.27) | copy-start | bytes 1572868
  248.8 69.3 %copy-start.55 = (f32[2048]{0:T(1024)}, f32[2048]{0:T(1024)S(1)}, u32[]{:S(2)}) copy-start(f32[2048]{0:T(1024)S(1)} %reshape.444) | copy-start | bytes 24580
  257.6 517.7 %reduce-scatter.5.cloned.1.call-start = ((), (), s32[]{:S(2)}) async-start(), calls=%async_computation.3 | async-start | bytes 3604480 | tf_op jit(solution)/shard_map/reduce_scatter | solution.py:819
  409.1 368.6 %reduce-scatter.3.cloned.1.call-start = ((), (), s32[]{:S(2)}) async-start(), calls=%async_computation.2 | async-start | bytes 7864320 | tf_op jit(solution)/shard_map/reduce_scatter | solution.py:816
  495.1 14.9 %collective-permute-start.1 = (bf16[256,2048]{1,0:T(8,128)(2,1)}, bf16[256,2048]{1,0:T(8,128)(2,1)S(1)}, u32[]{:S(2)}, u32[]{:S(2)}) collective-permute-start(bf16[256,2048]{1,0:T(8,128)(2,1)} %get-tuple-element.59), channel_id=1, source_target_pairs={{0,2},{2,0},{1,3},{3,1},{4,6},{6,4},{5,7},{7,5},{8,10},{10,8},{9,1... | collective-permute-start | bytes 3145736 | tf_op jit(solution)/shard_map/ppermute | solution.py:70
  495.1 14.8 %collective-permute-start.3 = (bf16[256,2048]{1,0:T(8,128)(2,1)}, bf16[256,2048]{1,0:T(8,128)(2,1)}, u32[]{:S(2)}, u32[]{:S(2)}) collective-permute-start(bf16[256,2048]{1,0:T(8,128)(2,1)} %get-tuple-element.58), channel_id=1, source_target_pairs={{0,2},{2,0},{1,3},{3,1},{4,6},{6,4},{5,7},{7,5},{8,10},{10,8},{9,1... | collective-permute-start | bytes 3145736 | tf_op jit(solution)/shard_map/ppermute | solution.py:70
  495.6 14.4 %collective-permute-start.5 = (bf16[256,2048]{1,0:T(8,128)(2,1)}, bf16[256,2048]{1,0:T(8,128)(2,1)}, u32[]{:S(2)}, u32[]{:S(2)}) collective-permute-start(bf16[256,2048]{1,0:T(8,128)(2,1)} %get-tuple-element.57), channel_id=1, source_target_pairs={{0,2},{2,0},{1,3},{3,1},{4,6},{6,4},{5,7},{7,5},{8,10},{10,8},{9,1... | collective-permute-start | bytes 3145736 | tf_op jit(solution)/shard_map/ppermute | solution.py:70
  509.5 29.0 %collective-permute-start = (bf16[256,2048]{1,0:T(8,128)(2,1)}, bf16[256,2048]{1,0:T(8,128)(2,1)}, u32[]{:S(2)}, u32[]{:S(2)}) collective-permute-start(bf16[256,2048]{1,0:T(8,128)(2,1)} %get-tuple-element.56), channel_id=1, source_target_pairs={{0,2},{2,0},{1,3},{3,1},{4,6},{6,4},{5,7},{7,5},{8,10},{10,8},{9,1... | collective-permute-start | bytes 3145736 | tf_op jit(solution)/shard_map/ppermute | solution.py:70
  515.9 26.3 %collective-permute-start.2 = (bf16[256,2048]{1,0:T(8,128)(2,1)}, bf16[256,2048]{1,0:T(8,128)(2,1)}, u32[]{:S(2)}, u32[]{:S(2)}) collective-permute-start(bf16[256,2048]{1,0:T(8,128)(2,1)} %get-tuple-element.52), channel_id=1, source_target_pairs={{0,4},{4,0},{1,5},{5,1},{2,6},{6,2},{3,7},{7,3},{8,12},{12,8},{9,1... | collective-permute-start | bytes 3145736 | tf_op jit(solution)/shard_map/ppermute | solution.py:72
  517.3 47.5 %collective-permute-start.4 = (bf16[256,2048]{1,0:T(8,128)(2,1)}, bf16[256,2048]{1,0:T(8,128)(2,1)}, u32[]{:S(2)}, u32[]{:S(2)}) collective-permute-start(bf16[256,2048]{1,0:T(8,128)(2,1)} %get-tuple-element.54), channel_id=1, source_target_pairs={{0,1},{1,0},{2,3},{3,2},{4,5},{5,4},{6,7},{7,6},{8,9},{9,8},{10,11... | collective-permute-start | bytes 3145736 | tf_op jit(solution)/shard_map/ppermute | solution.py:71
  517.9 19.8 %copy-start.65 = (f32[256]{0:T(256)S(1)}, f32[256]{0:T(256)}, u32[]{:S(2)}) copy-start(f32[256]{0:T(256)} %copy-done.64) | copy-start | bytes 3076
  517.9 46.9 %collective-permute-start.6 = (bf16[256,2048]{1,0:T(8,128)(2,1)}, bf16[256,2048]{1,0:T(8,128)(2,1)}, u32[]{:S(2)}, u32[]{:S(2)}) collective-permute-start(bf16[256,2048]{1,0:T(8,128)(2,1)} %get-tuple-element.53), channel_id=1, source_target_pairs={{0,5},{5,0},{1,4},{4,1},{2,7},{7,2},{3,6},{6,3},{8,13},{13,8},{9,1... | collective-permute-start | bytes 3145736 | tf_op jit(solution)/shard_map/ppermute | solution.py:73
  538.4 26.4 %copy-start.28 = (bf16[256,2048]{1,0:T(8,128)(2,1)S(1)}, bf16[256,2048]{1,0:T(8,128)(2,1)}, u32[]{:S(2)}) copy-start(bf16[256,2048]{1,0:T(8,128)(2,1)} %rows_ref.1) | copy-start | bytes 3145732
  538.5 26.4 %copy-start.72 = (f32[256]{0:T(256)S(1)}, f32[256]{0:T(256)}, u32[]{:S(2)}) copy-start(f32[256]{0:T(256)} %get-tuple-element.98) | copy-start | bytes 3076
  571.3 38.9 %copy-start.35 = (bf16[512,2048]{1,0:T(8,128)(2,1)S(1)}, bf16[512,2048]{1,0:T(8,128)(2,1)}, u32[]{:S(2)}) copy-start(bf16[512,2048]{1,0:T(8,128)(2,1)} %copy.224) | copy-start | bytes 6291460
  620.8 149.8 %collective-permute-start.8 = (bf16[2,1,128,2048]{3,2,1,0:T(8,128)(2,1)}, bf16[2,1,128,2048]{3,2,1,0:T(8,128)(2,1)}, u32[]{:S(2)}, u32[]{:S(2)}) collective-permute-start(bf16[2,1,128,2048]{3,2,1,0:T(8,128)(2,1)} %dynamic-slice_convert_fusion), channel_id=1, source_target_pairs={{0,1},{1,0},{2,3},{3,2},{4,5},{5,4},{6,7},{7,6},{8,9},{9,8},{10,11... | collective-permute-start | bytes 3145736 | tf_op jit(solution)/shard_map/ppermute | solution.py:854
  664.5 103.6 %collective-permute-start.7 = (bf16[512,2,256]{2,0,1:T(8,128)(2,1)}, bf16[512,2,256]{2,0,1:T(8,128)(2,1)}, u32[]{:S(2)}, u32[]{:S(2)}) collective-permute-start(bf16[512,2,256]{2,0,1:T(8,128)(2,1)} %fusion.58), channel_id=1, source_target_pairs={{0,1},{1,0},{2,3},{3,2},{4,5},{5,4},{6,7},{7,6},{8,9},{9,8},{10,11... | collective-permute-start | bytes 1572872 | tf_op jit(solution)/shard_map/ppermute | solution.py:854
  668.2 40.1 %copy-start.3 = (bf16[256,2048]{1,0:T(8,128)(2,1)S(1)}, bf16[256,2048]{1,0:T(8,128)(2,1)}, u32[]{:S(2)}) copy-start(bf16[256,2048]{1,0:T(8,128)(2,1)} %param.13) | copy-start | bytes 3145732
  668.2 40.1 %copy-start.54 = (f32[2048]{0:T(1024)S(1)}, f32[2048]{0:T(1024)}, u32[]{:S(2)}) copy-start(f32[2048]{0:T(1024)} %copy-done.53) | copy-start | bytes 24580
  668.2 40.1 %copy-start.69 = (f32[256]{0:T(256)S(1)}, f32[256]{0:T(256)}, u32[]{:S(2)}) copy-start(f32[256]{0:T(256)} %copy-done.68) | copy-start | bytes 3076
  (68 other events, 345.4 us)
Sparse Core Ops, SparseCore 0:
  142.7 114.8 all-gather.4
  259.7 58.0 all-gather.6
  409.2 56.4 reduce-scatter.4
  538.6 111.8 reduce-scatter.2

commit v3 on v2

v3 whole, which is shorter than its diff:
```python
import functools
import math

import jax
import jax.numpy as jnp
from jax import lax
from jax.experimental import pallas as pl
from jax.experimental.pallas import tpu as pltpu
from jax.sharding import Mesh
from jax.sharding import PartitionSpec as P

HEADS = 16
HEAD_DIM = 256
EPS = 1e-06
NEGATIVE = -1e30
F32 = jnp.float32
BF16 = jnp.bfloat16


def contract(left, right, left_dim, right_dim):
    return lax.dot_general(
        left, right, (((left_dim,), (right_dim,)), ((), ())), preferred_element_type=F32
    )


def after(value, *first):
    return lax.optimization_barrier((value, *first))[0]


def layout(lengths, count):
    spots = jnp.arange(lengths.shape[-1], dtype=jnp.int32)
    ends = jnp.sum(jnp.where(spots[None, :] <= spots[:, None], lengths[..., None, :], 0), axis=-1)
    places = jnp.arange(count, dtype=jnp.int32)
    passed = places[:, None] >= ends[..., None, :]
    segment = jnp.sum(passed.astype(jnp.int32), axis=-1)
    offset = jnp.sum(jnp.where(passed, lengths[..., None, :], 0), axis=-1)
    position = (places - offset).astype(F32)
    same = segment[..., :, None] == segment[..., None, :]
    return position, same & (places[None, :] <= places[:, None])


def rope_tables(position, width):
    half = width // 2
    steps = jnp.arange(half, dtype=F32)
    freqs = jnp.exp(steps * (-math.log(10000.0) / half))
    angles = position[..., None] * freqs
    return jnp.cos(angles), jnp.sin(angles)


def rotate(values, cosine, sine):
    half = values.shape[-1] // 2
    first, second = values[..., :half], values[..., half:]
    return jnp.concatenate(
        [first * cosine - second * sine, second * cosine + first * sine], axis=-1
    )


def unrotate(grads, cosine, sine):
    return rotate(grads, cosine, -sine)


SWAP = [(0, 1), (1, 0)]
DIAGONAL = [(0, 3), (3, 0), (1, 2), (2, 1)]


def plane_scatter(parts):
    low = parts.astype(BF16)
    sums = []
    for near, far in ((0, 2), (1, 3), (4, 6), (5, 7)):
        sums.append(parts[near].astype(F32) + lax.ppermute(low[far], "c", SWAP).astype(F32))
    by_y = lax.ppermute(sums[1].astype(BF16), "y", SWAP)
    by_x = lax.ppermute(sums[2].astype(BF16), "x", SWAP)
    by_both = lax.ppermute(sums[3].astype(BF16), ("x", "y"), DIAGONAL)
    return sums[0], by_x, by_y, by_both


X_BIT, C_BIT, Y_BIT = 4, 2, 1
VMEM_MOST = 56 * 2**20


def other(bits):
    flips = {"x": bits // 4, "c": bits // 2 % 2, "y": bits % 2}
    return {name: 1 - lax.axis_index(name) for name, flip in flips.items() if flip}


def greet(partners):
    barrier = pltpu.get_barrier_semaphore()
    for partner in partners:
        pl.semaphore_signal(barrier, inc=1, device_id=partner)
    pl.semaphore_wait(barrier, len(partners))


def send(source, target, send_sem, recv_sem, device):
    return pltpu.make_async_remote_copy(
        src_ref=source, dst_ref=target, send_sem=send_sem, recv_sem=recv_sem, device_id=device
    )


def gathering(chunks, in_ref, out_ref, send_sem, recv_sem):
    rows = in_ref.shape[0] // chunks
    both = X_BIT | Y_BIT

    def to(slot, k, bits, source):
        part = pl.ds(k * rows, rows)
        return send(
            source.at[part], out_ref.at[slot, part], send_sem.at[slot, k], recv_sem.at[slot, k], other(bits)
        )

    def own():
        for k in range(chunks):
            to(X_BIT, k, X_BIT, in_ref).start()
            to(Y_BIT, k, Y_BIT, in_ref).start()
        for k in range(chunks):
            to(C_BIT, k, C_BIT, in_ref).start()

    def relay(first, last):
        for k in range(first, last):
            to(X_BIT, k, X_BIT, in_ref).wait_recv()
            if k < chunks // 2:
                to(both, k, Y_BIT, out_ref.at[X_BIT]).start()
            to(X_BIT | C_BIT, k, C_BIT, out_ref.at[X_BIT]).start()
            to(Y_BIT, k, Y_BIT, in_ref).wait_recv()
            if k >= chunks // 2:
                to(both, k, X_BIT, out_ref.at[Y_BIT]).start()
            to(Y_BIT | C_BIT, k, C_BIT, out_ref.at[Y_BIT]).start()

    def far():
        for k in range(chunks):
            to(both, k, Y_BIT, in_ref).wait_recv()
            to(7, k, C_BIT, out_ref.at[both]).start()

    def end():
        for slot in range(1, 8):
            for k in range(chunks):
                copy = to(slot, k, slot, in_ref)
                if slot & C_BIT:
                    copy.wait_recv()
                copy.wait_send()

    return own, relay, far, end


def gather_kernel(chunks, in_ref, out_ref, own_sem, send_sem, recv_sem):
    greet([other(C_BIT), other(X_BIT), other(Y_BIT)])
    copy = pltpu.make_async_copy(in_ref, out_ref.at[0], own_sem)
    copy.start()
    own, relay, far, end = gathering(chunks, in_ref, out_ref, send_sem, recv_sem)
    own()
    relay(0, chunks)
    far()
    copy.wait()
    end()


def plane_gather(block, name, chunks=4):
    return pl.pallas_call(
        functools.partial(gather_kernel, chunks),
        out_shape=jax.ShapeDtypeStruct((8, *block.shape), block.dtype),
        in_specs=[pl.BlockSpec(memory_space=pl.ANY)],
        out_specs=pl.BlockSpec(memory_space=pl.ANY),
        scratch_shapes=[
            pltpu.SemaphoreType.DMA,
            pltpu.SemaphoreType.DMA((8, chunks)),
            pltpu.SemaphoreType.DMA((8, chunks)),
        ],
        compiler_params=pltpu.CompilerParams(collective_id=name, has_side_effects=True),
        cost_estimate=pl.CostEstimate(flops=0, bytes_accessed=160 * 2**20, transcendentals=0),
    )(block)


def matmul_scatter_kernel(flip, wide, *refs):
    left_ref, right_ref, *more_ref, out_ref, part_ref, near_ref, sum_ref, far_ref = refs[:-4]
    near_send, near_recv, chip_send, chip_recv = refs[-4:]
    tokens = out_ref.shape[0]
    step = 256
    greet([other(C_BIT), other(X_BIT), other(Y_BIT), other(X_BIT | Y_BIT)])

    def product(slot, target):
        @pl.loop(0, wide // step)
        def _(i):
            at = pl.ds(pl.multiple_of(i * step, step), step)
            rows = left_ref[slot * tokens : (slot + 1) * tokens, :]
            if flip:
                got = contract(rows, right_ref[at, :], 1, 1)
            else:
                got = contract(rows, right_ref[:, at], 1, 0)
            target[:, at] = got.astype(BF16)

        for ref in more_ref:
            target[:, wide:] = ref[slot * tokens : (slot + 1) * tokens, :].astype(BF16)

    chips = (X_BIT | Y_BIT, X_BIT, Y_BIT, 0)
    near, far = [], []
    for i, chip in enumerate(chips):
        product(chip | C_BIT, part_ref.at[i])
        copy = send(part_ref.at[i], near_ref.at[i], near_send.at[i], near_recv.at[i], other(C_BIT))
        copy.start()
        near.append(copy)
        product(chip, sum_ref.at[i])
        copy.wait_recv()

        @pl.loop(0, tokens // 32)
        def _(r):
            at = pl.ds(pl.multiple_of(r * 32, 32), 32)
            total = sum_ref[i, at, :].astype(F32) + near_ref[i, at, :].astype(F32)
            if chip:
                sum_ref[i, at, :] = total.astype(BF16)
            else:
                out_ref[at, :] = total

        if chip:
            copy = send(sum_ref.at[i], far_ref.at[i], chip_send.at[i], chip_recv.at[i], other(chip))
            copy.start()
            far.append(copy)
    for copy in far:
        copy.wait_recv()

    @pl.loop(0, tokens // 32)
    def _(r):
        at = pl.ds(pl.multiple_of(r * 32, 32), 32)
        total = out_ref[at, :]
        for i in range(3):
            total = total + far_ref[i, at, :].astype(F32)
        out_ref[at, :] = total

    for copy in (*near, *far):
        copy.wait_send()


def matmul_scatter(left, right, name, flip=False, *more):
    tokens, depth = left.shape[0] // 8, left.shape[1]
    wide = right.shape[0 if flip else 1]
    full = wide + sum(array.shape[1] for array in more)
    block = pltpu.VMEM((4, tokens, full), BF16)
    return pl.pallas_call(
        functools.partial(matmul_scatter_kernel, flip, wide),
        out_shape=jax.ShapeDtypeStruct((tokens, full), F32),
        in_specs=[pl.BlockSpec(memory_space=pltpu.VMEM)] * (2 + len(more)),
        out_specs=pl.BlockSpec(memory_space=pltpu.VMEM),
        scratch_shapes=[
            block,
            block,
            block,
            pltpu.VMEM((3, tokens, full), BF16),
            *[pltpu.SemaphoreType.DMA((4,))] * 2,
            *[pltpu.SemaphoreType.DMA((3,))] * 2,
        ],
        compiler_params=pltpu.CompilerParams(
            collective_id=name, has_side_effects=True, vmem_limit_bytes=VMEM_MOST
        ),
        cost_estimate=pl.CostEstimate(
            flops=16 * tokens * wide * depth, bytes_accessed=160 * 2**20, transcendentals=0
        ),
    )(left, right, *more)


def in_plane():
    return 4 * lax.axis_index("x") + 2 * lax.axis_index("c") + lax.axis_index("y")


class Parcel:
    def __init__(self, count, f_first, rank_rows, columns, kv_rows):
        self.count, self.f_first = count, f_first
        self.rank_rows, self.columns, self.kv_rows = rank_rows, columns, kv_rows
        self.windows = columns % 128 == 0

    def down_shape(self):
        if self.windows:
            return (2 * self.rank_rows, 4 * self.count * self.columns)
        return (8, self.count, self.rank_rows, self.columns)

    def down_from(self, array):
        if self.windows:
            return array
        array = array.reshape(2, 2, 2, self.count, self.rank_rows, self.columns)
        array = array.transpose((2, 4, 3, 0, 1, 5) if self.f_first else (2, 4, 0, 1, 3, 5))
        return array.reshape(2 * self.rank_rows, -1)

    def down_to(self, array):
        if self.windows:
            return array
        inner = (self.count, 2, 2) if self.f_first else (2, 2, self.count)
        array = array.reshape(2, self.rank_rows, *inner, self.columns)
        array = array.transpose((3, 4, 0, 2, 1, 5) if self.f_first else (2, 3, 0, 4, 1, 5))
        return array.reshape(self.down_shape())

    def blocks(self, refs, place, j):
        down, kv, small = refs
        pair, y = place // 2, place % 2
        at = j * 4 + pair if self.f_first else pair * self.count + j
        if self.windows:
            down = down.at[
                pl.ds(pl.multiple_of(y * self.rank_rows, self.rank_rows), self.rank_rows),
                pl.ds(pl.multiple_of(at * self.columns, self.columns), self.columns),
            ]
        else:
            down = down.at[place, j]
        start_row = pl.multiple_of((2 * at + y) * self.kv_rows, self.kv_rows)
        return down, kv.at[pl.ds(start_row, self.kv_rows)], small.at[place, j]

    def unit_pieces(self):
        for shard in range(8 * self.count):
            if self.f_first:
                yield shard % 8, shard // 8, shard
            else:
                yield shard // (2 * self.count) * 2 + shard % 2, shard // 2 % self.count, shard


def greet_all(count):
    f = lax.axis_index("f")
    lower, upper = f > 0, f < count - 1
    barrier = pltpu.get_barrier_semaphore()
    for bits in range(1, 8):
        pl.semaphore_signal(barrier, inc=1, device_id=other(bits))
    pl.when(lower)(lambda: pl.semaphore_signal(barrier, inc=1, device_id={"f": f - 1}))
    pl.when(upper)(lambda: pl.semaphore_signal(barrier, inc=1, device_id={"f": f + 1}))
    pl.semaphore_wait(barrier, 7 + lower.astype(jnp.int32) + upper.astype(jnp.int32))
    return lower, upper


def begin(copies):
    for copy in copies:
        copy.start()


def arrive(copies):
    for copy in copies:
        copy.wait_recv()


def gone(copies):
    for copy in copies:
        copy.wait_send()


FAR_FIRST = (7, 5, 6, 4, 3, 1, 2)


def start_kernel(
    parcel, chunks, units, padded, down_ref, kv_ref, small_ref, gate_ref, up_ref, rows_ref,
    down_all, kv_all, small_all, wide_all, rows_all,
    down_low, kv_low, wide_ref,
    local_sem, line_send, line_recv, plane_send, plane_recv, wide_send, wide_recv, rows_send, rows_recv,
):
    count = parcel.count
    f, me = lax.axis_index("f"), in_plane()
    lower, upper = greet_all(count)
    own = (down_low, kv_low, small_ref)
    alls = (down_all, kv_all, small_all)
    down_low[...] = down_ref[...].astype(BF16)
    kv_low[...] = kv_ref[...].astype(BF16)

    def hop(j, up, sources):
        return [
            send(
                source, target, line_send.at[i, 0 if up else 1, j], line_recv.at[i, j],
                {"f": f + 1 if up else f - 1},
            )
            for i, (source, target) in enumerate(zip(sources, parcel.blocks(alls, me, j)))
        ]

    def spread(slot, bits, j, sources):
        targets = parcel.blocks(alls, me ^ bits ^ slot, j)
        return [
            send(source, target, plane_send.at[i, slot, j], plane_recv.at[i, slot, j], other(bits))
            for i, (source, target) in enumerate(zip(sources, targets))
        ]

    def to_plane(j, sources):
        for bits in (X_BIT, Y_BIT, C_BIT):
            begin(spread(bits, bits, j, sources))

    def line_step(step):
        @pl.when(f - step >= 0)
        def _():
            j = f - step
            blocks = parcel.blocks(alls, me, j)
            arrive(hop(j, True, blocks))
            pl.when(upper)(lambda: begin(hop(j, True, blocks)))
            to_plane(j, blocks)

        @pl.when(f + step <= count - 1)
        def _():
            j = f + step
            blocks = parcel.blocks(alls, me, j)
            arrive(hop(j, False, blocks))
            pl.when(lower)(lambda: begin(hop(j, False, blocks)))
            to_plane(j, blocks)

    def relay(j):
        by_x, by_y = parcel.blocks(alls, me ^ X_BIT, j), parcel.blocks(alls, me ^ Y_BIT, j)
        arrive(spread(X_BIT, X_BIT, j, by_x))
        pl.when(j % 2 == 0)(lambda: begin(spread(5, Y_BIT, j, by_x)))
        begin(spread(6, C_BIT, j, by_x))
        arrive(spread(Y_BIT, Y_BIT, j, by_y))
        pl.when(j % 2 == 1)(lambda: begin(spread(5, X_BIT, j, by_y)))
        begin(spread(3, C_BIT, j, by_y))

    def relay_far(j):
        by_both = parcel.blocks(alls, me ^ 5, j)
        arrive(spread(5, Y_BIT, j, by_both))
        begin(spread(7, C_BIT, j, by_both))

    def in_order(do):
        do(f)
        for step in range(1, count):
            pl.when(f - step >= 0)(lambda: do(f - step))
            pl.when(f + step <= count - 1)(lambda: do(f + step))

    def wide(bits):
        return send(wide_ref.at[me ^ bits], wide_all.at[me], wide_send.at[bits], wide_recv.at[bits], other(bits))

    pl.when(upper)(lambda: begin(hop(f, True, own)))
    pl.when(lower)(lambda: begin(hop(f, False, own)))
    to_plane(f, own)
    for place, j, shard in parcel.unit_pieces():
        for first, ref in ((0, gate_ref), (padded, up_ref)):
            piece = ref[:, shard * units : (shard + 1) * units].astype(BF16)
            wide_ref[place, :, first + j * units : first + (j + 1) * units] = piece
    for first in (count * units, padded + count * units):
        size = padded - count * units
        wide_ref[:, :, first : first + size] = jnp.zeros((8, wide_ref.shape[1], size), BF16)
    for bits in FAR_FIRST:
        wide(bits).start()
    locals_ = [
        pltpu.make_async_copy(source, target, local_sem.at[i])
        for i, (source, target) in enumerate(
            (
                *zip(own, parcel.blocks(alls, me, f)),
                (wide_ref.at[me], wide_all.at[me]),
                (rows_ref, rows_all.at[0]),
            )
        )
    ]
    begin(locals_)
    rows_own, rows_relay, rows_far, rows_end = gathering(chunks, rows_ref, rows_all, rows_send, rows_recv)
    for step in range(1, count):
        line_step(step)
    rows_own()
    in_order(relay)
    rows_relay(0, chunks // 2)
    in_order(relay_far)
    rows_relay(chunks // 2, chunks)
    rows_far()
    for copy in locals_:
        copy.wait()
    for j in range(count):
        pl.when(upper & (f >= j))(lambda: gone(hop(j, True, own)))
        pl.when(lower & (f <= j))(lambda: gone(hop(j, False, own)))
    for slot in range(1, 8):
        for j in range(count):
            for copy in spread(slot, slot, j, own):
                if slot & C_BIT:
                    copy.wait_recv()
                copy.wait_send()
    for bits in range(1, 8):
        wide(bits).wait_recv()
        wide(bits).wait_send()
    rows_end()


def start(parcel, down, kv, small, gate, up, rows, units, padded, name, chunks=4):
    count = parcel.count
    any_space, vmem = pl.BlockSpec(memory_space=pl.ANY), pl.BlockSpec(memory_space=pltpu.VMEM)
    dma = pltpu.SemaphoreType.DMA
    wide = (8, gate.shape[0], 2 * padded)
    return pl.pallas_call(
        functools.partial(start_kernel, parcel, chunks, units, padded),
        out_shape=[
            jax.ShapeDtypeStruct(parcel.down_shape(), BF16),
            jax.ShapeDtypeStruct((8 * count * kv.shape[0], kv.shape[1]), BF16),
            jax.ShapeDtypeStruct((8, count, *small.shape), BF16),
            jax.ShapeDtypeStruct(wide, BF16),
            jax.ShapeDtypeStruct((8, *rows.shape), BF16),
        ],
        in_specs=[vmem] * 5 + [any_space],
        out_specs=[any_space] * 5,
        scratch_shapes=[
            pltpu.VMEM(down.shape, BF16),
            pltpu.VMEM(kv.shape, BF16),
            pltpu.VMEM(wide, BF16),
            dma((5,)),
            dma((3, 2, count)), dma((3, count)),
            dma((3, 8, count)), dma((3, 8, count)),
            dma((8,)), dma((8,)),
            dma((8, chunks)), dma((8, chunks)),
        ],
        compiler_params=pltpu.CompilerParams(
            collective_id=name, has_side_effects=True, vmem_limit_bytes=VMEM_MOST
        ),
        cost_estimate=pl.CostEstimate(flops=0, bytes_accessed=240 * 2**20, transcendentals=0),
    )(down, kv, small, gate, up, rows)


def end_kernel(
    parcel, units, padded, down_ref, kv_ref, small_ref, wide_ref,
    down_sum, kv_sum, small_sum, gate_sum, up_sum, *rest,
):
    count = parcel.count
    held = [rest[8 * i : 8 * i + 8] for i in range(3)]
    wide_all, near_send, near_recv, chip_send, chip_recv, line_send, line_recv, wide_send, wide_recv = rest[24:]
    f, me = lax.axis_index("f"), in_plane()
    lower, upper = greet_all(count)
    parts = (down_ref, kv_ref, small_ref)
    sums = (down_sum, kv_sum, small_sum)
    chips = (X_BIT | Y_BIT, X_BIT, Y_BIT, 0)

    def rows(amount, do):
        size = 16 if amount % 64 else 64

        @pl.loop(0, amount // size)
        def _(r):
            do(pl.ds(pl.multiple_of(r * size, size), size))

    def near(n, j):
        sources = parcel.blocks(parts, me ^ (chips[n] | C_BIT), j)
        return [
            send(source, held[i][1].at[n, j], near_send.at[i, n, j], near_recv.at[i, n, j], other(C_BIT))
            for i, source in enumerate(sources)
        ]

    def far(n):
        return [
            send(held[i][2].at[n], held[i][3].at[n], chip_send.at[i, n], chip_recv.at[i, n], other(chips[n]))
            for i in range(3)
        ]

    def wide(bits):
        return send(wide_ref.at[me ^ bits], wide_all.at[me], wide_send.at[bits], wide_recv.at[bits], other(bits))

    def hop(d, up):
        way = 0 if up else 1
        return [
            send(
                held[i][4 + 2 * way].at[d], held[i][5 + 2 * way].at[d],
                line_send.at[i, way, d], line_recv.at[i, way, d],
                {"f": f + 1 if up else f - 1},
            )
            for i in range(3)
        ]

    def pass_on(d, up):
        way = 0 if up else 1
        behind = lower if up else upper

        @pl.when((d > f) if up else (d < f))
        def _():
            @pl.when(behind)
            def _():
                for copy in hop(d, up):
                    copy.wait_recv()
                for total, outgoing, incoming in ((h[0], h[4 + 2 * way], h[5 + 2 * way]) for h in held):

                    def add(at, total=total, outgoing=outgoing, incoming=incoming):
                        outgoing[d, at, :] = (total[d, at, :] + incoming[d, at, :].astype(F32)).astype(BF16)

                    rows(total.shape[1], add)

            @pl.when(jnp.logical_not(behind))
            def _():
                for total, outgoing in ((h[0], h[4 + 2 * way]) for h in held):

                    def keep(at, total=total, outgoing=outgoing):
                        outgoing[d, at, :] = total[d, at, :].astype(BF16)

                    rows(total.shape[1], keep)

            for copy in hop(d, up):
                copy.start()

    for n in range(4):
        for j in range(count):
            for copy in near(n, j):
                copy.start()
    for bits in FAR_FIRST:
        wide(bits).start()
    for n in range(4):
        for j in range(count):
            for copy in near(n, j):
                copy.wait_recv()
            for i, source in enumerate(parcel.blocks(parts, me ^ chips[n], j)):
                total, near_ref, chip_ref = held[i][:3]

                def add(at, source=source, total=total, near_ref=near_ref, chip_ref=chip_ref):
                    both = source[at, :].astype(F32) + near_ref[n, j, at, :].astype(F32)
                    if n < 3:
                        chip_ref[n, j, at, :] = both.astype(BF16)
                    else:
                        total[j, at, :] = both

                rows(total.shape[1], add)
        if n < 3:
            for copy in far(n):
                copy.start()

    wide_all[me] = wide_ref[me]
    for bits in range(1, 8):
        wide(bits).wait_recv()
    for place, j, shard in parcel.unit_pieces():
        for first, ref in ((0, gate_sum), (padded, up_sum)):
            piece = wide_all[place, :, first + j * units : first + (j + 1) * units]
            ref[:, shard * units : (shard + 1) * units] = piece.astype(F32)

    for n in range(3):
        for copy in far(n):
            copy.wait_recv()
    for i in range(3):
        total, far_ref = held[i][0], held[i][3]
        for j in range(count):

            def add(at, total=total, far_ref=far_ref, j=j):
                value = total[j, at, :]
                for n in range(3):
                    value = value + far_ref[n, j, at, :].astype(F32)
                total[j, at, :] = value

            rows(total.shape[1], add)
    for step in range(1, count):
        pass_on(count - step, True)
        pass_on(step - 1, False)
    for i in range(3):

        def keep(at, i=i):
            sums[i][at, :] = held[i][0][f, at, :]

        rows(sums[i].shape[0], keep)
    for up, there in ((True, lower), (False, upper)):

        @pl.when(there)
        def _(up=up):
            for copy in hop(f, up):
                copy.wait_recv()
            for i in range(3):
                incoming = held[i][5 if up else 7]

                def add(at, i=i, incoming=incoming):
                    sums[i][at, :] = sums[i][at, :] + incoming[f, at, :].astype(F32)

                rows(sums[i].shape[0], add)

    for d in range(count):
        pl.when(f < d)(lambda: gone(hop(d, True)))
        pl.when(f > d)(lambda: gone(hop(d, False)))
    for n in range(4):
        for j in range(count):
            for copy in near(n, j):
                copy.wait_send()
    for n in range(3):
        for copy in far(n):
            copy.wait_send()
    for bits in range(1, 8):
        wide(bits).wait_send()


def end(parcel, down, kv, small, wide, units, padded, name):
    vmem = pl.BlockSpec(memory_space=pltpu.VMEM)
    dma = pltpu.SemaphoreType.DMA
    count = parcel.count
    bodies = (
        (count, parcel.rank_rows, parcel.columns),
        (count, parcel.kv_rows, kv.shape[1]),
        (count, *small.shape[2:]),
    )
    scratch = []
    for body in bodies:
        low = pltpu.VMEM(body, BF16)
        three = pltpu.VMEM((3, *body), BF16)
        scratch += [pltpu.VMEM(body, F32), pltpu.VMEM((4, *body), BF16), three, three, low, low, low, low]
    every = 8 * count * units
    return pl.pallas_call(
        functools.partial(end_kernel, parcel, units, padded),
        out_shape=[
            *[jax.ShapeDtypeStruct(body[1:], F32) for body in bodies],
            *[jax.ShapeDtypeStruct((wide.shape[1], every), F32)] * 2,
        ],
        in_specs=[vmem] * 4,
        out_specs=[vmem] * 5,
        scratch_shapes=[
            *scratch,
            pltpu.VMEM(wide.shape, BF16),
            dma((3, 4, count)), dma((3, 4, count)),
            dma((3, 3)), dma((3, 3)),
            dma((3, 2, count)), dma((3, 2, count)),
            dma((8,)), dma((8,)),
        ],
        compiler_params=pltpu.CompilerParams(
            collective_id=name, has_side_effects=True, vmem_limit_bytes=VMEM_MOST
        ),
        cost_estimate=pl.CostEstimate(flops=0, bytes_accessed=240 * 2**20, transcendentals=0),
    )(down, kv, small, wide)


def by_owner(array, axis, count, f_first):
    lead, size, tail = array.shape[:axis], array.shape[axis], array.shape[axis + 1 :]
    part = size // (8 * count)
    n = len(lead)
    rest = [*range(n), n + 4, *range(n + 5, n + 5 + len(tail))]
    if f_first:
        array = array.reshape(*lead, count, 2, 2, 2, part, *tail)
        array = array.transpose(n, n + 1, n + 2, n + 3, *rest)
    else:
        array = array.reshape(*lead, 2, 2, count, 2, part, *tail)
        array = array.transpose(n + 2, n, n + 1, n + 3, *rest)
    return array.reshape(count, 8, *lead, part, *tail)


def from_owner(array, axis, f_first):
    count, _, *body = array.shape
    lead, part, tail = body[:axis], body[axis], body[axis + 1 :]
    n = axis
    array = array.reshape(count, 2, 2, 2, *body)
    inner = (0, 1, 2, 3) if f_first else (1, 2, 0, 3)
    array = array.transpose(
        *range(4, 4 + n), *inner, 4 + n, *range(5 + n, 5 + n + len(tail))
    )
    return array.reshape(*lead, 8 * count * part, *tail)


def scores_of(q_rot, k_rot, allowed):
    raw = jnp.einsum("bthd,bsd->bhts", q_rot, k_rot, preferred_element_type=F32)
    return jnp.where(allowed[:, None], raw * HEAD_DIM**-0.5, NEGATIVE)


def per_device(
    count,
    f_first,
    block_input,
    seq_lens,
    attn_gain,
    latent_down,
    latent_gain,
    latent_up,
    shared_kv,
    out_proj,
    mlp_gain,
    gate_weight,
    up_weight,
    down_weight,
    out_cotangent,
):
    tokens, width = block_input.shape
    rank = 2 * latent_down.shape[0]
    half_rank = latent_down.shape[0]
    units = down_weight.shape[0]
    mine = units * count
    padded = -(-mine // 256) * 256
    y = lax.axis_index("y")
    place = lax.axis_index("f")
    x_c = 2 * lax.axis_index("x") + lax.axis_index("c")

    def rows_of(array):
        flat = array.reshape(-1)
        lines = -(-flat.shape[0] // 128)
        return jnp.pad(flat, (0, lines * 128 - flat.shape[0])).reshape(lines, 128)

    gain_high = latent_gain.astype(BF16)
    gain_low = (latent_gain - gain_high.astype(F32)).astype(BF16)
    gain_rows = attn_gain.shape[0]
    lat_lines = half_rank // 128
    small = jnp.concatenate(
        [
            rows_of(gain_high),
            rows_of(gain_low),
            rows_of(attn_gain.astype(BF16)),
            rows_of(mlp_gain.astype(BF16)),
            rows_of(seq_lens.astype(BF16)),
        ]
    )
    at_gain = 2 * lat_lines
    small = jnp.pad(small, ((0, -small.shape[0] % 16), (0, 0)))
    parcel = Parcel(count, f_first, half_rank, latent_down.shape[1], shared_kv.shape[0])
    down_full, kv_full, small, both, g_all = start(
        parcel, latent_down, shared_kv, small, gate_weight, up_weight, out_cotangent, units, padded, 0
    )
    down_full = parcel.down_from(down_full)
    g_all = g_all.reshape(8 * tokens, width)

    half = count // 2
    per_head = count // 4
    up_line = lax.all_gather(latent_up.astype(BF16), "f", axis=0)
    out_line = lax.all_gather(after(out_proj.astype(BF16), up_line), "f", axis=0)

    def heads(line):
        own = lax.dynamic_slice_in_dim(line, half * y, half, 0)
        far = lax.dynamic_slice_in_dim(line, half - half * y, half, 0)
        return own, lax.ppermute(far, "y", SWAP)

    def join(own, other_part, axis):
        low = jnp.where(y == 0, own, other_part)
        high = jnp.where(y == 0, other_part, own)
        return jnp.stack([low, high], axis)

    up_full = join(*heads(up_line), 0).transpose(0, 2, 1, 3).reshape(rank, 2 * HEAD_DIM)
    out_full = join(*heads(out_line), 1).reshape(2 * HEAD_DIM, width)

    both = lax.all_gather(after(both, out_line), "f", axis=0)
    both = from_owner(both, 0, f_first)
    ff_down = lax.all_gather(after(down_weight.astype(BF16), both), "f", axis=0)
    ff_down = jnp.pad(ff_down.reshape(mine, width), ((0, padded - mine), (0, 0)))

    gain_lat = small[:2, 0, :lat_lines].astype(F32) + small[:2, 0, lat_lines:at_gain].astype(F32)
    gain_lat = gain_lat.reshape(rank)
    by_line = small.transpose(1, 0, 2, 3)
    gain_one = from_owner(by_line[:, :, at_gain, :gain_rows], 0, f_first).astype(F32)
    gain_two = from_owner(by_line[:, :, at_gain + 1, :gain_rows], 0, f_first).astype(F32)
    lengths = lax.dynamic_index_in_dim(small[:, :, at_gain + 2, :3], place, 1, keepdims=False)
    lengths = jnp.stack(
        [lax.dynamic_index_in_dim(lengths, in_plane() ^ i, 0, keepdims=False) for i in range(8)]
    ).astype(jnp.int32)

    inputs = block_input.astype(F32)
    rms_one = lax.rsqrt(jnp.mean(inputs * inputs, axis=-1, keepdims=True) + EPS)
    normed = (inputs * rms_one * gain_one).astype(BF16)
    latent = contract(normed, down_full, 1, 1)
    rms_lat = lax.rsqrt(jnp.mean(latent * latent, axis=-1, keepdims=True) + EPS)
    latent_n = (latent * rms_lat * gain_lat).astype(BF16)
    shared = jnp.dot(normed, kv_full, preferred_element_type=F32)
    position, allowed = layout(lengths, tokens)
    cosine, sine = rope_tables(position, HEAD_DIM)
    k_own = rotate(shared, cosine[0], sine[0]).astype(BF16)

    rows_all = plane_gather(jnp.concatenate([latent_n, k_own, shared.astype(BF16)], axis=1), 1)
    lat_all = rows_all[:, :, :rank].reshape(8 * tokens, rank)
    k_rot = rows_all[:, :, rank : rank + HEAD_DIM]
    values = rows_all[:, :, rank + HEAD_DIM :]
    queries = jnp.dot(lat_all, up_full, preferred_element_type=F32)
    wide_cos, wide_sin = cosine[:, :, None], sine[:, :, None]
    q_rot = rotate(queries.reshape(8, tokens, 2, HEAD_DIM), wide_cos, wide_sin).astype(BF16)
    scores = scores_of(q_rot, k_rot, allowed)
    peak = jnp.max(scores, axis=-1, keepdims=True)
    log_total = peak + jnp.log(jnp.sum(jnp.exp(scores - peak), axis=-1, keepdims=True))
    probs = jnp.exp(scores - log_total)
    attended = jnp.einsum("bhts,bsd->bthd", probs.astype(BF16), values, preferred_element_type=F32)
    attended = attended.reshape(8 * tokens, 2 * HEAD_DIM).astype(BF16)
    branch = matmul_scatter(attended, out_full, 2)

    middle = inputs + branch
    rms_two = lax.rsqrt(jnp.mean(middle * middle, axis=-1, keepdims=True) + EPS)
    normed_two = (middle * rms_two * gain_two).astype(BF16)
    two_all = plane_gather(normed_two, 3).reshape(8 * tokens, width)
    gate_up = jnp.dot(two_all, both, preferred_element_type=F32)
    gate, upval = gate_up[:, :padded], gate_up[:, padded:]
    sigma = jax.nn.sigmoid(gate)
    hidden = (gate * sigma * upval).astype(BF16)

    d_hidden = contract(g_all, ff_down, 1, 1)
    d_gate = (d_hidden * upval * sigma * (1.0 + gate * (1.0 - sigma))).astype(BF16)
    d_up = (d_hidden * gate * sigma).astype(BF16)
    d_both = jnp.concatenate([d_gate, d_up], axis=1)
    d_two = matmul_scatter(d_both, both, 4, True)

    result = jnp.dot(hidden, ff_down, preferred_element_type=F32)
    result = plane_scatter(after(result.reshape(8, tokens, width), d_two))

    both_grad = contract(two_all, d_both, 0, 0)
    both_grad = by_owner(both_grad.astype(BF16), 0, count, f_first)
    both_grad = lax.psum_scatter(both_grad, "f", scatter_dimension=0)

    down_grad = contract(hidden, g_all, 0, 0)[:mine].reshape(count, units, width)
    down_grad = lax.psum_scatter(down_grad.astype(BF16), "f", scatter_dimension=0).astype(F32)

    upstream = out_cotangent.astype(F32)
    gain_two_part = jnp.sum(d_two * middle * rms_two, axis=0)
    scaled_two = d_two * gain_two
    d_middle = (
        upstream
        + rms_two * scaled_two
        - middle * (rms_two**3) * jnp.mean(scaled_two * middle, axis=-1, keepdims=True)
    )

    d_branch = plane_gather(d_middle.astype(BF16), 5).reshape(8 * tokens, width)
    d_attended = contract(d_branch, out_full, 1, 1).astype(BF16)
    d_attended = d_attended.reshape(8, tokens, 2, HEAD_DIM)
    d_probs = jnp.einsum("bthd,bsd->bhts", d_attended, values, preferred_element_type=F32)
    inner = jnp.sum(probs * d_probs, axis=-1, keepdims=True)
    d_scores = (probs * (d_probs - inner)).astype(BF16)
    scale = HEAD_DIM**-0.5
    d_qrot = jnp.einsum("bhts,bsd->bthd", d_scores, k_rot, preferred_element_type=F32) * scale
    d_queries = unrotate(d_qrot, wide_cos, wide_sin).astype(BF16)
    d_queries = d_queries.reshape(8 * tokens, 2 * HEAD_DIM)
    d_krot = jnp.einsum("bhts,bthd->bsd", d_scores, q_rot, preferred_element_type=F32) * scale
    value_part = jnp.einsum(
        "bhts,bthd->bsd", probs.astype(BF16), d_attended, preferred_element_type=F32
    )
    shared_part = unrotate(d_krot, cosine, sine) + value_part
    back = matmul_scatter(d_queries, up_full, 6, True, shared_part.reshape(8 * tokens, HEAD_DIM))
    d_lat_n, d_shared = back[:, :rank], back[:, rank:].astype(BF16)

    own, *arrived = after(result, back)
    block_output = (middle + own + sum(part.astype(F32) for part in arrived)).astype(BF16)

    up_grad_heads = contract(lat_all, d_queries, 0, 0).reshape(2, half_rank, 2, HEAD_DIM)
    out_grad_heads = contract(attended, d_branch, 0, 0).reshape(2, per_head, 2, -1, width)

    def swap_halves(array, axis):
        own = lax.dynamic_index_in_dim(array, y, axis, keepdims=False)
        other = lax.dynamic_index_in_dim(array, 1 - y, axis, keepdims=False).astype(BF16)
        return own, lax.ppermute(other, "y", SWAP).astype(F32)

    up_line_grad = join(*swap_halves(up_grad_heads, 0), 1).reshape(half_rank, count, -1)
    up_line_grad = up_line_grad.transpose(1, 0, 2).astype(BF16)
    latent_up_grad = lax.psum_scatter(up_line_grad, "f", scatter_dimension=0).astype(F32)
    out_line_grad = join(*swap_halves(out_grad_heads, 2), 0)
    out_line_grad = out_line_grad.reshape(count, -1, width).astype(BF16)
    out_proj_grad = lax.psum_scatter(out_line_grad, "f", scatter_dimension=0).astype(F32)

    gain_lat_part = jnp.sum(d_lat_n * latent * rms_lat, axis=0)
    scaled_lat = d_lat_n * gain_lat
    inner_lat = jnp.sum(scaled_lat * latent, axis=-1, keepdims=True)
    d_latent = (rms_lat * scaled_lat - latent * (rms_lat**3) * inner_lat / rank).astype(BF16)
    d_normed = contract(d_shared, kv_full, 1, 1) + jnp.dot(
        d_latent, down_full, preferred_element_type=F32
    )
    gain_one_part = jnp.sum(d_normed * inputs * rms_one, axis=0)
    scaled_one = d_normed * gain_one
    input_grad = (
        d_middle
        + rms_one * scaled_one
        - inputs * (rms_one**3) * jnp.mean(scaled_one * inputs, axis=-1, keepdims=True)
    ).astype(BF16)

    down_part = parcel.down_to(contract(d_latent, normed, 0, 0).astype(BF16))
    kv_part = contract(normed, d_shared, 0, 0).astype(BF16)

    def gain_rows_of(part):
        part = by_owner(part.astype(BF16), 0, count, f_first).transpose(1, 0, 2)
        return jnp.pad(part, ((0, 0), (0, 0), (0, 128 - gain_rows)))[:, :, None]

    lat_rows = jnp.broadcast_to(
        gain_lat_part.astype(BF16).reshape(1, 2, 1, lat_lines, 128), (4, 2, count, lat_lines, 128)
    )
    small_part = jnp.concatenate(
        [
            lat_rows.reshape(8, count, lat_lines, 128),
            gain_rows_of(gain_one_part),
            gain_rows_of(gain_two_part),
        ],
        axis=2,
    )
    small_part = jnp.pad(small_part, ((0, 0), (0, 0), (0, -small_part.shape[2] % 16), (0, 0)))
    latent_down_grad, shared_kv_grad, small_sum, gate_grad, up_grad = end(
        parcel, down_part, kv_part, small_part, both_grad, units, padded, 7
    )
    latent_gain_grad = small_sum[:lat_lines].reshape(half_rank)
    attn_gain_grad = small_sum[lat_lines, :gain_rows]
    mlp_gain_grad = small_sum[lat_lines + 1, :gain_rows]
    return (
        block_output,
        input_grad,
        attn_gain_grad,
        latent_down_grad,
        latent_gain_grad,
        latent_up_grad,
        shared_kv_grad,
        out_proj_grad,
        mlp_gain_grad,
        gate_grad,
        up_grad,
        down_grad,
    )


def solution(mesh):
    devices = mesh.devices
    split = devices.shape[0]
    count = split // 4
    f_first = split == HEADS
    if f_first:
        names, sizes = ("f", "x", "c", "y"), (count, 2, 2, 2)
    else:
        names, sizes = ("x", "c", "f", "y"), (2, 2, count, 2)
    fine = Mesh(devices.reshape(sizes), names)
    dp = names[:3]
    return jax.shard_map(
        functools.partial(per_device, count, f_first),
        mesh=fine,
        in_specs=(
            P(names, None),
            P(names, None),
            P(names),
            P("y", dp),
            P("y"),
            P("y", dp),
            P(names, None),
            P(names, None),
            P(names),
            P(names, None),
            P(names, None),
            P(names, None),
            P(names, None),
        ),
        out_specs=(
            P(names, None),
            P(names, None),
            P(names),
            P("y", dp),
            P("y"),
            P("y", dp),
            P(names, None),
            P(names, None),
            P(names),
            P(names, None),
            P(names, None),
            P(names, None),
        ),
        check_vma=False,
    )
```

time: 931 us -> 924 us (level)
  waiting for transfers between devices: 34.2 us -> 161 us
  local copies, waits for them, and re-layouts: 163 us -> 76.7 us
  Pallas kernels: 488 us -> 437 us
  matrix products: 131 us -> 141 us
    reduce_scatter x1, waiting for transfers between devices: 0.01 us -> 59.8 us  [per_device(): both_grad = lax.psum_scatter(both_grad, 'f', scatter_dimension=0)]
    reshape x17 -> x1, local copies, waits for them, and re-layouts: 60.9 us -> 1.36 us  [per_device(): latent_gain_grad = small_sum[:lat_lines].reshape(half_rank)]
    pallas_call x2, Pallas kernels: 217 us -> 159 us  [the longest x1 83.9 us: start(): pl.pallas_call(functools.partial(start_kernel, parcel, chunks, units, pad...]
    concatenate x2 -> x1, local copies, waits for them, and re-layouts: 24 us -> 0.06 us  [per_device(): jnp.concatenate([rows_of(gain_high), rows_of(gain_low), rows_of(attn_gain...]
    ppermute x2, waiting for transfers between devices: 0.01 us -> 24 us  [swap_halves(): return (own, lax.ppermute(other, 'y', SWAP).astype(F32))]
    all_gather x2 -> x4, waiting for transfers between devices: 7.83 us -> 28.8 us  [the longest x1 28.1 us: per_device(): up_line = lax.all_gather(latent_up.astype(BF16), 'f', axis=0)]
    ppermute x1, waiting for transfers between devices: 3.71 us -> 16.7 us  [plane_scatter(): by_x = lax.ppermute(sums[2].astype(BF16), 'x', SWAP)]
    unnamed x163 -> x120, local copies, waits for them, and re-layouts: 12.6 us -> 23.3 us
  transfers between devices with their start and end apart: 13 -> 19, of which waited for: 3 -> 8; matrix products, arithmetic and copies ran while one was open for 31% -> 21% of each run, Pallas kernels for 29% -> 28%
where the time goes in v3:
time: 924 us; the launch traced here: 915 us
  Pallas kernels  437 us (47%)
  waiting for transfers between devices  161 us (17%)
  matrix products  141 us (15%)
  local copies, waits for them, and re-layouts  76.7 us (8%)
  other arithmetic  74.1 us (8%)
  between operations  15.4 us (2%)
  starting transfers between devices  10.1 us (1%)
    pallas_call x3, Pallas kernels, matmul_scatter(): pl.pallas_call(functools.partial(matmul_scatter_kernel, flip, wide), out_...  159 us
    pallas_call x3, Pallas kernels, plane_gather(): pl.pallas_call(functools.partial(gather_kernel, chunks), out_shape=jax.Sh...  119 us
    pallas_call x1, Pallas kernels, start(): pl.pallas_call(functools.partial(start_kernel, parcel, chunks, units, pad...  83.9 us
    dot_general x10, matrix products, contract(): lax.dot_general(left, right, (((left_dim,), (right_dim,)), ((), ())), pre...  82.1 us
    pallas_call x1, Pallas kernels, end(): pl.pallas_call(functools.partial(end_kernel, parcel, units, padded), out_...  74.8 us
    reduce_scatter x1, waiting for transfers between devices, per_device(): both_grad = lax.psum_scatter(both_grad, 'f', scatter_dimension=0)  59.8 us
    all_gather x1, waiting for transfers between devices, per_device(): up_line = lax.all_gather(latent_up.astype(BF16), 'f', axis=0)  28.1 us
    ppermute x2, waiting for transfers between devices, swap_halves(): return (own, lax.ppermute(other, 'y', SWAP).astype(F32))  24 us
  transfers between devices with their start and end apart: 19, of which 8 were waited for; matrix products, arithmetic and copies ran while one was open for 21% of the time, Pallas kernels for 28%

profile of v3, /device:TPU:10, one launch (start us, length us, event | category | flops | bytes accessed | tf_op | source)
XLA Modules:
  0.0 915.1 jit_solution(6720722132579682888)
XLA Ops:
  11.2 28.1 %all-gather.9.cloned.1.call-done = bf16[2048,256]{1,0:T(8,128)(2,1)} async-done(((bf16[512,256]{1,0:T(8,128)(2,1)}), bf16[2048,256]{1,0:T(8,128)(2,1)}) %all-gather.9.cloned.1.call-update) | async-done | bytes 1048592 | tf_op jit(solution)/shard_map/all_gather | solution.py:780
  40.1 83.9 %shard_map.220 = (bf16[1024,2048]{1,0:T(8,128)(2,1)}, bf16[2048,256]{1,0:T(8,128)(2,1)}, bf16[8,4,16,128]{3,2,1,0:T(8,128)(2,1)}, bf16[8,64,1536]{2,1,0:T(8,128)(2,1)}, bf16[8,256,2048]{2,1,0:T(8,128)(2,1)}) custom-call(f32[512,128]{1,0:T(8,128)} %down_ref.1, f32[64,256]{1,0:T(8,128)} %kv_ref.1, bf16[16,128]{1,0:T(8,128)(2,1)} %pad.33.small_ref, ...), custom_call_target="tpu_custom_call" | custom-call | bytes 251658240 | tf_op jit(solution)/shard_map/pallas_call | solution.py:467
  146.5 39.9 %shard_map.221 = bf16[8,256,1536]{2,1,0:T(8,128)(2,1)} custom-call(bf16[256,1536]{1,0:T(8,128)(2,1)} %pad_maximum_fusion.9.in_ref), custom_call_target="tpu_custom_call" | custom-call | bytes 167772160 | tf_op jit(solution)/shard_map/pallas_call | solution.py:156
  193.5 6.5 copy.198
  224.4 6.2 copy.181
  235.3 8.4 collective-permute-done.1
  247.7 58.1 %shard_map.222 = f32[256,2048]{1,0:T(8,128)} custom-call(bf16[2048,512]{1,0:T(8,128)(2,1)} %bitcast.289, bf16[512,2048]{1,0:T(8,128)(2,1)} %bitcast.301), custom_call_target="tpu_custom_call" | custom-call | flops 4294967296 | bytes 167772160 | tf_op jit(solution)/shard_map/pallas_call | solution.py:235
  309.0 39.7 %shard_map.223 = bf16[8,256,2048]{2,1,0:T(8,128)(2,1)} custom-call(bf16[256,2048]{1,0:T(8,128)(2,1)} %multiply_convert_fusion.3.in_ref), custom_call_target="tpu_custom_call" | custom-call | bytes 167772160 | tf_op jit(solution)/shard_map/pallas_call | solution.py:156
  348.7 19.3 %fusion.80 = f32[2048,1536]{1,0:T(8,128)} fusion(bf16[2048,2048]{1,0:T(8,128)(2,1)} %bitcast.281, bf16[2048,1536]{1,0:T(8,128)(2,1)} %bitcast.323), kind=kOutput, calls=%fused_computation.194 | convolution fusion | flops 12884901888 | bytes 27262976 | tf_op jit(solution)/shard_map/dot_general | solution.py:841
  367.9 17.0 %multiply_convert_fusion.1 = (bf16[2048,768]{1,0:T(8,128)(2,1)S(1)}, bf16[2048,768]{1,0:T(8,128)(2,1)S(1)}, bf16[2048,768]{1,0:T(8,128)(2,1)}) fusion(f32[2048,1536]{1,0:T(8,128)} %fusion.80, bf16[2048,2048]{1,0:T(8,128)(2,1)} %bitcast.321, bf16[704,2048]{1,0:T(8,128)(2,1)} %all-gather.15.cloned.1.call-done), kind=kOutput, calls=%fused_computation.3 | convolution fusion | flops 6467616768 | bytes 33292288 | tf_op jit(solution)/shard_map/dot_general | solution.py:21
  390.7 62.2 %shard_map.224 = f32[256,2048]{1,0:T(8,128)} custom-call(bf16[2048,1536]{1,0:T(8,128)(2,1)} %pad_maximum_fusion.refs_0_, bf16[2048,1536]{1,0:T(8,128)(2,1)} %bitcast.324), custom_call_target="tpu_custom_call" | custom-call | flops 12884901888 | bytes 167772160 | tf_op jit(solution)/shard_map/pallas_call | solution.py:235
  457.7 39.6 %shard_map.225 = bf16[8,256,2048]{2,1,0:T(8,128)(2,1)} custom-call(bf16[256,2048]{1,0:T(8,128)(2,1)} %get-tuple-element.56.in_ref), custom_call_target="tpu_custom_call" | custom-call | bytes 167772160 | tf_op jit(solution)/shard_map/pallas_call | solution.py:156
  497.3 9.9 %convolution_convert_fusion.2 = bf16[2048,512]{1,0:T(8,128)(2,1)} fusion(bf16[2048,2048]{1,0:T(8,128)(2,1)} %bitcast.283, bf16[512,2048]{1,0:T(8,128)(2,1)} %bitcast.302), kind=kOutput, calls=%fused_computation.26 | convolution fusion | flops 4296015872 | bytes 12582912 | tf_op jit(solution)/shard_map/dot_general | solution.py:21
  555.9 8.2 fusion.83
  570.7 20.5 %collective-permute-done.10 = bf16[2,1,128,2048]{3,2,1,0:T(8,128)(2,1)S(1)} collective-permute-done((bf16[2,1,128,2048]{3,2,1,0:T(8,128)(2,1)}, bf16[2,1,128,2048]{3,2,1,0:T(8,128)(2,1)S(1)}, u32[]{:S(2)}, u32[]{:S(2)}) %collective-permute-start.10) | collective-permute-done | bytes 1048608 | tf_op jit(solution)/shard_map/ppermute | solution.py:898
  594.9 10.2 %fusion.84 = bf16[768,2048]{1,0:T(8,128)(2,1)S(1)} fusion(bf16[2048,768]{1,0:T(8,128)(2,1)} %get-tuple-element.66, bf16[2048,2048]{1,0:T(8,128)(2,1)} %bitcast.322), kind=kOutput, calls=%fused_computation.198 | convolution fusion | flops 6442450944 | bytes 14680064 | tf_op jit(solution)/shard_map/dot_general | solution.py:21
  606.9 19.7 %convolution_convert_fusion = bf16[2048,1536]{1,0:T(8,128)(2,1)} fusion(bf16[2048,2048]{1,0:T(8,128)(2,1)} %bitcast.282, bf16[2048,768]{1,0:T(8,128)(2,1)} %copy-done.25, bf16[2048,768]{1,0:T(8,128)(2,1)} %copy-done.24), kind=kOutput, calls=%fused_computation | convolution fusion | flops 12900630528 | bytes 20971520 | tf_op jit(solution)/shard_map/dot_general | solution.py:21
  626.6 9.7 %fusion.8 = f32[2048,2048]{1,0:T(8,128)S(1)} fusion(bf16[2048,768]{1,0:T(8,128)(2,1)} %get-tuple-element.66, bf16[704,2048]{1,0:T(8,128)(2,1)} %all-gather.15.cloned.1.call-done), kind=kOutput, calls=%fused_computation.29 | convolution fusion | flops 6442450944 | bytes 22806528 | tf_op jit(solution)/shard_map/dot_general | solution.py:852
  651.1 39.0 %shard_map.226 = f32[256,1280]{1,0:T(8,128)} custom-call(bf16[2048,512]{1,0:T(8,128)(2,1)} %bitcast.287, bf16[1024,512]{1,0:T(8,128)(2,1)} %bitcast.295, f32[2048,256]{1,0:T(8,128)} %bitcast.325), custom_call_target="tpu_custom_call" | custom-call | flops 2147483648 | bytes 167772160 | tf_op jit(solution)/shard_map/pallas_call | solution.py:235
  700.9 6.2 fusion.23
  716.4 16.7 %collective-permute-done.4 = bf16[256,2048]{1,0:T(8,128)(2,1)S(1)} collective-permute-done((bf16[256,2048]{1,0:T(8,128)(2,1)S(1)}, bf16[256,2048]{1,0:T(8,128)(2,1)S(1)}, u32[]{:S(2)}, u32[]{:S(2)}) %collective-permute-start.4) | collective-permute-done | bytes 1048608 | tf_op jit(solution)/shard_map/ppermute | solution.py:72
  733.1 22.8 %collective-permute-done.6 = bf16[256,2048]{1,0:T(8,128)(2,1)S(1)} collective-permute-done((bf16[256,2048]{1,0:T(8,128)(2,1)S(1)}, bf16[256,2048]{1,0:T(8,128)(2,1)S(1)}, u32[]{:S(2)}, u32[]{:S(2)}) %collective-permute-start.6) | collective-permute-done | bytes 1048608 | tf_op jit(solution)/shard_map/ppermute | solution.py:71
  764.0 59.8 %reduce-scatter.5.cloned.1.call-done = bf16[1,8,64,1536]{3,2,1,0:T(8,128)(2,1)} async-done(((bf16[4,8,64,1536]{3,2,1,0:T(8,128)(2,1)}), bf16[1,8,64,1536]{3,2,1,0:T(8,128)(2,1)}) %reduce-scatter.5.cloned.1.call-update) | async-done | bytes 1572880 | tf_op jit(solution)/shard_map/reduce_scatter | solution.py:857
  823.8 74.8 %shard_map.227 = (f32[512,128]{1,0:T(8,128)}, f32[64,256]{1,0:T(8,128)}, f32[16,128]{1,0:T(8,128)}, f32[64,5632]{1,0:T(8,128)}, f32[64,5632]{1,0:T(8,128)}) custom-call(bf16[1024,2048]{1,0:T(8,128)(2,1)} %convolution_convert_fusion.1.down_ref, bf16[2048,256]{1,0:T(8,128)(2,1)} %convolution_convert_fusion.3.kv_ref, bf16[8,4,16,128]{3,2,1,0:T(8,128)(2,1)} %fusion.55.small_ref, ...), custom_call_target="tpu_custom_call" | custom-call | bytes 251658240 | tf_op jit(solution)/shard_map/pallas_call | solution.py:670
  (268 shorter events, 193.2 us)
Async XLA Ops:
  7.2 32.2 %copy-start.50 = (f32[512]{0:T(512)S(1)}, f32[512]{0:T(512)}, u32[]{:S(2)}) copy-start(f32[512]{0:T(512)} %param.17) | copy-start | bytes 6148
  7.2 32.0 %all-gather.9.cloned.1.call-start = ((), (), s32[]{:S(2)}) async-start(), calls=%async_computation.8 | async-start | bytes 1310720 | tf_op jit(solution)/shard_map/all_gather | solution.py:780
  9.1 115.0 %all-gather.11.cloned.1.call-start = ((), (), s32[]{:S(2)}) async-start(), calls=%async_computation.9 | async-start | bytes 2621440 | tf_op jit(solution)/shard_map/all_gather | solution.py:781
  39.3 208.3 %all-gather.13.cloned.1.call-start = ((), (), s32[]{:S(2)}) async-start(), calls=%async_computation.10 | async-start | bytes 7864320 | tf_op jit(solution)/shard_map/all_gather | solution.py:796
  124.1 243.8 %all-gather.15.cloned.1.call-start = ((), (), s32[]{:S(2)}) async-start(), calls=%async_computation.11 | async-start | bytes 3604480 | tf_op jit(solution)/shard_map/all_gather | solution.py:798
  133.7 79.4 %copy-start.8 = (f32[8,256,128]{1,2,0:T(8,128)}, f32[8,256,128]{1,2,0:T(8,128)S(1)}, u32[]{:S(2)}) copy-start(f32[8,256,128]{1,2,0:T(8,128)S(1)} %copy.176) | copy-start | bytes 3145732
  144.1 56.5 %collective-permute-start = (bf16[2,512,256]{2,0,1:T(2,128)(2,1)}, bf16[2,512,256]{2,0,1:T(2,128)(2,1)}, u32[]{:S(2)}, u32[]{:S(2)}) collective-permute-start(bf16[2,512,256]{2,0,1:T(2,128)(2,1)} %copy.230), channel_id=1, source_target_pairs={{0,1},{1,0},{2,3},{3,2},{4,5},{5,4},{6,7},{7,6},{8,9},{9,8},{10,11... | collective-permute-start | bytes 1572872 | tf_op jit(solution)/shard_map/ppermute | solution.py:786
  217.9 25.8 %collective-permute-start.1 = (bf16[2,128,2048]{2,1,0:T(8,128)(2,1)}, bf16[2,128,2048]{2,1,0:T(8,128)(2,1)}, u32[]{:S(2)}, u32[]{:S(2)}) collective-permute-start(bf16[2,128,2048]{2,1,0:T(8,128)(2,1)} %constant_dynamic-slice_fusion), channel_id=1, source_target_pairs={{0,1},{1,0},{2,3},{3,2},{4,5},{5,4},{6,7},{7,6},{8,9},{9,8},{10,11... | collective-permute-start | bytes 3145736 | tf_op jit(solution)/shard_map/ppermute | solution.py:786
  247.7 510.0 %reduce-scatter.7.cloned.1.call-start = ((), (), s32[]{:S(2)}) async-start(), calls=%async_computation.5 | async-start | bytes 1310720 | tf_op jit(solution)/shard_map/reduce_scatter | solution.py:902
  554.6 14.8 %collective-permute-start.9 = (bf16[512,2,256]{2,0,1:T(8,128)(2,1)S(1)}, bf16[512,2,256]{2,0,1:T(8,128)(2,1)S(1)}, u32[]{:S(2)}, u32[]{:S(2)}) collective-permute-start(bf16[512,2,256]{2,0,1:T(8,128)(2,1)S(1)} %fusion.47), channel_id=1, source_target_pairs={{0,1},{1,0},{2,3},{3,2},{4,5},{5,4},{6,7},{7,6},{8,9},{9,8},{10,11... | collective-permute-start | bytes 1572872 | tf_op jit(solution)/shard_map/ppermute | solution.py:898
  565.2 26.1 %collective-permute-start.10 = (bf16[2,1,128,2048]{3,2,1,0:T(8,128)(2,1)}, bf16[2,1,128,2048]{3,2,1,0:T(8,128)(2,1)S(1)}, u32[]{:S(2)}, u32[]{:S(2)}) collective-permute-start(bf16[2,1,128,2048]{3,2,1,0:T(8,128)(2,1)} %dynamic-slice_convert_fusion), channel_id=1, source_target_pairs={{0,1},{1,0},{2,3},{3,2},{4,5},{5,4},{6,7},{7,6},{8,9},{9,8},{10,11... | collective-permute-start | bytes 3145736 | tf_op jit(solution)/shard_map/ppermute | solution.py:898
  570.7 188.8 %reduce-scatter.9.cloned.1.call-start = ((), (), s32[]{:S(2)}) async-start(), calls=%async_computation.6 | async-start | bytes 2621440 | tf_op jit(solution)/shard_map/reduce_scatter | solution.py:905
  594.8 166.8 %reduce-scatter.11.cloned.1.call-start = ((), (), s32[]{:S(2)}) async-start(), calls=%async_computation.7 | async-start | bytes 3604480 | tf_op jit(solution)/shard_map/reduce_scatter | solution.py:860
  606.9 216.9 %reduce-scatter.5.cloned.1.call-start = ((), (), s32[]{:S(2)}) async-start(), calls=%async_computation.4 | async-start | bytes 7864320 | tf_op jit(solution)/shard_map/reduce_scatter | solution.py:857
  644.4 56.5 %collective-permute-start.2 = (bf16[256,2048]{1,0:T(8,128)(2,1)}, bf16[256,2048]{1,0:T(8,128)(2,1)}, u32[]{:S(2)}, u32[]{:S(2)}) collective-permute-start(bf16[256,2048]{1,0:T(8,128)(2,1)} %get-tuple-element.70), channel_id=1, source_target_pairs={{0,2},{2,0},{1,3},{3,1},{4,6},{6,4},{5,7},{7,5},{8,10},{10,8},{9,1... | collective-permute-start | bytes 3145736 | tf_op jit(solution)/shard_map/ppermute | solution.py:70
  644.4 56.5 %collective-permute-start.3 = (bf16[256,2048]{1,0:T(8,128)(2,1)}, bf16[256,2048]{1,0:T(8,128)(2,1)}, u32[]{:S(2)}, u32[]{:S(2)}) collective-permute-start(bf16[256,2048]{1,0:T(8,128)(2,1)} %get-tuple-element.69), channel_id=1, source_target_pairs={{0,2},{2,0},{1,3},{3,1},{4,6},{6,4},{5,7},{7,5},{8,10},{10,8},{9,1... | collective-permute-start | bytes 3145736 | tf_op jit(solution)/shard_map/ppermute | solution.py:70
  644.9 56.0 %collective-permute-start.5 = (bf16[256,2048]{1,0:T(8,128)(2,1)}, bf16[256,2048]{1,0:T(8,128)(2,1)}, u32[]{:S(2)}, u32[]{:S(2)}) collective-permute-start(bf16[256,2048]{1,0:T(8,128)(2,1)} %get-tuple-element.68), channel_id=1, source_target_pairs={{0,2},{2,0},{1,3},{3,1},{4,6},{6,4},{5,7},{7,5},{8,10},{10,8},{9,1... | collective-permute-start | bytes 3145736 | tf_op jit(solution)/shard_map/ppermute | solution.py:70
  644.9 56.0 %collective-permute-start.7 = (bf16[256,2048]{1,0:T(8,128)(2,1)}, bf16[256,2048]{1,0:T(8,128)(2,1)}, u32[]{:S(2)}, u32[]{:S(2)}) collective-permute-start(bf16[256,2048]{1,0:T(8,128)(2,1)} %get-tuple-element.67), channel_id=1, source_target_pairs={{0,2},{2,0},{1,3},{3,1},{4,6},{6,4},{5,7},{7,5},{8,10},{10,8},{9,1... | collective-permute-start | bytes 3145736 | tf_op jit(solution)/shard_map/ppermute | solution.py:70
  651.1 39.1 %copy-start.7 = (f32[256,1024]{1,0:T(8,128)S(1)}, f32[256,1024]{1,0:T(8,128)}, u32[]{:S(2)}) copy-start(f32[256,1024]{1,0:T(8,128)} %copy-done.6) | copy-start | bytes 3145732
  651.1 39.1 %copy-start.43 = (f32[2,1,4,128]{3,2,1,0:T(4,128)S(1)}, f32[2,1,4,128]{3,2,1,0:T(4,128)}, u32[]{:S(2)}) copy-start(f32[2,1,4,128]{3,2,1,0:T(4,128)} %copy-done.42) | copy-start | bytes 12292
  651.1 39.1 %copy-start.45 = (f32[256]{0:T(256)S(1)}, f32[256]{0:T(256)}, u32[]{:S(2)}) copy-start(f32[256]{0:T(256)} %copy-done.44) | copy-start | bytes 3076
  707.0 26.1 %collective-permute-start.4 = (bf16[256,2048]{1,0:T(8,128)(2,1)S(1)}, bf16[256,2048]{1,0:T(8,128)(2,1)S(1)}, u32[]{:S(2)}, u32[]{:S(2)}) collective-permute-start(bf16[256,2048]{1,0:T(8,128)(2,1)S(1)} %get-tuple-element.64), channel_id=1, source_target_pairs={{0,4},{4,0},{1,5},{5,1},{2,6},{6,2},{3,7},{7,3},{8,12},{12,8},{9,1... | collective-permute-start | bytes 3145736 | tf_op jit(solution)/shard_map/ppermute | solution.py:72
  708.4 47.5 %collective-permute-start.6 = (bf16[256,2048]{1,0:T(8,128)(2,1)S(1)}, bf16[256,2048]{1,0:T(8,128)(2,1)S(1)}, u32[]{:S(2)}, u32[]{:S(2)}) collective-permute-start(bf16[256,2048]{1,0:T(8,128)(2,1)S(1)} %get-tuple-element.63), channel_id=1, source_target_pairs={{0,1},{1,0},{2,3},{3,2},{4,5},{5,4},{6,7},{7,6},{8,9},{9,8},{10,11... | collective-permute-start | bytes 3145736 | tf_op jit(solution)/shard_map/ppermute | solution.py:71
  709.1 46.8 %collective-permute-start.8 = (bf16[256,2048]{1,0:T(8,128)(2,1)S(1)}, bf16[256,2048]{1,0:T(8,128)(2,1)S(1)}, u32[]{:S(2)}, u32[]{:S(2)}) collective-permute-start(bf16[256,2048]{1,0:T(8,128)(2,1)S(1)} %get-tuple-element.62), channel_id=1, source_target_pairs={{0,5},{5,0},{1,4},{4,1},{2,7},{7,2},{3,6},{6,3},{8,13},{13,8},{9,1... | collective-permute-start | bytes 3145736 | tf_op jit(solution)/shard_map/ppermute | solution.py:73
  (51 other events, 322.0 us)
Sparse Core Ops, SparseCore 0:
  10.2 29.0 all-gather.8
  41.4 49.0 all-gather.10
  124.2 123.3 all-gather.12
  249.0 66.1 all-gather.14
  570.8 35.2 reduce-scatter.6
  608.4 42.3 reduce-scatter.8
  653.0 57.0 reduce-scatter.10
  712.5 111.2 reduce-scatter.4

commit v4 on v3

--- a/solution.py
+++ b/solution.py
@@ -32,11 +32,8 @@
     ends = jnp.sum(jnp.where(spots[None, :] <= spots[:, None], lengths[..., None, :], 0), axis=-1)
     places = jnp.arange(count, dtype=jnp.int32)
     passed = places[:, None] >= ends[..., None, :]
-    segment = jnp.sum(passed.astype(jnp.int32), axis=-1)
     offset = jnp.sum(jnp.where(passed, lengths[..., None, :], 0), axis=-1)
-    position = (places - offset).astype(F32)
-    same = segment[..., :, None] == segment[..., None, :]
-    return position, same & (places[None, :] <= places[:, None])
+    return (places - offset).astype(F32), offset
 
 
 def rope_tables(position, width):
@@ -55,31 +52,17 @@
     )
 
 
-def unrotate(grads, cosine, sine):
-    return rotate(grads, cosine, -sine)
-
-
 SWAP = [(0, 1), (1, 0)]
 DIAGONAL = [(0, 3), (3, 0), (1, 2), (2, 1)]
 
 
-def plane_scatter(parts):
-    low = parts.astype(BF16)
-    sums = []
-    for near, far in ((0, 2), (1, 3), (4, 6), (5, 7)):
-        sums.append(parts[near].astype(F32) + lax.ppermute(low[far], "c", SWAP).astype(F32))
-    by_y = lax.ppermute(sums[1].astype(BF16), "y", SWAP)
-    by_x = lax.ppermute(sums[2].astype(BF16), "x", SWAP)
-    by_both = lax.ppermute(sums[3].astype(BF16), ("x", "y"), DIAGONAL)
-    return sums[0], by_x, by_y, by_both
-
-
-X_BIT, C_BIT, Y_BIT = 4, 2, 1
-VMEM_MOST = 56 * 2**20
+X_BIT, Y_BIT, C_BIT = 4, 2, 1
+BOTH = X_BIT | Y_BIT
+VMEM_MOST = 60 * 2**20
 
 
 def other(bits):
-    flips = {"x": bits // 4, "c": bits // 2 % 2, "y": bits % 2}
+    flips = {"x": bits // 4, "y": bits // 2 % 2, "c": bits % 2}
     return {name: 1 - lax.axis_index(name) for name, flip in flips.items() if flip}
 
 
@@ -96,66 +79,86 @@
     )
 
 
+def begin(copies):
+    for copy in copies:
+        copy.start()
+
+
+def arrive(copies):
+    for copy in copies:
+        copy.wait_recv()
+
+
+def gone(copies):
+    for copy in copies:
+        copy.wait_send()
+
+
 def gathering(chunks, in_ref, out_ref, send_sem, recv_sem):
-    rows = in_ref.shape[0] // chunks
-    both = X_BIT | Y_BIT
-
-    def to(slot, k, bits, source):
-        part = pl.ds(k * rows, rows)
-        return send(
-            source.at[part], out_ref.at[slot, part], send_sem.at[slot, k], recv_sem.at[slot, k], other(bits)
-        )
+    tokens = in_ref.shape[0]
+    rows = tokens // chunks
+
+    def to(slot, k, bits, source=None):
+        target = out_ref.at[pl.ds(slot * tokens + k * rows, rows)]
+        if source is None:
+            source = in_ref.at[pl.ds(k * rows, rows)]
+        else:
+            source = out_ref.at[pl.ds(source * tokens + k * rows, rows)]
+        return send(source, target, send_sem.at[slot, k], recv_sem.at[slot, k], other(bits))
 
     def own():
         for k in range(chunks):
-            to(X_BIT, k, X_BIT, in_ref).start()
-            to(Y_BIT, k, Y_BIT, in_ref).start()
+            to(X_BIT, k, X_BIT).start()
+            to(Y_BIT, k, Y_BIT).start()
         for k in range(chunks):
-            to(C_BIT, k, C_BIT, in_ref).start()
+            to(C_BIT, k, C_BIT).start()
 
     def relay(first, last):
         for k in range(first, last):
-            to(X_BIT, k, X_BIT, in_ref).wait_recv()
+            to(X_BIT, k, X_BIT).wait_recv()
             if k < chunks // 2:
-                to(both, k, Y_BIT, out_ref.at[X_BIT]).start()
-            to(X_BIT | C_BIT, k, C_BIT, out_ref.at[X_BIT]).start()
-            to(Y_BIT, k, Y_BIT, in_ref).wait_recv()
+                to(BOTH, k, Y_BIT, X_BIT).start()
+            to(X_BIT | C_BIT, k, C_BIT, X_BIT).start()
+            to(Y_BIT, k, Y_BIT).wait_recv()
             if k >= chunks // 2:
-                to(both, k, X_BIT, out_ref.at[Y_BIT]).start()
-            to(Y_BIT | C_BIT, k, C_BIT, out_ref.at[Y_BIT]).start()
+                to(BOTH, k, X_BIT, Y_BIT).start()
+            to(Y_BIT | C_BIT, k, C_BIT, Y_BIT).start()
 
     def far():
         for k in range(chunks):
-            to(both, k, Y_BIT, in_ref).wait_recv()
-            to(7, k, C_BIT, out_ref.at[both]).start()
-
-    def end():
+            to(BOTH, k, Y_BIT).wait_recv()
+            to(BOTH | C_BIT, k, C_BIT, BOTH).start()
+
+    def arrived(chip):
+        for k in range(chunks):
+            to(chip | C_BIT, k, C_BIT).wait_recv()
+
+    def sent():
         for slot in range(1, 8):
             for k in range(chunks):
-                copy = to(slot, k, slot, in_ref)
-                if slot & C_BIT:
-                    copy.wait_recv()
-                copy.wait_send()
-
-    return own, relay, far, end
+                to(slot, k, C_BIT).wait_send()
+
+    return own, relay, far, arrived, sent
 
 
 def gather_kernel(chunks, in_ref, out_ref, own_sem, send_sem, recv_sem):
     greet([other(C_BIT), other(X_BIT), other(Y_BIT)])
-    copy = pltpu.make_async_copy(in_ref, out_ref.at[0], own_sem)
+    copy = pltpu.make_async_copy(in_ref, out_ref.at[pl.ds(0, in_ref.shape[0])], own_sem)
     copy.start()
-    own, relay, far, end = gathering(chunks, in_ref, out_ref, send_sem, recv_sem)
+    own, relay, far, arrived, sent = gathering(chunks, in_ref, out_ref, send_sem, recv_sem)
     own()
     relay(0, chunks)
     far()
     copy.wait()
-    end()
+    for chip in (0, Y_BIT, X_BIT, BOTH):
+        arrived(chip)
+    sent()
 
 
 def plane_gather(block, name, chunks=4):
     return pl.pallas_call(
         functools.partial(gather_kernel, chunks),
-        out_shape=jax.ShapeDtypeStruct((8, *block.shape), block.dtype),
+        out_shape=jax.ShapeDtypeStruct((8 * block.shape[0], block.shape[1]), block.dtype),
         in_specs=[pl.BlockSpec(memory_space=pl.ANY)],
         out_specs=pl.BlockSpec(memory_space=pl.ANY),
         scratch_shapes=[
@@ -168,90 +171,443 @@
     )(block)
 
 
-def matmul_scatter_kernel(flip, wide, *refs):
-    left_ref, right_ref, *more_ref, out_ref, part_ref, near_ref, sum_ref, far_ref = refs[:-4]
-    near_send, near_recv, chip_send, chip_recv = refs[-4:]
+def row_loop(amount, do, size=32):
+    @pl.loop(0, amount // size)
+    def _(r):
+        do(pl.ds(pl.multiple_of(r * size, size), size))
+
+
+def scattering(
+    out_ref, work_ref, near_ref, far_ref, near_send, near_recv, far_send, far_recv, produce
+):
+    greet([other(C_BIT), other(X_BIT), other(Y_BIT)])
     tokens = out_ref.shape[0]
+    half = tokens // 2
+    low, high = pl.ds(0, half), pl.ds(half, half)
+
+    def near(n):
+        return send(
+            work_ref.at[n, pl.ds(tokens, tokens)], near_ref.at[n], near_send.at[n], near_recv.at[n], other(C_BIT)
+        )
+
+    def hop(i):
+        n, part, bits = (
+            (0, low, X_BIT), (0, high, Y_BIT), (1, low, X_BIT), (2, high, Y_BIT), (1, high, X_BIT), (2, low, Y_BIT)
+        )[i]
+        return send(work_ref.at[n, part], far_ref.at[i], far_send.at[i], far_recv.at[i], other(bits))
+
+    def chip_sum(n):
+        near(n).wait_recv()
+
+        def keep(at):
+            total = work_ref[n, at, :].astype(F32) + near_ref[n, at, :].astype(F32)
+            work_ref[n, at, :] = total.astype(BF16)
+
+        row_loop(tokens, keep)
+
+    @pl.loop(0, 4)
+    def _(n):
+        produce(3 - n, work_ref.at[n])
+        near(n).start()
+
+        @pl.when(n > 0)
+        def _():
+            chip_sum(n - 1)
+            pl.when(n == 1)(lambda: begin([hop(0), hop(1)]))
+            pl.when(n == 2)(lambda: hop(2).start())
+            pl.when(n == 3)(lambda: hop(3).start())
+
+    near(3).wait_recv()
+
+    def give(at):
+        out_ref[at, :] = work_ref[3, at, :].astype(F32) + near_ref[3, at, :].astype(F32)
+
+    row_loop(tokens, give)
+    for came, n, first, on in ((0, 2, 0, 5), (1, 1, half, 4)):
+        hop(came).wait_recv()
+
+        def add(at, came=came, n=n, first=first):
+            here = pl.ds(pl.multiple_of(first + at.start, 32), 32)
+            total = work_ref[n, here, :].astype(F32) + far_ref[came, at, :].astype(F32)
+            work_ref[n, here, :] = total.astype(BF16)
+
+        row_loop(half, add)
+        hop(on).start()
+
+    def last(came, first):
+        for i in came:
+            hop(i).wait_recv()
+
+        def add(at):
+            here = pl.ds(pl.multiple_of(first + at.start, 32), 32)
+            value = out_ref[here, :]
+            for i in came:
+                value = value + far_ref[i, at, :].astype(F32)
+            out_ref[here, :] = value
+
+        row_loop(half, add)
+
+    last((2, 5), 0)
+    last((3, 4), half)
+    gone([*[near(n) for n in range(4)], *[hop(i) for i in range(6)]])
+
+
+def scatter_scratch(tokens, wide):
+    dma = pltpu.SemaphoreType.DMA
+    return [
+        pltpu.VMEM((4, 2 * tokens, wide), BF16),
+        pltpu.VMEM((4, tokens, wide), BF16),
+        pltpu.VMEM((6, tokens // 2, wide), BF16),
+        dma((4,)), dma((4,)),
+        dma((6,)), dma((6,)),
+    ]
+
+
+def vmem_call(kernel, out_shape, amount, scratch, name, flops, *arrays):
+    vmem = pl.BlockSpec(memory_space=pltpu.VMEM)
+    return pl.pallas_call(
+        kernel,
+        out_shape=out_shape,
+        in_specs=[vmem] * amount,
+        out_specs=[vmem] * len(out_shape),
+        scratch_shapes=scratch,
+        compiler_params=pltpu.CompilerParams(
+            collective_id=name, has_side_effects=True, vmem_limit_bytes=VMEM_MOST
+        ),
+        cost_estimate=pl.CostEstimate(flops=flops, bytes_accessed=160 * 2**20, transcendentals=0),
+    )(*arrays)
+
+
+def turn(values, cosine, sine):
+    half = values.shape[-1] // 2
+    first, second = values[:, :half], values[:, half:]
+    return jnp.concatenate([first * cosine - second * sine, second * cosine + first * sine], axis=1)
+
+
+def masked_scores(queries, keys, begins):
+    raw = contract(queries, keys, 1, 1) * HEAD_DIM**-0.5
+    to = lax.broadcasted_iota(jnp.int32, raw.shape, 0)
+    of = lax.broadcasted_iota(jnp.int32, raw.shape, 1)
+    return jnp.where((of <= to) & (of >= begins), raw, NEGATIVE)
+
+
+def halves(rank):
+    half = rank // 2
+    y = lax.axis_index("y")
+    return (
+        pl.ds(pl.multiple_of(y * half, half), half),
+        pl.ds(pl.multiple_of(half - y * half, half), half),
+    )
+
+
+def attention_kernel(
+    rank, rows_ref, own_ref, far_ref, out_w_ref, cos_ref, sin_ref, begin_ref,
+    branch_ref, query_ref, lse_ref, att_ref, *rest,
+):
+    wide = out_w_ref.shape[1]
+    tokens = branch_ref.shape[0]
+    mine, theirs = halves(rank)
+
+    def produce(chip, target):
+        pair = pl.ds(pl.multiple_of(chip * 2 * tokens, 2 * tokens), 2 * tokens)
+        queries = contract(rows_ref[pair, mine], own_ref[...], 1, 0)
+        queries = queries + contract(rows_ref[pair, theirs], far_ref[...], 1, 0)
+        for c in range(2):
+            rows = pl.ds(pl.multiple_of((2 * chip + c) * tokens, tokens), tokens)
+            keys = rows_ref[rows, rank : rank + HEAD_DIM]
+            values = rows_ref[rows, rank + HEAD_DIM :]
+            cosine, sine, begins = cos_ref[rows, :], sin_ref[rows, :], begin_ref[rows, :]
+            for h in range(2):
+                at = slice(h * HEAD_DIM, (h + 1) * HEAD_DIM)
+                turned = turn(queries[c * tokens : (c + 1) * tokens, at], cosine, sine).astype(BF16)
+                query_ref[rows, at] = turned
+                scores = masked_scores(turned, keys, begins)
+                peak = jnp.max(scores, axis=1, keepdims=True)
+                lse = peak + jnp.log(jnp.sum(jnp.exp(scores - peak), axis=1, keepdims=True))
+                lse_ref[rows, h : h + 1] = lse
+                probs = jnp.exp(scores - lse).astype(BF16)
+                att_ref[rows, at] = contract(probs, values, 1, 0).astype(BF16)
+
+        @pl.loop(0, wide // 512)
+        def _(i):
+            at = pl.ds(pl.multiple_of(i * 512, 512), 512)
+            target[:, at] = contract(att_ref[pair, :], out_w_ref[:, at], 1, 0).astype(BF16)
+
+    scattering(branch_ref, *rest, produce)
+
+
+def attention(rows, own, far, out_w, cosine, sine, begins, name):
+    tokens, rank = rows.shape[0] // 8, 2 * own.shape[0]
+    wide = out_w.shape[1]
+    two = 2 * HEAD_DIM
+    return vmem_call(
+        functools.partial(attention_kernel, rank),
+        [
+            jax.ShapeDtypeStruct((tokens, wide), F32),
+            jax.ShapeDtypeStruct((8 * tokens, two), BF16),
+            jax.ShapeDtypeStruct((8 * tokens, 2), F32),
+            jax.ShapeDtypeStruct((8 * tokens, two), BF16),
+        ],
+        7,
+        scatter_scratch(tokens, wide),
+        name,
+        16 * tokens * two * (wide + rank + 2 * tokens),
+        rows, own, far, out_w, cosine, sine, begins,
+    )
+
+
+def attention_back_kernel(
+    rank, d_ref, rows_ref, own_ref, far_ref, out_w_ref, cos_ref, sin_ref, begin_ref, query_ref, lse_ref,
+    back_ref, dq_ref, *rest,
+):
+    tokens = back_ref.shape[0]
+    mine, theirs = halves(rank)
+    scale = HEAD_DIM**-0.5
+
+    def produce(chip, target):
+        pair = pl.ds(pl.multiple_of(chip * 2 * tokens, 2 * tokens), 2 * tokens)
+        d_pair = contract(d_ref[pair, :], out_w_ref[...], 1, 1).astype(BF16)
+        for c in range(2):
+            rows = pl.ds(pl.multiple_of((2 * chip + c) * tokens, tokens), tokens)
+            here = slice(c * tokens, (c + 1) * tokens)
+            keys = rows_ref[rows, rank : rank + HEAD_DIM]
+            values = rows_ref[rows, rank + HEAD_DIM :]
+            cosine, sine, begins = cos_ref[rows, :], sin_ref[rows, :], begin_ref[rows, :]
+            d_keys = d_values = None
+            for h in range(2):
+                at = slice(h * HEAD_DIM, (h + 1) * HEAD_DIM)
+                queries, d_att = query_ref[rows, at], d_pair[here, at]
+                probs = jnp.exp(masked_scores(queries, keys, begins) - lse_ref[rows, h : h + 1])
+                d_probs = contract(d_att, values, 1, 1)
+                inner = jnp.sum(probs * d_probs, axis=1, keepdims=True)
+                d_scores = (probs * (d_probs - inner)).astype(BF16)
+                d_query = contract(d_scores, keys, 1, 0) * scale
+                dq_ref[rows, at] = turn(d_query, cosine, -sine).astype(BF16)
+                d_k = contract(d_scores, queries, 0, 0)
+                d_v = contract(probs.astype(BF16), d_att, 0, 0)
+                d_keys = d_k if h == 0 else d_keys + d_k
+                d_values = d_v if h == 0 else d_values + d_v
+            shared = turn(d_keys * scale, cosine, -sine) + d_values
+            target[here, rank:] = shared.astype(BF16)
+        target[:, mine] = contract(dq_ref[pair, :], own_ref[...], 1, 1).astype(BF16)
+        target[:, theirs] = contract(dq_ref[pair, :], far_ref[...], 1, 1).astype(BF16)
+
+    scattering(back_ref, *rest, produce)
+
+
+def attention_back(d_rows, rows, own, far, out_w, cosine, sine, begins, queries, lse, name):
+    tokens, rank = rows.shape[0] // 8, 2 * own.shape[0]
+    wide = out_w.shape[1]
+    two = 2 * HEAD_DIM
+    full = rank + HEAD_DIM
+    return vmem_call(
+        functools.partial(attention_back_kernel, rank),
+        [jax.ShapeDtypeStruct((tokens, full), F32), jax.ShapeDtypeStruct((8 * tokens, two), BF16)],
+        10,
+        scatter_scratch(tokens, full),
+        name,
+        16 * tokens * two * (wide + rank + 5 * tokens),
+        d_rows, rows, own, far, out_w, cosine, sine, begins, queries, lse,
+    )
+
+
+def feed_kernel(
+    chunks, in_ref, g_ref, both_ref, down_ref, two_ref, hidden_ref, d_both_ref,
+    g_held, both_held, down_held, own_sem, load_sem, send_sem, recv_sem,
+):
     step = 256
-    greet([other(C_BIT), other(X_BIT), other(Y_BIT), other(X_BIT | Y_BIT)])
-
-    def product(slot, target):
-        @pl.loop(0, wide // step)
+    tokens = in_ref.shape[0]
+    padded = hidden_ref.shape[1]
+    units = down_ref.shape[0]
+    loads = [
+        pltpu.make_async_copy(both_ref, both_held, load_sem.at[0]),
+        pltpu.make_async_copy(g_ref, g_held, load_sem.at[1]),
+        pltpu.make_async_copy(down_ref, down_held.at[pl.ds(0, units)], load_sem.at[2]),
+        pltpu.make_async_copy(in_ref, two_ref.at[pl.ds(0, tokens)], own_sem),
+    ]
+    begin(loads)
+    greet([other(C_BIT), other(X_BIT), other(Y_BIT)])
+    own, relay, far, arrived, sent = gathering(chunks, in_ref, two_ref, send_sem, recv_sem)
+    own()
+    if units < padded:
+        down_held[units:, :] = jnp.zeros((padded - units, down_held.shape[1]), BF16)
+    for copy in loads:
+        copy.wait()
+
+    def units_of(chip):
+        arrived(chip)
+        pair = pl.ds(chip * tokens, 2 * tokens)
+
+        @pl.loop(0, padded // step)
         def _(i):
             at = pl.ds(pl.multiple_of(i * step, step), step)
-            rows = left_ref[slot * tokens : (slot + 1) * tokens, :]
-            if flip:
-                got = contract(rows, right_ref[at, :], 1, 1)
-            else:
-                got = contract(rows, right_ref[:, at], 1, 0)
-            target[:, at] = got.astype(BF16)
-
-        for ref in more_ref:
-            target[:, wide:] = ref[slot * tokens : (slot + 1) * tokens, :].astype(BF16)
-
-    chips = (X_BIT | Y_BIT, X_BIT, Y_BIT, 0)
-    near, far = [], []
-    for i, chip in enumerate(chips):
-        product(chip | C_BIT, part_ref.at[i])
-        copy = send(part_ref.at[i], near_ref.at[i], near_send.at[i], near_recv.at[i], other(C_BIT))
-        copy.start()
-        near.append(copy)
-        product(chip, sum_ref.at[i])
-        copy.wait_recv()
-
-        @pl.loop(0, tokens // 32)
-        def _(r):
-            at = pl.ds(pl.multiple_of(r * 32, 32), 32)
-            total = sum_ref[i, at, :].astype(F32) + near_ref[i, at, :].astype(F32)
-            if chip:
-                sum_ref[i, at, :] = total.astype(BF16)
-            else:
-                out_ref[at, :] = total
-
-        if chip:
-            copy = send(sum_ref.at[i], far_ref.at[i], chip_send.at[i], chip_recv.at[i], other(chip))
-            copy.start()
-            far.append(copy)
-    for copy in far:
-        copy.wait_recv()
-
-    @pl.loop(0, tokens // 32)
-    def _(r):
-        at = pl.ds(pl.multiple_of(r * 32, 32), 32)
-        total = out_ref[at, :]
-        for i in range(3):
-            total = total + far_ref[i, at, :].astype(F32)
-        out_ref[at, :] = total
-
-    for copy in (*near, *far):
-        copy.wait_send()
-
-
-def matmul_scatter(left, right, name, flip=False, *more):
-    tokens, depth = left.shape[0] // 8, left.shape[1]
-    wide = right.shape[0 if flip else 1]
-    full = wide + sum(array.shape[1] for array in more)
-    block = pltpu.VMEM((4, tokens, full), BF16)
+            up_at = pl.ds(pl.multiple_of(padded + i * step, step), step)
+            gate = contract(two_ref[pair, :], both_held[:, at], 1, 0)
+            upval = contract(two_ref[pair, :], both_held[:, up_at], 1, 0)
+            d_hidden = contract(g_held[pair, :], down_held[at, :], 1, 1)
+            sigma = 1.0 / (1.0 + jnp.exp(-gate))
+            silu = gate * sigma
+            hidden_ref[pair, at] = (silu * upval).astype(BF16)
+            d_gate = d_hidden * upval * sigma * (1.0 + gate * (1.0 - sigma))
+            d_both_ref[pair, at] = d_gate.astype(BF16)
+            d_both_ref[pair, up_at] = (d_hidden * silu).astype(BF16)
+
+    units_of(0)
+    relay(0, chunks)
+    units_of(X_BIT)
+    units_of(Y_BIT)
+    far()
+    units_of(BOTH)
+    sent()
+
+
+def feed(rows, g, both, down, padded, name, chunks=4):
+    tokens, width = rows.shape
+    any_space, vmem = pl.BlockSpec(memory_space=pl.ANY), pl.BlockSpec(memory_space=pltpu.VMEM)
+    dma = pltpu.SemaphoreType.DMA
     return pl.pallas_call(
-        functools.partial(matmul_scatter_kernel, flip, wide),
-        out_shape=jax.ShapeDtypeStruct((tokens, full), F32),
-        in_specs=[pl.BlockSpec(memory_space=pltpu.VMEM)] * (2 + len(more)),
-        out_specs=pl.BlockSpec(memory_space=pltpu.VMEM),
+        functools.partial(feed_kernel, chunks),
+        out_shape=[
+            jax.ShapeDtypeStruct((8 * tokens, width), BF16),
+            jax.ShapeDtypeStruct((8 * tokens, padded), BF16),
+            jax.ShapeDtypeStruct((8 * tokens, 2 * padded), BF16),
+        ],
+        in_specs=[any_space] * 4,
+        out_specs=[vmem] * 3,
         scratch_shapes=[
-            block,
-            block,
-            block,
-            pltpu.VMEM((3, tokens, full), BF16),
-            *[pltpu.SemaphoreType.DMA((4,))] * 2,
-            *[pltpu.SemaphoreType.DMA((3,))] * 2,
+            pltpu.VMEM(g.shape, BF16),
+            pltpu.VMEM(both.shape, BF16),
+            pltpu.VMEM((padded, width), BF16),
+            dma,
+            dma((3,)),
+            dma((8, chunks)), dma((8, chunks)),
         ],
         compiler_params=pltpu.CompilerParams(
             collective_id=name, has_side_effects=True, vmem_limit_bytes=VMEM_MOST
         ),
         cost_estimate=pl.CostEstimate(
-            flops=16 * tokens * wide * depth, bytes_accessed=160 * 2**20, transcendentals=0
+            flops=16 * tokens * 3 * width * padded, bytes_accessed=160 * 2**20, transcendentals=0
         ),
-    )(left, right, *more)
+    )(rows, g, both, down)
+
+
+def product_scatter_kernel(left_ref, right_ref, out_ref, *rest):
+    tokens = out_ref.shape[0]
+    step = 256
+
+    def produce(chip, target):
+        pair = pl.ds(pl.multiple_of(chip * 2 * tokens, 2 * tokens), 2 * tokens)
+
+        @pl.loop(0, out_ref.shape[1] // step)
+        def _(i):
+            at = pl.ds(pl.multiple_of(i * step, step), step)
+            target[:, at] = contract(left_ref[pair, :], right_ref[at, :], 1, 1).astype(BF16)
+
+    scattering(out_ref, *rest, produce)
+
+
+def product_scatter(left, right, name):
+    tokens, wide = left.shape[0] // 8, right.shape[0]
+    return vmem_call(
+        product_scatter_kernel,
+        [jax.ShapeDtypeStruct((tokens, wide), F32)],
+        2,
+        scatter_scratch(tokens, wide),
+        name,
+        16 * tokens * wide * left.shape[1],
+        left, right,
+    )[0]
+
+
+def branch_gather_kernel(
+    chunks, in_ref, hidden_ref, down_ref, out_ref, own_sum, chip_sums,
+    down_held, work_ref, near_ref, own_sem, load_sem, send_sem, recv_sem, near_send, near_recv,
+):
+    tokens = in_ref.shape[0]
+    wide = down_ref.shape[1]
+    units, padded = down_ref.shape[0], down_held.shape[0]
+    copies = [
+        pltpu.make_async_copy(in_ref, out_ref.at[pl.ds(0, tokens)], own_sem),
+        pltpu.make_async_copy(down_ref, down_held.at[pl.ds(0, units)], load_sem),
+    ]
+    begin(copies)
+    greet([other(C_BIT), other(X_BIT), other(Y_BIT)])
+    own, relay, far, arrived, sent = gathering(chunks, in_ref, out_ref, send_sem, recv_sem)
+    own()
+    if units < padded:
+        down_held[units:, :] = jnp.zeros((padded - units, wide), BF16)
+    for copy in copies:
+        copy.wait()
+
+    def near(n):
+        return send(
+            work_ref.at[n, pl.ds(tokens, tokens)], near_ref.at[n], near_send.at[n], near_recv.at[n], other(C_BIT)
+        )
+
+    def product(n):
+        pair = slice((3 - n) * 2 * tokens, (4 - n) * 2 * tokens)
+
+        @pl.loop(0, wide // 256)
+        def _(i):
+            at = pl.ds(pl.multiple_of(i * 256, 256), 256)
+            work_ref[n, :, at] = contract(hidden_ref[pair, :], down_held[:, at], 1, 0).astype(BF16)
+
+        near(n).start()
+
+    product(0)
+    product(1)
+    relay(0, chunks // 2)
+    product(2)
+    relay(chunks // 2, chunks)
+    product(3)
+    for n in range(4):
+        near(n).wait_recv()
+
+        def add(at, n=n):
+            total = work_ref[n, at, :].astype(F32) + near_ref[n, at, :].astype(F32)
+            if n < 3:
+                chip_sums[n, at, :] = total.astype(BF16)
+            else:
+                own_sum[at, :] = total
+
+        row_loop(tokens, add)
+    far()
+    for chip in (0, Y_BIT, X_BIT, BOTH):
+        arrived(chip)
+    sent()
+    gone([near(n) for n in range(4)])
+
+
+def branch_gather(rows, hidden, down, name, chunks=4):
+    tokens, width = rows.shape
+    wide = down.shape[1]
+    any_space, vmem = pl.BlockSpec(memory_space=pl.ANY), pl.BlockSpec(memory_space=pltpu.VMEM)
+    dma = pltpu.SemaphoreType.DMA
+    return pl.pallas_call(
+        functools.partial(branch_gather_kernel, chunks),
+        out_shape=[
+            jax.ShapeDtypeStruct((8 * tokens, width), BF16),
+            jax.ShapeDtypeStruct((tokens, wide), F32),
+            jax.ShapeDtypeStruct((3, tokens, wide), BF16),
+        ],
+        in_specs=[any_space, vmem, any_space],
+        out_specs=[any_space, vmem, vmem],
+        scratch_shapes=[
+            pltpu.VMEM((hidden.shape[1], wide), BF16),
+            pltpu.VMEM((4, 2 * tokens, wide), BF16),
+            pltpu.VMEM((4, tokens, wide), BF16),
+            dma,
+            dma,
+            dma((8, chunks)), dma((8, chunks)),
+            dma((4,)), dma((4,)),
+        ],
+        compiler_params=pltpu.CompilerParams(
+            collective_id=name, has_side_effects=True, vmem_limit_bytes=VMEM_MOST
+        ),
+        cost_estimate=pl.CostEstimate(
+            flops=16 * tokens * wide * hidden.shape[1], bytes_accessed=160 * 2**20, transcendentals=0
+        ),
+    )(rows, hidden, down)
 
 
 def in_plane():
@@ -318,22 +674,11 @@
     return lower, upper
 
 
-def begin(copies):
-    for copy in copies:
-        copy.start()
-
-
-def arrive(copies):
-    for copy in copies:
-        copy.wait_recv()
-
-
-def gone(copies):
-    for copy in copies:
-        copy.wait_send()
-
-
-FAR_FIRST = (7, 5, 6, 4, 3, 1, 2)
+FAR_FIRST = (7, 6, 5, 4, 3, 2, 1)
+
+
+def as_place(bits):
+    return (bits & 4) + 2 * (bits & 1) + (bits >> 1 & 1)
 
 
 def start_kernel(
@@ -360,7 +705,7 @@
         ]
 
     def spread(slot, bits, j, sources):
-        targets = parcel.blocks(alls, me ^ bits ^ slot, j)
+        targets = parcel.blocks(alls, me ^ as_place(bits) ^ as_place(slot), j)
         return [
             send(source, target, plane_send.at[i, slot, j], plane_recv.at[i, slot, j], other(bits))
             for i, (source, target) in enumerate(zip(sources, targets))
@@ -388,18 +733,18 @@
             to_plane(j, blocks)
 
     def relay(j):
-        by_x, by_y = parcel.blocks(alls, me ^ X_BIT, j), parcel.blocks(alls, me ^ Y_BIT, j)
+        by_x, by_y = parcel.blocks(alls, me ^ as_place(X_BIT), j), parcel.blocks(alls, me ^ as_place(Y_BIT), j)
         arrive(spread(X_BIT, X_BIT, j, by_x))
-        pl.when(j % 2 == 0)(lambda: begin(spread(5, Y_BIT, j, by_x)))
-        begin(spread(6, C_BIT, j, by_x))
+        pl.when(j % 2 == 0)(lambda: begin(spread(BOTH, Y_BIT, j, by_x)))
+        begin(spread(X_BIT | C_BIT, C_BIT, j, by_x))
         arrive(spread(Y_BIT, Y_BIT, j, by_y))
-        pl.when(j % 2 == 1)(lambda: begin(spread(5, X_BIT, j, by_y)))
-        begin(spread(3, C_BIT, j, by_y))
+        pl.when(j % 2 == 1)(lambda: begin(spread(BOTH, X_BIT, j, by_y)))
+        begin(spread(Y_BIT | C_BIT, C_BIT, j, by_y))
 
     def relay_far(j):
-        by_both = parcel.blocks(alls, me ^ 5, j)
-        arrive(spread(5, Y_BIT, j, by_both))
-        begin(spread(7, C_BIT, j, by_both))
+        by_both = parcel.blocks(alls, me ^ as_place(BOTH), j)
+        arrive(spread(BOTH, Y_BIT, j, by_both))
+        begin(spread(BOTH | C_BIT, C_BIT, j, by_both))
 
     def in_order(do):
         do(f)
@@ -408,7 +753,7 @@
             pl.when(f + step <= count - 1)(lambda: do(f + step))
 
     def wide(bits):
-        return send(wide_ref.at[me ^ bits], wide_all.at[me], wide_send.at[bits], wide_recv.at[bits], other(bits))
+        return send(wide_ref.at[me ^ as_place(bits)], wide_all.at[me], wide_send.at[bits], wide_recv.at[bits], other(bits))
 
     pl.when(upper)(lambda: begin(hop(f, True, own)))
     pl.when(lower)(lambda: begin(hop(f, False, own)))
@@ -428,12 +773,12 @@
             (
                 *zip(own, parcel.blocks(alls, me, f)),
                 (wide_ref.at[me], wide_all.at[me]),
-                (rows_ref, rows_all.at[0]),
+                (rows_ref, rows_all.at[pl.ds(0, rows_ref.shape[0])]),
             )
         )
     ]
     begin(locals_)
-    rows_own, rows_relay, rows_far, rows_end = gathering(chunks, rows_ref, rows_all, rows_send, rows_recv)
+    rows_own, rows_relay, rows_far, rows_arrived, rows_sent = gathering(chunks, rows_ref, rows_all, rows_send, rows_recv)
     for step in range(1, count):
         line_step(step)
     rows_own()
@@ -456,7 +801,9 @@
     for bits in range(1, 8):
         wide(bits).wait_recv()
         wide(bits).wait_send()
-    rows_end()
+    for chip in (0, Y_BIT, X_BIT, BOTH):
+        rows_arrived(chip)
+    rows_sent()
 
 
 def start(parcel, down, kv, small, gate, up, rows, units, padded, name, chunks=4):
@@ -471,7 +818,7 @@
             jax.ShapeDtypeStruct((8 * count * kv.shape[0], kv.shape[1]), BF16),
             jax.ShapeDtypeStruct((8, count, *small.shape), BF16),
             jax.ShapeDtypeStruct(wide, BF16),
-            jax.ShapeDtypeStruct((8, *rows.shape), BF16),
+            jax.ShapeDtypeStruct((8 * rows.shape[0], rows.shape[1]), BF16),
         ],
         in_specs=[vmem] * 5 + [any_space],
         out_specs=[any_space] * 5,
@@ -503,7 +850,7 @@
     lower, upper = greet_all(count)
     parts = (down_ref, kv_ref, small_ref)
     sums = (down_sum, kv_sum, small_sum)
-    chips = (X_BIT | Y_BIT, X_BIT, Y_BIT, 0)
+    chips = (BOTH, X_BIT, Y_BIT, 0)
 
     def rows(amount, do):
         size = 16 if amount % 64 else 64
@@ -513,7 +860,7 @@
             do(pl.ds(pl.multiple_of(r * size, size), size))
 
     def near(n, j):
-        sources = parcel.blocks(parts, me ^ (chips[n] | C_BIT), j)
+        sources = parcel.blocks(parts, me ^ as_place(chips[n] | C_BIT), j)
         return [
             send(source, held[i][1].at[n, j], near_send.at[i, n, j], near_recv.at[i, n, j], other(C_BIT))
             for i, source in enumerate(sources)
@@ -526,7 +873,7 @@
         ]
 
     def wide(bits):
-        return send(wide_ref.at[me ^ bits], wide_all.at[me], wide_send.at[bits], wide_recv.at[bits], other(bits))
+        return send(wide_ref.at[me ^ as_place(bits)], wide_all.at[me], wide_send.at[bits], wide_recv.at[bits], other(bits))
 
     def hop(d, up):
         way = 0 if up else 1
@@ -572,13 +919,11 @@
         for j in range(count):
             for copy in near(n, j):
                 copy.start()
-    for bits in FAR_FIRST:
-        wide(bits).start()
     for n in range(4):
         for j in range(count):
             for copy in near(n, j):
                 copy.wait_recv()
-            for i, source in enumerate(parcel.blocks(parts, me ^ chips[n], j)):
+            for i, source in enumerate(parcel.blocks(parts, me ^ as_place(chips[n]), j)):
                 total, near_ref, chip_ref = held[i][:3]
 
                 def add(at, source=source, total=total, near_ref=near_ref, chip_ref=chip_ref):
@@ -593,50 +938,52 @@
             for copy in far(n):
                 copy.start()
 
+    for bits in FAR_FIRST:
+        wide(bits).start()
     wide_all[me] = wide_ref[me]
+    for n in range(3):
+        for copy in far(n):
+            copy.wait_recv()
+    for i in range(3):
+        total, far_ref = held[i][0], held[i][3]
+        for j in range(count):
+
+            def add(at, total=total, far_ref=far_ref, j=j):
+                value = total[j, at, :]
+                for n in range(3):
+                    value = value + far_ref[n, j, at, :].astype(F32)
+                total[j, at, :] = value
+
+            rows(total.shape[1], add)
+    for step in range(1, count):
+        pass_on(count - step, True)
+        pass_on(step - 1, False)
+    for i in range(3):
+
+        def keep(at, i=i):
+            sums[i][at, :] = held[i][0][f, at, :]
+
+        rows(sums[i].shape[0], keep)
+    for up, there in ((True, lower), (False, upper)):
+
+        @pl.when(there)
+        def _(up=up):
+            for copy in hop(f, up):
+                copy.wait_recv()
+            for i in range(3):
+                incoming = held[i][5 if up else 7]
+
+                def add(at, i=i, incoming=incoming):
+                    sums[i][at, :] = sums[i][at, :] + incoming[f, at, :].astype(F32)
+
+                rows(sums[i].shape[0], add)
+
     for bits in range(1, 8):
         wide(bits).wait_recv()
     for place, j, shard in parcel.unit_pieces():
         for first, ref in ((0, gate_sum), (padded, up_sum)):
             piece = wide_all[place, :, first + j * units : first + (j + 1) * units]
             ref[:, shard * units : (shard + 1) * units] = piece.astype(F32)
-
-    for n in range(3):
-        for copy in far(n):
-            copy.wait_recv()
-    for i in range(3):
-        total, far_ref = held[i][0], held[i][3]
-        for j in range(count):
-
-            def add(at, total=total, far_ref=far_ref, j=j):
-                value = total[j, at, :]
-                for n in range(3):
-                    value = value + far_ref[n, j, at, :].astype(F32)
-                total[j, at, :] = value
-
-            rows(total.shape[1], add)
-    for step in range(1, count):
-        pass_on(count - step, True)
-        pass_on(step - 1, False)
-    for i in range(3):
-
-        def keep(at, i=i):
-            sums[i][at, :] = held[i][0][f, at, :]
-
-        rows(sums[i].shape[0], keep)
-    for up, there in ((True, lower), (False, upper)):
-
-        @pl.when(there)
-        def _(up=up):
-            for copy in hop(f, up):
-                copy.wait_recv()
-            for i in range(3):
-                incoming = held[i][5 if up else 7]
-
-                def add(at, i=i, incoming=incoming):
-                    sums[i][at, :] = sums[i][at, :] + incoming[f, at, :].astype(F32)
-
-                rows(sums[i].shape[0], add)
 
     for d in range(count):
         pl.when(f < d)(lambda: gone(hop(d, True)))
@@ -716,11 +1063,6 @@
     return array.reshape(*lead, 8 * count * part, *tail)
 
 
-def scores_of(q_rot, k_rot, allowed):
-    raw = jnp.einsum("bthd,bsd->bhts", q_rot, k_rot, preferred_element_type=F32)
-    return jnp.where(allowed[:, None], raw * HEAD_DIM**-0.5, NEGATIVE)
-
-
 def per_device(
     count,
     f_first,
@@ -773,12 +1115,11 @@
         parcel, latent_down, shared_kv, small, gate_weight, up_weight, out_cotangent, units, padded, 0
     )
     down_full = parcel.down_from(down_full)
-    g_all = g_all.reshape(8 * tokens, width)
 
     half = count // 2
     per_head = count // 4
     up_line = lax.all_gather(latent_up.astype(BF16), "f", axis=0)
-    out_line = lax.all_gather(after(out_proj.astype(BF16), up_line), "f", axis=0)
+    out_line = lax.all_gather(out_proj.astype(BF16), "f", axis=0)
 
     def heads(line):
         own = lax.dynamic_slice_in_dim(line, half * y, half, 0)
@@ -790,13 +1131,13 @@
         high = jnp.where(y == 0, other_part, own)
         return jnp.stack([low, high], axis)
 
-    up_full = join(*heads(up_line), 0).transpose(0, 2, 1, 3).reshape(rank, 2 * HEAD_DIM)
+    up_own, up_far = (part.transpose(1, 0, 2).reshape(half_rank, -1) for part in heads(up_line))
     out_full = join(*heads(out_line), 1).reshape(2 * HEAD_DIM, width)
 
-    both = lax.all_gather(after(both, out_line), "f", axis=0)
+    both = lax.all_gather(both, "f", axis=0)
     both = from_owner(both, 0, f_first)
-    ff_down = lax.all_gather(after(down_weight.astype(BF16), both), "f", axis=0)
-    ff_down = jnp.pad(ff_down.reshape(mine, width), ((0, padded - mine), (0, 0)))
+    ff_down = lax.all_gather(after(down_weight.astype(BF16), small), "f", axis=0)
+    ff_down = ff_down.reshape(mine, width)
 
     gain_lat = small[:2, 0, :lat_lines].astype(F32) + small[:2, 0, lat_lines:at_gain].astype(F32)
     gain_lat = gain_lat.reshape(rank)
@@ -805,7 +1146,7 @@
     gain_two = from_owner(by_line[:, :, at_gain + 1, :gain_rows], 0, f_first).astype(F32)
     lengths = lax.dynamic_index_in_dim(small[:, :, at_gain + 2, :3], place, 1, keepdims=False)
     lengths = jnp.stack(
-        [lax.dynamic_index_in_dim(lengths, in_plane() ^ i, 0, keepdims=False) for i in range(8)]
+        [lax.dynamic_index_in_dim(lengths, in_plane() ^ as_place(i), 0, keepdims=False) for i in range(8)]
     ).astype(jnp.int32)
 
     inputs = block_input.astype(F32)
@@ -815,49 +1156,26 @@
     rms_lat = lax.rsqrt(jnp.mean(latent * latent, axis=-1, keepdims=True) + EPS)
     latent_n = (latent * rms_lat * gain_lat).astype(BF16)
     shared = jnp.dot(normed, kv_full, preferred_element_type=F32)
-    position, allowed = layout(lengths, tokens)
-    cosine, sine = rope_tables(position, HEAD_DIM)
-    k_own = rotate(shared, cosine[0], sine[0]).astype(BF16)
+    position, begins = layout(lengths, tokens)
+    cosine, sine = rope_tables(position.reshape(-1), HEAD_DIM)
+    k_own = rotate(shared, cosine[:tokens], sine[:tokens]).astype(BF16)
 
     rows_all = plane_gather(jnp.concatenate([latent_n, k_own, shared.astype(BF16)], axis=1), 1)
-    lat_all = rows_all[:, :, :rank].reshape(8 * tokens, rank)
-    k_rot = rows_all[:, :, rank : rank + HEAD_DIM]
-    values = rows_all[:, :, rank + HEAD_DIM :]
-    queries = jnp.dot(lat_all, up_full, preferred_element_type=F32)
-    wide_cos, wide_sin = cosine[:, :, None], sine[:, :, None]
-    q_rot = rotate(queries.reshape(8, tokens, 2, HEAD_DIM), wide_cos, wide_sin).astype(BF16)
-    scores = scores_of(q_rot, k_rot, allowed)
-    peak = jnp.max(scores, axis=-1, keepdims=True)
-    log_total = peak + jnp.log(jnp.sum(jnp.exp(scores - peak), axis=-1, keepdims=True))
-    probs = jnp.exp(scores - log_total)
-    attended = jnp.einsum("bhts,bsd->bthd", probs.astype(BF16), values, preferred_element_type=F32)
-    attended = attended.reshape(8 * tokens, 2 * HEAD_DIM).astype(BF16)
-    branch = matmul_scatter(attended, out_full, 2)
+    begins = begins.reshape(-1, 1)
+    branch, q_rot, lse, attended = attention(
+        rows_all, up_own, up_far, out_full, cosine, sine, begins, 2
+    )
 
     middle = inputs + branch
     rms_two = lax.rsqrt(jnp.mean(middle * middle, axis=-1, keepdims=True) + EPS)
     normed_two = (middle * rms_two * gain_two).astype(BF16)
-    two_all = plane_gather(normed_two, 3).reshape(8 * tokens, width)
-    gate_up = jnp.dot(two_all, both, preferred_element_type=F32)
-    gate, upval = gate_up[:, :padded], gate_up[:, padded:]
-    sigma = jax.nn.sigmoid(gate)
-    hidden = (gate * sigma * upval).astype(BF16)
-
-    d_hidden = contract(g_all, ff_down, 1, 1)
-    d_gate = (d_hidden * upval * sigma * (1.0 + gate * (1.0 - sigma))).astype(BF16)
-    d_up = (d_hidden * gate * sigma).astype(BF16)
-    d_both = jnp.concatenate([d_gate, d_up], axis=1)
-    d_two = matmul_scatter(d_both, both, 4, True)
-
-    result = jnp.dot(hidden, ff_down, preferred_element_type=F32)
-    result = plane_scatter(after(result.reshape(8, tokens, width), d_two))
-
-    both_grad = contract(two_all, d_both, 0, 0)
-    both_grad = by_owner(both_grad.astype(BF16), 0, count, f_first)
+    two_all, hidden, d_both = feed(normed_two, g_all, both, ff_down, padded, 3)
+    down_grad = contract(hidden, g_all, 0, 0)[:mine].reshape(count, units, width).astype(BF16)
+    both_grad = by_owner(contract(two_all, d_both, 0, 0).astype(BF16), 0, count, f_first)
+    d_both, both_grad, down_grad = lax.optimization_barrier((d_both, both_grad, down_grad))
     both_grad = lax.psum_scatter(both_grad, "f", scatter_dimension=0)
-
-    down_grad = contract(hidden, g_all, 0, 0)[:mine].reshape(count, units, width)
-    down_grad = lax.psum_scatter(down_grad.astype(BF16), "f", scatter_dimension=0).astype(F32)
+    down_grad = lax.psum_scatter(down_grad, "f", scatter_dimension=0).astype(F32)
+    d_two = product_scatter(d_both, both, 4)
 
     upstream = out_cotangent.astype(F32)
     gain_two_part = jnp.sum(d_two * middle * rms_two, axis=0)
@@ -868,26 +1186,19 @@
         - middle * (rms_two**3) * jnp.mean(scaled_two * middle, axis=-1, keepdims=True)
     )
 
-    d_branch = plane_gather(d_middle.astype(BF16), 5).reshape(8 * tokens, width)
-    d_attended = contract(d_branch, out_full, 1, 1).astype(BF16)
-    d_attended = d_attended.reshape(8, tokens, 2, HEAD_DIM)
-    d_probs = jnp.einsum("bthd,bsd->bhts", d_attended, values, preferred_element_type=F32)
-    inner = jnp.sum(probs * d_probs, axis=-1, keepdims=True)
-    d_scores = (probs * (d_probs - inner)).astype(BF16)
-    scale = HEAD_DIM**-0.5
-    d_qrot = jnp.einsum("bhts,bsd->bthd", d_scores, k_rot, preferred_element_type=F32) * scale
-    d_queries = unrotate(d_qrot, wide_cos, wide_sin).astype(BF16)
-    d_queries = d_queries.reshape(8 * tokens, 2 * HEAD_DIM)
-    d_krot = jnp.einsum("bhts,bthd->bsd", d_scores, q_rot, preferred_element_type=F32) * scale
-    value_part = jnp.einsum(
-        "bhts,bthd->bsd", probs.astype(BF16), d_attended, preferred_element_type=F32
-    )
-    shared_part = unrotate(d_krot, cosine, sine) + value_part
-    back = matmul_scatter(d_queries, up_full, 6, True, shared_part.reshape(8 * tokens, HEAD_DIM))
+    d_branch, result, chip_sums = branch_gather(d_middle.astype(BF16), hidden, ff_down, 5)
+    back, d_queries = attention_back(
+        d_branch, rows_all, up_own, up_far, out_full, cosine, sine, begins, q_rot, lse, 6
+    )
     d_lat_n, d_shared = back[:, :rank], back[:, rank:].astype(BF16)
-
-    own, *arrived = after(result, back)
-    block_output = (middle + own + sum(part.astype(F32) for part in arrived)).astype(BF16)
+    lat_all = rows_all[:, :rank]
+
+    chip_sums = after(chip_sums, back)
+    arrived = (
+        lax.ppermute(chip_sums[0], ("x", "y"), DIAGONAL),
+        lax.ppermute(chip_sums[1], "x", SWAP),
+        lax.ppermute(chip_sums[2], "y", SWAP),
+    )
 
     up_grad_heads = contract(lat_all, d_queries, 0, 0).reshape(2, half_rank, 2, HEAD_DIM)
     out_grad_heads = contract(attended, d_branch, 0, 0).reshape(2, per_head, 2, -1, width)
@@ -899,10 +1210,10 @@
 
     up_line_grad = join(*swap_halves(up_grad_heads, 0), 1).reshape(half_rank, count, -1)
     up_line_grad = up_line_grad.transpose(1, 0, 2).astype(BF16)
-    latent_up_grad = lax.psum_scatter(up_line_grad, "f", scatter_dimension=0).astype(F32)
+    latent_up_grad = lax.psum_scatter(after(up_line_grad, both_grad, down_grad, back), "f", scatter_dimension=0).astype(F32)
     out_line_grad = join(*swap_halves(out_grad_heads, 2), 0)
     out_line_grad = out_line_grad.reshape(count, -1, width).astype(BF16)
-    out_proj_grad = lax.psum_scatter(out_line_grad, "f", scatter_dimension=0).astype(F32)
+    out_proj_grad = lax.psum_scatter(after(out_line_grad, both_grad, down_grad, back), "f", scatter_dimension=0).astype(F32)
 
     gain_lat_part = jnp.sum(d_lat_n * latent * rms_lat, axis=0)
     scaled_lat = d_lat_n * gain_lat
@@ -944,6 +1255,8 @@
     latent_gain_grad = small_sum[:lat_lines].reshape(half_rank)
     attn_gain_grad = small_sum[lat_lines, :gain_rows]
     mlp_gain_grad = small_sum[lat_lines + 1, :gain_rows]
+    arrived = after(arrived, small_sum)
+    block_output = (middle + result + sum(part.astype(F32) for part in arrived)).astype(BF16)
     return (
         block_output,
         input_grad,

time: 924 us -> 725 us (0.78)
  waiting for transfers between devices: 161 us -> 62.8 us
  matrix products: 141 us -> 57.1 us
  Pallas kernels: 437 us -> 494 us
  local copies, waits for them, and re-layouts: 76.7 us -> 33.8 us
  other arithmetic: 74.1 us -> 41.7 us
    pallas_call x3 -> x5, Pallas kernels: 159 us -> 261 us  [the longest x3 147 us: vmem_call(): pl.pallas_call(kernel, out_shape=out_shape, in_specs=[vmem] * amount, out...]
    pallas_call x3 -> x1, Pallas kernels: 119 us -> 57.6 us  [plane_gather(): pl.pallas_call(functools.partial(gather_kernel, chunks), out_shape=jax.Sh...]
    reduce_scatter x1, waiting for transfers between devices: 59.8 us -> 0.01 us  [per_device(): both_grad = lax.psum_scatter(both_grad, 'f', scatter_dimension=0)]
    dot_general x9 -> x0, matrix products: 54.6 us -> none  [the longest x1 19.3 us: per_device(): gate_up = jnp.dot(two_all, both, preferred_element_type=F32)]
    ppermute x7 -> x3, waiting for transfers between devices: 39.5 us -> 0.01 us  [the longest x1 0.01 us: per_device(): lax.ppermute(chip_sums[0], ('x', 'y'), DIAGONAL)]
    all_gather x3, waiting for transfers between devices: 0.74 us -> 40.1 us  [the longest x1 40.1 us: per_device(): both = lax.all_gather(both, 'f', axis=0)]
    dot_general x10 -> x8, matrix products: 82.1 us -> 52.9 us  [contract(): lax.dot_general(left, right, (((left_dim,), (right_dim,)), ((), ())), pre...]
    all_gather x1, waiting for transfers between devices: 28.1 us -> 0.01 us  [per_device(): up_line = lax.all_gather(latent_up.astype(BF16), 'f', axis=0)]
  transfers between devices with their start and end apart: 19 -> 15, of which waited for: 8 -> 3; matrix products, arithmetic and copies ran while one was open for 21% -> 13% of each run, Pallas kernels for 28% -> 62%
where the time goes in v4:
time: 725 us; the launch traced here: 714 us
  Pallas kernels  494 us (68%)
  waiting for transfers between devices  62.8 us (9%)
  matrix products  57.1 us (8%)
  other arithmetic  41.7 us (6%)
  local copies, waits for them, and re-layouts  33.8 us (5%)
  between operations  15 us (2%)
  starting transfers between devices  9.76 us (1%)
    pallas_call x3, Pallas kernels, vmem_call(): pl.pallas_call(kernel, out_shape=out_shape, in_specs=[vmem] * amount, out...  147 us
    pallas_call x1, Pallas kernels, end(): pl.pallas_call(functools.partial(end_kernel, parcel, units, padded), out_...  91.6 us
    pallas_call x1, Pallas kernels, start(): pl.pallas_call(functools.partial(start_kernel, parcel, chunks, units, pad...  83.9 us
    pallas_call x1, Pallas kernels, branch_gather(): pl.pallas_call(functools.partial(branch_gather_kernel, chunks), out_shape...  60.9 us
    pallas_call x1, Pallas kernels, plane_gather(): pl.pallas_call(functools.partial(gather_kernel, chunks), out_shape=jax.Sh...  57.6 us
    pallas_call x1, Pallas kernels, feed(): pl.pallas_call(functools.partial(feed_kernel, chunks), out_shape=[jax.Sha...  53.7 us
    dot_general x8, matrix products, contract(): lax.dot_general(left, right, (((left_dim,), (right_dim,)), ((), ())), pre...  52.9 us
    all_gather x1, waiting for transfers between devices, per_device(): both = lax.all_gather(both, 'f', axis=0)  40.1 us
  transfers between devices with their start and end apart: 15, of which 3 were waited for; matrix products, arithmetic and copies ran while one was open for 13% of the time, Pallas kernels for 62%

profile of v4, /device:TPU:10, one launch (start us, length us, event | category | flops | bytes accessed | tf_op | source)
XLA Modules:
  0.0 714.4 jit_solution(3135459510870887683)
XLA Ops:
  12.1 83.9 %shard_map.220 = (bf16[1024,2048]{1,0:T(8,128)(2,1)}, bf16[2048,256]{1,0:T(8,128)(2,1)}, bf16[8,4,16,128]{3,2,1,0:T(8,128)(2,1)}, bf16[8,64,1536]{2,1,0:T(8,128)(2,1)}, bf16[2048,2048]{1,0:T(8,128)(2,1)}) custom-call(f32[512,128]{1,0:T(8,128)} %down_ref.1, f32[64,256]{1,0:T(8,128)} %kv_ref.1, bf16[16,128]{1,0:T(8,128)(2,1)} %pad.29.small_ref, ...), custom_call_target="tpu_custom_call" | custom-call | bytes 251658240 | tf_op jit(solution)/shard_map/pallas_call | solution.py:814
  100.4 3.7 multiply_cosine_fusion
  106.8 2.7 constant_dynamic-slice_fusion
  116.8 57.6 %shard_map.221.rows_ref = bf16[2048,1536]{1,0:T(8,128)(2,1)} custom-call(bf16[256,1536]{1,0:T(8,128)(2,1)} %pad_maximum_fusion.3.in_ref), custom_call_target="tpu_custom_call" | custom-call | bytes 167772160 | tf_op jit(solution)/shard_map/pallas_call | solution.py:159
  183.2 51.7 %shard_map.222 = (f32[256,2048]{1,0:T(8,128)}, bf16[2048,512]{1,0:T(8,128)(2,1)}, f32[2048,2]{1,0:T(8,128)}, bf16[2048,512]{1,0:T(8,128)(2,1)}) custom-call(bf16[2048,1536]{1,0:T(8,128)(2,1)} %shard_map.221.rows_ref, bf16[512,512]{1,0:T(8,128)(2,1)} %bitcast.152, bf16[512,512]{1,0:T(8,128)(2,1)} %bitcast.154, bf16[512,2048]{1,0:T(8,128)(2,1)} %bitcast.145, ...), custom_call_target="tpu_custom_call" | custom-call | flops 7516192768 | bytes 167772160 | tf_op jit(solution)/shard_map/pallas_call | solution.py:268
  238.1 40.1 %all-gather.13.cloned.1.call-done = bf16[32,64,1536]{2,1,0:T(8,128)(2,1)} async-done(((bf16[8,64,1536]{2,1,0:T(8,128)(2,1)}), bf16[32,64,1536]{2,1,0:T(8,128)(2,1)}) %all-gather.13.cloned.1.call-update) | async-done | bytes 6291472 | tf_op jit(solution)/shard_map/all_gather | solution.py:1137
  278.2 53.7 %shard_map.223 = (bf16[2048,2048]{1,0:T(8,128)(2,1)}, bf16[2048,768]{1,0:T(8,128)(2,1)}, bf16[2048,1536]{1,0:T(8,128)(2,1)}) custom-call(bf16[256,2048]{1,0:T(8,128)(2,1)} %multiply_convert_fusion.in_ref, bf16[2048,2048]{1,0:T(8,128)(2,1)} %get-tuple-element.48.g_ref, bf16[2048,1536]{1,0:T(8,128)(2,1)} %bitcast.167, ...), custom_call_target="tpu_custom_call" | custom-call | flops 19327352832 | bytes 167772160 | tf_op jit(solution)/shard_map/pallas_call | solution.py:468
  331.9 10.3 %fusion.43 = bf16[768,2048]{1,0:T(8,128)(2,1)S(1)} fusion(bf16[2048,768]{1,0:T(8,128)(2,1)} %get-tuple-element.53.hidden_ref, bf16[2048,2048]{1,0:T(8,128)(2,1)} %get-tuple-element.48.g_ref), kind=kOutput, calls=%fused_computation.124 | convolution fusion | flops 6442450944 | bytes 14680064 | tf_op jit(solution)/shard_map/dot_general | solution.py:21
  344.0 15.9 %convolution_convert_fusion = bf16[2048,1536]{1,0:T(8,128)(2,1)} fusion(bf16[2048,2048]{1,0:T(8,128)(2,1)S(1)} %copy-done.27, bf16[2048,1536]{1,0:T(8,128)(2,1)S(1)} %copy-done.28), kind=kOutput, calls=%fused_computation | convolution fusion | flops 12888047616 | bytes 20971520 | tf_op jit(solution)/shard_map/dot_general | solution.py:21
  360.5 52.9 %shard_map.224 = f32[256,2048]{1,0:T(8,128)} custom-call(bf16[2048,1536]{1,0:T(8,128)(2,1)} %get-tuple-element.54.left_ref, bf16[2048,1536]{1,0:T(8,128)(2,1)} %bitcast.168), custom_call_target="tpu_custom_call" | custom-call | flops 12884901888 | bytes 167772160 | tf_op jit(solution)/shard_map/pallas_call | solution.py:268
  418.3 60.9 %shard_map.225 = (bf16[2048,2048]{1,0:T(8,128)(2,1)}, f32[256,2048]{1,0:T(8,128)}, bf16[3,256,2048]{2,1,0:T(8,128)(2,1)}) custom-call(bf16[256,2048]{1,0:T(8,128)(2,1)} %get-tuple-element.82.in_ref, bf16[2048,768]{1,0:T(8,128)(2,1)} %get-tuple-element.53.hidden_ref, bf16[704,2048]{1,0:T(8,128)(2,1)} %all-gather.15.cloned.1.call-done.down_ref), custom_call_target="tpu_custom_call" | custom-call | flops 6442450944 | bytes 167772160 | tf_op jit(solution)/shard_map/pallas_call | solution.py:586
  479.2 41.9 %shard_map.226 = (f32[256,1280]{1,0:T(8,128)}, bf16[2048,512]{1,0:T(8,128)(2,1)}) custom-call(bf16[2048,2048]{1,0:T(8,128)(2,1)} %get-tuple-element.57.d_ref, bf16[2048,1536]{1,0:T(8,128)(2,1)} %shard_map.221.rows_ref, bf16[512,512]{1,0:T(8,128)(2,1)} %bitcast.153, bf16[512,512]{1,0:T(8,128)(2,1)} %bitcast.155, bf16[512,2048]{1,0:T(8,128)(2,1)} %bitcast.146, ...), custom_call_target="tpu_custom_call" | custom-call | flops 9126805504 | bytes 167772160 | tf_op jit(solution)/shard_map/pallas_call | solution.py:268
  521.1 6.3 fusion
  527.4 2.5 reshape.288
  532.9 10.0 %fusion.45 = bf16[512,2048]{1,0:T(8,128)(2,1)} fusion(bf16[2048,512]{1,0:T(8,128)(2,1)} %get-tuple-element.72, bf16[2048,2048]{1,0:T(8,128)(2,1)} %get-tuple-element.57.d_ref), kind=kOutput, calls=%fused_computation.126 | convolution fusion | flops 4294967296 | bytes 12582912 | tf_op jit(solution)/shard_map/dot_general | solution.py:21
  548.4 2.4 bitcast_convert_fusion
  556.8 19.7 %collective-permute-done.6 = bf16[2,1,128,2048]{3,2,0,1:T(8,128)(2,1)S(1)} collective-permute-done((bf16[2,1,128,2048]{3,2,0,1:T(8,128)(2,1)S(1)}, bf16[2,1,128,2048]{3,2,0,1:T(8,128)(2,1)S(1)}, u32[]{:S(2)}, u32[]{:S(2)}) %collective-permute-start.6) | collective-permute-done | bytes 1048608 | tf_op jit(solution)/shard_map/ppermute | solution.py:1209
  578.6 3.7 fusion.44
  582.3 3.1 fusion.12
  585.6 3.9 slice_bitcast_fusion
  593.0 2.5 convolution_convert_fusion.2.kv_ref
  596.3 3.4 convolution_convert_fusion.1.down_ref
  601.4 91.6 %shard_map.227 = (f32[512,128]{1,0:T(8,128)}, f32[64,256]{1,0:T(8,128)}, f32[16,128]{1,0:T(8,128)}, f32[64,5632]{1,0:T(8,128)}, f32[64,5632]{1,0:T(8,128)}) custom-call(bf16[1024,2048]{1,0:T(8,128)(2,1)} %convolution_convert_fusion.1.down_ref, bf16[2048,256]{1,0:T(8,128)(2,1)} %convolution_convert_fusion.2.kv_ref, bf16[8,4,16,128]{3,2,1,0:T(8,128)(2,1)} %fusion.25.small_ref, ...), custom_call_target="tpu_custom_call" | custom-call | bytes 251658240 | tf_op jit(solution)/shard_map/pallas_call | solution.py:1017
  695.5 4.3 add_convert_fusion
  (174 shorter events, 70.8 us)
Async XLA Ops:
  7.2 99.6 %all-gather.11.cloned.1.call-start = ((), (), s32[]{:S(2)}) async-start(), calls=%async_computation.9 | async-start | bytes 2621440 | tf_op jit(solution)/shard_map/all_gather | solution.py:1122
  9.5 102.3 %all-gather.9.cloned.1.call-start = ((), (), s32[]{:S(2)}) async-start(), calls=%async_computation.8 | async-start | bytes 1310720 | tf_op jit(solution)/shard_map/all_gather | solution.py:1121
  10.3 227.8 %all-gather.15.cloned.1.call-start = ((), (), s32[]{:S(2)}) async-start(), calls=%async_computation.11 | async-start | bytes 3604480 | tf_op jit(solution)/shard_map/all_gather | solution.py:1139
  96.1 182.1 %all-gather.13.cloned.1.call-start = ((), (), s32[]{:S(2)}) async-start(), calls=%async_computation.10 | async-start | bytes 7864320 | tf_op jit(solution)/shard_map/all_gather | solution.py:1137
  96.6 451.8 %reduce-scatter.7.cloned.1.call-start = ((), (), s32[]{:S(2)}) async-start(), calls=%async_computation.5 | async-start | bytes 3604480 | tf_op jit(solution)/shard_map/reduce_scatter | solution.py:1177
  99.9 5.5 copy-start.23
  106.8 8.9 %copy-start.1 = (f32[256,1024]{1,0:T(8,128)}, f32[256,1024]{1,0:T(8,128)S(1)}, u32[]{:S(2)}) copy-start(f32[256,1024]{1,0:T(8,128)S(1)} %get-tuple-element.124) | copy-start | bytes 3145732
  109.5 70.8 %collective-permute-start.1 = (bf16[2,128,2048]{2,1,0:T(8,128)(2,1)}, bf16[2,128,2048]{2,1,0:T(8,128)(2,1)}, u32[]{:S(2)}, u32[]{:S(2)}) collective-permute-start(bf16[2,128,2048]{2,1,0:T(8,128)(2,1)} %constant_dynamic-slice_fusion), channel_id=1, source_target_pairs={{0,1},{1,0},{2,3},{3,2},{4,5},{5,4},{6,7},{7,6},{8,9},{9,8},{10,11... | collective-permute-start | bytes 3145736 | tf_op jit(solution)/shard_map/ppermute | solution.py:1127
  115.2 63.1 %collective-permute-start = (bf16[2,512,256]{2,0,1:T(2,128)(2,1)}, bf16[2,512,256]{2,0,1:T(2,128)(2,1)}, u32[]{:S(2)}, u32[]{:S(2)}) collective-permute-start(bf16[2,512,256]{2,0,1:T(2,128)(2,1)} %copy.90), channel_id=1, source_target_pairs={{0,1},{1,0},{2,3},{3,2},{4,5},{5,4},{6,7},{7,6},{8,9},{9,8},{10,11... | collective-permute-start | bytes 1572872 | tf_op jit(solution)/shard_map/ppermute | solution.py:1127
  174.4 5.9 copy-start.10
  331.9 12.1 %copy-start.27 = (bf16[2048,2048]{1,0:T(8,128)(2,1)S(1)}, bf16[2048,2048]{1,0:T(8,128)(2,1)}, u32[]{:S(2)}) copy-start(bf16[2048,2048]{1,0:T(8,128)(2,1)} %get-tuple-element.52) | copy-start | bytes 25165828
  331.9 12.1 %copy-start.28 = (bf16[2048,1536]{1,0:T(8,128)(2,1)S(1)}, bf16[2048,1536]{1,0:T(8,128)(2,1)}, u32[]{:S(2)}) copy-start(bf16[2048,1536]{1,0:T(8,128)(2,1)} %get-tuple-element.54.left_ref) | copy-start | bytes 18874372
  359.9 190.9 %reduce-scatter.5.cloned.1.call-start = ((), (), s32[]{:S(2)}) async-start(), calls=%async_computation.4 | async-start | bytes 7864320 | tf_op jit(solution)/shard_map/reduce_scatter | solution.py:1176
  360.5 339.3 %reduce-scatter.9.cloned.1.call-start = ((), (), s32[]{:S(2)}) async-start(), calls=%async_computation.6 | async-start | bytes 1310720 | tf_op jit(solution)/shard_map/reduce_scatter | solution.py:1213
  531.3 13.6 %collective-permute-start.5 = (bf16[512,2,256]{2,1,0:T(2,128)(2,1)S(1)}, bf16[512,2,256]{2,1,0:T(2,128)(2,1)S(1)}, u32[]{:S(2)}, u32[]{:S(2)}) collective-permute-start(bf16[512,2,256]{2,1,0:T(2,128)(2,1)S(1)} %fusion.18), channel_id=1, source_target_pairs={{0,1},{1,0},{2,3},{3,2},{4,5},{5,4},{6,7},{7,6},{8,9},{9,8},{10,11... | collective-permute-start | bytes 1572872 | tf_op jit(solution)/shard_map/ppermute | solution.py:1209
  532.9 12.0 %copy-start.7 = (bf16[2,512,2,256]{3,2,1,0:T(2,128)(2,1)S(1)}, bf16[2,512,2,256]{3,2,1,0:T(2,128)(2,1)}, u32[]{:S(2)}) copy-start(bf16[2,512,2,256]{3,2,1,0:T(2,128)(2,1)} %reshape.288) | copy-start | bytes 3145732
  550.8 150.9 %reduce-scatter.11.cloned.1.call-start = ((), (), s32[]{:S(2)}) async-start(), calls=%async_computation.7 | async-start | bytes 2621440 | tf_op jit(solution)/shard_map/reduce_scatter | solution.py:1216
  552.5 23.9 %copy-start.11 = (bf16[512,2048]{1,0:T(8,128)(2,1)S(1)}, bf16[512,2048]{1,0:T(8,128)(2,1)}, u32[]{:S(2)}) copy-start(bf16[512,2048]{1,0:T(8,128)(2,1)} %fusion.45) | copy-start | bytes 6291460
  552.5 23.9 %collective-permute-start.6 = (bf16[2,1,128,2048]{3,2,0,1:T(8,128)(2,1)S(1)}, bf16[2,1,128,2048]{3,2,0,1:T(8,128)(2,1)S(1)}, u32[]{:S(2)}, u32[]{:S(2)}) collective-permute-start(bf16[2,1,128,2048]{3,2,0,1:T(8,128)(2,1)S(1)} %fusion.15), channel_id=1, source_target_pairs={{0,1},{1,0},{2,3},{3,2},{4,5},{5,4},{6,7},{7,6},{8,9},{9,8},{10,11... | collective-permute-start | bytes 3145736 | tf_op jit(solution)/shard_map/ppermute | solution.py:1209
  589.5 6.8 copy-start.9
  589.5 103.4 %collective-permute-start.2 = (bf16[256,2048]{1,0:T(8,128)(2,1)}, bf16[256,2048]{1,0:T(8,128)(2,1)}, u32[]{:S(2)}, u32[]{:S(2)}) collective-permute-start(bf16[256,2048]{1,0:T(8,128)(2,1)} %get-tuple-element.90), channel_id=1, source_target_pairs={{0,5},{5,0},{1,4},{4,1},{2,7},{7,2},{3,6},{6,3},{8,13},{13,8},{9,1... | collective-permute-start | bytes 3145736 | tf_op jit(solution)/shard_map/ppermute | solution.py:1198
  590.9 102.1 %collective-permute-start.3 = (bf16[256,2048]{1,0:T(8,128)(2,1)}, bf16[256,2048]{1,0:T(8,128)(2,1)}, u32[]{:S(2)}, u32[]{:S(2)}) collective-permute-start(bf16[256,2048]{1,0:T(8,128)(2,1)} %get-tuple-element.89), channel_id=1, source_target_pairs={{0,4},{4,0},{1,5},{5,1},{2,6},{6,2},{3,7},{7,3},{8,12},{12,8},{9,1... | collective-permute-start | bytes 3145736 | tf_op jit(solution)/shard_map/ppermute | solution.py:1199
  592.6 100.4 %collective-permute-start.4 = (bf16[256,2048]{1,0:T(8,128)(2,1)}, bf16[256,2048]{1,0:T(8,128)(2,1)}, u32[]{:S(2)}, u32[]{:S(2)}) collective-permute-start(bf16[256,2048]{1,0:T(8,128)(2,1)} %get-tuple-element.88), channel_id=1, source_target_pairs={{0,1},{1,0},{2,3},{3,2},{4,5},{5,4},{6,7},{7,6},{8,9},{9,8},{10,11... | collective-permute-start | bytes 3145736 | tf_op jit(solution)/shard_map/ppermute | solution.py:1200
  699.8 5.4 copy-start.14
  (20 other events, 59.8 us)
Sparse Core Ops, SparseCore 0:
  10.2 50.6 all-gather.10
  63.0 30.0 all-gather.8
  96.2 67.1 all-gather.14
  164.8 113.3 all-gather.12
  360.0 56.4 reduce-scatter.6
  418.7 111.2 reduce-scatter.4
  550.9 26.7 reduce-scatter.8
  580.1 42.2 reduce-scatter.10

commit v5 on v4

--- a/solution.py
+++ b/solution.py
@@ -178,7 +178,8 @@
 
 
 def scattering(
-    out_ref, work_ref, near_ref, far_ref, near_send, near_recv, far_send, far_recv, produce
+    out_ref, work_ref, near_ref, far_ref, near_send, near_recv, far_send, far_recv, produce,
+    at_start=None, meanwhile=None, at_end=None,
 ):
     greet([other(C_BIT), other(X_BIT), other(Y_BIT)])
     tokens = out_ref.shape[0]
@@ -204,6 +205,9 @@
             work_ref[n, at, :] = total.astype(BF16)
 
         row_loop(tokens, keep)
+
+    if at_start is not None:
+        at_start()
 
     @pl.loop(0, 4)
     def _(n):
@@ -233,6 +237,8 @@
 
         row_loop(half, add)
         hop(on).start()
+    if meanwhile is not None:
+        meanwhile()
 
     def last(came, first):
         for i in came:
@@ -250,6 +256,8 @@
     last((2, 5), 0)
     last((3, 4), half)
     gone([*[near(n) for n in range(4)], *[hop(i) for i in range(6)]])
+    if at_end is not None:
+        at_end()
 
 
 def scatter_scratch(tokens, wide):
@@ -263,13 +271,13 @@
     ]
 
 
-def vmem_call(kernel, out_shape, amount, scratch, name, flops, *arrays):
-    vmem = pl.BlockSpec(memory_space=pltpu.VMEM)
+def vmem_call(kernel, out_shape, stay, scratch, name, flops, *arrays):
+    vmem, any_space = pl.BlockSpec(memory_space=pltpu.VMEM), pl.BlockSpec(memory_space=pl.ANY)
     return pl.pallas_call(
         kernel,
         out_shape=out_shape,
-        in_specs=[vmem] * amount,
-        out_specs=[vmem] * len(out_shape),
+        in_specs=[vmem] * (len(arrays) - stay) + [any_space] * stay,
+        out_specs=[vmem] * (len(out_shape) - stay) + [any_space] * stay,
         scratch_shapes=scratch,
         compiler_params=pltpu.CompilerParams(
             collective_id=name, has_side_effects=True, vmem_limit_bytes=VMEM_MOST
@@ -301,7 +309,7 @@
 
 
 def attention_kernel(
-    rank, rows_ref, own_ref, far_ref, out_w_ref, cos_ref, sin_ref, begin_ref,
+    rank, rows_ref, head_ref, out_w_ref, cos_ref, sin_ref, begin_ref,
     branch_ref, query_ref, lse_ref, att_ref, *rest,
 ):
     wide = out_w_ref.shape[1]
@@ -310,8 +318,10 @@
 
     def produce(chip, target):
         pair = pl.ds(pl.multiple_of(chip * 2 * tokens, 2 * tokens), 2 * tokens)
-        queries = contract(rows_ref[pair, mine], own_ref[...], 1, 0)
-        queries = queries + contract(rows_ref[pair, theirs], far_ref[...], 1, 0)
+        queries = [
+            contract(rows_ref[pair, mine], head_ref[h], 1, 0) + contract(rows_ref[pair, theirs], head_ref[2 + h], 1, 0)
+            for h in range(2)
+        ]
         for c in range(2):
             rows = pl.ds(pl.multiple_of((2 * chip + c) * tokens, tokens), tokens)
             keys = rows_ref[rows, rank : rank + HEAD_DIM]
@@ -319,7 +329,7 @@
             cosine, sine, begins = cos_ref[rows, :], sin_ref[rows, :], begin_ref[rows, :]
             for h in range(2):
                 at = slice(h * HEAD_DIM, (h + 1) * HEAD_DIM)
-                turned = turn(queries[c * tokens : (c + 1) * tokens, at], cosine, sine).astype(BF16)
+                turned = turn(queries[h][c * tokens : (c + 1) * tokens], cosine, sine).astype(BF16)
                 query_ref[rows, at] = turned
                 scores = masked_scores(turned, keys, begins)
                 peak = jnp.max(scores, axis=1, keepdims=True)
@@ -331,13 +341,13 @@
         @pl.loop(0, wide // 512)
         def _(i):
             at = pl.ds(pl.multiple_of(i * 512, 512), 512)
-            target[:, at] = contract(att_ref[pair, :], out_w_ref[:, at], 1, 0).astype(BF16)
+            target[:, at] = contract(att_ref[pair, :], out_w_ref[: 2 * HEAD_DIM, at], 1, 0).astype(BF16)
 
     scattering(branch_ref, *rest, produce)
 
 
-def attention(rows, own, far, out_w, cosine, sine, begins, name):
-    tokens, rank = rows.shape[0] // 8, 2 * own.shape[0]
+def attention(rows, heads, out_w, cosine, sine, begins, name):
+    tokens, rank = rows.shape[0] // 8, 2 * heads.shape[1]
     wide = out_w.shape[1]
     two = 2 * HEAD_DIM
     return vmem_call(
@@ -348,17 +358,17 @@
             jax.ShapeDtypeStruct((8 * tokens, 2), F32),
             jax.ShapeDtypeStruct((8 * tokens, two), BF16),
         ],
-        7,
+        0,
         scatter_scratch(tokens, wide),
         name,
         16 * tokens * two * (wide + rank + 2 * tokens),
-        rows, own, far, out_w, cosine, sine, begins,
+        rows, heads, out_w, cosine, sine, begins,
     )
 
 
 def attention_back_kernel(
-    rank, d_ref, rows_ref, own_ref, far_ref, out_w_ref, cos_ref, sin_ref, begin_ref, query_ref, lse_ref,
-    back_ref, dq_ref, *rest,
+    rank, d_ref, rows_ref, head_ref, out_w_ref, cos_ref, sin_ref, begin_ref, query_ref, lse_ref, give_ref,
+    back_ref, dq_ref, grad_ref, got_ref, *rest,
 ):
     tokens = back_ref.shape[0]
     mine, theirs = halves(rank)
@@ -366,7 +376,7 @@
 
     def produce(chip, target):
         pair = pl.ds(pl.multiple_of(chip * 2 * tokens, 2 * tokens), 2 * tokens)
-        d_pair = contract(d_ref[pair, :], out_w_ref[...], 1, 1).astype(BF16)
+        d_pair = contract(d_ref[pair, :], out_w_ref[: 2 * HEAD_DIM, :], 1, 1).astype(BF16)
         for c in range(2):
             rows = pl.ds(pl.multiple_of((2 * chip + c) * tokens, tokens), tokens)
             here = slice(c * tokens, (c + 1) * tokens)
@@ -389,31 +399,47 @@
                 d_values = d_v if h == 0 else d_values + d_v
             shared = turn(d_keys * scale, cosine, -sine) + d_values
             target[here, rank:] = shared.astype(BF16)
-        target[:, mine] = contract(dq_ref[pair, :], own_ref[...], 1, 1).astype(BF16)
-        target[:, theirs] = contract(dq_ref[pair, :], far_ref[...], 1, 1).astype(BF16)
-
-    scattering(back_ref, *rest, produce)
-
-
-def attention_back(d_rows, rows, own, far, out_w, cosine, sine, begins, queries, lse, name):
-    tokens, rank = rows.shape[0] // 8, 2 * own.shape[0]
+        for first, part in ((0, mine), (2, theirs)):
+            got = contract(dq_ref[pair, :HEAD_DIM], head_ref[first], 1, 1)
+            got = got + contract(dq_ref[pair, HEAD_DIM:], head_ref[first + 1], 1, 1)
+            target[:, part] = got.astype(BF16)
+
+    *rest, send_sem, recv_sem = rest
+    copy = send(give_ref, got_ref, send_sem, recv_sem, other(Y_BIT))
+
+    def meanwhile():
+        @pl.loop(0, rank // 256)
+        def _(i):
+            at = pl.ds(pl.multiple_of(i * 256, 256), 256)
+            grad_ref[at, :] = contract(rows_ref[:, at], dq_ref[...], 0, 0).astype(BF16)
+
+    scattering(back_ref, *rest, produce, at_start=copy.start, meanwhile=meanwhile, at_end=copy.wait)
+
+
+def attention_back(d_rows, rows, heads, out_w, cosine, sine, begins, queries, lse, give, name):
+    tokens, rank = rows.shape[0] // 8, 2 * heads.shape[1]
     wide = out_w.shape[1]
     two = 2 * HEAD_DIM
     full = rank + HEAD_DIM
     return vmem_call(
         functools.partial(attention_back_kernel, rank),
-        [jax.ShapeDtypeStruct((tokens, full), F32), jax.ShapeDtypeStruct((8 * tokens, two), BF16)],
-        10,
-        scatter_scratch(tokens, full),
+        [
+            jax.ShapeDtypeStruct((tokens, full), F32),
+            jax.ShapeDtypeStruct((8 * tokens, two), BF16),
+            jax.ShapeDtypeStruct((rank, two), BF16),
+            jax.ShapeDtypeStruct(give.shape, give.dtype),
+        ],
+        1,
+        [*scatter_scratch(tokens, full), pltpu.SemaphoreType.DMA, pltpu.SemaphoreType.DMA],
         name,
         16 * tokens * two * (wide + rank + 5 * tokens),
-        d_rows, rows, own, far, out_w, cosine, sine, begins, queries, lse,
+        d_rows, rows, heads, out_w, cosine, sine, begins, queries, lse, give,
     )
 
 
 def feed_kernel(
-    chunks, in_ref, g_ref, both_ref, down_ref, two_ref, hidden_ref, d_both_ref,
-    g_held, both_held, down_held, own_sem, load_sem, send_sem, recv_sem,
+    chunks, in_ref, g_ref, both_ref, down_ref, two_ref, hidden_ref, d_both_ref, own_sum, chip_sums,
+    g_held, both_held, down_held, work_ref, near_ref, own_sem, load_sem, send_sem, recv_sem, near_send, near_recv,
 ):
     step = 256
     tokens = in_ref.shape[0]
@@ -434,6 +460,34 @@
     for copy in loads:
         copy.wait()
 
+    def near(n):
+        return send(
+            work_ref.at[n, pl.ds(tokens, tokens)], near_ref.at[n], near_send.at[n], near_recv.at[n], other(C_BIT)
+        )
+
+    def chip_sum(n):
+        near(n).wait_recv()
+
+        def add(at):
+            total = work_ref[n, at, :].astype(F32) + near_ref[n, at, :].astype(F32)
+            if n:
+                chip_sums[n - 1, at, :] = total.astype(BF16)
+            else:
+                own_sum[at, :] = total
+
+        row_loop(tokens, add)
+
+    def outputs_of(chip):
+        pair = pl.ds(chip * tokens, 2 * tokens)
+        n = chip // 2
+
+        @pl.loop(0, down_held.shape[1] // step)
+        def _(i):
+            at = pl.ds(pl.multiple_of(i * step, step), step)
+            work_ref[n, :, at] = contract(hidden_ref[pair, :], down_held[:, at], 1, 0).astype(BF16)
+
+        near(n).start()
+
     def units_of(chip):
         arrived(chip)
         pair = pl.ds(chip * tokens, 2 * tokens)
@@ -456,9 +510,16 @@
     relay(0, chunks)
     units_of(X_BIT)
     units_of(Y_BIT)
+    outputs_of(0)
     far()
     units_of(BOTH)
+    outputs_of(X_BIT)
+    outputs_of(Y_BIT)
+    outputs_of(BOTH)
+    for n in range(4):
+        chip_sum(n)
     sent()
+    gone([near(n) for n in range(4)])
 
 
 def feed(rows, g, both, down, padded, name, chunks=4):
@@ -471,16 +532,21 @@
             jax.ShapeDtypeStruct((8 * tokens, width), BF16),
             jax.ShapeDtypeStruct((8 * tokens, padded), BF16),
             jax.ShapeDtypeStruct((8 * tokens, 2 * padded), BF16),
+            jax.ShapeDtypeStruct((tokens, width), F32),
+            jax.ShapeDtypeStruct((3, tokens, width), BF16),
         ],
         in_specs=[any_space] * 4,
-        out_specs=[vmem] * 3,
+        out_specs=[vmem] * 5,
         scratch_shapes=[
             pltpu.VMEM(g.shape, BF16),
             pltpu.VMEM(both.shape, BF16),
             pltpu.VMEM((padded, width), BF16),
+            pltpu.VMEM((4, 2 * tokens, width), BF16),
+            pltpu.VMEM((4, tokens, width), BF16),
             dma,
             dma((3,)),
             dma((8, chunks)), dma((8, chunks)),
+            dma((4,)), dma((4,)),
         ],
         compiler_params=pltpu.CompilerParams(
             collective_id=name, has_side_effects=True, vmem_limit_bytes=VMEM_MOST
@@ -491,7 +557,7 @@
     )(rows, g, both, down)
 
 
-def product_scatter_kernel(left_ref, right_ref, out_ref, *rest):
+def product_scatter_kernel(left_ref, right_ref, side_ref, out_ref, grad_ref, *rest):
     tokens = out_ref.shape[0]
     step = 256
 
@@ -503,111 +569,29 @@
             at = pl.ds(pl.multiple_of(i * step, step), step)
             target[:, at] = contract(left_ref[pair, :], right_ref[at, :], 1, 1).astype(BF16)
 
-    scattering(out_ref, *rest, produce)
-
-
-def product_scatter(left, right, name):
+    def meanwhile():
+        @pl.loop(0, grad_ref.shape[0] // step)
+        def _(i):
+            at = pl.ds(pl.multiple_of(i * step, step), step)
+            grad_ref[at, :] = contract(side_ref[:, at], left_ref[...], 0, 0).astype(BF16)
+
+    scattering(out_ref, *rest, produce, meanwhile=meanwhile)
+
+
+def product_scatter(left, right, side, name):
     tokens, wide = left.shape[0] // 8, right.shape[0]
     return vmem_call(
         product_scatter_kernel,
-        [jax.ShapeDtypeStruct((tokens, wide), F32)],
-        2,
+        [
+            jax.ShapeDtypeStruct((tokens, wide), F32),
+            jax.ShapeDtypeStruct((side.shape[1], left.shape[1]), BF16),
+        ],
+        0,
         scatter_scratch(tokens, wide),
         name,
-        16 * tokens * wide * left.shape[1],
-        left, right,
-    )[0]
-
-
-def branch_gather_kernel(
-    chunks, in_ref, hidden_ref, down_ref, out_ref, own_sum, chip_sums,
-    down_held, work_ref, near_ref, own_sem, load_sem, send_sem, recv_sem, near_send, near_recv,
-):
-    tokens = in_ref.shape[0]
-    wide = down_ref.shape[1]
-    units, padded = down_ref.shape[0], down_held.shape[0]
-    copies = [
-        pltpu.make_async_copy(in_ref, out_ref.at[pl.ds(0, tokens)], own_sem),
-        pltpu.make_async_copy(down_ref, down_held.at[pl.ds(0, units)], load_sem),
-    ]
-    begin(copies)
-    greet([other(C_BIT), other(X_BIT), other(Y_BIT)])
-    own, relay, far, arrived, sent = gathering(chunks, in_ref, out_ref, send_sem, recv_sem)
-    own()
-    if units < padded:
-        down_held[units:, :] = jnp.zeros((padded - units, wide), BF16)
-    for copy in copies:
-        copy.wait()
-
-    def near(n):
-        return send(
-            work_ref.at[n, pl.ds(tokens, tokens)], near_ref.at[n], near_send.at[n], near_recv.at[n], other(C_BIT)
-        )
-
-    def product(n):
-        pair = slice((3 - n) * 2 * tokens, (4 - n) * 2 * tokens)
-
-        @pl.loop(0, wide // 256)
-        def _(i):
-            at = pl.ds(pl.multiple_of(i * 256, 256), 256)
-            work_ref[n, :, at] = contract(hidden_ref[pair, :], down_held[:, at], 1, 0).astype(BF16)
-
-        near(n).start()
-
-    product(0)
-    product(1)
-    relay(0, chunks // 2)
-    product(2)
-    relay(chunks // 2, chunks)
-    product(3)
-    for n in range(4):
-        near(n).wait_recv()
-
-        def add(at, n=n):
-            total = work_ref[n, at, :].astype(F32) + near_ref[n, at, :].astype(F32)
-            if n < 3:
-                chip_sums[n, at, :] = total.astype(BF16)
-            else:
-                own_sum[at, :] = total
-
-        row_loop(tokens, add)
-    far()
-    for chip in (0, Y_BIT, X_BIT, BOTH):
-        arrived(chip)
-    sent()
-    gone([near(n) for n in range(4)])
-
-
-def branch_gather(rows, hidden, down, name, chunks=4):
-    tokens, width = rows.shape
-    wide = down.shape[1]
-    any_space, vmem = pl.BlockSpec(memory_space=pl.ANY), pl.BlockSpec(memory_space=pltpu.VMEM)
-    dma = pltpu.SemaphoreType.DMA
-    return pl.pallas_call(
-        functools.partial(branch_gather_kernel, chunks),
-        out_shape=[
-            jax.ShapeDtypeStruct((8 * tokens, width), BF16),
-            jax.ShapeDtypeStruct((tokens, wide), F32),
-            jax.ShapeDtypeStruct((3, tokens, wide), BF16),
-        ],
-        in_specs=[any_space, vmem, any_space],
-        out_specs=[any_space, vmem, vmem],
-        scratch_shapes=[
-            pltpu.VMEM((hidden.shape[1], wide), BF16),
-            pltpu.VMEM((4, 2 * tokens, wide), BF16),
-            pltpu.VMEM((4, tokens, wide), BF16),
-            dma,
-            dma,
-            dma((8, chunks)), dma((8, chunks)),
-            dma((4,)), dma((4,)),
-        ],
-        compiler_params=pltpu.CompilerParams(
-            collective_id=name, has_side_effects=True, vmem_limit_bytes=VMEM_MOST
-        ),
-        cost_estimate=pl.CostEstimate(
-            flops=16 * tokens * wide * hidden.shape[1], bytes_accessed=160 * 2**20, transcendentals=0
-        ),
-    )(rows, hidden, down)
+        32 * tokens * wide * left.shape[1],
+        left, right, side,
+    )
 
 
 def in_plane():
@@ -618,12 +602,13 @@
     def __init__(self, count, f_first, rank_rows, columns, kv_rows):
         self.count, self.f_first = count, f_first
         self.rank_rows, self.columns, self.kv_rows = rank_rows, columns, kv_rows
-        self.windows = columns % 128 == 0
+        self.windows = columns == 128
+        self.lines = rank_rows * columns // 128
 
     def down_shape(self):
         if self.windows:
             return (2 * self.rank_rows, 4 * self.count * self.columns)
-        return (8, self.count, self.rank_rows, self.columns)
+        return (8, self.count, self.lines, 128)
 
     def down_from(self, array):
         if self.windows:
@@ -682,10 +667,11 @@
 
 
 def start_kernel(
-    parcel, chunks, units, padded, down_ref, kv_ref, small_ref, gate_ref, up_ref, rows_ref,
-    down_all, kv_all, small_all, wide_all, rows_all,
-    down_low, kv_low, wide_ref,
+    parcel, chunks, units, padded, down_ref, kv_ref, small_ref, head_ref, out_ref, ff_ref, gate_ref, up_ref, rows_ref,
+    down_all, kv_all, small_all, head_all, out_all, ff_all, wide_all, rows_all,
+    down_low, kv_low, head_low, out_low, ff_low, wide_ref,
     local_sem, line_send, line_recv, plane_send, plane_recv, wide_send, wide_recv, rows_send, rows_recv,
+    head_send, head_recv, far_send, far_recv,
 ):
     count = parcel.count
     f, me = lax.axis_index("f"), in_plane()
@@ -694,6 +680,61 @@
     alls = (down_all, kv_all, small_all)
     down_low[...] = down_ref[...].astype(BF16)
     kv_low[...] = kv_ref[...].astype(BF16)
+    head_low[...] = head_ref[...].astype(BF16)
+    out_low[...] = out_ref[...].astype(BF16)
+    ff_low[...] = ff_ref[...].astype(BF16)
+
+    half = count // 2
+    y = lax.axis_index("y")
+
+    def head_blocks(j):
+        kept = (j // half == y).astype(jnp.int32)
+        spare = (1 - kept) * (2 * half + j % half)
+        return (
+            head_all.at[kept * (j % half) + spare],
+            out_all.at[kept * (2 * (j % half) + y) + spare],
+            ff_all.at[j],
+        )
+
+    def head_hop(j, up, sources):
+        return [
+            send(
+                source, target, head_send.at[i, 0 if up else 1, j], head_recv.at[i, j],
+                {"f": f + 1 if up else f - 1},
+            )
+            for i, (source, target) in enumerate(zip(sources, head_blocks(j)))
+        ]
+
+    def across(slot, sources):
+        targets = (head_all.at[half + slot], out_all.at[2 * slot + y])
+        return [
+            send(source, target, far_send.at[i, slot], far_recv.at[i, slot], other(Y_BIT))
+            for i, (source, target) in enumerate(zip(sources, targets))
+        ]
+
+    def head_own():
+        pl.when(upper)(lambda: begin(head_hop(f, True, own_heads)))
+        pl.when(lower)(lambda: begin(head_hop(f, False, own_heads)))
+        pl.when(f // half != y)(lambda: begin(across(f % half, own_heads)))
+
+    def head_step(step):
+        @pl.when(f - step >= 0)
+        def _():
+            j = f - step
+            blocks = head_blocks(j)
+            arrive(head_hop(j, True, blocks))
+            pl.when(upper)(lambda: begin(head_hop(j, True, blocks)))
+            pl.when(j // half != y)(lambda: begin(across(j % half, blocks)))
+
+        @pl.when(f + step <= count - 1)
+        def _():
+            j = f + step
+            blocks = head_blocks(j)
+            arrive(head_hop(j, False, blocks))
+            pl.when(lower)(lambda: begin(head_hop(j, False, blocks)))
+            pl.when(j // half != y)(lambda: begin(across(j % half, blocks)))
+
+    own_heads = (head_low, out_low, ff_low)
 
     def hop(j, up, sources):
         return [
@@ -772,6 +813,7 @@
         for i, (source, target) in enumerate(
             (
                 *zip(own, parcel.blocks(alls, me, f)),
+                *zip(own_heads, head_blocks(f)),
                 (wide_ref.at[me], wide_all.at[me]),
                 (rows_ref, rows_all.at[pl.ds(0, rows_ref.shape[0])]),
             )
@@ -781,17 +823,28 @@
     rows_own, rows_relay, rows_far, rows_arrived, rows_sent = gathering(chunks, rows_ref, rows_all, rows_send, rows_recv)
     for step in range(1, count):
         line_step(step)
+        if step == min(2, count - 1):
+            head_own()
     rows_own()
     in_order(relay)
+    head_step(1)
     rows_relay(0, chunks // 2)
     in_order(relay_far)
     rows_relay(chunks // 2, chunks)
-    rows_far()
+    for step in range(2, count):
+        head_step(step)
+        if step == 2:
+            rows_far()
     for copy in locals_:
         copy.wait()
     for j in range(count):
         pl.when(upper & (f >= j))(lambda: gone(hop(j, True, own)))
         pl.when(lower & (f <= j))(lambda: gone(hop(j, False, own)))
+        pl.when(upper & (f >= j))(lambda: gone(head_hop(j, True, own_heads)))
+        pl.when(lower & (f <= j))(lambda: gone(head_hop(j, False, own_heads)))
+    for slot in range(half):
+        arrive(across(slot, own_heads))
+        gone(across(slot, own_heads))
     for slot in range(1, 8):
         for j in range(count):
             for copy in spread(slot, slot, j, own):
@@ -806,7 +859,7 @@
     rows_sent()
 
 
-def start(parcel, down, kv, small, gate, up, rows, units, padded, name, chunks=4):
+def start(parcel, down, kv, small, head, out, ff, gate, up, rows, units, padded, name, chunks=4):
     count = parcel.count
     any_space, vmem = pl.BlockSpec(memory_space=pl.ANY), pl.BlockSpec(memory_space=pltpu.VMEM)
     dma = pltpu.SemaphoreType.DMA
@@ -817,39 +870,102 @@
             jax.ShapeDtypeStruct(parcel.down_shape(), BF16),
             jax.ShapeDtypeStruct((8 * count * kv.shape[0], kv.shape[1]), BF16),
             jax.ShapeDtypeStruct((8, count, *small.shape), BF16),
+            jax.ShapeDtypeStruct((3 * count // 2, *head.shape), BF16),
+            jax.ShapeDtypeStruct((3 * count // 2, *out.shape), BF16),
+            jax.ShapeDtypeStruct((count, *ff.shape), BF16),
             jax.ShapeDtypeStruct(wide, BF16),
             jax.ShapeDtypeStruct((8 * rows.shape[0], rows.shape[1]), BF16),
         ],
-        in_specs=[vmem] * 5 + [any_space],
-        out_specs=[any_space] * 5,
+        in_specs=[vmem] * 8 + [any_space],
+        out_specs=[any_space] * 8,
         scratch_shapes=[
             pltpu.VMEM(down.shape, BF16),
             pltpu.VMEM(kv.shape, BF16),
+            pltpu.VMEM(head.shape, BF16),
+            pltpu.VMEM(out.shape, BF16),
+            pltpu.VMEM(ff.shape, BF16),
             pltpu.VMEM(wide, BF16),
-            dma((5,)),
+            dma((8,)),
             dma((3, 2, count)), dma((3, count)),
             dma((3, 8, count)), dma((3, 8, count)),
             dma((8,)), dma((8,)),
             dma((8, chunks)), dma((8, chunks)),
+            dma((3, 2, count)), dma((3, count)),
+            dma((2, count // 2)), dma((2, count // 2)),
         ],
         compiler_params=pltpu.CompilerParams(
             collective_id=name, has_side_effects=True, vmem_limit_bytes=VMEM_MOST
         ),
         cost_estimate=pl.CostEstimate(flops=0, bytes_accessed=240 * 2**20, transcendentals=0),
-    )(down, kv, small, gate, up, rows)
+    )(down, kv, small, head, out, ff, gate, up, rows)
+
+
+def own_back_kernel(
+    back_ref, latent_ref, rms_lat_ref, gain_lat_ref, normed_ref, down_ref, kv_ref, in_ref, rms_ref, gain_ref, d_mid_ref,
+    down_part, kv_part, d_in_ref, lat_sum, gain_sum, d_normed,
+):
+    rank = latent_ref.shape[1]
+    width = in_ref.shape[1]
+    step = 512
+    d_lat_n, d_shared = back_ref[:, :rank], back_ref[:, rank:].astype(BF16)
+    latent, rms_lat = latent_ref[...], rms_lat_ref[...]
+    lat_sum[...] = jnp.sum(d_lat_n * latent * rms_lat, axis=0, keepdims=True)
+    scaled = d_lat_n * gain_lat_ref[...]
+    inner = jnp.sum(scaled * latent, axis=1, keepdims=True)
+    d_latent = (rms_lat * scaled - latent * (rms_lat * rms_lat * rms_lat) * inner / rank).astype(BF16)
+
+    @pl.loop(0, width // step)
+    def _(i):
+        at = pl.ds(pl.multiple_of(i * step, step), step)
+        down_part[:, at] = contract(d_latent, normed_ref[:, at], 0, 0).astype(BF16)
+        kv_part[at, :] = contract(normed_ref[:, at], d_shared, 0, 0).astype(BF16)
+        d_normed[:, at] = contract(d_shared, kv_ref[at, :], 1, 1) + contract(d_latent, down_ref[:, at], 1, 0)
+
+    inputs, rms = in_ref[...].astype(F32), rms_ref[...]
+    gain_sum[...] = jnp.sum(d_normed[...] * inputs * rms, axis=0, keepdims=True)
+    mean = jnp.sum(d_normed[...] * gain_ref[...] * inputs, axis=1, keepdims=True) / width
+    k = d_normed[...] * gain_ref[...]
+    d_in_ref[...] = (d_mid_ref[...] + rms * k - inputs * (rms * rms * rms) * mean).astype(BF16)
+
+
+def own_back(back, latent, rms_lat, gain_lat, normed, down, kv, inputs, rms, gain, d_middle):
+    vmem = pl.BlockSpec(memory_space=pltpu.VMEM)
+    tokens, width = inputs.shape
+    rank = latent.shape[1]
+    return pl.pallas_call(
+        own_back_kernel,
+        out_shape=[
+            jax.ShapeDtypeStruct((rank, width), BF16),
+            jax.ShapeDtypeStruct(kv.shape, BF16),
+            jax.ShapeDtypeStruct((tokens, width), BF16),
+            jax.ShapeDtypeStruct((1, rank), F32),
+            jax.ShapeDtypeStruct((1, width), F32),
+        ],
+        in_specs=[vmem] * 11,
+        out_specs=[vmem] * 5,
+        scratch_shapes=[pltpu.VMEM((tokens, width), F32)],
+        compiler_params=pltpu.CompilerParams(vmem_limit_bytes=VMEM_MOST),
+        cost_estimate=pl.CostEstimate(
+            flops=4 * tokens * width * (rank + kv.shape[1]), bytes_accessed=16 * 2**20, transcendentals=0
+        ),
+    )(back, latent, rms_lat, gain_lat, normed, down, kv, inputs, rms, gain, d_middle)
 
 
 def end_kernel(
-    parcel, units, padded, down_ref, kv_ref, small_ref, wide_ref,
-    down_sum, kv_sum, small_sum, gate_sum, up_sum, *rest,
+    parcel, units, padded, down_ref, kv_ref, small_ref, wide_ref, head_ref,
+    down_sum, kv_sum, small_sum, gate_sum, up_sum, head_sum, *rest,
 ):
     count = parcel.count
     held = [rest[8 * i : 8 * i + 8] for i in range(3)]
-    wide_all, near_send, near_recv, chip_send, chip_recv, line_send, line_recv, wide_send, wide_recv = rest[24:]
+    head_held = (rest[24], None, None, None, *rest[25:29])
+    head_got = rest[29]
+    held.append(head_held)
+    wide_all, near_send, near_recv, chip_send, chip_recv, line_send, line_recv, wide_send, wide_recv = rest[30:39]
+    far_send, far_recv = rest[39:]
     f, me = lax.axis_index("f"), in_plane()
     lower, upper = greet_all(count)
     parts = (down_ref, kv_ref, small_ref)
-    sums = (down_sum, kv_sum, small_sum)
+    sums = (down_sum, kv_sum, small_sum, head_sum)
     chips = (BOTH, X_BIT, Y_BIT, 0)
 
     def rows(amount, do):
@@ -866,16 +982,20 @@
             for i, source in enumerate(sources)
         ]
 
-    def far(n):
+    def far(n, j):
         return [
-            send(held[i][2].at[n], held[i][3].at[n], chip_send.at[i, n], chip_recv.at[i, n], other(chips[n]))
+            send(held[i][2].at[n, j], held[i][3].at[n, j], chip_send.at[i, n, j], chip_recv.at[i, n, j], other(chips[n]))
             for i in range(3)
         ]
 
+    order = []
+    for j in range(count // 2):
+        order += [count - 1 - j, j]
+
     def wide(bits):
         return send(wide_ref.at[me ^ as_place(bits)], wide_all.at[me], wide_send.at[bits], wide_recv.at[bits], other(bits))
 
-    def hop(d, up):
+    def hop(d, up, group):
         way = 0 if up else 1
         return [
             send(
@@ -883,10 +1003,10 @@
                 line_send.at[i, way, d], line_recv.at[i, way, d],
                 {"f": f + 1 if up else f - 1},
             )
-            for i in range(3)
+            for i in group
         ]
 
-    def pass_on(d, up):
+    def pass_on(d, up, group):
         way = 0 if up else 1
         behind = lower if up else upper
 
@@ -894,9 +1014,8 @@
         def _():
             @pl.when(behind)
             def _():
-                for copy in hop(d, up):
-                    copy.wait_recv()
-                for total, outgoing, incoming in ((h[0], h[4 + 2 * way], h[5 + 2 * way]) for h in held):
+                arrive(hop(d, up, group))
+                for total, outgoing, incoming in ((held[i][0], held[i][4 + 2 * way], held[i][5 + 2 * way]) for i in group):
 
                     def add(at, total=total, outgoing=outgoing, incoming=incoming):
                         outgoing[d, at, :] = (total[d, at, :] + incoming[d, at, :].astype(F32)).astype(BF16)
@@ -905,28 +1024,38 @@
 
             @pl.when(jnp.logical_not(behind))
             def _():
-                for total, outgoing in ((h[0], h[4 + 2 * way]) for h in held):
+                for total, outgoing in ((held[i][0], held[i][4 + 2 * way]) for i in group):
 
                     def keep(at, total=total, outgoing=outgoing):
                         outgoing[d, at, :] = total[d, at, :].astype(BF16)
 
                     rows(total.shape[1], keep)
 
-            for copy in hop(d, up):
-                copy.start()
-
-    for n in range(4):
-        for j in range(count):
-            for copy in near(n, j):
-                copy.start()
-    for n in range(4):
-        for j in range(count):
-            for copy in near(n, j):
-                copy.wait_recv()
+            begin(hop(d, up, group))
+
+    def line_step(step, group):
+        pass_on(count - step, True, group)
+        pass_on(step - 1, False, group)
+
+    half = count // 2
+    y = lax.axis_index("y")
+    rank_rows, columns = head_got.shape[0], head_got.shape[1] // half
+
+    def half_rows(which):
+        return pl.ds(pl.multiple_of(which * rank_rows, rank_rows), rank_rows)
+
+    swap = send(head_ref.at[half_rows(1 - y)], head_got, far_send, far_recv, other(Y_BIT))
+    swap.start()
+    for j in order:
+        for n in range(4):
+            begin(near(n, j))
+    for j in order:
+        for n in range(4):
+            arrive(near(n, j))
             for i, source in enumerate(parcel.blocks(parts, me ^ as_place(chips[n]), j)):
                 total, near_ref, chip_ref = held[i][:3]
 
-                def add(at, source=source, total=total, near_ref=near_ref, chip_ref=chip_ref):
+                def add(at, n=n, j=j, source=source, total=total, near_ref=near_ref, chip_ref=chip_ref):
                     both = source[at, :].astype(F32) + near_ref[n, j, at, :].astype(F32)
                     if n < 3:
                         chip_ref[n, j, at, :] = both.astype(BF16)
@@ -934,31 +1063,38 @@
                         total[j, at, :] = both
 
                 rows(total.shape[1], add)
-        if n < 3:
-            for copy in far(n):
-                copy.start()
+            if n < 3:
+                begin(far(n, j))
 
     for bits in FAR_FIRST:
         wide(bits).start()
     wide_all[me] = wide_ref[me]
-    for n in range(3):
-        for copy in far(n):
-            copy.wait_recv()
-    for i in range(3):
-        total, far_ref = held[i][0], held[i][3]
-        for j in range(count):
-
-            def add(at, total=total, far_ref=far_ref, j=j):
+    swap.wait_recv()
+    for slot in range(half):
+        at_columns = slice(slot * columns, (slot + 1) * columns)
+        head_held[0][y * half + slot] = head_ref[half_rows(y), at_columns].astype(F32)
+        head_held[0][(1 - y) * half + slot] = head_got[:, at_columns].astype(F32)
+    pair, head = (0, 1, 2), (3,)
+    line_step(1, head)
+    for at_order, j in enumerate(order):
+        for n in range(3):
+            arrive(far(n, j))
+        for i in range(3):
+            total, far_ref = held[i][0], held[i][3]
+
+            def add(at, j=j, total=total, far_ref=far_ref):
                 value = total[j, at, :]
                 for n in range(3):
                     value = value + far_ref[n, j, at, :].astype(F32)
                 total[j, at, :] = value
 
             rows(total.shape[1], add)
-    for step in range(1, count):
-        pass_on(count - step, True)
-        pass_on(step - 1, False)
-    for i in range(3):
+        pass_on(j, True, pair)
+        pass_on(j, False, pair)
+        if at_order == 1:
+            for step in range(2, count):
+                line_step(step, head)
+    for i in range(4):
 
         def keep(at, i=i):
             sums[i][at, :] = held[i][0][f, at, :]
@@ -968,9 +1104,8 @@
 
         @pl.when(there)
         def _(up=up):
-            for copy in hop(f, up):
-                copy.wait_recv()
-            for i in range(3):
+            arrive(hop(f, up, range(4)))
+            for i in range(4):
                 incoming = held[i][5 if up else 7]
 
                 def add(at, i=i, incoming=incoming):
@@ -983,28 +1118,29 @@
     for place, j, shard in parcel.unit_pieces():
         for first, ref in ((0, gate_sum), (padded, up_sum)):
             piece = wide_all[place, :, first + j * units : first + (j + 1) * units]
-            ref[:, shard * units : (shard + 1) * units] = piece.astype(F32)
+            ref[:, shard * units : (shard + 1) * units] = piece
 
     for d in range(count):
-        pl.when(f < d)(lambda: gone(hop(d, True)))
-        pl.when(f > d)(lambda: gone(hop(d, False)))
+        pl.when(f < d)(lambda: gone(hop(d, True, range(4))))
+        pl.when(f > d)(lambda: gone(hop(d, False, range(4))))
     for n in range(4):
         for j in range(count):
             for copy in near(n, j):
                 copy.wait_send()
     for n in range(3):
-        for copy in far(n):
-            copy.wait_send()
+        for j in range(count):
+            gone(far(n, j))
     for bits in range(1, 8):
         wide(bits).wait_send()
-
-
-def end(parcel, down, kv, small, wide, units, padded, name):
+    swap.wait_send()
+
+
+def end(parcel, down, kv, small, wide, head, units, padded, name):
     vmem = pl.BlockSpec(memory_space=pltpu.VMEM)
     dma = pltpu.SemaphoreType.DMA
     count = parcel.count
     bodies = (
-        (count, parcel.rank_rows, parcel.columns),
+        (count, parcel.lines, 128),
         (count, parcel.kv_rows, kv.shape[1]),
         (count, *small.shape[2:]),
     )
@@ -1013,28 +1149,34 @@
         low = pltpu.VMEM(body, BF16)
         three = pltpu.VMEM((3, *body), BF16)
         scratch += [pltpu.VMEM(body, F32), pltpu.VMEM((4, *body), BF16), three, three, low, low, low, low]
+    lines = (count, parcel.rank_rows, 2 * head.shape[1] // count)
     every = 8 * count * units
     return pl.pallas_call(
         functools.partial(end_kernel, parcel, units, padded),
         out_shape=[
             *[jax.ShapeDtypeStruct(body[1:], F32) for body in bodies],
-            *[jax.ShapeDtypeStruct((wide.shape[1], every), F32)] * 2,
+            *[jax.ShapeDtypeStruct((wide.shape[1], every), BF16)] * 2,
+            jax.ShapeDtypeStruct(lines[1:], F32),
         ],
-        in_specs=[vmem] * 4,
-        out_specs=[vmem] * 5,
+        in_specs=[vmem] * 5,
+        out_specs=[vmem] * 6,
         scratch_shapes=[
             *scratch,
+            pltpu.VMEM(lines, F32),
+            *[pltpu.VMEM(lines, BF16)] * 4,
+            pltpu.VMEM((parcel.rank_rows, head.shape[1]), BF16),
             pltpu.VMEM(wide.shape, BF16),
             dma((3, 4, count)), dma((3, 4, count)),
-            dma((3, 3)), dma((3, 3)),
-            dma((3, 2, count)), dma((3, 2, count)),
+            dma((3, 3, count)), dma((3, 3, count)),
+            dma((4, 2, count)), dma((4, 2, count)),
             dma((8,)), dma((8,)),
+            dma, dma,
         ],
         compiler_params=pltpu.CompilerParams(
             collective_id=name, has_side_effects=True, vmem_limit_bytes=VMEM_MOST
         ),
         cost_estimate=pl.CostEstimate(flops=0, bytes_accessed=240 * 2**20, transcendentals=0),
-    )(down, kv, small, wide)
+    )(down, kv, small, wide, head)
 
 
 def by_owner(array, axis, count, f_first):
@@ -1111,32 +1253,32 @@
     at_gain = 2 * lat_lines
     small = jnp.pad(small, ((0, -small.shape[0] % 16), (0, 0)))
     parcel = Parcel(count, f_first, half_rank, latent_down.shape[1], shared_kv.shape[0])
-    down_full, kv_full, small, both, g_all = start(
-        parcel, latent_down, shared_kv, small, gate_weight, up_weight, out_cotangent, units, padded, 0
+    down_full, kv_full, small, heads, out_full, ff_down, both, g_all = start(
+        parcel,
+        latent_down.reshape(-1, 128),
+        shared_kv,
+        small,
+        latent_up,
+        out_proj,
+        down_weight,
+        gate_weight,
+        up_weight,
+        out_cotangent,
+        units,
+        padded,
+        0,
     )
     down_full = parcel.down_from(down_full)
 
     half = count // 2
     per_head = count // 4
-    up_line = lax.all_gather(latent_up.astype(BF16), "f", axis=0)
-    out_line = lax.all_gather(out_proj.astype(BF16), "f", axis=0)
-
-    def heads(line):
-        own = lax.dynamic_slice_in_dim(line, half * y, half, 0)
-        far = lax.dynamic_slice_in_dim(line, half - half * y, half, 0)
-        return own, lax.ppermute(far, "y", SWAP)
-
-    def join(own, other_part, axis):
-        low = jnp.where(y == 0, own, other_part)
-        high = jnp.where(y == 0, other_part, own)
-        return jnp.stack([low, high], axis)
-
-    up_own, up_far = (part.transpose(1, 0, 2).reshape(half_rank, -1) for part in heads(up_line))
-    out_full = join(*heads(out_line), 1).reshape(2 * HEAD_DIM, width)
+    if per_head > 1:
+        heads = heads[: 2 * half].reshape(2, 2, per_head, half_rank, -1).transpose(0, 1, 3, 2, 4)
+        heads = heads.reshape(4, half_rank, HEAD_DIM)
+    out_full = out_full.reshape(-1, width)
 
     both = lax.all_gather(both, "f", axis=0)
     both = from_owner(both, 0, f_first)
-    ff_down = lax.all_gather(after(down_weight.astype(BF16), small), "f", axis=0)
     ff_down = ff_down.reshape(mine, width)
 
     gain_lat = small[:2, 0, :lat_lines].astype(F32) + small[:2, 0, lat_lines:at_gain].astype(F32)
@@ -1162,20 +1304,23 @@
 
     rows_all = plane_gather(jnp.concatenate([latent_n, k_own, shared.astype(BF16)], axis=1), 1)
     begins = begins.reshape(-1, 1)
-    branch, q_rot, lse, attended = attention(
-        rows_all, up_own, up_far, out_full, cosine, sine, begins, 2
-    )
+    branch, q_rot, lse, attended = attention(rows_all, heads, out_full, cosine, sine, begins, 2)
 
     middle = inputs + branch
     rms_two = lax.rsqrt(jnp.mean(middle * middle, axis=-1, keepdims=True) + EPS)
     normed_two = (middle * rms_two * gain_two).astype(BF16)
-    two_all, hidden, d_both = feed(normed_two, g_all, both, ff_down, padded, 3)
+    two_all, hidden, d_both, result, chip_sums = feed(normed_two, g_all, both, ff_down, padded, 3)
     down_grad = contract(hidden, g_all, 0, 0)[:mine].reshape(count, units, width).astype(BF16)
-    both_grad = by_owner(contract(two_all, d_both, 0, 0).astype(BF16), 0, count, f_first)
-    d_both, both_grad, down_grad = lax.optimization_barrier((d_both, both_grad, down_grad))
+    d_both, down_grad, chip_sums = lax.optimization_barrier((d_both, down_grad, chip_sums))
+    down_grad = lax.psum_scatter(down_grad, "f", scatter_dimension=0).astype(F32)
+    arrived = (
+        lax.ppermute(chip_sums[2], ("x", "y"), DIAGONAL),
+        lax.ppermute(chip_sums[1], "x", SWAP),
+        lax.ppermute(chip_sums[0], "y", SWAP),
+    )
+    d_two, both_grad = product_scatter(d_both, both, two_all, 4)
+    both_grad = by_owner(both_grad, 0, count, f_first)
     both_grad = lax.psum_scatter(both_grad, "f", scatter_dimension=0)
-    down_grad = lax.psum_scatter(down_grad, "f", scatter_dimension=0).astype(F32)
-    d_two = product_scatter(d_both, both, 4)
 
     upstream = out_cotangent.astype(F32)
     gain_two_part = jnp.sum(d_two * middle * rms_two, axis=0)
@@ -1186,52 +1331,32 @@
         - middle * (rms_two**3) * jnp.mean(scaled_two * middle, axis=-1, keepdims=True)
     )
 
-    d_branch, result, chip_sums = branch_gather(d_middle.astype(BF16), hidden, ff_down, 5)
-    back, d_queries = attention_back(
-        d_branch, rows_all, up_own, up_far, out_full, cosine, sine, begins, q_rot, lse, 6
-    )
-    d_lat_n, d_shared = back[:, :rank], back[:, rank:].astype(BF16)
-    lat_all = rows_all[:, :rank]
-
-    chip_sums = after(chip_sums, back)
-    arrived = (
-        lax.ppermute(chip_sums[0], ("x", "y"), DIAGONAL),
-        lax.ppermute(chip_sums[1], "x", SWAP),
-        lax.ppermute(chip_sums[2], "y", SWAP),
-    )
-
-    up_grad_heads = contract(lat_all, d_queries, 0, 0).reshape(2, half_rank, 2, HEAD_DIM)
-    out_grad_heads = contract(attended, d_branch, 0, 0).reshape(2, per_head, 2, -1, width)
-
-    def swap_halves(array, axis):
+    d_branch = plane_gather(d_middle.astype(BF16), 5)
+
+    def join(own, other_part, axis):
+        low = jnp.where(y == 0, own, other_part)
+        high = jnp.where(y == 0, other_part, own)
+        return jnp.stack([low, high], axis)
+
+    def halves_of(array, axis):
+        array = array.astype(BF16)
         own = lax.dynamic_index_in_dim(array, y, axis, keepdims=False)
-        other = lax.dynamic_index_in_dim(array, 1 - y, axis, keepdims=False).astype(BF16)
-        return own, lax.ppermute(other, "y", SWAP).astype(F32)
-
-    up_line_grad = join(*swap_halves(up_grad_heads, 0), 1).reshape(half_rank, count, -1)
-    up_line_grad = up_line_grad.transpose(1, 0, 2).astype(BF16)
-    latent_up_grad = lax.psum_scatter(after(up_line_grad, both_grad, down_grad, back), "f", scatter_dimension=0).astype(F32)
-    out_line_grad = join(*swap_halves(out_grad_heads, 2), 0)
-    out_line_grad = out_line_grad.reshape(count, -1, width).astype(BF16)
-    out_proj_grad = lax.psum_scatter(after(out_line_grad, both_grad, down_grad, back), "f", scatter_dimension=0).astype(F32)
-
-    gain_lat_part = jnp.sum(d_lat_n * latent * rms_lat, axis=0)
-    scaled_lat = d_lat_n * gain_lat
-    inner_lat = jnp.sum(scaled_lat * latent, axis=-1, keepdims=True)
-    d_latent = (rms_lat * scaled_lat - latent * (rms_lat**3) * inner_lat / rank).astype(BF16)
-    d_normed = contract(d_shared, kv_full, 1, 1) + jnp.dot(
-        d_latent, down_full, preferred_element_type=F32
-    )
-    gain_one_part = jnp.sum(d_normed * inputs * rms_one, axis=0)
-    scaled_one = d_normed * gain_one
-    input_grad = (
-        d_middle
-        + rms_one * scaled_one
-        - inputs * (rms_one**3) * jnp.mean(scaled_one * inputs, axis=-1, keepdims=True)
-    ).astype(BF16)
-
-    down_part = parcel.down_to(contract(d_latent, normed, 0, 0).astype(BF16))
-    kv_part = contract(normed, d_shared, 0, 0).astype(BF16)
+        return own, lax.dynamic_index_in_dim(array, 1 - y, axis, keepdims=False)
+
+    out_grad = contract(attended, d_branch, 0, 0).reshape(2, per_head, 2, -1, width)
+    out_own, out_far = halves_of(out_grad, 2)
+    back, d_queries, up_grad_part, out_far = attention_back(
+        d_branch, rows_all, heads, out_full, cosine, sine, begins, q_rot, lse, out_far, 6
+    )
+    out_line_grad = join(out_own, out_far, 0).reshape(count, -1, width)
+    out_proj_grad = lax.psum_scatter(after(out_line_grad, both_grad, down_grad), "f", scatter_dimension=0).astype(F32)
+
+    down_part, kv_part, input_grad, gain_lat_part, gain_one_part = own_back(
+        back, latent, rms_lat, gain_lat[None], normed, down_full, kv_full, block_input, rms_one, gain_one[None], d_middle
+    )
+    gain_one_part = gain_one_part.reshape(width)
+
+    down_part = parcel.down_to(down_part)
 
     def gain_rows_of(part):
         part = by_owner(part.astype(BF16), 0, count, f_first).transpose(1, 0, 2)
@@ -1249,9 +1374,11 @@
         axis=2,
     )
     small_part = jnp.pad(small_part, ((0, 0), (0, 0), (0, -small_part.shape[2] % 16), (0, 0)))
-    latent_down_grad, shared_kv_grad, small_sum, gate_grad, up_grad = end(
-        parcel, down_part, kv_part, small_part, both_grad, units, padded, 7
-    )
+    latent_down_grad, shared_kv_grad, small_sum, gate_grad, up_grad, latent_up_grad = end(
+        parcel, down_part, kv_part, small_part, both_grad, up_grad_part, units, padded, 7
+    )
+    gate_grad, up_grad = gate_grad.astype(F32), up_grad.astype(F32)
+    latent_down_grad = latent_down_grad.reshape(latent_down.shape)
     latent_gain_grad = small_sum[:lat_lines].reshape(half_rank)
     attn_gain_grad = small_sum[lat_lines, :gain_rows]
     mlp_gain_grad = small_sum[lat_lines + 1, :gain_rows]

time: 725 us -> 679 us (0.937)
  Pallas kernels: 494 us -> 547 us
  matrix products: 57.1 us -> 23.3 us
  waiting for transfers between devices: 62.8 us -> 29.7 us
  local copies, waits for them, and re-layouts: 33.8 us -> 18.9 us
    pallas_call x1, Pallas kernels: 83.9 us -> 121 us  [start(): pl.pallas_call(functools.partial(start_kernel, parcel, chunks, units, pad...]
    dot_general x8 -> x3, matrix products: 52.9 us -> 22.9 us  [contract(): lax.dot_general(left, right, (((left_dim,), (right_dim,)), ((), ())), pre...]
    pallas_call x4, Pallas kernels: 207 us -> 180 us  [the longest x3 169 us: vmem_call(): pl.pallas_call(kernel, out_shape=out_shape, in_specs=[vmem] * (len(arrays...]
    ppermute x6 -> x2, waiting for transfers between devices: 21.6 us -> 0.01 us  [the longest x1 0.01 us: per_device(): lax.ppermute(chip_sums[2], ('x', 'y'), DIAGONAL)]
    pallas_call x1, Pallas kernels: 53.7 us -> 71.3 us  [feed(): pl.pallas_call(functools.partial(feed_kernel, chunks), out_shape=[jax.Sha...]
    pallas_call x1, Pallas kernels: 91.6 us -> 105 us  [end(): pl.pallas_call(functools.partial(end_kernel, parcel, units, padded), out_...]
    pallas_call x1 -> x2, Pallas kernels: 57.6 us -> 70.4 us  [plane_gather(): pl.pallas_call(functools.partial(gather_kernel, chunks), out_shape=jax.Sh...]
    all_gather x1, waiting for transfers between devices: 40.1 us -> 29.6 us  [per_device(): both = lax.all_gather(both, 'f', axis=0)]
  transfers between devices with their start and end apart: 15 -> 7, of which waited for: 3 -> 1; matrix products, arithmetic and copies ran while one was open for 13% -> 8% of each run, Pallas kernels for 62% -> 53%
where the time goes in v5:
time: 679 us; the launch traced here: 673 us
  Pallas kernels  547 us (81%)
  other arithmetic  35.6 us (5%)
  waiting for transfers between devices  29.7 us (4%)
  matrix products  23.3 us (3%)
  local copies, waits for them, and re-layouts  18.9 us (3%)
  between operations  14.7 us (2%)
    pallas_call x3, Pallas kernels, vmem_call(): pl.pallas_call(kernel, out_shape=out_shape, in_specs=[vmem] * (len(arrays...  169 us
    pallas_call x1, Pallas kernels, start(): pl.pallas_call(functools.partial(start_kernel, parcel, chunks, units, pad...  121 us
    pallas_call x1, Pallas kernels, end(): pl.pallas_call(functools.partial(end_kernel, parcel, units, padded), out_...  105 us
    pallas_call x1, Pallas kernels, feed(): pl.pallas_call(functools.partial(feed_kernel, chunks), out_shape=[jax.Sha...  71.3 us
    pallas_call x2, Pallas kernels, plane_gather(): pl.pallas_call(functools.partial(gather_kernel, chunks), out_shape=jax.Sh...  70.4 us
    all_gather x1, waiting for transfers between devices, per_device(): both = lax.all_gather(both, 'f', axis=0)  29.6 us
    dot_general x3, matrix products, contract(): lax.dot_general(left, right, (((left_dim,), (right_dim,)), ((), ())), pre...  22.9 us
  transfers between devices with their start and end apart: 7, of which 1 were waited for; matrix products, arithmetic and copies ran while one was open for 8% of the time, Pallas kernels for 53%

profile of v5, /device:TPU:10, one launch (start us, length us, event | category | flops | bytes accessed | tf_op | source)
XLA Modules:
  0.0 673.2 jit_solution(3491018417528460428)
XLA Ops:
  10.6 120.6 %shard_map.220 = (bf16[1024,2048]{1,0:T(8,128)(2,1)}, bf16[2048,256]{1,0:T(8,128)(2,1)}, bf16[8,4,16,128]{3,2,1,0:T(8,128)(2,1)}, bf16[6,512,256]{2,1,0:T(8,128)...) custom-call(f32[512,128]{1,0:T(8,128)} %down_ref.1, ...), custom_call_target="tpu_custom_call" | custom-call | bytes 251658240 | tf_op jit(solution)/shard_map/pallas_call | solution.py:867
  134.9 4.0 multiply_reduce_fusion.3
  140.0 3.7 multiply_cosine_fusion
  145.2 30.4 %shard_map.221.rows_ref = bf16[2048,1536]{1,0:T(8,128)(2,1)} custom-call(bf16[256,1536]{1,0:T(8,128)(2,1)} %pad_maximum_fusion.1.in_ref), custom_call_target="tpu_custom_call" | custom-call | bytes 167772160 | tf_op jit(solution)/shard_map/pallas_call | solution.py:159
  177.1 52.8 %shard_map.222 = (f32[256,2048]{1,0:T(8,128)}, bf16[2048,512]{1,0:T(8,128)(2,1)}, f32[2048,2]{1,0:T(8,128)}, bf16[2048,512]{1,0:T(8,128)(2,1)}) custom-call(bf16[2048,1536]{1,0:T(8,128)(2,1)} %shard_map.221.rows_ref, bf16[6,512,256]{2,1,0:T(8,128)(2,1)} %get-tuple-element.55.head_ref, bf16[768,2048]{1,0:T(8,128)(2,1)} %bitcast.141, f32[2048,128]{1,0:T(8,128)} %copy-done.10, ...), custom_call_target="tpu_custom_call" | custom-call | flops 7516192768 | bytes 167772160 | tf_op jit(solution)/shard_map/pallas_call | solution.py:276
  229.9 2.0 multiply_reduce_fusion.2
  233.1 29.6 %all-gather.3.cloned.1.call-done = bf16[32,64,1536]{2,1,0:T(8,128)(2,1)} async-done(((bf16[8,64,1536]{2,1,0:T(8,128)(2,1)}), bf16[32,64,1536]{2,1,0:T(8,128)(2,1)}) %all-gather.3.cloned.1.call-update) | async-done | bytes 6291472 | tf_op jit(solution)/shard_map/all_gather | solution.py:1280
  262.8 71.3 %shard_map.223 = (bf16[2048,2048]{1,0:T(8,128)(2,1)}, bf16[2048,768]{1,0:T(8,128)(2,1)}, bf16[2048,1536]{1,0:T(8,128)(2,1)}, f32[256,2048]{1,0:T(8,128)}, bf16[3,256,2048]{2,1,0:T(8,128)(2,1)}) custom-call(bf16[256,2048]{1,0:T(8,128)(2,1)} %multiply_convert_fusion.in_ref, bf16[2048,2048]{1,0:T(8,128)(2,1)} %get-tuple-element.58.g_ref, ...), custom_call_target="tpu_custom_call" | custom-call | flops 19327352832 | bytes 167772160 | tf_op jit(solution)/shard_map/pallas_call | solution.py:529
  334.1 10.4 %fusion.21 = bf16[768,2048]{1,0:T(8,128)(2,1)S(1)} fusion(bf16[2048,768]{1,0:T(8,128)(2,1)} %get-tuple-element.63, bf16[2048,2048]{1,0:T(8,128)(2,1)} %get-tuple-element.58.g_ref), kind=kOutput, calls=%fused_computation.84 | convolution fusion | flops 6442450944 | bytes 14680064 | tf_op jit(solution)/shard_map/dot_general | solution.py:21
  344.5 1.8 slice.91
  346.4 57.9 %shard_map.224 = (f32[256,2048]{1,0:T(8,128)}, bf16[2048,1536]{1,0:T(8,128)(2,1)}) custom-call(bf16[2048,1536]{1,0:T(8,128)(2,1)} %get-tuple-element.66.left_ref, bf16[2048,1536]{1,0:T(8,128)(2,1)} %bitcast.140, bf16[2048,2048]{1,0:T(8,128)(2,1)} %get-tuple-element.67.side_ref), custom_call_target="tpu_custom_call" | custom-call | flops 25769803776 | bytes 167772160 | tf_op jit(solution)/shard_map/pallas_call | solution.py:276
  404.4 2.3 multiply_reduce_fusion
  406.9 2.3 fusion.19
  409.1 40.0 %shard_map.225.d_ref = bf16[2048,2048]{1,0:T(8,128)(2,1)} custom-call(bf16[256,2048]{1,0:T(8,128)(2,1)} %get-tuple-element.94.in_ref), custom_call_target="tpu_custom_call" | custom-call | bytes 167772160 | tf_op jit(solution)/shard_map/pallas_call | solution.py:159
  449.1 8.6 %convolution_convert_fusion = bf16[512,2048]{1,0:T(8,128)(2,1)S(1)} fusion(bf16[2048,512]{1,0:T(8,128)(2,1)} %get-tuple-element.71, bf16[2048,2048]{1,0:T(8,128)(2,1)} %shard_map.225.d_ref), kind=kOutput, calls=%fused_computation.4 | convolution fusion | flops 4296015872 | bytes 12582912 | tf_op jit(solution)/shard_map/dot_general | solution.py:21
  460.1 57.8 %shard_map.226 = (f32[256,1280]{1,0:T(8,128)}, bf16[2048,512]{1,0:T(8,128)(2,1)}, bf16[1024,512]{1,0:T(8,128)(2,1)}, bf16[2,1,128,2048]{3,2,1,0:T(8,128)(2,1)}) custom-call(bf16[2048,2048]{1,0:T(8,128)(2,1)} %shard_map.225.d_ref, bf16[2048,1536]{1,0:T(8,128)(2,1)} %shard_map.221.rows_ref, bf16[6,512,256]{2,1,0:T(8,128)(2,1)} %get-tuple-element.55.head_ref, ...), custom_call_target="tpu_custom_call" | custom-call | flops 9126805504 | bytes 167772160 | tf_op jit(solution)/shard_map/pallas_call | solution.py:276
  517.9 1.8 fusion.4
  522.0 2.4 bitcast_convert_fusion
  524.4 3.5 slice_bitcast_fusion
  533.7 11.1 %shard_map.227 = (bf16[1024,2048]{1,0:T(8,128)(2,1)}, bf16[2048,256]{1,0:T(8,128)(2,1)}, bf16[256,2048]{1,0:T(8,128)(2,1)}, f32[1,1024]{1,0:T(1,128)}, f32[1,2048]{1,0:T(1,128)}) custom-call(f32[256,1280]{1,0:T(8,128)} %get-tuple-element.72.back_ref, f32[256,1024]{1,0:T(8,128)} %copy-done.6, f32[256,1]{1,0:T(8,128)} %copy.98.rms_lat_ref, ...), custom_call_target="tpu_custom_call" | custom-call | flops 2684354560 | bytes 16777216 | tf_op jit(solution)/shard_map/pallas_call | solution.py:935
  547.2 104.9 %shard_map.228 = (f32[512,128]{1,0:T(8,128)}, f32[64,256]{1,0:T(8,128)}, f32[16,128]{1,0:T(8,128)}, bf16[64,5632]{1,0:T(8,128)(2,1)}, bf16[64,5632]{1,0:T(8,128)(2,1)}, /*index=5*/f32[512,256]{1,0:T(8,128)}) custom-call(bf16[1024,2048]{1,0:T(8,128)(2,1)} %get-tuple-element.73.down_ref, bf16[2048,256]{1,0:T(8,128)(2,1)} %get-tuple-element.74.kv_ref, ...), custom_call_target="tpu_custom_call" | custom-call | bytes 251658240 | tf_op jit(solution)/shard_map/pallas_call | solution.py:1154
  652.1 2.5 convert_element_type.229
  658.3 3.6 add_convert_fusion
  661.9 2.2 bitcast_convert_fusion.1
  (112 shorter events, 31.2 us)
Async XLA Ops:
  7.2 255.6 %all-gather.3.cloned.1.call-start = ((), (), s32[]{:S(2)}) async-start(), calls=%async_computation.6 | async-start | bytes 7864320 | tf_op jit(solution)/shard_map/all_gather | solution.py:1280
  131.3 2.9 copy-start
  131.3 390.7 %reduce-scatter.6.cloned.1.call-start = ((), (), s32[]{:S(2)}) async-start(), calls=%async_computation.4 | async-start | bytes 3604480 | tf_op jit(solution)/shard_map/reduce_scatter | solution.py:1315
  134.8 4.8 copy-start.1
  134.9 4.7 copy-start.5
  138.8 5.0 copy-start.6
  139.6 4.2 copy-start.16
  143.7 31.9 %copy-start.10 = (f32[2048,128]{1,0:T(8,128)}, f32[2048,128]{1,0:T(8,128)S(1)}, u32[]{:S(2)}) copy-start(f32[2048,128]{1,0:T(8,128)S(1)} %get-tuple-element.113.cos_ref) | copy-start | bytes 3145732
  143.7 31.9 %copy-start.11 = (f32[2048,128]{1,0:T(8,128)}, f32[2048,128]{1,0:T(8,128)S(1)}, u32[]{:S(2)}) copy-start(f32[2048,128]{1,0:T(8,128)S(1)} %get-tuple-element.114.sin_ref) | copy-start | bytes 3145732
  346.3 178.1 %reduce-scatter.4.cloned.1.call-start = ((), (), s32[]{:S(2)}) async-start(), calls=%async_computation.3 | async-start | bytes 7864320 | tf_op jit(solution)/shard_map/reduce_scatter | solution.py:1323
  404.3 257.6 %reduce-scatter.8.cloned.1.call-start = ((), (), s32[]{:S(2)}) async-start(), calls=%async_computation.5 | async-start | bytes 2621440 | tf_op jit(solution)/shard_map/reduce_scatter | solution.py:1352
  404.4 2.3 copy-start.2
  404.4 2.5 copy-start.8
  457.7 1.3 copy-start.3
  517.9 2.2 copy-start.4
  517.9 2.5 copy-start.7
  527.9 127.8 %collective-permute-start = (bf16[256,2048]{1,0:T(8,128)(2,1)}, bf16[256,2048]{1,0:T(8,128)(2,1)}, u32[]{:S(2)}, u32[]{:S(2)}) collective-permute-start(bf16[256,2048]{1,0:T(8,128)(2,1)} %get-tuple-element.100), channel_id=1, source_target_pairs={{0,5},{5,0},{1,4},{4,1},{2,7},{7,2},{3,6},{6,3},{8,13},{13,8},{9,1... | collective-permute-start | bytes 3145736 | tf_op jit(solution)/shard_map/ppermute | solution.py:1317
  529.4 126.4 %collective-permute-start.1 = (bf16[256,2048]{1,0:T(8,128)(2,1)}, bf16[256,2048]{1,0:T(8,128)(2,1)}, u32[]{:S(2)}, u32[]{:S(2)}) collective-permute-start(bf16[256,2048]{1,0:T(8,128)(2,1)} %get-tuple-element.99), channel_id=1, source_target_pairs={{0,4},{4,0},{1,5},{5,1},{2,6},{6,2},{3,7},{7,3},{8,12},{12,8},{9,1... | collective-permute-start | bytes 3145736 | tf_op jit(solution)/shard_map/ppermute | solution.py:1318
  530.9 124.8 %collective-permute-start.2 = (bf16[256,2048]{1,0:T(8,128)(2,1)S(1)}, bf16[256,2048]{1,0:T(8,128)(2,1)}, u32[]{:S(2)}, u32[]{:S(2)}) collective-permute-start(bf16[256,2048]{1,0:T(8,128)(2,1)S(1)} %get-tuple-element.98), channel_id=1, source_target_pairs={{0,1},{1,0},{2,3},{3,2},{4,5},{5,4},{6,7},{7,6},{8,9},{9,8},{10,11... | collective-permute-start | bytes 3145736 | tf_op jit(solution)/shard_map/ppermute | solution.py:1319
  652.1 2.5 copy-start.12
  652.1 6.2 copy-start.9
  658.3 5.8 copy-start.14
  661.9 2.9 copy-start.13
  661.9 3.7 copy-start.15
Sparse Core Ops, SparseCore 0:
  131.4 131.3 all-gather.2
  346.5 56.8 reduce-scatter.5
  405.6 111.2 reduce-scatter.3
  524.5 42.6 reduce-scatter.7

commit v6 on v5

--- a/solution.py
+++ b/solution.py
@@ -52,7 +52,6 @@
     )
 
 
-SWAP = [(0, 1), (1, 0)]
 DIAGONAL = [(0, 3), (3, 0), (1, 2), (2, 1)]
 
 
@@ -260,6 +259,27 @@
         at_end()
 
 
+class PairLoads:
+    def __init__(self, pairs, sem):
+        self.pairs, self.sem = pairs, sem
+        self.rows = pairs[0][0].shape[0] // 4
+
+    def copies(self, chip):
+        rows = pl.ds(pl.multiple_of(chip * self.rows, self.rows), self.rows)
+        return [
+            pltpu.make_async_copy(source.at[rows], target.at[rows], self.sem.at[i, chip])
+            for i, (source, target) in enumerate(self.pairs)
+        ]
+
+    def start(self):
+        for chip in (3, 2, 1, 0):
+            begin(self.copies(chip))
+
+    def wait(self, chip):
+        for copy in self.copies(chip):
+            copy.wait()
+
+
 def scatter_scratch(tokens, wide):
     dma = pltpu.SemaphoreType.DMA
     return [
@@ -272,12 +292,13 @@
 
 
 def vmem_call(kernel, out_shape, stay, scratch, name, flops, *arrays):
+    stay_in, stay_out = stay
     vmem, any_space = pl.BlockSpec(memory_space=pltpu.VMEM), pl.BlockSpec(memory_space=pl.ANY)
     return pl.pallas_call(
         kernel,
         out_shape=out_shape,
-        in_specs=[vmem] * (len(arrays) - stay) + [any_space] * stay,
-        out_specs=[vmem] * (len(out_shape) - stay) + [any_space] * stay,
+        in_specs=[vmem] * (len(arrays) - stay_in) + [any_space] * stay_in,
+        out_specs=[vmem] * (len(out_shape) - stay_out) + [any_space] * stay_out,
         scratch_shapes=scratch,
         compiler_params=pltpu.CompilerParams(
             collective_id=name, has_side_effects=True, vmem_limit_bytes=VMEM_MOST
@@ -309,14 +330,18 @@
 
 
 def attention_kernel(
-    rank, rows_ref, head_ref, out_w_ref, cos_ref, sin_ref, begin_ref,
+    rank, head_ref, out_w_ref, cos_ref, sin_ref, begin_ref, rows_in,
     branch_ref, query_ref, lse_ref, att_ref, *rest,
 ):
     wide = out_w_ref.shape[1]
     tokens = branch_ref.shape[0]
     mine, theirs = halves(rank)
+    *rest, rows_ref, load_sem = rest
+    loads = PairLoads([(rows_in, rows_ref)], load_sem)
+    loads.start()
 
     def produce(chip, target):
+        loads.wait(chip)
         pair = pl.ds(pl.multiple_of(chip * 2 * tokens, 2 * tokens), 2 * tokens)
         queries = [
             contract(rows_ref[pair, mine], head_ref[h], 1, 0) + contract(rows_ref[pair, theirs], head_ref[2 + h], 1, 0)
@@ -358,23 +383,27 @@
             jax.ShapeDtypeStruct((8 * tokens, 2), F32),
             jax.ShapeDtypeStruct((8 * tokens, two), BF16),
         ],
-        0,
-        scatter_scratch(tokens, wide),
+        (1, 0),
+        [*scatter_scratch(tokens, wide), pltpu.VMEM(rows.shape, BF16), pltpu.SemaphoreType.DMA((1, 4))],
         name,
         16 * tokens * two * (wide + rank + 2 * tokens),
-        rows, heads, out_w, cosine, sine, begins,
+        heads, out_w, cosine, sine, begins, rows,
     )
 
 
 def attention_back_kernel(
-    rank, d_ref, rows_ref, head_ref, out_w_ref, cos_ref, sin_ref, begin_ref, query_ref, lse_ref, give_ref,
+    rank, head_ref, out_w_ref, cos_ref, sin_ref, begin_ref, lse_ref, d_in, rows_in, query_in, give_ref,
     back_ref, dq_ref, grad_ref, got_ref, *rest,
 ):
     tokens = back_ref.shape[0]
     mine, theirs = halves(rank)
     scale = HEAD_DIM**-0.5
+    *rest, d_ref, rows_ref, query_ref, load_sem, send_sem, recv_sem = rest
+    loads = PairLoads([(d_in, d_ref), (rows_in, rows_ref), (query_in, query_ref)], load_sem)
+    loads.start()
 
     def produce(chip, target):
+        loads.wait(chip)
         pair = pl.ds(pl.multiple_of(chip * 2 * tokens, 2 * tokens), 2 * tokens)
         d_pair = contract(d_ref[pair, :], out_w_ref[: 2 * HEAD_DIM, :], 1, 1).astype(BF16)
         for c in range(2):
@@ -404,7 +433,6 @@
             got = got + contract(dq_ref[pair, HEAD_DIM:], head_ref[first + 1], 1, 1)
             target[:, part] = got.astype(BF16)
 
-    *rest, send_sem, recv_sem = rest
     copy = send(give_ref, got_ref, send_sem, recv_sem, other(Y_BIT))
 
     def meanwhile():
@@ -429,21 +457,27 @@
             jax.ShapeDtypeStruct((rank, two), BF16),
             jax.ShapeDtypeStruct(give.shape, give.dtype),
         ],
-        1,
-        [*scatter_scratch(tokens, full), pltpu.SemaphoreType.DMA, pltpu.SemaphoreType.DMA],
+        (4, 1),
+        [
+            *scatter_scratch(tokens, full),
+            *[pltpu.VMEM(array.shape, BF16) for array in (d_rows, rows, queries)],
+            pltpu.SemaphoreType.DMA((3, 4)),
+            pltpu.SemaphoreType.DMA,
+            pltpu.SemaphoreType.DMA,
+        ],
         name,
         16 * tokens * two * (wide + rank + 5 * tokens),
-        d_rows, rows, heads, out_w, cosine, sine, begins, queries, lse, give,
+        heads, out_w, cosine, sine, begins, lse, d_rows, rows, queries, give,
     )
 
 
 def feed_kernel(
-    chunks, in_ref, g_ref, both_ref, down_ref, two_ref, hidden_ref, d_both_ref, own_sum, chip_sums,
-    g_held, both_held, down_held, work_ref, near_ref, own_sem, load_sem, send_sem, recv_sem, near_send, near_recv,
+    chunks, in_ref, g_ref, both_ref, down_ref, two_out, hidden_out, d_both_out, own_sum, chip_sums,
+    two_ref, hidden_ref, d_both_ref, g_held, both_held, down_held, work_ref, near_ref, own_sem, load_sem, send_sem, recv_sem, near_send, near_recv, out_sem,
 ):
     step = 256
     tokens = in_ref.shape[0]
-    padded = hidden_ref.shape[1]
+    padded = hidden_out.shape[1]
     units = down_ref.shape[0]
     loads = [
         pltpu.make_async_copy(both_ref, both_held, load_sem.at[0]),
@@ -477,6 +511,14 @@
 
         row_loop(tokens, add)
 
+    def leave(chip):
+        pair = pl.ds(chip * tokens, 2 * tokens)
+        results = ((two_ref, two_out), (hidden_ref, hidden_out), (d_both_ref, d_both_out))
+        return [
+            pltpu.make_async_copy(held.at[pair], result.at[pair], out_sem.at[i, chip // 2])
+            for i, (held, result) in enumerate(results)
+        ]
+
     def outputs_of(chip):
         pair = pl.ds(chip * tokens, 2 * tokens)
         n = chip // 2
@@ -506,18 +548,24 @@
             d_both_ref[pair, at] = d_gate.astype(BF16)
             d_both_ref[pair, up_at] = (d_hidden * silu).astype(BF16)
 
+        begin(leave(chip))
+
     units_of(0)
+    outputs_of(0)
+    chip_sum(0)
     relay(0, chunks)
     units_of(X_BIT)
+    outputs_of(X_BIT)
     units_of(Y_BIT)
-    outputs_of(0)
     far()
+    outputs_of(Y_BIT)
     units_of(BOTH)
-    outputs_of(X_BIT)
-    outputs_of(Y_BIT)
     outputs_of(BOTH)
-    for n in range(4):
+    for n in (2, 1, 3):
         chip_sum(n)
+    for chip in (0, Y_BIT, X_BIT, BOTH):
+        for copy in leave(chip):
+            copy.wait()
     sent()
     gone([near(n) for n in range(4)])
 
@@ -536,8 +584,11 @@
             jax.ShapeDtypeStruct((3, tokens, width), BF16),
         ],
         in_specs=[any_space] * 4,
-        out_specs=[vmem] * 5,
+        out_specs=[any_space] * 3 + [vmem] * 2,
         scratch_shapes=[
+            pltpu.VMEM((8 * tokens, width), BF16),
+            pltpu.VMEM((8 * tokens, padded), BF16),
+            pltpu.VMEM((8 * tokens, 2 * padded), BF16),
             pltpu.VMEM(g.shape, BF16),
             pltpu.VMEM(both.shape, BF16),
             pltpu.VMEM((padded, width), BF16),
@@ -547,6 +598,7 @@
             dma((3,)),
             dma((8, chunks)), dma((8, chunks)),
             dma((4,)), dma((4,)),
+            dma((3, 4)),
         ],
         compiler_params=pltpu.CompilerParams(
             collective_id=name, has_side_effects=True, vmem_limit_bytes=VMEM_MOST
@@ -557,11 +609,19 @@
     )(rows, g, both, down)
 
 
-def product_scatter_kernel(left_ref, right_ref, side_ref, out_ref, grad_ref, *rest):
+def product_scatter_kernel(left_in, right_in, side_in, give_ref, out_ref, grad_ref, got_ref, *rest):
     tokens = out_ref.shape[0]
     step = 256
+    *rest, left_ref, right_ref, side_ref, grad_held, load_sem, pair_sem, grad_sem, give_send, give_recv = rest
+    right_load = pltpu.make_async_copy(right_in, right_ref, load_sem.at[0])
+    side_load = pltpu.make_async_copy(side_in, side_ref, load_sem.at[1])
+    loads = PairLoads([(left_in, left_ref)], pair_sem)
+    right_load.start()
+    loads.start()
+    side_load.start()
 
     def produce(chip, target):
+        loads.wait(chip)
         pair = pl.ds(pl.multiple_of(chip * 2 * tokens, 2 * tokens), 2 * tokens)
 
         @pl.loop(0, out_ref.shape[1] // step)
@@ -569,28 +629,63 @@
             at = pl.ds(pl.multiple_of(i * step, step), step)
             target[:, at] = contract(left_ref[pair, :], right_ref[at, :], 1, 1).astype(BF16)
 
+    copies = [
+        send(give_ref.at[i], got_ref.at[i], give_send.at[i], give_recv.at[i], other(bits))
+        for i, bits in enumerate((Y_BIT, X_BIT))
+    ]
+
+    def grad_out(i):
+        at = pl.ds(pl.multiple_of(i * step, step), step)
+        return pltpu.make_async_copy(grad_held.at[at], grad_ref.at[at], grad_sem.at[i])
+
+    steps = grad_ref.shape[0] // step
+
+    def at_start():
+        begin(copies)
+        right_load.wait()
+
     def meanwhile():
-        @pl.loop(0, grad_ref.shape[0] // step)
+        side_load.wait()
+
+        @pl.loop(0, steps)
         def _(i):
             at = pl.ds(pl.multiple_of(i * step, step), step)
-            grad_ref[at, :] = contract(side_ref[:, at], left_ref[...], 0, 0).astype(BF16)
-
-    scattering(out_ref, *rest, produce, meanwhile=meanwhile)
-
-
-def product_scatter(left, right, side, name):
+            grad_held[at, :] = contract(side_ref[:, at], left_ref[...], 0, 0).astype(BF16)
+            grad_out(i).start()
+
+    def at_end():
+        for copy in copies:
+            copy.wait()
+        for i in range(steps):
+            grad_out(i).wait()
+
+    scattering(out_ref, *rest, produce, at_start, meanwhile, at_end)
+
+
+def product_scatter(left, right, side, give, name):
     tokens, wide = left.shape[0] // 8, right.shape[0]
+    grad = (side.shape[1], left.shape[1])
+    dma = pltpu.SemaphoreType.DMA
     return vmem_call(
         product_scatter_kernel,
         [
             jax.ShapeDtypeStruct((tokens, wide), F32),
-            jax.ShapeDtypeStruct((side.shape[1], left.shape[1]), BF16),
+            jax.ShapeDtypeStruct(grad, BF16),
+            jax.ShapeDtypeStruct((2, *give.shape[1:]), BF16),
         ],
-        0,
-        scatter_scratch(tokens, wide),
+        (4, 2),
+        [
+            *scatter_scratch(tokens, wide),
+            *[pltpu.VMEM(array.shape, BF16) for array in (left, right, side)],
+            pltpu.VMEM(grad, BF16),
+            dma((2,)),
+            dma((1, 4)),
+            dma((grad[0] // 256,)),
+            dma((2,)), dma((2,)),
+        ],
         name,
         32 * tokens * wide * left.shape[1],
-        left, right, side,
+        left, right, side, give,
     )
 
 
@@ -696,13 +791,13 @@
             ff_all.at[j],
         )
 
-    def head_hop(j, up, sources):
+    def head_hop(j, up, sources, group):
         return [
             send(
-                source, target, head_send.at[i, 0 if up else 1, j], head_recv.at[i, j],
+                sources[i], head_blocks(j)[i], head_send.at[i, 0 if up else 1, j], head_recv.at[i, j],
                 {"f": f + 1 if up else f - 1},
             )
-            for i, (source, target) in enumerate(zip(sources, head_blocks(j)))
+            for i in group
         ]
 
     def across(slot, sources):
@@ -712,27 +807,32 @@
             for i, (source, target) in enumerate(zip(sources, targets))
         ]
 
-    def head_own():
-        pl.when(upper)(lambda: begin(head_hop(f, True, own_heads)))
-        pl.when(lower)(lambda: begin(head_hop(f, False, own_heads)))
-        pl.when(f // half != y)(lambda: begin(across(f % half, own_heads)))
-
-    def head_step(step):
+    heads, ff = (0, 1), (2,)
+
+    def head_own(group):
+        pl.when(upper)(lambda: begin(head_hop(f, True, own_heads, group)))
+        pl.when(lower)(lambda: begin(head_hop(f, False, own_heads, group)))
+        if group == heads:
+            pl.when(f // half != y)(lambda: begin(across(f % half, own_heads)))
+
+    def head_step(step, group):
         @pl.when(f - step >= 0)
         def _():
             j = f - step
             blocks = head_blocks(j)
-            arrive(head_hop(j, True, blocks))
-            pl.when(upper)(lambda: begin(head_hop(j, True, blocks)))
-            pl.when(j // half != y)(lambda: begin(across(j % half, blocks)))
+            arrive(head_hop(j, True, blocks, group))
+            pl.when(upper)(lambda: begin(head_hop(j, True, blocks, group)))
+            if group == heads:
+                pl.when(j // half != y)(lambda: begin(across(j % half, blocks)))
 
         @pl.when(f + step <= count - 1)
         def _():
             j = f + step
             blocks = head_blocks(j)
-            arrive(head_hop(j, False, blocks))
-            pl.when(lower)(lambda: begin(head_hop(j, False, blocks)))
-            pl.when(j // half != y)(lambda: begin(across(j % half, blocks)))
+            arrive(head_hop(j, False, blocks, group))
+            pl.when(lower)(lambda: begin(head_hop(j, False, blocks, group)))
+            if group == heads:
+                pl.when(j // half != y)(lambda: begin(across(j % half, blocks)))
 
     own_heads = (head_low, out_low, ff_low)
 
@@ -799,6 +899,7 @@
     pl.when(upper)(lambda: begin(hop(f, True, own)))
     pl.when(lower)(lambda: begin(hop(f, False, own)))
     to_plane(f, own)
+    head_own(heads)
     for place, j, shard in parcel.unit_pieces():
         for first, ref in ((0, gate_ref), (padded, up_ref)):
             piece = ref[:, shard * units : (shard + 1) * units].astype(BF16)
@@ -823,25 +924,27 @@
     rows_own, rows_relay, rows_far, rows_arrived, rows_sent = gathering(chunks, rows_ref, rows_all, rows_send, rows_recv)
     for step in range(1, count):
         line_step(step)
-        if step == min(2, count - 1):
-            head_own()
-    rows_own()
+        if step == 1:
+            rows_own()
+        if step < count - 1:
+            head_step(step, heads)
+    head_own(ff)
     in_order(relay)
-    head_step(1)
+    head_step(count - 1, heads)
     rows_relay(0, chunks // 2)
     in_order(relay_far)
+    head_step(1, ff)
     rows_relay(chunks // 2, chunks)
+    rows_far()
     for step in range(2, count):
-        head_step(step)
-        if step == 2:
-            rows_far()
+        head_step(step, ff)
     for copy in locals_:
         copy.wait()
     for j in range(count):
         pl.when(upper & (f >= j))(lambda: gone(hop(j, True, own)))
         pl.when(lower & (f <= j))(lambda: gone(hop(j, False, own)))
-        pl.when(upper & (f >= j))(lambda: gone(head_hop(j, True, own_heads)))
-        pl.when(lower & (f <= j))(lambda: gone(head_hop(j, False, own_heads)))
+        pl.when(upper & (f >= j))(lambda: gone(head_hop(j, True, own_heads, (0, 1, 2))))
+        pl.when(lower & (f <= j))(lambda: gone(head_hop(j, False, own_heads, (0, 1, 2))))
     for slot in range(half):
         arrive(across(slot, own_heads))
         gone(across(slot, own_heads))
@@ -1313,12 +1416,8 @@
     down_grad = contract(hidden, g_all, 0, 0)[:mine].reshape(count, units, width).astype(BF16)
     d_both, down_grad, chip_sums = lax.optimization_barrier((d_both, down_grad, chip_sums))
     down_grad = lax.psum_scatter(down_grad, "f", scatter_dimension=0).astype(F32)
-    arrived = (
-        lax.ppermute(chip_sums[2], ("x", "y"), DIAGONAL),
-        lax.ppermute(chip_sums[1], "x", SWAP),
-        lax.ppermute(chip_sums[0], "y", SWAP),
-    )
-    d_two, both_grad = product_scatter(d_both, both, two_all, 4)
+    d_two, both_grad, arrived = product_scatter(d_both, both, two_all, chip_sums, 4)
+    farthest = lax.ppermute(chip_sums[2], ("x", "y"), DIAGONAL)
     both_grad = by_owner(both_grad, 0, count, f_first)
     both_grad = lax.psum_scatter(both_grad, "f", scatter_dimension=0)
 
@@ -1382,8 +1481,8 @@
     latent_gain_grad = small_sum[:lat_lines].reshape(half_rank)
     attn_gain_grad = small_sum[lat_lines, :gain_rows]
     mlp_gain_grad = small_sum[lat_lines + 1, :gain_rows]
-    arrived = after(arrived, small_sum)
-    block_output = (middle + result + sum(part.astype(F32) for part in arrived)).astype(BF16)
+    farthest = after(farthest, small_sum).astype(F32)
+    block_output = (middle + result + arrived[0].astype(F32) + arrived[1].astype(F32) + farthest).astype(BF16)
     return (
         block_output,
         input_grad,

time: 679 us -> 639 us (0.941)
  Pallas kernels: 547 us -> 528 us
  waiting for transfers between devices: 29.7 us -> 12.9 us
    pallas_call x1, Pallas kernels: 105 us -> 83.8 us  [end(): pl.pallas_call(functools.partial(end_kernel, parcel, units, padded), out_...]
    all_gather x1, waiting for transfers between devices: 29.6 us -> 12.8 us  [per_device(): both = lax.all_gather(both, 'f', axis=0)]
    pallas_call x1, Pallas kernels: 121 us -> 135 us  [start(): pl.pallas_call(functools.partial(start_kernel, parcel, chunks, units, pad...]
    pallas_call x1, Pallas kernels: 71.3 us -> 59.7 us  [feed(): pl.pallas_call(functools.partial(feed_kernel, chunks), out_shape=[jax.Sha...]
  transfers between devices with their start and end apart: 7 -> 5, of which waited for: 1 -> 1; matrix products, arithmetic and copies ran while one was open for 8% -> 9% of each run, Pallas kernels for 53% -> 53%
where the time goes in v6:
time: 639 us; the launch traced here: 634 us
  Pallas kernels  528 us (83%)
  other arithmetic  36 us (6%)
  matrix products  23.3 us (4%)
  local copies, waits for them, and re-layouts  16.7 us (3%)
  between operations  14.7 us (2%)
  waiting for transfers between devices  12.9 us (2%)
    pallas_call x3, Pallas kernels, vmem_call(): pl.pallas_call(kernel, out_shape=out_shape, in_specs=[vmem] * (len(arrays...  166 us
    pallas_call x1, Pallas kernels, start(): pl.pallas_call(functools.partial(start_kernel, parcel, chunks, units, pad...  135 us
    pallas_call x1, Pallas kernels, end(): pl.pallas_call(functools.partial(end_kernel, parcel, units, padded), out_...  83.8 us
    pallas_call x2, Pallas kernels, plane_gather(): pl.pallas_call(functools.partial(gather_kernel, chunks), out_shape=jax.Sh...  71.6 us
    pallas_call x1, Pallas kernels, feed(): pl.pallas_call(functools.partial(feed_kernel, chunks), out_shape=[jax.Sha...  59.7 us
    dot_general x3, matrix products, contract(): lax.dot_general(left, right, (((left_dim,), (right_dim,)), ((), ())), pre...  22.9 us
    all_gather x1, waiting for transfers between devices, per_device(): both = lax.all_gather(both, 'f', axis=0)  12.8 us
  transfers between devices with their start and end apart: 5, of which 1 were waited for; matrix products, arithmetic and copies ran while one was open for 9% of the time, Pallas kernels for 53%

profile of v6, /device:TPU:10, one launch (start us, length us, event | category | flops | bytes accessed | tf_op | source)
XLA Modules:
  0.0 633.7 jit_solution(13808912543490750021)
XLA Ops:
  10.6 135.5 %shard_map.220 = (bf16[1024,2048]{1,0:T(8,128)(2,1)}, bf16[2048,256]{1,0:T(8,128)(2,1)}, bf16[8,4,16,128]{3,2,1,0:T(8,128)(2,1)}, bf16[6,512,256]{2,1,0:T(8,128)...) custom-call(f32[512,128]{1,0:T(8,128)} %down_ref.1, ...), custom_call_target="tpu_custom_call" | custom-call | bytes 251658240 | tf_op jit(solution)/shard_map/pallas_call | solution.py:970
  149.7 4.0 multiply_reduce_fusion.3
  154.9 3.7 multiply_sine_fusion
  160.0 32.3 %shard_map.221.rows_in = bf16[2048,1536]{1,0:T(8,128)(2,1)} custom-call(bf16[256,1536]{1,0:T(8,128)(2,1)} %pad_maximum_fusion.1.in_ref), custom_call_target="tpu_custom_call" | custom-call | bytes 167772160 | tf_op jit(solution)/shard_map/pallas_call | solution.py:158
  193.8 51.5 %shard_map.222 = (f32[256,2048]{1,0:T(8,128)}, bf16[2048,512]{1,0:T(8,128)(2,1)}, f32[2048,2]{1,0:T(8,128)}, bf16[2048,512]{1,0:T(8,128)(2,1)}) custom-call(bf16[6,512,256]{2,1,0:T(8,128)(2,1)} %get-tuple-element.51.head_ref, bf16[768,2048]{1,0:T(8,128)(2,1)} %bitcast.143, f32[2048,128]{1,0:T(8,128)} %copy-done.12, f32[2048,128]{1,0:T(8,128)} %copy-done.11, ...), custom_call_target="tpu_custom_call" | custom-call | flops 7516192768 | bytes 167772160 | tf_op jit(solution)/shard_map/pallas_call | solution.py:297
  245.3 1.9 multiply_reduce_fusion.2
  248.5 12.8 %all-gather.3.cloned.1.call-done = bf16[32,64,1536]{2,1,0:T(8,128)(2,1)} async-done(((bf16[8,64,1536]{2,1,0:T(8,128)(2,1)}), bf16[32,64,1536]{2,1,0:T(8,128)(2,1)}) %all-gather.3.cloned.1.call-update) | async-done | bytes 6291472 | tf_op jit(solution)/shard_map/all_gather | solution.py:1383
  261.3 59.7 %shard_map.223 = (bf16[2048,2048]{1,0:T(8,128)(2,1)}, bf16[2048,768]{1,0:T(8,128)(2,1)}, bf16[2048,1536]{1,0:T(8,128)(2,1)}, f32[256,2048]{1,0:T(8,128)}, bf16[3,256,2048]{2,1,0:T(8,128)(2,1)}) custom-call(bf16[256,2048]{1,0:T(8,128)(2,1)} %multiply_convert_fusion.in_ref, bf16[2048,2048]{1,0:T(8,128)(2,1)} %get-tuple-element.57.g_ref, ...), custom_call_target="tpu_custom_call" | custom-call | flops 19327352832 | bytes 167772160 | tf_op jit(solution)/shard_map/pallas_call | solution.py:577
  321.0 10.4 %fusion.23 = bf16[768,2048]{1,0:T(8,128)(2,1)S(1)} fusion(bf16[2048,768]{1,0:T(8,128)(2,1)} %get-tuple-element.62, bf16[2048,2048]{1,0:T(8,128)(2,1)} %get-tuple-element.57.g_ref), kind=kOutput, calls=%fused_computation.85 | convolution fusion | flops 6442450944 | bytes 14680064 | tf_op jit(solution)/shard_map/dot_general | solution.py:21
  331.3 1.7 slice.91
  333.1 61.4 %shard_map.224 = (f32[256,2048]{1,0:T(8,128)}, bf16[2048,1536]{1,0:T(8,128)(2,1)}, bf16[2,256,2048]{2,1,0:T(8,128)(2,1)}) custom-call(bf16[2048,1536]{1,0:T(8,128)(2,1)} %get-tuple-element.64.left_in, bf16[2048,1536]{1,0:T(8,128)(2,1)} %bitcast.142, bf16[2048,2048]{1,0:T(8,128)(2,1)} %get-tuple-element.65.side_in, ...), custom_call_target="tpu_custom_call" | custom-call | flops 25769803776 | bytes 167772160 | tf_op jit(solution)/shard_map/pallas_call | solution.py:297
  394.7 2.3 multiply_reduce_fusion
  397.1 2.3 fusion.21
  399.4 39.3 %shard_map.225.d_in = bf16[2048,2048]{1,0:T(8,128)(2,1)} custom-call(bf16[256,2048]{1,0:T(8,128)(2,1)} %get-tuple-element.92.in_ref), custom_call_target="tpu_custom_call" | custom-call | bytes 167772160 | tf_op jit(solution)/shard_map/pallas_call | solution.py:158
  438.7 8.6 %convolution_convert_fusion = bf16[512,2048]{1,0:T(8,128)(2,1)S(1)} fusion(bf16[2048,512]{1,0:T(8,128)(2,1)} %get-tuple-element.71, bf16[2048,2048]{1,0:T(8,128)(2,1)} %shard_map.225.d_in), kind=kOutput, calls=%fused_computation.4 | convolution fusion | flops 4296015872 | bytes 12582912 | tf_op jit(solution)/shard_map/dot_general | solution.py:21
  449.7 53.0 %shard_map.226 = (f32[256,1280]{1,0:T(8,128)}, bf16[2048,512]{1,0:T(8,128)(2,1)}, bf16[1024,512]{1,0:T(8,128)(2,1)}, bf16[2,1,128,2048]{3,2,1,0:T(8,128)(2,1)}) custom-call(bf16[6,512,256]{2,1,0:T(8,128)(2,1)} %get-tuple-element.51.head_ref, bf16[768,2048]{1,0:T(8,128)(2,1)} %bitcast.144, f32[2048,128]{1,0:T(8,128)} %copy-done.12, f32[2048,128]{1,0:T(8,128)} %copy-done.11, ...), custom_call_target="tpu_custom_call" | custom-call | flops 9126805504 | bytes 167772160 | tf_op jit(solution)/shard_map/pallas_call | solution.py:297
  502.7 1.8 fusion.6
  506.8 2.4 bitcast_convert_fusion
  514.3 11.5 %shard_map.227 = (bf16[1024,2048]{1,0:T(8,128)(2,1)}, bf16[2048,256]{1,0:T(8,128)(2,1)}, bf16[256,2048]{1,0:T(8,128)(2,1)}, f32[1,1024]{1,0:T(1,128)}, f32[1,2048]{1,0:T(1,128)}) custom-call(f32[256,1280]{1,0:T(8,128)} %get-tuple-element.72.back_ref, f32[256,1024]{1,0:T(8,128)} %copy-done.6, f32[256,1]{1,0:T(8,128)} %copy.98.rms_lat_ref, ...), custom_call_target="tpu_custom_call" | custom-call | flops 2684354560 | bytes 16777216 | tf_op jit(solution)/shard_map/pallas_call | solution.py:1038
  528.2 83.8 %shard_map.228 = (f32[512,128]{1,0:T(8,128)}, f32[64,256]{1,0:T(8,128)}, f32[16,128]{1,0:T(8,128)}, bf16[64,5632]{1,0:T(8,128)(2,1)}, bf16[64,5632]{1,0:T(8,128)(2,1)}, /*index=5*/f32[512,256]{1,0:T(8,128)}) custom-call(bf16[1024,2048]{1,0:T(8,128)(2,1)} %get-tuple-element.73.down_ref, bf16[2048,256]{1,0:T(8,128)(2,1)} %get-tuple-element.74.kv_ref, ...), custom_call_target="tpu_custom_call" | custom-call | bytes 251658240 | tf_op jit(solution)/shard_map/pallas_call | solution.py:1257
  612.1 2.5 convert_element_type.237
  614.5 2.3 convert_element_type.238
  619.4 3.0 fusion.4
  622.4 2.2 bitcast_convert_fusion.1
  (108 shorter events, 29.3 us)
Async XLA Ops:
  7.2 254.1 %all-gather.3.cloned.1.call-start = ((), (), s32[]{:S(2)}) async-start(), calls=%async_computation.6 | async-start | bytes 7864320 | tf_op jit(solution)/shard_map/all_gather | solution.py:1383
  146.1 2.9 copy-start
  146.1 360.7 %reduce-scatter.6.cloned.1.call-start = ((), (), s32[]{:S(2)}) async-start(), calls=%async_computation.4 | async-start | bytes 3604480 | tf_op jit(solution)/shard_map/reduce_scatter | solution.py:1418
  149.7 4.8 copy-start.1
  149.7 4.8 copy-start.5
  153.6 5.0 copy-start.6
  154.4 4.2 copy-start.16
  158.6 33.8 %copy-start.11 = (f32[2048,128]{1,0:T(8,128)}, f32[2048,128]{1,0:T(8,128)S(1)}, u32[]{:S(2)}) copy-start(f32[2048,128]{1,0:T(8,128)S(1)} %get-tuple-element.108.sin_ref) | copy-start | bytes 3145732
  158.6 33.8 %copy-start.12 = (f32[2048,128]{1,0:T(8,128)}, f32[2048,128]{1,0:T(8,128)S(1)}, u32[]{:S(2)}) copy-start(f32[2048,128]{1,0:T(8,128)S(1)} %get-tuple-element.109.cos_ref) | copy-start | bytes 3145732
  333.1 176.1 %reduce-scatter.4.cloned.1.call-start = ((), (), s32[]{:S(2)}) async-start(), calls=%async_computation.3 | async-start | bytes 7864320 | tf_op jit(solution)/shard_map/reduce_scatter | solution.py:1422
  394.6 227.8 %reduce-scatter.8.cloned.1.call-start = ((), (), s32[]{:S(2)}) async-start(), calls=%async_computation.5 | async-start | bytes 2621440 | tf_op jit(solution)/shard_map/reduce_scatter | solution.py:1451
  394.6 2.3 copy-start.2
  394.6 2.5 copy-start.8
  447.3 1.3 copy-start.3
  502.7 2.2 copy-start.4
  502.7 2.5 copy-start.7
  510.5 106.3 %collective-permute-start = (bf16[256,2048]{1,0:T(8,128)(2,1)S(1)}, bf16[256,2048]{1,0:T(8,128)(2,1)}, u32[]{:S(2)}, u32[]{:S(2)}) collective-permute-start(bf16[256,2048]{1,0:T(8,128)(2,1)S(1)} %slice_bitcast_fusion), channel_id=1, source_target_pairs={{0,5},{5,0},{1,4},{4,1},{2,7},{7,2},{3,6},{6,3},{8,13},{13,8},{9,1... | collective-permute-start | bytes 3145736 | tf_op jit(solution)/shard_map/ppermute | solution.py:1420
  612.1 7.3 %copy-start.9 = (f32[256,2048]{1,0:T(8,128)S(1)}, f32[256,2048]{1,0:T(8,128)}, u32[]{:S(2)}) copy-start(f32[256,2048]{1,0:T(8,128)} %get-tuple-element.60) | copy-start | bytes 6291460
  612.1 7.3 %copy-start.10 = (bf16[2,256,2048]{2,1,0:T(8,128)(2,1)S(1)}, bf16[2,256,2048]{2,1,0:T(8,128)(2,1)}, u32[]{:S(2)}) copy-start(bf16[2,256,2048]{2,1,0:T(8,128)(2,1)} %get-tuple-element.67) | copy-start | bytes 6291460
  619.4 5.2 copy-start.14
  622.4 2.9 copy-start.13
  622.4 3.7 copy-start.15
Sparse Core Ops, SparseCore 0:
  146.3 114.9 all-gather.2
  333.2 56.4 reduce-scatter.5
  394.7 111.2 reduce-scatter.3
  509.3 42.4 reduce-scatter.7

commit v7 on v6

--- a/solution.py
+++ b/solution.py
@@ -398,7 +398,7 @@
     tokens = back_ref.shape[0]
     mine, theirs = halves(rank)
     scale = HEAD_DIM**-0.5
-    *rest, d_ref, rows_ref, query_ref, load_sem, send_sem, recv_sem = rest
+    *rest, d_ref, rows_ref, query_ref, load_sem, keep_sem, send_sem, recv_sem = rest
     loads = PairLoads([(d_in, d_ref), (rows_in, rows_ref), (query_in, query_ref)], load_sem)
     loads.start()
 
@@ -433,7 +433,26 @@
             got = got + contract(dq_ref[pair, HEAD_DIM:], head_ref[first + 1], 1, 1)
             target[:, part] = got.astype(BF16)
 
-    copy = send(give_ref, got_ref, send_sem, recv_sem, other(Y_BIT))
+    y = lax.axis_index("y")
+    half = got_ref.shape[0] // 2
+    size = got_ref.shape[1]
+
+    def grad_copies(s):
+        rows = [pl.ds(pl.multiple_of((2 * s + which) * size, size), size) for which in (y, 1 - y)]
+        target = got_ref.at[y * half + s]
+        return (
+            pltpu.make_async_copy(give_ref.at[rows[0]], target, keep_sem.at[s]),
+            send(give_ref.at[rows[1]], target, send_sem.at[s], recv_sem.at[s], other(Y_BIT)),
+        )
+
+    def at_start():
+        for s in range(half):
+            begin(grad_copies(s))
+
+    def at_end():
+        for s in range(half):
+            for copy in grad_copies(s):
+                copy.wait()
 
     def meanwhile():
         @pl.loop(0, rank // 256)
@@ -441,10 +460,10 @@
             at = pl.ds(pl.multiple_of(i * 256, 256), 256)
             grad_ref[at, :] = contract(rows_ref[:, at], dq_ref[...], 0, 0).astype(BF16)
 
-    scattering(back_ref, *rest, produce, at_start=copy.start, meanwhile=meanwhile, at_end=copy.wait)
-
-
-def attention_back(d_rows, rows, heads, out_w, cosine, sine, begins, queries, lse, give, name):
+    scattering(back_ref, *rest, produce, at_start, meanwhile, at_end)
+
+
+def attention_back(d_rows, rows, heads, out_w, cosine, sine, begins, queries, lse, give, lines, name):
     tokens, rank = rows.shape[0] // 8, 2 * heads.shape[1]
     wide = out_w.shape[1]
     two = 2 * HEAD_DIM
@@ -455,15 +474,14 @@
             jax.ShapeDtypeStruct((tokens, full), F32),
             jax.ShapeDtypeStruct((8 * tokens, two), BF16),
             jax.ShapeDtypeStruct((rank, two), BF16),
-            jax.ShapeDtypeStruct(give.shape, give.dtype),
+            jax.ShapeDtypeStruct((lines, give.shape[0] // lines, give.shape[1]), give.dtype),
         ],
         (4, 1),
         [
             *scatter_scratch(tokens, full),
             *[pltpu.VMEM(array.shape, BF16) for array in (d_rows, rows, queries)],
             pltpu.SemaphoreType.DMA((3, 4)),
-            pltpu.SemaphoreType.DMA,
-            pltpu.SemaphoreType.DMA,
+            *[pltpu.SemaphoreType.DMA((lines // 2,))] * 3,
         ],
         name,
         16 * tokens * two * (wide + rank + 5 * tokens),
@@ -689,6 +707,77 @@
     )
 
 
+def branch_gather_kernel(
+    chunks, in_ref, att_ref, out_ref, grad_ref, held_ref, total_ref, own_sem, out_sem, send_sem, recv_sem
+):
+    tokens = in_ref.shape[0]
+    step = 512
+    copy = pltpu.make_async_copy(in_ref, held_ref.at[pl.ds(0, tokens)], own_sem)
+    copy.start()
+    greet([other(C_BIT), other(X_BIT), other(Y_BIT)])
+    own, relay, far, arrived, sent = gathering(chunks, in_ref, held_ref, send_sem, recv_sem)
+
+    def leave(chip):
+        pair = pl.ds(chip * tokens, 2 * tokens)
+        return pltpu.make_async_copy(held_ref.at[pair], out_ref.at[pair], out_sem.at[chip // 2])
+
+    def grad_of(chip):
+        arrived(chip)
+        leave(chip).start()
+        pair = pl.ds(chip * tokens, 2 * tokens)
+
+        @pl.loop(0, grad_ref.shape[1] // step)
+        def _(i):
+            at = pl.ds(pl.multiple_of(i * step, step), step)
+            got = contract(att_ref[pair, :], held_ref[pair, at], 0, 0)
+            if chip == 0:
+                total_ref[:, at] = got
+            elif chip == BOTH:
+                grad_ref[:, at] = (total_ref[:, at] + got).astype(BF16)
+            else:
+                total_ref[:, at] = total_ref[:, at] + got
+
+    own()
+    copy.wait()
+    grad_of(0)
+    relay(0, chunks)
+    grad_of(X_BIT)
+    grad_of(Y_BIT)
+    far()
+    grad_of(BOTH)
+    sent()
+    for chip in (0, Y_BIT, X_BIT, BOTH):
+        leave(chip).wait()
+
+
+def branch_gather(rows, att, name, chunks=4):
+    tokens, width = rows.shape
+    any_space, vmem = pl.BlockSpec(memory_space=pl.ANY), pl.BlockSpec(memory_space=pltpu.VMEM)
+    dma = pltpu.SemaphoreType.DMA
+    return pl.pallas_call(
+        functools.partial(branch_gather_kernel, chunks),
+        out_shape=[
+            jax.ShapeDtypeStruct((8 * tokens, width), BF16),
+            jax.ShapeDtypeStruct((att.shape[1], width), BF16),
+        ],
+        in_specs=[any_space, vmem],
+        out_specs=[any_space, vmem],
+        scratch_shapes=[
+            pltpu.VMEM((8 * tokens, width), BF16),
+            pltpu.VMEM((att.shape[1], width), F32),
+            dma,
+            dma((4,)),
+            dma((8, chunks)), dma((8, chunks)),
+        ],
+        compiler_params=pltpu.CompilerParams(
+            collective_id=name, has_side_effects=True, vmem_limit_bytes=VMEM_MOST
+        ),
+        cost_estimate=pl.CostEstimate(
+            flops=16 * tokens * width * att.shape[1], bytes_accessed=160 * 2**20, transcendentals=0
+        ),
+    )(rows, att)
+
+
 def in_plane():
     return 4 * lax.axis_index("x") + 2 * lax.axis_index("c") + lax.axis_index("y")
 
@@ -899,6 +988,8 @@
     pl.when(upper)(lambda: begin(hop(f, True, own)))
     pl.when(lower)(lambda: begin(hop(f, False, own)))
     to_plane(f, own)
+    rows_own, rows_relay, rows_far, rows_arrived, rows_sent = gathering(chunks, rows_ref, rows_all, rows_send, rows_recv)
+    rows_own()
     head_own(heads)
     for place, j, shard in parcel.unit_pieces():
         for first, ref in ((0, gate_ref), (padded, up_ref)):
@@ -921,20 +1012,16 @@
         )
     ]
     begin(locals_)
-    rows_own, rows_relay, rows_far, rows_arrived, rows_sent = gathering(chunks, rows_ref, rows_all, rows_send, rows_recv)
     for step in range(1, count):
         line_step(step)
-        if step == 1:
-            rows_own()
         if step < count - 1:
             head_step(step, heads)
     head_own(ff)
+    rows_relay(0, chunks)
     in_order(relay)
     head_step(count - 1, heads)
-    rows_relay(0, chunks // 2)
+    head_step(1, ff)
     in_order(relay_far)
-    head_step(1, ff)
-    rows_relay(chunks // 2, chunks)
     rows_far()
     for step in range(2, count):
         head_step(step, ff)
@@ -1221,7 +1308,7 @@
     for place, j, shard in parcel.unit_pieces():
         for first, ref in ((0, gate_sum), (padded, up_sum)):
             piece = wide_all[place, :, first + j * units : first + (j + 1) * units]
-            ref[:, shard * units : (shard + 1) * units] = piece
+            ref[:, shard * units : (shard + 1) * units] = piece.astype(F32)
 
     for d in range(count):
         pl.when(f < d)(lambda: gone(hop(d, True, range(4))))
@@ -1258,7 +1345,7 @@
         functools.partial(end_kernel, parcel, units, padded),
         out_shape=[
             *[jax.ShapeDtypeStruct(body[1:], F32) for body in bodies],
-            *[jax.ShapeDtypeStruct((wide.shape[1], every), BF16)] * 2,
+            *[jax.ShapeDtypeStruct((wide.shape[1], every), F32)] * 2,
             jax.ShapeDtypeStruct(lines[1:], F32),
         ],
         in_specs=[vmem] * 5,
@@ -1331,9 +1418,7 @@
     units = down_weight.shape[0]
     mine = units * count
     padded = -(-mine // 256) * 256
-    y = lax.axis_index("y")
     place = lax.axis_index("f")
-    x_c = 2 * lax.axis_index("x") + lax.axis_index("c")
 
     def rows_of(array):
         flat = array.reshape(-1)
@@ -1430,30 +1515,16 @@
         - middle * (rms_two**3) * jnp.mean(scaled_two * middle, axis=-1, keepdims=True)
     )
 
-    d_branch = plane_gather(d_middle.astype(BF16), 5)
-
-    def join(own, other_part, axis):
-        low = jnp.where(y == 0, own, other_part)
-        high = jnp.where(y == 0, other_part, own)
-        return jnp.stack([low, high], axis)
-
-    def halves_of(array, axis):
-        array = array.astype(BF16)
-        own = lax.dynamic_index_in_dim(array, y, axis, keepdims=False)
-        return own, lax.dynamic_index_in_dim(array, 1 - y, axis, keepdims=False)
-
-    out_grad = contract(attended, d_branch, 0, 0).reshape(2, per_head, 2, -1, width)
-    out_own, out_far = halves_of(out_grad, 2)
-    back, d_queries, up_grad_part, out_far = attention_back(
-        d_branch, rows_all, heads, out_full, cosine, sine, begins, q_rot, lse, out_far, 6
-    )
-    out_line_grad = join(out_own, out_far, 0).reshape(count, -1, width)
-    out_proj_grad = lax.psum_scatter(after(out_line_grad, both_grad, down_grad), "f", scatter_dimension=0).astype(F32)
-
+    d_branch, out_grad = branch_gather(d_middle.astype(BF16), attended, 5)
+    back, d_queries, up_grad_part, out_grad = attention_back(
+        d_branch, rows_all, heads, out_full, cosine, sine, begins, q_rot, lse, out_grad, count, 6
+    )
     down_part, kv_part, input_grad, gain_lat_part, gain_one_part = own_back(
         back, latent, rms_lat, gain_lat[None], normed, down_full, kv_full, block_input, rms_one, gain_one[None], d_middle
     )
     gain_one_part = gain_one_part.reshape(width)
+    out_grad = after(out_grad, both_grad, down_grad, gain_one_part)
+    out_proj_grad = lax.psum_scatter(out_grad, "f", scatter_dimension=0).astype(F32)
 
     down_part = parcel.down_to(down_part)
 
@@ -1476,7 +1547,6 @@
     latent_down_grad, shared_kv_grad, small_sum, gate_grad, up_grad, latent_up_grad = end(
         parcel, down_part, kv_part, small_part, both_grad, up_grad_part, units, padded, 7
     )
-    gate_grad, up_grad = gate_grad.astype(F32), up_grad.astype(F32)
     latent_down_grad = latent_down_grad.reshape(latent_down.shape)
     latent_gain_grad = small_sum[:lat_lines].reshape(half_rank)
     attn_gain_grad = small_sum[lat_lines, :gain_rows]

time: 639 us -> 630 us (0.986)
  matrix products: 23.3 us -> 14.7 us
  waiting for transfers between devices: 12.9 us -> 21.5 us
  other arithmetic: 36 us -> 29.2 us
    pallas_call x0 -> x1, Pallas kernels: none -> 42.7 us  [branch_gather(): pl.pallas_call(functools.partial(branch_gather_kernel, chunks), out_shape...]
    pallas_call x2 -> x1, Pallas kernels: 71.6 us -> 31.2 us  [plane_gather(): pl.pallas_call(functools.partial(gather_kernel, chunks), out_shape=jax.Sh...]
    dot_general x3 -> x2, matrix products: 22.9 us -> 14.3 us  [contract(): lax.dot_general(left, right, (((left_dim,), (right_dim,)), ((), ())), pre...]
    reduce_scatter x1, waiting for transfers between devices: 0.01 us -> 7.49 us  [per_device(): both_grad = lax.psum_scatter(both_grad, 'f', scatter_dimension=0)]
  transfers between devices with their start and end apart: 5 -> 5, of which waited for: 1 -> 2; matrix products, arithmetic and copies ran while one was open for 9% -> 6% of each run, Pallas kernels for 53% -> 54%
where the time goes in v7:
time: 630 us; the launch traced here: 625 us
  Pallas kernels  527 us (84%)
  other arithmetic  29.2 us (5%)
  waiting for transfers between devices  21.5 us (3%)
  local copies, waits for them, and re-layouts  15.8 us (3%)
  matrix products  14.7 us (2%)
  between operations  14.5 us (2%)
    pallas_call x3, Pallas kernels, vmem_call(): pl.pallas_call(kernel, out_shape=out_shape, in_specs=[vmem] * (len(arrays...  167 us
    pallas_call x1, Pallas kernels, start(): pl.pallas_call(functools.partial(start_kernel, parcel, chunks, units, pad...  131 us
    pallas_call x1, Pallas kernels, end(): pl.pallas_call(functools.partial(end_kernel, parcel, units, padded), out_...  84.5 us
    pallas_call x1, Pallas kernels, feed(): pl.pallas_call(functools.partial(feed_kernel, chunks), out_shape=[jax.Sha...  59.7 us
    pallas_call x1, Pallas kernels, branch_gather(): pl.pallas_call(functools.partial(branch_gather_kernel, chunks), out_shape...  42.7 us
    pallas_call x1, Pallas kernels, plane_gather(): pl.pallas_call(functools.partial(gather_kernel, chunks), out_shape=jax.Sh...  31.2 us
    dot_general x2, matrix products, contract(): lax.dot_general(left, right, (((left_dim,), (right_dim,)), ((), ())), pre...  14.3 us
    all_gather x1, waiting for transfers between devices, per_device(): both = lax.all_gather(both, 'f', axis=0)  13.9 us
  transfers between devices with their start and end apart: 5, of which 2 were waited for; matrix products, arithmetic and copies ran while one was open for 6% of the time, Pallas kernels for 54%

profile of v7, /device:TPU:10, one launch (start us, length us, event | category | flops | bytes accessed | tf_op | source)
XLA Modules:
  0.0 625.4 jit_solution(10926582554780321702)
XLA Ops:
  10.6 131.3 %shard_map.220 = (bf16[1024,2048]{1,0:T(8,128)(2,1)}, bf16[2048,256]{1,0:T(8,128)(2,1)}, bf16[8,4,16,128]{3,2,1,0:T(8,128)(2,1)}, bf16[6,512,256]{2,1,0:T(8,128)...) custom-call(f32[512,128]{1,0:T(8,128)} %down_ref.1, ...), custom_call_target="tpu_custom_call" | custom-call | bytes 251658240 | tf_op jit(solution)/shard_map/pallas_call | solution.py:1057
  145.6 3.9 multiply_reduce_fusion.3
  150.8 3.7 multiply_sine_fusion
  155.9 31.2 %shard_map.221.rows_in = bf16[2048,1536]{1,0:T(8,128)(2,1)} custom-call(bf16[256,1536]{1,0:T(8,128)(2,1)} %pad_maximum_fusion.in_ref), custom_call_target="tpu_custom_call" | custom-call | bytes 167772160 | tf_op jit(solution)/shard_map/pallas_call | solution.py:158
  187.2 1.3 copy.84
  188.6 51.3 %shard_map.222 = (f32[256,2048]{1,0:T(8,128)}, bf16[2048,512]{1,0:T(8,128)(2,1)}, f32[2048,2]{1,0:T(8,128)}, bf16[2048,512]{1,0:T(8,128)(2,1)}) custom-call(bf16[6,512,256]{2,1,0:T(8,128)(2,1)} %get-tuple-element.53.head_ref, bf16[768,2048]{1,0:T(8,128)(2,1)} %bitcast.111, f32[2048,128]{1,0:T(8,128)} %copy-done.9, f32[2048,128]{1,0:T(8,128)} %copy-done.8, ...), custom_call_target="tpu_custom_call" | custom-call | flops 7516192768 | bytes 167772160 | tf_op jit(solution)/shard_map/pallas_call | solution.py:297
  239.9 1.9 multiply_reduce_fusion.2
  243.1 13.9 %all-gather.3.cloned.1.call-done = bf16[32,64,1536]{2,1,0:T(8,128)(2,1)} async-done(((bf16[8,64,1536]{2,1,0:T(8,128)(2,1)}), bf16[32,64,1536]{2,1,0:T(8,128)(2,1)}) %all-gather.3.cloned.1.call-update) | async-done | bytes 6291472 | tf_op jit(solution)/shard_map/all_gather | solution.py:1468
  256.9 59.7 %shard_map.223 = (bf16[2048,2048]{1,0:T(8,128)(2,1)}, bf16[2048,768]{1,0:T(8,128)(2,1)}, bf16[2048,1536]{1,0:T(8,128)(2,1)}, f32[256,2048]{1,0:T(8,128)}, bf16[3,256,2048]{2,1,0:T(8,128)(2,1)}) custom-call(bf16[256,2048]{1,0:T(8,128)(2,1)} %multiply_convert_fusion.in_ref, bf16[2048,2048]{1,0:T(8,128)(2,1)} %get-tuple-element.59.g_ref, ...), custom_call_target="tpu_custom_call" | custom-call | flops 19327352832 | bytes 167772160 | tf_op jit(solution)/shard_map/pallas_call | solution.py:595
  316.7 10.4 %fusion.21 = bf16[768,2048]{1,0:T(8,128)(2,1)S(1)} fusion(bf16[2048,768]{1,0:T(8,128)(2,1)} %get-tuple-element.64, bf16[2048,2048]{1,0:T(8,128)(2,1)} %get-tuple-element.59.g_ref), kind=kOutput, calls=%fused_computation.78 | convolution fusion | flops 6442450944 | bytes 14680064 | tf_op jit(solution)/shard_map/dot_general | solution.py:21
  327.0 1.8 slice.91
  328.9 61.2 %shard_map.224 = (f32[256,2048]{1,0:T(8,128)}, bf16[2048,1536]{1,0:T(8,128)(2,1)}, bf16[2,256,2048]{2,1,0:T(8,128)(2,1)}) custom-call(bf16[2048,1536]{1,0:T(8,128)(2,1)} %get-tuple-element.66.left_in, bf16[2048,1536]{1,0:T(8,128)(2,1)} %bitcast.110, bf16[2048,2048]{1,0:T(8,128)(2,1)} %get-tuple-element.67.side_in, ...), custom_call_target="tpu_custom_call" | custom-call | flops 25769803776 | bytes 167772160 | tf_op jit(solution)/shard_map/pallas_call | solution.py:297
  390.2 2.3 multiply_reduce_fusion
  392.7 2.3 fusion.19
  395.0 42.7 %shard_map.225 = (bf16[2048,2048]{1,0:T(8,128)(2,1)}, bf16[512,2048]{1,0:T(8,128)(2,1)}) custom-call(bf16[256,2048]{1,0:T(8,128)(2,1)} %get-tuple-element.96.in_ref, bf16[2048,512]{1,0:T(8,128)(2,1)} %get-tuple-element.72.att_ref), custom_call_target="tpu_custom_call" | custom-call | flops 4294967296 | bytes 167772160 | tf_op jit(solution)/shard_map/pallas_call | solution.py:757
  437.6 54.1 %shard_map.226 = (f32[256,1280]{1,0:T(8,128)}, bf16[2048,512]{1,0:T(8,128)(2,1)}, bf16[1024,512]{1,0:T(8,128)(2,1)}, bf16[4,128,2048]{2,1,0:T(8,128)(2,1)}) custom-call(bf16[6,512,256]{2,1,0:T(8,128)(2,1)} %get-tuple-element.53.head_ref, bf16[768,2048]{1,0:T(8,128)(2,1)} %bitcast.112, f32[2048,128]{1,0:T(8,128)} %copy-done.9, f32[2048,128]{1,0:T(8,128)} %copy-done.8, ...), custom_call_target="tpu_custom_call" | custom-call | flops 9126805504 | bytes 167772160 | tf_op jit(solution)/shard_map/pallas_call | solution.py:297
  491.7 2.4 bitcast_convert_fusion
  494.1 7.5 %reduce-scatter.4.cloned.1.call-done = bf16[1,8,64,1536]{3,2,1,0:T(8,128)(2,1)} async-done(((bf16[4,8,64,1536]{3,2,1,0:T(8,128)(2,1)}), bf16[1,8,64,1536]{3,2,1,0:T(8,128)(2,1)}) %reduce-scatter.4.cloned.1.call-update) | async-done | bytes 1572880 | tf_op jit(solution)/shard_map/reduce_scatter | solution.py:1507
  501.6 1.3 slice_bitcast_fusion
  502.9 1.5 collective-permute-start
  506.7 11.4 %shard_map.227 = (bf16[1024,2048]{1,0:T(8,128)(2,1)}, bf16[2048,256]{1,0:T(8,128)(2,1)}, bf16[256,2048]{1,0:T(8,128)(2,1)}, f32[1,1024]{1,0:T(1,128)}, f32[1,2048]{1,0:T(1,128)}) custom-call(f32[256,1280]{1,0:T(8,128)} %get-tuple-element.76.back_ref, f32[256,1024]{1,0:T(8,128)} %copy-done.4, f32[256,1]{1,0:T(8,128)} %copy.77.rms_lat_ref, ...), custom_call_target="tpu_custom_call" | custom-call | flops 2684354560 | bytes 16777216 | tf_op jit(solution)/shard_map/pallas_call | solution.py:1125
  520.6 84.5 %shard_map.228 = (f32[512,128]{1,0:T(8,128)}, f32[64,256]{1,0:T(8,128)}, f32[16,128]{1,0:T(8,128)}, f32[64,5632]{1,0:T(8,128)}, f32[64,5632]{1,0:T(8,128)}, /*index=5*/f32[512,256]{1,0:T(8,128)}) custom-call(bf16[1024,2048]{1,0:T(8,128)(2,1)} %get-tuple-element.77.down_ref, bf16[2048,256]{1,0:T(8,128)(2,1)} %get-tuple-element.78.kv_ref, ...), custom_call_target="tpu_custom_call" | custom-call | bytes 251658240 | tf_op jit(solution)/shard_map/pallas_call | solution.py:1344
  607.7 4.3 fusion.4
  612.0 2.3 bitcast_convert_fusion.1
  (97 shorter events, 22.8 us)
Async XLA Ops:
  7.2 249.8 %all-gather.3.cloned.1.call-start = ((), (), s32[]{:S(2)}) async-start(), calls=%async_computation.6 | async-start | bytes 7864320 | tf_op jit(solution)/shard_map/all_gather | solution.py:1468
  141.9 3.0 copy-start
  142.0 349.8 %reduce-scatter.6.cloned.1.call-start = ((), (), s32[]{:S(2)}) async-start(), calls=%async_computation.4 | async-start | bytes 3604480 | tf_op jit(solution)/shard_map/reduce_scatter | solution.py:1503
  145.6 4.8 copy-start.1
  145.6 4.7 copy-start.3
  149.5 5.0 copy-start.4
  150.3 4.2 copy-start.13
  154.5 32.7 %copy-start.8 = (f32[2048,128]{1,0:T(8,128)}, f32[2048,128]{1,0:T(8,128)S(1)}, u32[]{:S(2)}) copy-start(f32[2048,128]{1,0:T(8,128)S(1)} %get-tuple-element.112.sin_ref) | copy-start | bytes 3145732
  154.5 32.7 %copy-start.9 = (f32[2048,128]{1,0:T(8,128)}, f32[2048,128]{1,0:T(8,128)S(1)}, u32[]{:S(2)}) copy-start(f32[2048,128]{1,0:T(8,128)S(1)} %get-tuple-element.113.cos_ref) | copy-start | bytes 3145732
  328.8 172.8 %reduce-scatter.4.cloned.1.call-start = ((), (), s32[]{:S(2)}) async-start(), calls=%async_computation.3 | async-start | bytes 7864320 | tf_op jit(solution)/shard_map/reduce_scatter | solution.py:1507
  390.1 221.8 %reduce-scatter.8.cloned.1.call-start = ((), (), s32[]{:S(2)}) async-start(), calls=%async_computation.5 | async-start | bytes 2621440 | tf_op jit(solution)/shard_map/reduce_scatter | solution.py:1527
  390.2 2.3 copy-start.2
  390.2 2.5 copy-start.5
  502.9 102.2 %collective-permute-start = (bf16[256,2048]{1,0:T(8,128)(2,1)S(1)}, bf16[256,2048]{1,0:T(8,128)(2,1)}, u32[]{:S(2)}, u32[]{:S(2)}) collective-permute-start(bf16[256,2048]{1,0:T(8,128)(2,1)S(1)} %slice_bitcast_fusion), channel_id=1, source_target_pairs={{0,5},{5,0},{1,4},{4,1},{2,7},{7,2},{3,6},{6,3},{8,13},{13,8},{9,1... | collective-permute-start | bytes 3145736 | tf_op jit(solution)/shard_map/ppermute | solution.py:1505
  607.7 6.6 %copy-start.11 = (f32[512,128]{1,0:T(8,128)S(1)}, f32[512,128]{1,0:T(8,128)}, u32[]{:S(2)}) copy-start(f32[512,128]{1,0:T(8,128)} %get-tuple-element.141) | copy-start | bytes 786436
  611.9 3.0 copy-start.10
  611.9 3.8 copy-start.12
  611.9 4.4 copy-start.7
  614.9 2.5 copy-start.6
Sparse Core Ops, SparseCore 0:
  142.1 114.8 all-gather.2
  328.9 56.4 reduce-scatter.5
  390.3 111.2 reduce-scatter.3
  503.7 42.1 reduce-scatter.7

commit v8 on v7

--- a/solution.py
+++ b/solution.py
@@ -1159,7 +1159,7 @@
     chips = (BOTH, X_BIT, Y_BIT, 0)
 
     def rows(amount, do):
-        size = 16 if amount % 64 else 64
+        size = amount if amount % 256 else 256
 
         @pl.loop(0, amount // size)
         def _(r):
@@ -1172,9 +1172,15 @@
             for i, source in enumerate(sources)
         ]
 
-    def far(n, j):
+    def far(step, j):
+        by_x = (step != 2) == (j % 2 == 0)
+        n = 0 if step == 0 else (1 if by_x else 2)
+        slot = (2, 0, 1)[step]
         return [
-            send(held[i][2].at[n, j], held[i][3].at[n, j], chip_send.at[i, n, j], chip_recv.at[i, n, j], other(chips[n]))
+            send(
+                held[i][2].at[n, j], held[i][3].at[slot, j], chip_send.at[i, step, j], chip_recv.at[i, step, j],
+                other(X_BIT if by_x else Y_BIT),
+            )
             for i in range(3)
         ]
 
@@ -1253,8 +1259,23 @@
                         total[j, at, :] = both
 
                 rows(total.shape[1], add)
-            if n < 3:
-                begin(far(n, j))
+            if n == 0:
+                begin(far(0, j))
+            if n == 2:
+                begin(far(1, j))
+
+    for j in order:
+        arrive(far(0, j))
+        n = 2 if j % 2 == 0 else 1
+        for i in range(3):
+            chip_ref, far_ref = held[i][2:4]
+
+            def add(at, n=n, j=j, chip_ref=chip_ref, far_ref=far_ref):
+                both = chip_ref[n, j, at, :].astype(F32) + far_ref[2, j, at, :].astype(F32)
+                chip_ref[n, j, at, :] = both.astype(BF16)
+
+            rows(chip_ref.shape[2], add)
+        begin(far(2, j))
 
     for bits in FAR_FIRST:
         wide(bits).start()
@@ -1267,14 +1288,14 @@
     pair, head = (0, 1, 2), (3,)
     line_step(1, head)
     for at_order, j in enumerate(order):
-        for n in range(3):
-            arrive(far(n, j))
+        arrive(far(1, j))
+        arrive(far(2, j))
         for i in range(3):
             total, far_ref = held[i][0], held[i][3]
 
             def add(at, j=j, total=total, far_ref=far_ref):
                 value = total[j, at, :]
-                for n in range(3):
+                for n in range(2):
                     value = value + far_ref[n, j, at, :].astype(F32)
                 total[j, at, :] = value
 

time: 630 us -> 626 us (level)
  no operation moved by 1% of the time
where the time goes in v8:
time: 626 us; the launch traced here: 621 us
  Pallas kernels  523 us (84%)
  other arithmetic  29.2 us (5%)
  waiting for transfers between devices  21.9 us (3%)
  local copies, waits for them, and re-layouts  15.8 us (3%)
  matrix products  14.8 us (2%)
  between operations  14.4 us (2%)
    pallas_call x3, Pallas kernels, vmem_call(): pl.pallas_call(kernel, out_shape=out_shape, in_specs=[vmem] * (len(arrays...  167 us
    pallas_call x1, Pallas kernels, start(): pl.pallas_call(functools.partial(start_kernel, parcel, chunks, units, pad...  131 us
    pallas_call x1, Pallas kernels, end(): pl.pallas_call(functools.partial(end_kernel, parcel, units, padded), out_...  80.6 us
    pallas_call x1, Pallas kernels, feed(): pl.pallas_call(functools.partial(feed_kernel, chunks), out_shape=[jax.Sha...  59.7 us
    pallas_call x1, Pallas kernels, branch_gather(): pl.pallas_call(functools.partial(branch_gather_kernel, chunks), out_shape...  42.7 us
    pallas_call x1, Pallas kernels, plane_gather(): pl.pallas_call(functools.partial(gather_kernel, chunks), out_shape=jax.Sh...  31.2 us
    dot_general x2, matrix products, contract(): lax.dot_general(left, right, (((left_dim,), (right_dim,)), ((), ())), pre...  14.3 us
    all_gather x1, waiting for transfers between devices, per_device(): both = lax.all_gather(both, 'f', axis=0)  14.3 us
  transfers between devices with their start and end apart: 5, of which 2 were waited for; matrix products, arithmetic and copies ran while one was open for 6% of the time, Pallas kernels for 54%

profile of v8, /device:TPU:10, one launch (start us, length us, event | category | flops | bytes accessed | tf_op | source)
XLA Modules:
  0.0 621.4 jit_solution(5288992637575452370)
XLA Ops:
  10.6 131.3 %shard_map.220 = (bf16[1024,2048]{1,0:T(8,128)(2,1)}, bf16[2048,256]{1,0:T(8,128)(2,1)}, bf16[8,4,16,128]{3,2,1,0:T(8,128)(2,1)}, bf16[6,512,256]{2,1,0:T(8,128)...) custom-call(f32[512,128]{1,0:T(8,128)} %down_ref.1, ...), custom_call_target="tpu_custom_call" | custom-call | bytes 251658240 | tf_op jit(solution)/shard_map/pallas_call | solution.py:1057
  145.2 3.9 multiply_reduce_fusion.3
  150.3 3.7 multiply_sine_fusion
  155.5 31.2 %shard_map.221.rows_in = bf16[2048,1536]{1,0:T(8,128)(2,1)} custom-call(bf16[256,1536]{1,0:T(8,128)(2,1)} %pad_maximum_fusion.in_ref), custom_call_target="tpu_custom_call" | custom-call | bytes 167772160 | tf_op jit(solution)/shard_map/pallas_call | solution.py:158
  186.8 1.3 copy.84
  188.2 51.3 %shard_map.222 = (f32[256,2048]{1,0:T(8,128)}, bf16[2048,512]{1,0:T(8,128)(2,1)}, f32[2048,2]{1,0:T(8,128)}, bf16[2048,512]{1,0:T(8,128)(2,1)}) custom-call(bf16[6,512,256]{2,1,0:T(8,128)(2,1)} %get-tuple-element.53.head_ref, bf16[768,2048]{1,0:T(8,128)(2,1)} %bitcast.111, f32[2048,128]{1,0:T(8,128)} %copy-done.9, f32[2048,128]{1,0:T(8,128)} %copy-done.8, ...), custom_call_target="tpu_custom_call" | custom-call | flops 7516192768 | bytes 167772160 | tf_op jit(solution)/shard_map/pallas_call | solution.py:297
  239.5 1.9 multiply_reduce_fusion.2
  242.7 14.3 %all-gather.3.cloned.1.call-done = bf16[32,64,1536]{2,1,0:T(8,128)(2,1)} async-done(((bf16[8,64,1536]{2,1,0:T(8,128)(2,1)}), bf16[32,64,1536]{2,1,0:T(8,128)(2,1)}) %all-gather.3.cloned.1.call-update) | async-done | bytes 6291472 | tf_op jit(solution)/shard_map/all_gather | solution.py:1489
  256.9 59.7 %shard_map.223 = (bf16[2048,2048]{1,0:T(8,128)(2,1)}, bf16[2048,768]{1,0:T(8,128)(2,1)}, bf16[2048,1536]{1,0:T(8,128)(2,1)}, f32[256,2048]{1,0:T(8,128)}, bf16[3,256,2048]{2,1,0:T(8,128)(2,1)}) custom-call(bf16[256,2048]{1,0:T(8,128)(2,1)} %multiply_convert_fusion.in_ref, bf16[2048,2048]{1,0:T(8,128)(2,1)} %get-tuple-element.59.g_ref, ...), custom_call_target="tpu_custom_call" | custom-call | flops 19327352832 | bytes 167772160 | tf_op jit(solution)/shard_map/pallas_call | solution.py:595
  316.7 10.4 %fusion.21 = bf16[768,2048]{1,0:T(8,128)(2,1)S(1)} fusion(bf16[2048,768]{1,0:T(8,128)(2,1)} %get-tuple-element.64, bf16[2048,2048]{1,0:T(8,128)(2,1)} %get-tuple-element.59.g_ref), kind=kOutput, calls=%fused_computation.78 | convolution fusion | flops 6442450944 | bytes 14680064 | tf_op jit(solution)/shard_map/dot_general | solution.py:21
  327.1 1.8 slice.91
  328.9 61.3 %shard_map.224 = (f32[256,2048]{1,0:T(8,128)}, bf16[2048,1536]{1,0:T(8,128)(2,1)}, bf16[2,256,2048]{2,1,0:T(8,128)(2,1)}) custom-call(bf16[2048,1536]{1,0:T(8,128)(2,1)} %get-tuple-element.66.left_in, bf16[2048,1536]{1,0:T(8,128)(2,1)} %bitcast.110, bf16[2048,2048]{1,0:T(8,128)(2,1)} %get-tuple-element.67.side_in, ...), custom_call_target="tpu_custom_call" | custom-call | flops 25769803776 | bytes 167772160 | tf_op jit(solution)/shard_map/pallas_call | solution.py:297
  390.3 2.3 multiply_reduce_fusion
  392.7 2.3 fusion.19
  395.0 42.7 %shard_map.225 = (bf16[2048,2048]{1,0:T(8,128)(2,1)}, bf16[512,2048]{1,0:T(8,128)(2,1)}) custom-call(bf16[256,2048]{1,0:T(8,128)(2,1)} %get-tuple-element.96.in_ref, bf16[2048,512]{1,0:T(8,128)(2,1)} %get-tuple-element.72.att_ref), custom_call_target="tpu_custom_call" | custom-call | flops 4294967296 | bytes 167772160 | tf_op jit(solution)/shard_map/pallas_call | solution.py:757
  437.7 54.1 %shard_map.226 = (f32[256,1280]{1,0:T(8,128)}, bf16[2048,512]{1,0:T(8,128)(2,1)}, bf16[1024,512]{1,0:T(8,128)(2,1)}, bf16[4,128,2048]{2,1,0:T(8,128)(2,1)}) custom-call(bf16[6,512,256]{2,1,0:T(8,128)(2,1)} %get-tuple-element.53.head_ref, bf16[768,2048]{1,0:T(8,128)(2,1)} %bitcast.112, f32[2048,128]{1,0:T(8,128)} %copy-done.9, f32[2048,128]{1,0:T(8,128)} %copy-done.8, ...), custom_call_target="tpu_custom_call" | custom-call | flops 9126805504 | bytes 167772160 | tf_op jit(solution)/shard_map/pallas_call | solution.py:297
  491.8 2.4 bitcast_convert_fusion
  494.2 7.5 %reduce-scatter.4.cloned.1.call-done = bf16[1,8,64,1536]{3,2,1,0:T(8,128)(2,1)} async-done(((bf16[4,8,64,1536]{3,2,1,0:T(8,128)(2,1)}), bf16[1,8,64,1536]{3,2,1,0:T(8,128)(2,1)}) %reduce-scatter.4.cloned.1.call-update) | async-done | bytes 1572880 | tf_op jit(solution)/shard_map/reduce_scatter | solution.py:1528
  501.7 1.3 slice_bitcast_fusion
  503.0 1.5 collective-permute-start
  506.8 11.4 %shard_map.227 = (bf16[1024,2048]{1,0:T(8,128)(2,1)}, bf16[2048,256]{1,0:T(8,128)(2,1)}, bf16[256,2048]{1,0:T(8,128)(2,1)}, f32[1,1024]{1,0:T(1,128)}, f32[1,2048]{1,0:T(1,128)}) custom-call(f32[256,1280]{1,0:T(8,128)} %get-tuple-element.76.back_ref, f32[256,1024]{1,0:T(8,128)} %copy-done.4, f32[256,1]{1,0:T(8,128)} %copy.77.rms_lat_ref, ...), custom_call_target="tpu_custom_call" | custom-call | flops 2684354560 | bytes 16777216 | tf_op jit(solution)/shard_map/pallas_call | solution.py:1125
  520.6 80.6 %shard_map.228 = (f32[512,128]{1,0:T(8,128)}, f32[64,256]{1,0:T(8,128)}, f32[16,128]{1,0:T(8,128)}, f32[64,5632]{1,0:T(8,128)}, f32[64,5632]{1,0:T(8,128)}, /*index=5*/f32[512,256]{1,0:T(8,128)}) custom-call(bf16[1024,2048]{1,0:T(8,128)(2,1)} %get-tuple-element.77.down_ref, bf16[2048,256]{1,0:T(8,128)(2,1)} %get-tuple-element.78.kv_ref, ...), custom_call_target="tpu_custom_call" | custom-call | bytes 251658240 | tf_op jit(solution)/shard_map/pallas_call | solution.py:1365
  603.8 4.3 fusion.4
  608.1 2.3 bitcast_convert_fusion.1
  (97 shorter events, 22.4 us)
Async XLA Ops:
  7.2 249.8 %all-gather.3.cloned.1.call-start = ((), (), s32[]{:S(2)}) async-start(), calls=%async_computation.6 | async-start | bytes 7864320 | tf_op jit(solution)/shard_map/all_gather | solution.py:1489
  141.9 2.6 copy-start
  142.0 349.8 %reduce-scatter.6.cloned.1.call-start = ((), (), s32[]{:S(2)}) async-start(), calls=%async_computation.4 | async-start | bytes 3604480 | tf_op jit(solution)/shard_map/reduce_scatter | solution.py:1524
  145.1 4.8 copy-start.1
  145.2 4.7 copy-start.3
  149.1 5.0 copy-start.4
  149.9 4.2 copy-start.13
  154.0 32.7 %copy-start.8 = (f32[2048,128]{1,0:T(8,128)}, f32[2048,128]{1,0:T(8,128)S(1)}, u32[]{:S(2)}) copy-start(f32[2048,128]{1,0:T(8,128)S(1)} %get-tuple-element.112.sin_ref) | copy-start | bytes 3145732
  154.1 32.7 %copy-start.9 = (f32[2048,128]{1,0:T(8,128)}, f32[2048,128]{1,0:T(8,128)S(1)}, u32[]{:S(2)}) copy-start(f32[2048,128]{1,0:T(8,128)S(1)} %get-tuple-element.113.cos_ref) | copy-start | bytes 3145732
  328.8 172.8 %reduce-scatter.4.cloned.1.call-start = ((), (), s32[]{:S(2)}) async-start(), calls=%async_computation.3 | async-start | bytes 7864320 | tf_op jit(solution)/shard_map/reduce_scatter | solution.py:1528
  390.2 217.9 %reduce-scatter.8.cloned.1.call-start = ((), (), s32[]{:S(2)}) async-start(), calls=%async_computation.5 | async-start | bytes 2621440 | tf_op jit(solution)/shard_map/reduce_scatter | solution.py:1548
  390.2 2.3 copy-start.2
  390.2 2.5 copy-start.5
  503.0 98.3 %collective-permute-start = (bf16[256,2048]{1,0:T(8,128)(2,1)S(1)}, bf16[256,2048]{1,0:T(8,128)(2,1)}, u32[]{:S(2)}, u32[]{:S(2)}) collective-permute-start(bf16[256,2048]{1,0:T(8,128)(2,1)S(1)} %slice_bitcast_fusion), channel_id=1, source_target_pairs={{0,5},{5,0},{1,4},{4,1},{2,7},{7,2},{3,6},{6,3},{8,13},{13,8},{9,1... | collective-permute-start | bytes 3145736 | tf_op jit(solution)/shard_map/ppermute | solution.py:1526
  603.8 6.6 %copy-start.11 = (f32[512,128]{1,0:T(8,128)S(1)}, f32[512,128]{1,0:T(8,128)}, u32[]{:S(2)}) copy-start(f32[512,128]{1,0:T(8,128)} %get-tuple-element.141) | copy-start | bytes 786436
  608.0 3.0 copy-start.10
  608.0 3.8 copy-start.12
  608.0 4.4 copy-start.7
  611.0 2.5 copy-start.6
Sparse Core Ops, SparseCore 0:
  142.1 114.8 all-gather.2
  329.0 56.4 reduce-scatter.5
  390.3 111.2 reduce-scatter.3
  503.8 42.1 reduce-scatter.7

commit v9 on v8

--- a/solution.py
+++ b/solution.py
@@ -1547,6 +1547,8 @@
     out_grad = after(out_grad, both_grad, down_grad, gain_one_part)
     out_proj_grad = lax.psum_scatter(out_grad, "f", scatter_dimension=0).astype(F32)
 
+    nearer = middle + result + arrived[0].astype(F32) + arrived[1].astype(F32)
+    down_part, nearer = lax.optimization_barrier((down_part, nearer))
     down_part = parcel.down_to(down_part)
 
     def gain_rows_of(part):
@@ -1573,7 +1575,7 @@
     attn_gain_grad = small_sum[lat_lines, :gain_rows]
     mlp_gain_grad = small_sum[lat_lines + 1, :gain_rows]
     farthest = after(farthest, small_sum).astype(F32)
-    block_output = (middle + result + arrived[0].astype(F32) + arrived[1].astype(F32) + farthest).astype(BF16)
+    block_output = (nearer + farthest).astype(BF16)
     return (
         block_output,
         input_grad,

time: 626 us -> 624 us (level)
  no operation moved by 1% of the time
where the time goes in v9:
time: 624 us; the launch traced here: 620 us
  Pallas kernels  523 us (84%)
  other arithmetic  31 us (5%)
  waiting for transfers between devices  18.3 us (3%)
  local copies, waits for them, and re-layouts  15.8 us (3%)
  matrix products  14.8 us (2%)
  between operations  14.4 us (2%)
    pallas_call x3, Pallas kernels, vmem_call(): pl.pallas_call(kernel, out_shape=out_shape, in_specs=[vmem] * (len(arrays...  166 us
    pallas_call x1, Pallas kernels, start(): pl.pallas_call(functools.partial(start_kernel, parcel, chunks, units, pad...  131 us
    pallas_call x1, Pallas kernels, end(): pl.pallas_call(functools.partial(end_kernel, parcel, units, padded), out_...  80.4 us
    pallas_call x1, Pallas kernels, feed(): pl.pallas_call(functools.partial(feed_kernel, chunks), out_shape=[jax.Sha...  59.6 us
    pallas_call x1, Pallas kernels, branch_gather(): pl.pallas_call(functools.partial(branch_gather_kernel, chunks), out_shape...  42.8 us
    pallas_call x1, Pallas kernels, plane_gather(): pl.pallas_call(functools.partial(gather_kernel, chunks), out_shape=jax.Sh...  31.2 us
    dot_general x2, matrix products, contract(): lax.dot_general(left, right, (((left_dim,), (right_dim,)), ((), ())), pre...  14.3 us
    all_gather x1, waiting for transfers between devices, per_device(): both = lax.all_gather(both, 'f', axis=0)  13.9 us
  transfers between devices with their start and end apart: 5, of which 2 were waited for; matrix products, arithmetic and copies ran while one was open for 6% of the time, Pallas kernels for 54%

profile of v9, /device:TPU:10, one launch (start us, length us, event | category | flops | bytes accessed | tf_op | source)
XLA Modules:
  0.0 619.5 jit_solution(12070241454185585230)
XLA Ops:
  10.6 131.3 %shard_map.220 = (bf16[1024,2048]{1,0:T(8,128)(2,1)}, bf16[2048,256]{1,0:T(8,128)(2,1)}, bf16[8,4,16,128]{3,2,1,0:T(8,128)(2,1)}, bf16[6,512,256]{2,1,0:T(8,128)...) custom-call(f32[512,128]{1,0:T(8,128)} %down_ref.1, ...), custom_call_target="tpu_custom_call" | custom-call | bytes 251658240 | tf_op jit(solution)/shard_map/pallas_call | solution.py:1057
  145.5 4.0 multiply_reduce_fusion.3
  150.7 3.7 multiply_sine_fusion
  155.9 31.2 %shard_map.221.rows_in = bf16[2048,1536]{1,0:T(8,128)(2,1)} custom-call(bf16[256,1536]{1,0:T(8,128)(2,1)} %pad_maximum_fusion.in_ref), custom_call_target="tpu_custom_call" | custom-call | bytes 167772160 | tf_op jit(solution)/shard_map/pallas_call | solution.py:158
  187.2 1.3 copy.84
  188.6 51.3 %shard_map.222 = (f32[256,2048]{1,0:T(8,128)}, bf16[2048,512]{1,0:T(8,128)(2,1)}, f32[2048,2]{1,0:T(8,128)}, bf16[2048,512]{1,0:T(8,128)(2,1)}) custom-call(bf16[6,512,256]{2,1,0:T(8,128)(2,1)} %get-tuple-element.55.head_ref, bf16[768,2048]{1,0:T(8,128)(2,1)} %bitcast.111, f32[2048,128]{1,0:T(8,128)} %copy-done.10, f32[2048,128]{1,0:T(8,128)} %copy-done.9, ...), custom_call_target="tpu_custom_call" | custom-call | flops 7516192768 | bytes 167772160 | tf_op jit(solution)/shard_map/pallas_call | solution.py:297
  239.9 1.9 multiply_reduce_fusion.2
  243.0 13.9 %all-gather.3.cloned.1.call-done = bf16[32,64,1536]{2,1,0:T(8,128)(2,1)} async-done(((bf16[8,64,1536]{2,1,0:T(8,128)(2,1)}), bf16[32,64,1536]{2,1,0:T(8,128)(2,1)}) %all-gather.3.cloned.1.call-update) | async-done | bytes 6291472 | tf_op jit(solution)/shard_map/all_gather | solution.py:1489
  256.9 59.6 %shard_map.223 = (bf16[2048,2048]{1,0:T(8,128)(2,1)}, bf16[2048,768]{1,0:T(8,128)(2,1)}, bf16[2048,1536]{1,0:T(8,128)(2,1)}, f32[256,2048]{1,0:T(8,128)}, bf16[3,256,2048]{2,1,0:T(8,128)(2,1)}) custom-call(bf16[256,2048]{1,0:T(8,128)(2,1)} %multiply_convert_fusion.in_ref, bf16[2048,2048]{1,0:T(8,128)(2,1)} %get-tuple-element.62.g_ref, ...), custom_call_target="tpu_custom_call" | custom-call | flops 19327352832 | bytes 167772160 | tf_op jit(solution)/shard_map/pallas_call | solution.py:595
  316.6 10.4 %fusion.19 = bf16[768,2048]{1,0:T(8,128)(2,1)S(1)} fusion(bf16[2048,768]{1,0:T(8,128)(2,1)} %get-tuple-element.66, bf16[2048,2048]{1,0:T(8,128)(2,1)} %get-tuple-element.62.g_ref), kind=kOutput, calls=%fused_computation.77 | convolution fusion | flops 6442450944 | bytes 14680064 | tf_op jit(solution)/shard_map/dot_general | solution.py:21
  326.9 1.8 slice.91
  328.9 61.3 %shard_map.224 = (f32[256,2048]{1,0:T(8,128)}, bf16[2048,1536]{1,0:T(8,128)(2,1)}, bf16[2,256,2048]{2,1,0:T(8,128)(2,1)}) custom-call(bf16[2048,1536]{1,0:T(8,128)(2,1)} %get-tuple-element.68.left_in, bf16[2048,1536]{1,0:T(8,128)(2,1)} %bitcast.110, bf16[2048,2048]{1,0:T(8,128)(2,1)} %get-tuple-element.69.side_in, ...), custom_call_target="tpu_custom_call" | custom-call | flops 25769803776 | bytes 167772160 | tf_op jit(solution)/shard_map/pallas_call | solution.py:297
  390.2 5.4 multiply_reduce_fusion
  395.6 2.7 fusion.17
  398.4 42.8 %shard_map.225 = (bf16[2048,2048]{1,0:T(8,128)(2,1)}, bf16[512,2048]{1,0:T(8,128)(2,1)}) custom-call(bf16[256,2048]{1,0:T(8,128)(2,1)} %get-tuple-element.100.in_ref, bf16[2048,512]{1,0:T(8,128)(2,1)} %get-tuple-element.72.att_ref), custom_call_target="tpu_custom_call" | custom-call | flops 4294967296 | bytes 167772160 | tf_op jit(solution)/shard_map/pallas_call | solution.py:757
  441.2 53.8 %shard_map.226 = (f32[256,1280]{1,0:T(8,128)}, bf16[2048,512]{1,0:T(8,128)(2,1)}, bf16[1024,512]{1,0:T(8,128)(2,1)}, bf16[4,128,2048]{2,1,0:T(8,128)(2,1)}) custom-call(bf16[6,512,256]{2,1,0:T(8,128)(2,1)} %get-tuple-element.55.head_ref, bf16[768,2048]{1,0:T(8,128)(2,1)} %bitcast.112, f32[2048,128]{1,0:T(8,128)} %copy-done.10, f32[2048,128]{1,0:T(8,128)} %copy-done.9, ...), custom_call_target="tpu_custom_call" | custom-call | flops 9126805504 | bytes 167772160 | tf_op jit(solution)/shard_map/pallas_call | solution.py:297
  495.0 2.4 bitcast_convert_fusion
  497.4 4.2 reduce-scatter.4.cloned.1.call-done
  501.6 1.3 slice_bitcast_fusion
  503.0 1.5 collective-permute-start
  506.8 11.4 %shard_map.227 = (bf16[1024,2048]{1,0:T(8,128)(2,1)}, bf16[2048,256]{1,0:T(8,128)(2,1)}, bf16[256,2048]{1,0:T(8,128)(2,1)}, f32[1,1024]{1,0:T(1,128)}, f32[1,2048]{1,0:T(1,128)}) custom-call(f32[256,1280]{1,0:T(8,128)} %get-tuple-element.76.back_ref, f32[256,1024]{1,0:T(8,128)} %copy-done.5, f32[256,1]{1,0:T(8,128)} %copy.77.rms_lat_ref, ...), custom_call_target="tpu_custom_call" | custom-call | flops 2684354560 | bytes 16777216 | tf_op jit(solution)/shard_map/pallas_call | solution.py:1125
  520.6 80.4 %shard_map.228 = (f32[512,128]{1,0:T(8,128)}, f32[64,256]{1,0:T(8,128)}, f32[16,128]{1,0:T(8,128)}, f32[64,5632]{1,0:T(8,128)}, f32[64,5632]{1,0:T(8,128)}, /*index=5*/f32[512,256]{1,0:T(8,128)}) custom-call(bf16[1024,2048]{1,0:T(8,128)(2,1)} %get-tuple-element.81.down_ref, bf16[2048,256]{1,0:T(8,128)(2,1)} %get-tuple-element.82.kv_ref, ...), custom_call_target="tpu_custom_call" | custom-call | bytes 251658240 | tf_op jit(solution)/shard_map/pallas_call | solution.py:1365
  603.6 2.5 add_convert_fusion
  606.1 2.3 bitcast_convert_fusion.1
  (99 shorter events, 22.6 us)
Async XLA Ops:
  7.2 249.8 %all-gather.3.cloned.1.call-start = ((), (), s32[]{:S(2)}) async-start(), calls=%async_computation.6 | async-start | bytes 7864320 | tf_op jit(solution)/shard_map/all_gather | solution.py:1489
  141.9 2.9 copy-start
  142.0 353.0 %reduce-scatter.6.cloned.1.call-start = ((), (), s32[]{:S(2)}) async-start(), calls=%async_computation.4 | async-start | bytes 3604480 | tf_op jit(solution)/shard_map/reduce_scatter | solution.py:1524
  145.5 4.8 copy-start.1
  145.5 4.8 copy-start.4
  149.5 5.0 copy-start.5
  150.2 4.2 copy-start.14
  154.4 32.7 %copy-start.9 = (f32[2048,128]{1,0:T(8,128)}, f32[2048,128]{1,0:T(8,128)S(1)}, u32[]{:S(2)}) copy-start(f32[2048,128]{1,0:T(8,128)S(1)} %get-tuple-element.117.sin_ref) | copy-start | bytes 3145732
  154.4 32.7 %copy-start.10 = (f32[2048,128]{1,0:T(8,128)}, f32[2048,128]{1,0:T(8,128)S(1)}, u32[]{:S(2)}) copy-start(f32[2048,128]{1,0:T(8,128)S(1)} %get-tuple-element.118.cos_ref) | copy-start | bytes 3145732
  328.8 172.8 %reduce-scatter.4.cloned.1.call-start = ((), (), s32[]{:S(2)}) async-start(), calls=%async_computation.3 | async-start | bytes 7864320 | tf_op jit(solution)/shard_map/reduce_scatter | solution.py:1528
  390.2 216.0 %reduce-scatter.8.cloned.1.call-start = ((), (), s32[]{:S(2)}) async-start(), calls=%async_computation.5 | async-start | bytes 2621440 | tf_op jit(solution)/shard_map/reduce_scatter | solution.py:1548
  390.2 5.4 copy-start.3
  390.2 5.4 copy-start.6
  503.0 98.1 %collective-permute-start = (bf16[256,2048]{1,0:T(8,128)(2,1)S(1)}, bf16[256,2048]{1,0:T(8,128)(2,1)}, u32[]{:S(2)}, u32[]{:S(2)}) collective-permute-start(bf16[256,2048]{1,0:T(8,128)(2,1)S(1)} %slice_bitcast_fusion), channel_id=1, source_target_pairs={{0,5},{5,0},{1,4},{4,1},{2,7},{7,2},{3,6},{6,3},{8,13},{13,8},{9,1... | collective-permute-start | bytes 3145736 | tf_op jit(solution)/shard_map/ppermute | solution.py:1526
  520.6 83.0 %copy-start.2 = (f32[256,2048]{1,0:T(8,128)S(1)}, f32[256,2048]{1,0:T(8,128)}, u32[]{:S(2)}) copy-start(f32[256,2048]{1,0:T(8,128)} %get-tuple-element.80) | copy-start | bytes 6291460
  603.6 4.8 copy-start.12
  606.1 3.0 copy-start.11
  606.1 3.8 copy-start.13
  606.1 4.4 copy-start.8
  609.1 2.5 copy-start.7
Sparse Core Ops, SparseCore 0:
  142.1 114.8 all-gather.2
  328.9 56.4 reduce-scatter.5
  390.3 111.2 reduce-scatter.3
  503.8 42.1 reduce-scatter.7
